TPU v7x, 32 devices: a whole 2x2x4 slice. The times are simulated.
32 devices in a mesh: ctx: 16 (over z, y, x), wt: 2 (over core).
Axes of the slice: x: 2, y: 2, z: 4, core: 2. Of those that a mesh axis runs over, the one named last changes fastest.
Arguments:
- inputs: bfloat16 [16, 256, 4, 768], P('ctx'), may hold values from -6 to 6
- cotangent: bfloat16 [16, 256, 4, 768], P('ctx'), may hold values from -6 to 6
- lengths: int32 [4], replicated, may hold values from 1024 to 4096, as said below
- block_pairs: int32 [16], replicated, may hold values from 0 to 15, each once
- routes: int32 [16, 256, 4, 2], P('ctx'), may hold values from 0 to 15, all different within a row; in each aligned block of 1024 rows (0 to 1023, 1024 to 2047, ..., all dimensions but the last counted through in order) at most 160 rows name the same one
- attn_gain: float32 [768], replicated, may hold values from 0.25 to 1.75
- query_weight: bfloat16 [768, 768], P(None, 'wt'), may hold values from -0.21875 to 0.21875
- key_weight: bfloat16 [768, 768], P(None, 'wt'), may hold values from -0.21875 to 0.21875
- value_weight: bfloat16 [768, 768], P(None, 'wt'), may hold values from -0.21875 to 0.21875
- out_weight: bfloat16 [768, 768], P('wt'), may hold values from -1.75 to 1.75
- ffn_gain: float32 [768], replicated, may hold values from 0.25 to 1.75
- router_weight: bfloat16 [768, 16], replicated, may hold values from -0.15625 to 0.15625
- expert_gate: bfloat16 [16, 768, 2048], P(None, None, 'wt'), may hold values from -0.21875 to 0.21875
- expert_up: bfloat16 [16, 768, 2048], P(None, None, 'wt'), may hold values from -0.21875 to 0.21875
- expert_down: bfloat16 [16, 2048, 768], P(None, 'wt'), may hold values from -0.125 to 0.125
- dense_gate: bfloat16 [768, 2048], P(None, 'wt'), may hold values from -0.21875 to 0.21875
- dense_up: bfloat16 [768, 2048], P(None, 'wt'), may hold values from -0.21875 to 0.21875
- dense_down: bfloat16 [2048, 768], P('wt'), may hold values from -0.125 to 0.125
Outputs:
- output: bfloat16 [16, 256, 4, 768], P('ctx')
- grad_inputs: bfloat16 [16, 256, 4, 768], P('ctx')
- grad_attn_gain: float32 [768], P('ctx')
- grad_query: float32 [768, 768], P('ctx', 'wt')
- grad_key: float32 [768, 768], P('ctx', 'wt')
- grad_value: float32 [768, 768], P('ctx', 'wt')
- grad_out: float32 [768, 768], P('wt', 'ctx')
- grad_ffn_gain: float32 [768], P('ctx')
- grad_router: float32 [768, 16], P('ctx')
- grad_expert_gate: float32 [16, 768, 2048], P(None, 'ctx', 'wt')
- grad_expert_up: float32 [16, 768, 2048], P(None, 'ctx', 'wt')
- grad_expert_down: float32 [16, 2048, 768], P(None, 'wt', 'ctx')
- grad_dense_gate: float32 [768, 2048], P('ctx', 'wt')
- grad_dense_up: float32 [768, 2048], P('ctx', 'wt')
- grad_dense_down: float32 [2048, 768], P('wt', 'ctx')
Inputs may be any that keep to these rules, and one draw needn't show every extreme that they name: `lengths`: one slot chosen by the seed is 4096 tokens long and another one 4096 // 4. `block_pairs`: every pair number once. `routes`: two different experts a token; among the 1024 tokens of one ctx index no expert is named more than 160 times, a bound that some block reaches.
All inputs are finite; a program needn't handle non-finite values.
Results may differ from a plain program's by a relative error of at most 0.015.
Values may be sent and summed in bfloat16 or wider, within the bound.
No kernel may reach another device: no remote copies, remote signals or barrier semaphores. Data moves between devices by JAX's collectives and lax.ppermute only.
A program may use at most 448 MiB of HBM per device.

v0:
```python
import math

import jax
import jax.numpy as jnp
from jax import lax
from jax.sharding import PartitionSpec as P

HEAD_DIM = 64
CAPACITY = 160


EPS = 1e-06
THETA = 10000.0


def place_table(block_pairs, pair_rows):
    members = block_pairs.shape[0]
    half = pair_rows // 2
    within = jnp.arange(pair_rows, dtype=jnp.int32)
    which = jnp.where(
        within[None, :] < half, block_pairs[:, None], 2 * members - 1 - block_pairs[:, None]
    )
    return (which * half + within[None, :] % half).reshape(-1)


def turn_tables(places, width):
    half = width // 2
    freqs = THETA ** (-jnp.arange(half, dtype=jnp.float32) / half)
    angles = places.astype(jnp.float32)[:, None] * freqs[None, :]
    cosine = jnp.concatenate([jnp.cos(angles), jnp.cos(angles)], axis=-1)[:, None, None, :]
    sine = jnp.concatenate([jnp.sin(angles), jnp.sin(angles)], axis=-1)[:, None, None, :]
    return (cosine, sine)


def rotate_fwd(values, cosine, sine):
    half = values.shape[-1] // 2
    turned = jnp.concatenate([-values[..., half:], values[..., :half]], axis=-1)
    return values * cosine + turned * sine


def rotate_back(grads, cosine, sine):
    half = grads.shape[-1] // 2
    scaled = grads * sine
    return grads * cosine + jnp.concatenate([scaled[..., half:], -scaled[..., :half]], axis=-1)


def norm_fwd(values, gain):
    scale = lax.rsqrt(jnp.mean(values * values, axis=-1, keepdims=True) + EPS)
    return (values * scale * gain, scale)


def norm_back(values, scale, gain, upstream):
    unit = values * scale
    pulled = upstream * gain
    result = scale * (pulled - unit * jnp.mean(pulled * unit, axis=-1, keepdims=True))
    return (result, jnp.sum(upstream * unit, axis=0))


def swiglu(gate_part, up_part):
    return jax.nn.silu(gate_part) * up_part


def per_device(
    inputs,
    cotangent,
    lengths,
    block_pairs,
    routes,
    attn_gain,
    query_weight,
    key_weight,
    value_weight,
    out_weight,
    ffn_gain,
    router_weight,
    expert_gate,
    expert_up,
    expert_down,
    dense_gate,
    dense_up,
    dense_down,
):
    pair_rows, seqs_here, width = (inputs.shape[1], inputs.shape[2], inputs.shape[3])
    heads_here = query_weight.shape[1] // HEAD_DIM
    local_width = heads_here * HEAD_DIM
    experts = expert_gate.shape[0]
    members = lax.axis_size("ctx")
    whole_rows = members * pair_rows
    key_block = min(512, whole_rows)
    factor = HEAD_DIM ** (-0.5)
    bf_type = jnp.bfloat16
    fl_type = jnp.float32
    tokens = inputs.reshape(-1, width).astype(fl_type)
    places = place_table(block_pairs, pair_rows)
    my_places = lax.dynamic_slice_in_dim(places, lax.axis_index("ctx") * pair_rows, pair_rows)
    valid = (my_places[:, None] < lengths[None, :]).reshape(-1, 1)
    masked_cot = jnp.where(valid, cotangent.reshape(-1, width), jnp.zeros((), bf_type))
    cot_float = masked_cot.astype(fl_type)
    normed_one, scale_one = norm_fwd(tokens, attn_gain)
    first = normed_one.astype(bf_type)
    query_raw = jnp.dot(first, query_weight, preferred_element_type=fl_type)
    key_raw = jnp.dot(first, key_weight, preferred_element_type=fl_type)
    value_raw = jnp.dot(first, value_weight, preferred_element_type=fl_type)
    cosine, sine = turn_tables(my_places, HEAD_DIM)
    head_shape = (pair_rows, seqs_here, heads_here, HEAD_DIM)
    queries = rotate_fwd(query_raw.reshape(head_shape), cosine, sine).astype(bf_type)
    keys_local = (
        rotate_fwd(key_raw.reshape(head_shape), cosine, sine).astype(bf_type).reshape(pair_rows, -1)
    )
    values_local = value_raw.astype(bf_type).reshape(pair_rows, -1)
    all_keys, all_values = (
        lax.all_gather(keys_local, "ctx", axis=0, tiled=True),
        lax.all_gather(values_local, "ctx", axis=0, tiled=True),
    )

    def key_tiles(key_rows, value_rows, place_rows, tile):
        pieces = key_rows.shape[0] // tile
        shape = (pieces, tile, seqs_here, heads_here, HEAD_DIM)
        return (
            key_rows.reshape(shape),
            value_rows.reshape(shape),
            place_rows.reshape(pieces, tile),
        )

    def scores_of(key_tile, tile_places):
        raw = (
            jnp.einsum("jshd,kshd->shjk", queries, key_tile, preferred_element_type=fl_type)
            * factor
        )
        allowed = (tile_places[None, None, :] <= my_places[None, :, None]) & (
            tile_places[None, None, :] < lengths[:, None, None]
        )
        return jnp.where(allowed[:, None], raw, -1e30)

    tiles = key_tiles(all_keys, all_values, places, key_block)
    stat_shape = (seqs_here, heads_here, pair_rows)

    def stat_step(carry, tile):
        top, total = carry
        scores = scores_of(tile[0], tile[2])
        new_top = jnp.maximum(top, jnp.max(scores, axis=-1))
        total = total * jnp.exp(top - new_top) + jnp.sum(
            jnp.exp(scores - new_top[..., None]), axis=-1
        )
        return ((new_top, total), None)

    (row_top, row_total), unused = lax.scan(
        stat_step, (jnp.full(stat_shape, -1e30, fl_type), jnp.zeros(stat_shape, fl_type)), tiles
    )

    def probs_of(scores):
        return jnp.exp(scores - row_top[..., None]) / row_total[..., None]

    def out_step(carry, tile):
        weights = probs_of(scores_of(tile[0], tile[2])).astype(bf_type)
        return (
            carry + jnp.einsum("shjk,kshd->jshd", weights, tile[1], preferred_element_type=fl_type),
            None,
        )

    mixed, unused = lax.scan(out_step, jnp.zeros(head_shape, fl_type), tiles)
    mixed = mixed.astype(bf_type).reshape(-1, local_width)
    partial_mix = jnp.dot(mixed, out_weight, preferred_element_type=fl_type)
    state = tokens + lax.psum(partial_mix, "wt")
    normed_two, scale_two = norm_fwd(state, ffn_gain)
    second = normed_two.astype(bf_type)
    logits = jnp.dot(second, router_weight, preferred_element_type=fl_type)
    chosen = routes.reshape(-1, 2)
    picks = chosen[:, :, None] == jnp.arange(experts, dtype=jnp.int32)[None, None, :]
    selected = jnp.sum(jnp.where(picks, logits[:, None, :], 0.0), axis=-1)
    weights_two = jnp.exp(selected - jnp.max(selected, axis=-1, keepdims=True))
    gates = weights_two / jnp.sum(weights_two, axis=-1, keepdims=True)
    flat = chosen.reshape(-1)
    marks = (flat[:, None] == jnp.arange(experts, dtype=jnp.int32)[None, :]).astype(jnp.int32)
    order = jnp.sum(
        (jnp.cumsum(marks, axis=0, dtype=jnp.int32) - 1) * marks, axis=1, dtype=jnp.int32
    )
    target = flat * CAPACITY + order
    pair_target = target.reshape(-1, 2)
    slot_ids = jnp.arange(experts * CAPACITY, dtype=jnp.int32)[:, None]
    spread = ((slot_ids == pair_target[None, :, 0]) | (slot_ids == pair_target[None, :, 1])).astype(
        bf_type
    )
    routed_flat = jnp.dot(spread, second, preferred_element_type=fl_type).astype(bf_type)
    routed = routed_flat.reshape(experts, CAPACITY, width)
    gate_weights, up_weights, down_weights = (expert_gate, expert_up, expert_down)
    gate_part = jnp.einsum("ecd,edf->ecf", routed, gate_weights, preferred_element_type=fl_type)
    up_part = jnp.einsum("ecd,edf->ecf", routed, up_weights, preferred_element_type=fl_type)
    expert_hidden = swiglu(gate_part, up_part).astype(bf_type)
    made = jnp.einsum("ecf,efd->ecd", expert_hidden, down_weights, preferred_element_type=fl_type)
    produced = made.reshape(-1, width)
    picked = jnp.take(produced, target, axis=0).reshape(-1, 2, width)
    mixture = jnp.sum(picked * gates[:, :, None], axis=1)
    dense_gate_part = jnp.dot(second, dense_gate, preferred_element_type=fl_type)
    dense_up_part = jnp.dot(second, dense_up, preferred_element_type=fl_type)
    dense_hidden = swiglu(dense_gate_part, dense_up_part).astype(bf_type)
    dense_out = jnp.dot(dense_hidden, dense_down, preferred_element_type=fl_type)
    branch = lax.psum((mixture + dense_out).astype(jnp.bfloat16), "wt").astype(jnp.float32)
    output = (state + branch).astype(bf_type).reshape(inputs.shape)
    dense_back = jnp.einsum("rd,fd->rf", masked_cot, dense_down, preferred_element_type=fl_type)
    unused, pull_dense = jax.vjp(swiglu, dense_gate_part, dense_up_part)
    dense_dgate, dense_dup = pull_dense(dense_back)
    dense_dgate = dense_dgate.astype(bf_type)
    dense_dup = dense_dup.astype(bf_type)
    grad_dense_down = jnp.einsum(
        "rf,rd->fd", dense_hidden, masked_cot, preferred_element_type=fl_type
    )
    grad_dense_gate = jnp.einsum("rd,rf->df", second, dense_dgate, preferred_element_type=fl_type)
    grad_dense_up = jnp.einsum("rd,rf->df", second, dense_dup, preferred_element_type=fl_type)
    back_two = jnp.einsum(
        "rf,df->rd", dense_dgate, dense_gate, preferred_element_type=fl_type
    ) + jnp.einsum("rf,df->rd", dense_dup, dense_up, preferred_element_type=fl_type)
    spread_cot = (cot_float[:, None, :] * gates[:, :, None]).reshape(-1, width)
    cot_flat = (
        jnp.zeros((experts * CAPACITY, width), fl_type).at[target].add(spread_cot).astype(bf_type)
    )
    expert_cot = cot_flat.reshape(experts, CAPACITY, width)
    expert_back = jnp.einsum(
        "ecd,efd->ecf", expert_cot, down_weights, preferred_element_type=fl_type
    )
    unused, pull_expert = jax.vjp(swiglu, gate_part, up_part)
    expert_dgate, expert_dup = pull_expert(expert_back)
    expert_dgate = expert_dgate.astype(bf_type)
    expert_dup = expert_dup.astype(bf_type)
    grad_expert_down = jnp.einsum(
        "ecf,ecd->efd", expert_hidden, expert_cot, preferred_element_type=fl_type
    )
    grad_expert_gate = jnp.einsum(
        "ecd,ecf->edf", routed, expert_dgate, preferred_element_type=fl_type
    )
    grad_expert_up = jnp.einsum("ecd,ecf->edf", routed, expert_dup, preferred_element_type=fl_type)
    routed_made = jnp.einsum(
        "ecf,edf->ecd", expert_dgate, gate_weights, preferred_element_type=fl_type
    ) + jnp.einsum("ecf,edf->ecd", expert_dup, up_weights, preferred_element_type=fl_type)
    routed_back = routed_made.reshape(-1, width)
    back_two = back_two + jnp.sum(
        jnp.take(routed_back, target, axis=0).reshape(-1, 2, width), axis=1
    )
    gate_back = jnp.sum(picked * cot_float[:, None, :], axis=-1)
    back_two, gate_back = lax.psum((back_two, gate_back), "wt")
    select_back = gates * (gate_back - jnp.sum(gates * gate_back, axis=-1, keepdims=True))
    logit_back = jnp.sum(jnp.where(picks, select_back[:, :, None], 0.0), axis=1).astype(bf_type)
    back_two = back_two + jnp.einsum(
        "re,de->rd", logit_back, router_weight, preferred_element_type=fl_type
    )
    grad_router = jnp.einsum("rd,re->de", second, logit_back, preferred_element_type=fl_type)
    state_back, grad_ffn_gain = norm_back(state, scale_two, ffn_gain, back_two)
    state_back = cot_float + state_back
    state_low = state_back.astype(bf_type)
    grad_out = jnp.einsum("rq,rd->qd", mixed, state_low, preferred_element_type=fl_type)
    mixed_back = (
        jnp.einsum("rd,qd->rq", state_low, out_weight, preferred_element_type=fl_type)
        .astype(bf_type)
        .reshape(head_shape)
    )
    back_keys, back_values = (
        lax.all_gather(keys_local, "ctx", axis=0, tiled=True),
        lax.all_gather(values_local, "ctx", axis=0, tiled=True),
    )
    back_tiles = key_tiles(back_keys, back_values, places, key_block)

    def delta_step(carry, tile):
        weights = probs_of(scores_of(tile[0], tile[2]))
        pulled = jnp.einsum("jshd,kshd->shjk", mixed_back, tile[1], preferred_element_type=fl_type)
        return (carry + jnp.sum(weights * pulled, axis=-1), None)

    delta, unused = lax.scan(delta_step, jnp.zeros(stat_shape, fl_type), back_tiles)

    def score_grads(key_tile, value_tile, tile_places):
        weights = probs_of(scores_of(key_tile, tile_places))
        pulled = jnp.einsum(
            "jshd,kshd->shjk", mixed_back, value_tile, preferred_element_type=fl_type
        )
        return (weights, (weights * (pulled - delta[..., None])).astype(bf_type))

    def query_step(carry, tile):
        weights, score_back = score_grads(tile[0], tile[1], tile[2])
        return (
            carry
            + jnp.einsum("shjk,kshd->jshd", score_back, tile[0], preferred_element_type=fl_type),
            None,
        )

    query_back, unused = lax.scan(query_step, jnp.zeros(head_shape, fl_type), back_tiles)
    query_back = (
        rotate_back(query_back * factor, cosine, sine).astype(bf_type).reshape(-1, local_width)
    )
    rows_count = pair_rows * lax.axis_size("ctx")
    tile = math.gcd(rows_count, key_block)
    parts = key_tiles(back_keys, back_values, places, tile)

    def single(item):
        weights, score_back = score_grads(item[0], item[1], item[2])
        key_part = (
            jnp.einsum("shjk,jshd->kshd", score_back, queries, preferred_element_type=fl_type)
            * factor
        )
        value_part = jnp.einsum(
            "shjk,jshd->kshd", weights.astype(bf_type), mixed_back, preferred_element_type=fl_type
        )
        return jnp.concatenate([key_part.reshape(tile, -1), value_part.reshape(tile, -1)], axis=-1)

    key_value_back = lax.psum_scatter(
        lax.map(single, parts).reshape(rows_count, -1), "ctx", scatter_dimension=0, tiled=True
    )
    span = seqs_here * local_width
    key_back = (
        rotate_back(key_value_back[:, :span].reshape(head_shape), cosine, sine)
        .astype(bf_type)
        .reshape(-1, local_width)
    )
    value_back = key_value_back[:, span:].astype(bf_type).reshape(-1, local_width)
    grad_query = jnp.einsum("rd,rq->dq", first, query_back, preferred_element_type=fl_type)
    grad_key = jnp.einsum("rd,rq->dq", first, key_back, preferred_element_type=fl_type)
    grad_value = jnp.einsum("rd,rq->dq", first, value_back, preferred_element_type=fl_type)
    first_back = (
        jnp.einsum("rq,dq->rd", query_back, query_weight, preferred_element_type=fl_type)
        + jnp.einsum("rq,dq->rd", key_back, key_weight, preferred_element_type=fl_type)
        + jnp.einsum("rq,dq->rd", value_back, value_weight, preferred_element_type=fl_type)
    )
    first_back = lax.psum(first_back, "wt")
    token_back, grad_attn_gain = norm_back(tokens, scale_one, attn_gain, first_back)
    grad_inputs = (state_back + token_back).astype(bf_type).reshape(inputs.shape)
    summed = (
        lax.psum_scatter(grad_attn_gain, "ctx", scatter_dimension=0, tiled=True),
        lax.psum_scatter(grad_query, "ctx", scatter_dimension=0, tiled=True),
        lax.psum_scatter(grad_key, "ctx", scatter_dimension=0, tiled=True),
        lax.psum_scatter(grad_value, "ctx", scatter_dimension=0, tiled=True),
        lax.psum_scatter(grad_out, "ctx", scatter_dimension=1, tiled=True),
        lax.psum_scatter(grad_ffn_gain, "ctx", scatter_dimension=0, tiled=True),
        lax.psum_scatter(grad_router, "ctx", scatter_dimension=0, tiled=True),
        lax.psum_scatter(grad_expert_gate, "ctx", scatter_dimension=1, tiled=True),
        lax.psum_scatter(grad_expert_up, "ctx", scatter_dimension=1, tiled=True),
        lax.psum_scatter(grad_expert_down, "ctx", scatter_dimension=2, tiled=True),
        lax.psum_scatter(grad_dense_gate, "ctx", scatter_dimension=0, tiled=True),
        lax.psum_scatter(grad_dense_up, "ctx", scatter_dimension=0, tiled=True),
        lax.psum_scatter(grad_dense_down, "ctx", scatter_dimension=1, tiled=True),
    )
    return (
        output,
        grad_inputs,
        summed[0],
        summed[1],
        summed[2],
        summed[3],
        summed[4],
        summed[5],
        summed[6],
        summed[7],
        summed[8],
        summed[9],
        summed[10],
        summed[11],
        summed[12],
    )


def solution(mesh):
    placed = (
        P("ctx", None, None, None),
        P("ctx", None, None, None),
        P(),
        P(),
        P("ctx", None, None, None),
        P(),
        P(None, "wt"),
        P(None, "wt"),
        P(None, "wt"),
        P("wt", None),
        P(),
        P(),
        P(None, None, "wt"),
        P(None, None, "wt"),
        P(None, "wt", None),
        P(None, "wt"),
        P(None, "wt"),
        P("wt", None),
    )
    return jax.shard_map(
        per_device,
        mesh=mesh,
        in_specs=placed,
        out_specs=(
            P("ctx", None, None, None),
            P("ctx", None, None, None),
            P("ctx"),
            P("ctx", "wt"),
            P("ctx", "wt"),
            P("ctx", "wt"),
            P("wt", "ctx"),
            P("ctx"),
            P("ctx", None),
            P(None, "ctx", "wt"),
            P(None, "ctx", "wt"),
            P(None, "wt", "ctx"),
            P("ctx", "wt"),
            P("ctx", "wt"),
            P("wt", "ctx"),
        ),
        check_vma=False,
    )
```

profile of v0, /device:TPU:0, one launch (start us, length us, event | category | flops | bytes accessed | tf_op | source)
XLA Modules:
  0.0 5234.9 jit_solution(15284177010679515293)
XLA Ops:
  34.0 176.4 %all-gather.3.cloned.1.call-done = bf16[4096,1536]{0,1:T(8,128)(2,1)} async-done(((bf16[256,1536]{0,1:T(8,128)(2,1)}), bf16[4096,1536]{0,1:T(8,128)(2,1)}) %all-gather.3.cloned.1.call-update) | async-done | bytes 12582928 | tf_op jit(solution)/shard_map/all_gather | solution.py:113
  229.1 168.1 %all-gather.5.cloned.1.call-done = bf16[4096,1536]{0,1:T(8,128)(2,1)} async-done(((bf16[256,1536]{0,1:T(8,128)(2,1)}), bf16[4096,1536]{0,1:T(8,128)(2,1)}) %all-gather.5.cloned.1.call-update) | async-done | bytes 12582928 | tf_op jit(solution)/shard_map/all_gather | solution.py:112
  415.8 68.0 %while.57 = (s32[]{:T(128)}, f32[4,6,256]{2,1,0:T(8,128)S(1)}, f32[4,6,256]{2,1,0:T(8,128)S(1)}, s32[8,512]{1,0:T(8,128)S(1)}, s32[256]{0:T(256)S(1)}, /*index=5...) while((s32[]{:T(128)}, f32[4,6,256]{2,1,0:T(8,128)S(1)}, ...), condition=%wide.region_4.5_spmd.clone, body=%wide.region_1.4_spmd.clone.sunk | while | flops 425361408 | bytes 31790252 | solution.py:147
  483.8 71.9 %while.58 = (s32[]{:T(128)}, f32[256,4,6,64]{0,3,2,1:T(8,128)}, bf16[8,512,4,6,64]{1,4,3,2,0:T(8,128)(2,1)}, s32[8,512]{1,0:T(8,128)S(1)}, s32[256]{0:T(256)S(1)...) while((s32[]{:T(128)}, f32[256,4,6,64]{0,3,2,1:T(8,128)}, ...), condition=%wide.region_6.7_spmd.clone, body=%wide.region_5.6_spmd.clone.sunk | while | flops 822478848 | bytes 8452762 | solution.py:161
  618.5 17.6 fusion.146
  636.1 23.1 multiply_convert_fusion.1
  659.2 17.1 fusion.147
  676.3 13.9 gather_fusion
  701.4 19.2 scatter_custom_fusion
  726.0 21.6 multiply_convert_fusion
  747.7 17.7 fusion.152
  765.4 19.3 convolution_add_fusion
  784.6 13.9 gather_fusion.1
  811.8 11.9 reduce_sum.158
  839.7 31.2 multiply_reduce_fusion.1
  880.5 12.8 all-reduce.10.cloned.1.call-done
  905.9 89.5 %while.59 = (s32[]{:T(128)}, f32[4,6,256]{2,1,0:T(8,128)S(1)}, s32[8,512]{1,0:T(8,128)}, s32[256]{0:T(256)S(1)}, s32[4]{0:T(128)S(1)}, /*index=5*/bf16[8,512,4,6...) while((s32[]{:T(128)}, f32[4,6,256]{2,1,0:T(8,128)S(1)}, ...), condition=%wide.region_27.29_spmd.clone, body=%wide.region_25.28_spmd.clone.sunk | while | flops 824844288 | bytes 31356072 | solution.py:267
  995.4 344.0 %while.56 = (s32[]{:T(128)}, f32[8,512,3072]{2,1,0:T(8,128)}, s32[8,512]{1,0:T(8,128)}, s32[256]{0:T(256)S(1)}, s32[4]{0:T(128)S(1)}, /*index=5*/bf16[8,512,4,6,...) while((s32[]{:T(128)}, f32[8,512,3072]{2,1,0:T(8,128)}, ...), condition=%wide.region_31.33_spmd, body=%wide.region_30.32_spmd.sunk | while | flops 1638795264 | bytes 102061248 | solution.py:304
  1005.1 10.5 fusion.274
  1048.1 10.5 fusion.274
  1091.1 10.5 fusion.274
  1134.0 10.5 fusion.274
  1263.0 10.5 fusion.274
  1306.0 10.5 fusion.274
  1348.9 180.8 %while.60 = (s32[]{:T(128)}, f32[256,4,6,64]{0,3,2,1:T(8,128)}, bf16[8,512,4,6,64]{1,4,3,2,0:T(8,128)(2,1)}, s32[8,512]{1,0:T(8,128)}, s32[256]{0:T(256)S(1)}, /...) while((s32[]{:T(128)}, f32[256,4,6,64]{0,3,2,1:T(8,128)}, ...), condition=%wide.region_29.31_spmd.clone, body=%wide.region_28.30_spmd.clone.sunk | while | flops 1231423488 | bytes 36002476 | solution.py:284
  1359.0 12.0 bitcast_add_fusion.5
  1380.9 13.0 bitcast_add_fusion.5
  1403.8 12.7 bitcast_add_fusion.5
  1426.4 12.5 bitcast_add_fusion.5
  1448.7 13.0 bitcast_add_fusion.5
  1471.6 12.7 bitcast_add_fusion.5
  1494.3 12.5 bitcast_add_fusion.5
  1516.7 13.0 bitcast_add_fusion.5
  1541.7 498.4 %reduce-scatter.15.cloned.1.call-done = f32[256,3072]{1,0:T(8,128)} async-done(((f32[4096,3072]{1,0:T(8,128)}), f32[256,3072]{1,0:T(8,128)}) %reduce-scatter.15.cloned.1.call-update) | async-done | bytes 3145744 | tf_op jit(solution)/shard_map/reduce_scatter | solution.py:303
  2101.8 21.6 fusion.159
  2123.4 21.6 fusion.158
  2145.1 21.6 fusion.157
  2193.9 42.6 all-reduce.2
  2243.6 76.6 %reduce-scatter.23.cloned.1.call-done = f32[384,48]{0,1:T(8,128)} async-done(((f32[384,768]{0,1:T(8,128)}), f32[384,48]{0,1:T(8,128)}) %reduce-scatter.23.cloned.1.call-update) | async-done | bytes 73744 | tf_op jit(solution)/shard_map/reduce_scatter | solution.py:329
  2320.2 127.8 %reduce-scatter.17.cloned.1.call-done = f32[48,384]{1,0:T(8,128)} async-done(((f32[768,384]{1,0:T(8,128)}), f32[48,384]{1,0:T(8,128)}) %reduce-scatter.17.cloned.1.call-update) | async-done | bytes 73744 | tf_op jit(solution)/shard_map/reduce_scatter | solution.py:326
  2448.0 135.4 %reduce-scatter.33.cloned.1.call-done = f32[48,1024]{1,0:T(8,128)} async-done(((f32[768,1024]{1,0:T(8,128)}), f32[48,1024]{1,0:T(8,128)}) %reduce-scatter.33.cloned.1.call-update) | async-done | bytes 196624 | tf_op jit(solution)/shard_map/reduce_scatter | solution.py:336
  2583.4 135.4 %reduce-scatter.31.cloned.1.call-done = f32[48,1024]{1,0:T(8,128)} async-done(((f32[768,1024]{1,0:T(8,128)}), f32[48,1024]{1,0:T(8,128)}) %reduce-scatter.31.cloned.1.call-update) | async-done | bytes 196624 | tf_op jit(solution)/shard_map/reduce_scatter | solution.py:335
  2718.8 135.4 %reduce-scatter.35.cloned.1.call-done = f32[1024,48]{0,1:T(8,128)} async-done(((f32[1024,768]{0,1:T(8,128)}), f32[1024,48]{0,1:T(8,128)}) %reduce-scatter.35.cloned.1.call-update) | async-done | bytes 196624 | tf_op jit(solution)/shard_map/reduce_scatter | solution.py:337
  2854.1 705.3 %reduce-scatter.29.cloned.1.call-done = f32[16,1024,48]{1,2,0:T(8,128)} async-done(((f32[16,1024,768]{1,2,0:T(8,128)}), f32[16,1024,48]{1,2,0:T(8,128)}) %reduce-scatter.29.cloned.1.call-update) | async-done | bytes 3145744 | tf_op jit(solution)/shard_map/reduce_scatter | solution.py:334
  3559.4 706.4 %reduce-scatter.27.cloned.1.call-done = f32[16,48,1024]{2,1,0:T(8,128)} async-done(((f32[16,768,1024]{2,1,0:T(8,128)}), f32[16,48,1024]{2,1,0:T(8,128)}) %reduce-scatter.27.cloned.1.call-update) | async-done | bytes 3145744 | tf_op jit(solution)/shard_map/reduce_scatter | solution.py:333
  4265.8 705.2 %reduce-scatter.25.cloned.1.call-done = f32[16,48,1024]{2,1,0:T(8,128)} async-done(((f32[16,768,1024]{2,1,0:T(8,128)}), f32[16,48,1024]{2,1,0:T(8,128)}) %reduce-scatter.25.cloned.1.call-update) | async-done | bytes 3145744 | tf_op jit(solution)/shard_map/reduce_scatter | solution.py:332
  4971.0 128.4 %reduce-scatter.21.cloned.1.call-done = f32[48,384]{1,0:T(8,128)} async-done(((f32[768,384]{1,0:T(8,128)}), f32[48,384]{1,0:T(8,128)}) %reduce-scatter.21.cloned.1.call-update) | async-done | bytes 73744 | tf_op jit(solution)/shard_map/reduce_scatter | solution.py:328
  5099.4 128.5 %reduce-scatter.19.cloned.1.call-done = f32[48,384]{1,0:T(8,128)} async-done(((f32[768,384]{1,0:T(8,128)}), f32[48,384]{1,0:T(8,128)}) %reduce-scatter.19.cloned.1.call-update) | async-done | bytes 73744 | tf_op jit(solution)/shard_map/reduce_scatter | solution.py:327
  (650 shorter events, 897.4 us)
Async XLA Ops:
  7.2 595.5 %copy-start = (bf16[1024,768]{1,0:T(8,128)(2,1)S(1)}, bf16[1024,768]{1,0:T(8,128)(2,1)}, u32[]{:S(2)}) copy-start(bf16[1024,768]{1,0:T(8,128)(2,1)} %param.47) | copy-start | bytes 4718596
  7.2 203.2 %all-gather.3.cloned.1.call-start = ((), (), s32[]{:S(2)}) async-start(), calls=%async_computation.12 | async-start | bytes 13369344 | tf_op jit(solution)/shard_map/all_gather | solution.py:113
  13.7 14.1 copy-start.32
  13.9 8.5 copy-start.61
  13.9 8.6 copy-start.71
  17.7 10.1 copy-start.9
  22.4 374.7 %all-gather.5.cloned.1.call-start = ((), (), s32[]{:S(2)}) async-start(), calls=%async_computation.13 | async-start | bytes 13369344 | tf_op jit(solution)/shard_map/all_gather | solution.py:112
  33.1 559.3 %all-reduce.8.cloned.1.call-start = ((), (), s32[]{:S(2)}) async-start(), calls=%async_computation.14 | async-start | bytes 6291456 | tf_op jit(solution)/shard_map/psum | solution.py:164
  406.5 9.3 copy-start.46
  555.7 8.5 copy-start.20
  555.7 8.5 copy-start.38
  555.7 8.5 copy-start.51
  555.7 12.6 copy-start.40
  555.7 12.6 copy-start.47
  557.3 7.0 copy-start.27
  566.9 307.2 %all-reduce.12.cloned.1.call-start = ((), (), s32[]{:S(2)}) async-start(), calls=%async_computation.16 | async-start | bytes 6291456 | tf_op jit(solution)/shard_map/psum | solution.py:240
  568.6 34.0 copy-start.68
  568.8 28.2 copy-start.54
  596.5 14.9 copy-start.7
  831.1 62.1 %all-reduce.10.cloned.1.call-start = ((), (), s32[]{:S(2)}) async-start(), calls=%async_computation.15 | async-start | bytes 3145728 | tf_op jit(solution)/shard_map/psum | solution.py:198
  839.7 31.3 copy-start.74
  874.0 1166.1 %reduce-scatter.15.cloned.1.call-start = ((), (), s32[]{:S(2)}) async-start(), calls=%async_computation.17 | async-start | bytes 53477376 | tf_op jit(solution)/shard_map/reduce_scatter | solution.py:303
  874.1 19.1 copy-start.13
  874.2 19.1 copy-start.69
  893.3 6.9 copy-start.28
  1015.7 6.7 copy-start.3
  1058.6 6.7 copy-start.3
  1101.6 6.7 copy-start.3
  1144.5 6.7 copy-start.3
  1339.4 843.6 %reduce-scatter.37.cloned.1.call-start = ((), (), s32[]{:S(2)}) async-start(), calls=%async_computation.29 | async-start | bytes 417792
  1348.9 841.3 %all-reduce.14.cloned.1.call-start = ((), (), s32[]{:S(2)}) async-start(), calls=%async_computation.18 | async-start | bytes 6291456 | tf_op jit(solution)/shard_map/psum | solution.py:321
  1348.9 180.8 %copy-start.53 = (f32[256,64]{0,1:T(8,128)S(1)}, f32[256,64]{0,1:T(8,128)}, u32[]{:S(2)}) copy-start(f32[256,64]{0,1:T(8,128)} %get-tuple-element.780) | copy-start | bytes 196612
  1532.0 7.0 copy-start.29
  1539.0 501.1 %copy-start.23 = (bf16[1024,384]{1,0:T(8,128)(2,1)}, bf16[1024,384]{1,0:T(8,128)(2,1)S(1)}, u32[]{:S(2)}) copy-start(bf16[1024,384]{1,0:T(8,128)(2,1)S(1)} %reshape.771) | copy-start | bytes 2359300
  2044.7 7.8 copy-start.43
  2070.8 249.4 %reduce-scatter.23.cloned.1.call-start = ((), (), s32[]{:S(2)}) async-start(), calls=%async_computation.22 | async-start | bytes 1253376 | tf_op jit(solution)/shard_map/reduce_scatter | solution.py:329
  2075.2 372.8 %reduce-scatter.17.cloned.1.call-start = ((), (), s32[]{:S(2)}) async-start(), calls=%async_computation.19 | async-start | bytes 1253376 | tf_op jit(solution)/shard_map/reduce_scatter | solution.py:326
  2084.7 498.8 %reduce-scatter.33.cloned.1.call-start = ((), (), s32[]{:S(2)}) async-start(), calls=%async_computation.27 | async-start | bytes 3342336 | tf_op jit(solution)/shard_map/reduce_scatter | solution.py:336
  2089.9 628.9 %reduce-scatter.31.cloned.1.call-start = ((), (), s32[]{:S(2)}) async-start(), calls=%async_computation.26 | async-start | bytes 3342336 | tf_op jit(solution)/shard_map/reduce_scatter | solution.py:335
  2095.1 759.1 %reduce-scatter.35.cloned.1.call-start = ((), (), s32[]{:S(2)}) async-start(), calls=%async_computation.28 | async-start | bytes 3342336 | tf_op jit(solution)/shard_map/reduce_scatter | solution.py:337
  2101.7 1457.7 %reduce-scatter.29.cloned.1.call-start = ((), (), s32[]{:S(2)}) async-start(), calls=%async_computation.25 | async-start | bytes 53477376 | tf_op jit(solution)/shard_map/reduce_scatter | solution.py:334
  2123.4 2142.4 %reduce-scatter.27.cloned.1.call-start = ((), (), s32[]{:S(2)}) async-start(), calls=%async_computation.24 | async-start | bytes 53477376 | tf_op jit(solution)/shard_map/reduce_scatter | solution.py:333
  2145.0 2825.9 %reduce-scatter.25.cloned.1.call-start = ((), (), s32[]{:S(2)}) async-start(), calls=%async_computation.23 | async-start | bytes 53477376 | tf_op jit(solution)/shard_map/reduce_scatter | solution.py:332
  2166.7 2932.6 %reduce-scatter.21.cloned.1.call-start = ((), (), s32[]{:S(2)}) async-start(), calls=%async_computation.21 | async-start | bytes 1253376 | tf_op jit(solution)/shard_map/reduce_scatter | solution.py:328
  2170.4 3057.5 %reduce-scatter.19.cloned.1.call-start = ((), (), s32[]{:S(2)}) async-start(), calls=%async_computation.20 | async-start | bytes 1253376 | tf_op jit(solution)/shard_map/reduce_scatter | solution.py:327
  2181.7 8.5 copy-start.62
  2185.8 8.1 copy-start.67
  2237.6 2990.2 %copy-start.1 = (bf16[1024,768]{1,0:T(8,128)(2,1)S(1)}, bf16[1024,768]{1,0:T(8,128)(2,1)}, u32[]{:S(2)}) copy-start(bf16[1024,768]{1,0:T(8,128)(2,1)} %param.47) | copy-start | bytes 4718596
  (59 other events, 216.3 us)
Sparse Core Ops, SparseCore 0:
  22.5 187.8 all-gather.2
  213.7 183.3 all-gather.4
  567.1 21.4 all-reduce.7
  831.3 21.6 all-reduce.11
  874.1 19.0 all-reduce.9
  1339.5 700.5 reduce-scatter.14
  2044.8 120.6 reduce-scatter.36
  2167.9 22.2 all-reduce.13
  2195.5 124.6 reduce-scatter.22
  2325.4 122.5 reduce-scatter.16
  2453.6 129.7 reduce-scatter.32
  2588.8 129.9 reduce-scatter.30
  2724.3 129.7 reduce-scatter.34
  2860.6 698.8 reduce-scatter.28
  3566.9 698.8 reduce-scatter.26
  4272.2 698.7 reduce-scatter.24
  4976.9 122.4 reduce-scatter.20
  5105.3 122.5 reduce-scatter.18
where the time goes:
time: 5250 us; the launch traced here: 5230 us
  waiting for transfers between devices  3840 us (73%)
  matrix products  810 us (15%)
  local copies, waits for them, and re-layouts  309 us (6%)
  other arithmetic  206 us (4%)
    reduce_scatter x1, waiting for transfers between devices, per_device(): lax.psum_scatter(grad_expert_up, 'ctx', scatter_dimension=1, tiled=True)  706 us
    reduce_scatter x1, waiting for transfers between devices, per_device(): lax.psum_scatter(grad_expert_down, 'ctx', scatter_dimension=2, tiled=True)  705 us
    reduce_scatter x1, waiting for transfers between devices, per_device(): lax.psum_scatter(grad_expert_gate, 'ctx', scatter_dimension=1, tiled=True)  705 us
    reduce_scatter x1, waiting for transfers between devices, per_device(): lax.psum_scatter(lax.map(single, parts).reshape(rows_count, -1), 'ctx', s...  498 us
    dot_general x32, matrix products, scores_of(): jnp.einsum('jshd,kshd->shjk', queries, key_tile, preferred_element_type=f...  186 us
    all_gather x1, waiting for transfers between devices, per_device(): lax.all_gather(values_local, 'ctx', axis=0, tiled=True)  176 us
    all_gather x1, waiting for transfers between devices, per_device(): lax.all_gather(keys_local, 'ctx', axis=0, tiled=True)  168 us
    reduce_scatter x1, waiting for transfers between devices, per_device(): lax.psum_scatter(grad_dense_up, 'ctx', scatter_dimension=0, tiled=True)  135 us
  transfers between devices with their start and end apart: 18, of which 15 were waited for; matrix products, arithmetic and copies ran while one was open for 9% of the time, Pallas kernels for 0%

commit v1 on v0

v1 whole, which is shorter than its diff:
```python
import functools

import jax
import jax.numpy as jnp
from jax import lax
from jax.experimental import pallas as pl
from jax.experimental.pallas import tpu as pltpu
from jax.sharding import PartitionSpec as P

HEAD_DIM = 64
CAPACITY = 160
EPS = 1e-06
THETA = 10000.0
LANES = 128
BF = jnp.bfloat16
F4 = jnp.float32
TQ = 256
TK = 512
VMEM_LIMIT = 56 * 1024 * 1024


def dot(a, b):
    return jnp.dot(a, b, preferred_element_type=F4)


def dot_nt(a, b):
    return lax.dot_general(a, b, (((1,), (1,)), ((), ())), preferred_element_type=F4)


def dot_tn(a, b):
    return lax.dot_general(a, b, (((0,), (0,)), ((), ())), preferred_element_type=F4)


def wt_gather(x):
    size = lax.axis_size("wt")
    return [x] + [
        lax.ppermute(x, "wt", [(i, (i - k) % size) for i in range(size)]) for k in range(1, size)
    ]


def wt_scatter(pieces):
    size = lax.axis_size("wt")
    total = pieces[0]
    for k in range(1, size):
        moved = lax.ppermute(pieces[k], "wt", [(i, (i + k) % size) for i in range(size)])
        total = total + moved.astype(total.dtype)
    return total


def wt_sum(x):
    if lax.axis_size("wt") == 2:
        return x + lax.ppermute(x, "wt", [(0, 1), (1, 0)])
    return lax.psum(x, "wt")


def in_order(parts):
    size = len(parts)
    start = (size - lax.axis_index("wt")) % size
    return lax.dynamic_slice_in_dim(jnp.stack(parts + parts[:-1]), start, size, 0)


def lane_of(shape):
    return lax.broadcasted_iota(jnp.int32, shape, len(shape) - 1)


def pair_swap(a, b):
    low = lane_of(a.shape) < HEAD_DIM
    return (
        jnp.where(low, a, pltpu.roll(b, HEAD_DIM, 1)),
        jnp.where(low, pltpu.roll(a, HEAD_DIM, 1), b),
    )


def turn_halves(t):
    first = lane_of(t.shape) % HEAD_DIM < HEAD_DIM // 2
    return jnp.where(
        first,
        pltpu.roll(t, LANES - HEAD_DIM // 2, 1),
        pltpu.roll(t, HEAD_DIM // 2, 1),
    )


def params(count):
    return pltpu.CompilerParams(
        vmem_limit_bytes=VMEM_LIMIT, dimension_semantics=("arbitrary",) * count
    )


def whole(shape):
    return pl.BlockSpec(shape, lambda *i: (0,) * len(shape))


def project_kernel(members, heads, units, x_ref, gain_ref, w_ref, cos_ref, sin_ref, msg_ref, a1_ref):
    s = pl.program_id(0)
    rows = x_ref.shape[1]
    chunk = rows // 2
    width = heads * HEAD_DIM
    x = x_ref[0].astype(F4)
    scale = lax.rsqrt(jnp.mean(x * x, axis=-1, keepdims=True) + EPS)
    a1 = (x * scale * gain_ref[...]).astype(BF)
    a1_ref[0] = a1
    cosine, sine = cos_ref[...], sin_ref[...]
    query = dot(a1, w_ref[:, :width])
    key = dot(a1, w_ref[:, width : 2 * width])
    value = dot(a1, w_ref[:, 2 * width :])
    if units * members > (heads * pl.num_programs(0)):

        @pl.when(s == 0)
        def _():
            msg_ref[...] = jnp.zeros_like(msg_ref)

    def rope(t):
        return t * cosine + turn_halves(t) * sine

    for g in range(heads // 2):
        part = slice(g * LANES, (g + 1) * LANES)
        pairs = pair_swap(rope(key[:, part]), value[:, part])
        turned = rope(query[:, part])
        asked = pair_swap(turned[:chunk], turned[chunk:])
        for c in range(2):
            unit = s * heads + 2 * g + c
            chip, u = unit % members, unit // members
            msg_ref[chip, 3 * u] = pairs[c][:chunk].astype(BF)
            msg_ref[chip, 3 * u + 1] = pairs[c][chunk:].astype(BF)
            msg_ref[chip, 3 * u + 2] = asked[c].astype(BF)


def project(x, gain, weights, cosine, sine, members, units):
    seqs, rows, width = x.shape
    heads = weights.shape[1] // 3 // HEAD_DIM
    msg = (members, 3 * units, rows // 2, LANES)
    return pl.pallas_call(
        functools.partial(project_kernel, members, heads, units),
        grid=(seqs,),
        in_specs=[
            pl.BlockSpec((1, rows, width), lambda s: (s, 0, 0)),
            whole((1, width)),
            whole(weights.shape),
            whole(cosine.shape),
            whole(sine.shape),
        ],
        out_specs=[whole(msg), pl.BlockSpec((1, rows, width), lambda s: (s, 0, 0))],
        out_shape=[
            jax.ShapeDtypeStruct(msg, BF),
            jax.ShapeDtypeStruct((seqs, rows, width), BF),
        ],
        compiler_params=params(1),
        name="project",
    )(x, gain, weights, cosine, sine)


def gather_keys(inv_ref, w, kv_refs, kv_s, members, chunk):
    size = len(kv_refs)
    for block in range(2 * members):
        half = 0 if block < members else 1
        chip = inv_ref[block if half == 0 else 2 * members - 1 - block]
        for k, ref in enumerate(kv_refs):
            core = lax.rem(w + k, size)
            start = pl.multiple_of(block * size * chunk + core * chunk, chunk)
            kv_s[pl.ds(start, chunk), :] = ref[chip, half]


def gather_rows(inv_ref, read, put, members, to_high):
    for block in range(2 * members):
        half = 0 if block < members else 1
        chip = inv_ref[block if half == 0 else 2 * members - 1 - block]
        rows = read(chip).astype(F4)
        if (half == 1) != to_high:
            rows = pltpu.roll(rows, HEAD_DIM, 1)
        low = lane_of(rows.shape) < HEAD_DIM
        rows = jnp.where(low, 0.0, rows) if to_high else jnp.where(low, rows, 0.0)
        put(block, rows)


def attend_kernel(members, size, inv_ref, len_ref, w_ref, *refs):
    kv_refs = refs[:size]
    o_ref, of_ref, lse_ref = refs[size : size + 3]
    kv_s, vt_s, q_s, o_s = refs[size + 3 :]
    u = pl.program_id(0)
    chunk = kv_refs[0].shape[2]
    own_rows = q_s.shape[0]
    slot = kv_s.shape[0]
    w = w_ref[0]
    length = len_ref[u]
    gather_keys(inv_ref, w, kv_refs, kv_s, members, chunk)

    def put(block, rows):
        q_s[block * chunk : (block + 1) * chunk, :] = rows * HEAD_DIM ** (-0.5)

    gather_rows(inv_ref, lambda chip: kv_refs[0][chip, 2], put, members, False)

    def flip(i, carry):
        tile = kv_s[pl.ds(pl.multiple_of(i * TK, TK), TK), :].astype(F4)
        vt_s[i] = tile.T[HEAD_DIM:].astype(BF)
        return carry

    lax.fori_loop(0, slot // TK, flip, 0)
    span = TQ * size

    def row_tile(t, carry):
        row = pl.multiple_of(t * TQ, TQ)
        qt = q_s[pl.ds(row, TQ), :].T.astype(BF)
        index = lax.broadcasted_iota(jnp.int32, (1, TQ), 1)
        place = t * span + (index // chunk) * (size * chunk) + w * chunk + index % chunk
        limit = jnp.minimum(place, length - 1)

        def step(masked, kt, state):
            top, total, acc = state
            start = pl.multiple_of(kt * TK, TK)
            scores = dot(kv_s[pl.ds(start, TK), :], qt)
            if masked:
                keys = kt * TK + lax.broadcasted_iota(jnp.int32, (TK, 1), 0)
                scores = jnp.where(keys <= limit, scores, -1e30)
            new_top = jnp.maximum(top, jnp.max(scores, axis=0, keepdims=True))
            weights = jnp.exp(scores - new_top)
            fade = jnp.exp(top - new_top)
            total = total * fade + jnp.sum(weights, axis=0, keepdims=True)
            acc = acc * fade + dot(vt_s[kt], weights.astype(BF))
            return new_top, total, acc

        clear = jnp.minimum(t * span, length) // TK
        last = jnp.minimum(pl.cdiv((t + 1) * span, TK), pl.cdiv(length, TK))
        state = (
            jnp.full((1, TQ), -1e30, F4),
            jnp.zeros((1, TQ), F4),
            jnp.zeros((HEAD_DIM, TQ), F4),
        )
        state = lax.fori_loop(0, clear, functools.partial(step, False), state)
        top, total, acc = lax.fori_loop(clear, last, functools.partial(step, True), state)
        result = acc / total
        of_ref[0, t] = result
        lse_ref[0, t] = top + jnp.log(total)
        blank = jnp.zeros_like(result)
        first = 2 * t * TQ < own_rows
        both = jnp.concatenate(
            [jnp.where(first, result, blank), jnp.where(first, blank, result)], axis=0
        )
        o_s[pl.ds(row, TQ), :] = both.T
        return carry

    lax.fori_loop(0, own_rows // TQ, row_tile, 0)
    for b in range(members):
        other = 2 * members - 1 - b
        rows = (
            o_s[b * chunk : (b + 1) * chunk, :] + o_s[other * chunk : (other + 1) * chunk, :]
        )
        o_ref[inv_ref[b], 0] = rows.astype(BF)


def attend(inv, lengths, w, blocks, units):
    members, _, chunk, _ = blocks[0].shape
    size = len(blocks)
    slot = 2 * members * chunk * size
    rows = 2 * members * chunk
    spec = pl.BlockSpec((members, 3, chunk, LANES), lambda u, *_: (0, u, 0, 0))
    return pl.pallas_call(
        functools.partial(attend_kernel, members, size),
        grid_spec=pltpu.PrefetchScalarGridSpec(
            num_scalar_prefetch=3,
            grid=(units,),
            in_specs=[spec] * size,
            out_specs=[
                pl.BlockSpec((members, 1, chunk, LANES), lambda u, *_: (0, u, 0, 0)),
                pl.BlockSpec((1, rows // TQ, HEAD_DIM, TQ), lambda u, *_: (u, 0, 0, 0)),
                pl.BlockSpec((1, rows // TQ, 1, TQ), lambda u, *_: (u, 0, 0, 0)),
            ],
            scratch_shapes=[
                pltpu.VMEM((slot, LANES), BF),
                pltpu.VMEM((slot // TK, HEAD_DIM, TK), BF),
                pltpu.VMEM((rows, LANES), F4),
                pltpu.VMEM((rows, LANES), F4),
            ],
        ),
        out_shape=[
            jax.ShapeDtypeStruct((members, units, chunk, LANES), BF),
            jax.ShapeDtypeStruct((units, rows // TQ, HEAD_DIM, TQ), F4),
            jax.ShapeDtypeStruct((units, rows // TQ, 1, TQ), F4),
        ],
        compiler_params=params(1),
        name="attend",
    )(inv, lengths, w, *blocks)


def attend_back_kernel(members, size, inv_ref, len_ref, w_ref, *refs):
    kv_refs = refs[:size]
    do_ref, of_ref, lse_ref = refs[size : size + 3]
    dq_ref = refs[size + 3]
    dkv_refs = refs[size + 4 : 2 * size + 4]
    kv_s, kt_s, q_s, do_s, dq_s, dkv_s = refs[2 * size + 4 :]
    u = pl.program_id(0)
    chunk = kv_refs[0].shape[2]
    own_rows = q_s.shape[0]
    slot = kv_s.shape[0]
    w = w_ref[0]
    length = len_ref[u]
    gather_keys(inv_ref, w, kv_refs, kv_s, members, chunk)

    def put_q(block, rows):
        q_s[block * chunk : (block + 1) * chunk, :] = rows * HEAD_DIM ** (-0.5)

    def put_do(block, rows):
        do_s[block * chunk : (block + 1) * chunk, :] = rows

    gather_rows(inv_ref, lambda chip: kv_refs[0][chip, 2], put_q, members, False)
    gather_rows(inv_ref, lambda chip: do_ref[chip, 0], put_do, members, True)

    def flip(i, carry):
        tile = kv_s[pl.ds(pl.multiple_of(i * TK, TK), TK), :].astype(F4)
        kt_s[i] = tile.T[:HEAD_DIM].astype(BF)
        return carry

    lax.fori_loop(0, slot // TK, flip, 0)
    dkv_s[...] = jnp.zeros_like(dkv_s)
    dq_s[...] = jnp.zeros_like(dq_s)
    span = TQ * size

    def row_tile(t, carry):
        row = pl.multiple_of(t * TQ, TQ)
        q_rows = q_s[pl.ds(row, TQ), :]
        do_rows = do_s[pl.ds(row, TQ), :]
        qt, dot_ = q_rows.T, do_rows.T
        delta = jnp.sum(dot_[HEAD_DIM:] * of_ref[0, t], axis=0, keepdims=True)
        qt, dot_ = qt.astype(BF), dot_.astype(BF)
        stacked = jnp.concatenate([do_rows.astype(BF), q_rows.astype(BF)], axis=0)
        lse = lse_ref[0, t]
        index = lax.broadcasted_iota(jnp.int32, (1, TQ), 1)
        place = t * span + (index // chunk) * (size * chunk) + w * chunk + index % chunk
        limit = jnp.minimum(place, length - 1)

        def step(masked, kt, dqt):
            start = pl.multiple_of(kt * TK, TK)
            kv = kv_s[pl.ds(start, TK), :]
            weights = jnp.exp(dot(kv, qt) - lse)
            if masked:
                keys = kt * TK + lax.broadcasted_iota(jnp.int32, (TK, 1), 0)
                weights = jnp.where(keys <= limit, weights, 0.0)
            pulled = dot(kv, dot_)
            back = (weights * (pulled - delta)).astype(BF)
            dkv_s[pl.ds(start, TK), :] += dot(
                jnp.concatenate([weights.astype(BF), back], axis=1), stacked
            )
            return dqt + dot(kt_s[kt], back)

        clear = jnp.minimum(t * span, length) // TK
        last = jnp.minimum(pl.cdiv((t + 1) * span, TK), pl.cdiv(length, TK))
        dqt = jnp.zeros((HEAD_DIM, TQ), F4)
        dqt = lax.fori_loop(0, clear, functools.partial(step, False), dqt)
        dqt = lax.fori_loop(clear, last, functools.partial(step, True), dqt)
        dqt = dqt * HEAD_DIM ** (-0.5)
        blank = jnp.zeros_like(dqt)
        first = 2 * t * TQ < own_rows
        both = jnp.concatenate(
            [jnp.where(first, dqt, blank), jnp.where(first, blank, dqt)], axis=0
        )
        dq_s[pl.ds(row, TQ), :] = both.T
        return carry

    lax.fori_loop(0, jnp.minimum(pl.cdiv(length, span), own_rows // TQ), row_tile, 0)
    for b in range(members):
        other = 2 * members - 1 - b
        chip = inv_ref[b]
        rows = (
            dq_s[b * chunk : (b + 1) * chunk, :] + dq_s[other * chunk : (other + 1) * chunk, :]
        )
        dq_ref[chip, 0] = rows.astype(BF)
        for half, block in ((0, b), (1, other)):
            for k, ref in enumerate(dkv_refs):
                core = lax.rem(w + k, size)
                start = pl.multiple_of(block * size * chunk + core * chunk, chunk)
                ref[chip, half] = dkv_s[pl.ds(start, chunk), :]


def attend_back(inv, lengths, w, blocks, do_msg, kept, lse, units):
    members, _, chunk, _ = blocks[0].shape
    size = len(blocks)
    slot = 2 * members * chunk * size
    rows = 2 * members * chunk
    spec = pl.BlockSpec((members, 3, chunk, LANES), lambda u, *_: (0, u, 0, 0))
    one = pl.BlockSpec((members, 1, chunk, LANES), lambda u, *_: (0, u, 0, 0))
    two = pl.BlockSpec((members, 2, chunk, LANES), lambda u, *_: (0, u, 0, 0))
    return pl.pallas_call(
        functools.partial(attend_back_kernel, members, size),
        grid_spec=pltpu.PrefetchScalarGridSpec(
            num_scalar_prefetch=3,
            grid=(units,),
            in_specs=[spec] * size
            + [
                one,
                pl.BlockSpec((1, rows // TQ, HEAD_DIM, TQ), lambda u, *_: (u, 0, 0, 0)),
                pl.BlockSpec((1, rows // TQ, 1, TQ), lambda u, *_: (u, 0, 0, 0)),
            ],
            out_specs=[one] + [two] * size,
            scratch_shapes=[
                pltpu.VMEM((slot, LANES), BF),
                pltpu.VMEM((slot // TK, HEAD_DIM, TK), BF),
                pltpu.VMEM((rows, LANES), F4),
                pltpu.VMEM((rows, LANES), F4),
                pltpu.VMEM((rows, LANES), F4),
                pltpu.VMEM((slot, LANES), F4),
            ],
        ),
        out_shape=[jax.ShapeDtypeStruct((members, units, chunk, LANES), BF)]
        + [jax.ShapeDtypeStruct((members, 2 * units, chunk, LANES), F4)] * size,
        compiler_params=params(1),
        name="attend_back",
    )(inv, lengths, w, *blocks, do_msg, kept, lse)


def mix_kernel(members, heads, o_ref, x_ref, w_ref, gain_ref, mixed_ref, state_ref, a2_ref):
    s = pl.program_id(0)
    chunk = o_ref.shape[2]
    for g in range(heads // 2):
        pair = []
        for c in range(2):
            unit = s * heads + 2 * g + c
            pair.append(o_ref[unit % members, unit // members].astype(F4))
        early, late = pair_swap(*pair)
        part = slice(g * LANES, (g + 1) * LANES)
        mixed_ref[0, :chunk, part] = early.astype(BF)
        mixed_ref[0, chunk:, part] = late.astype(BF)
    state = x_ref[0].astype(F4) + dot(mixed_ref[0], w_ref[...])
    state_ref[0] = state
    scale = lax.rsqrt(jnp.mean(state * state, axis=-1, keepdims=True) + EPS)
    a2_ref[0] = (state * scale * gain_ref[...]).astype(BF)


def mix(o_msg, x, out_weight, gain):
    members, units, chunk, _ = o_msg.shape
    seqs, rows, width = x.shape
    inner = out_weight.shape[0]
    per_slot = pl.BlockSpec((1, rows, width), lambda s: (s, 0, 0))
    return pl.pallas_call(
        functools.partial(mix_kernel, members, inner // HEAD_DIM),
        grid=(seqs,),
        in_specs=[whole(o_msg.shape), per_slot, whole(out_weight.shape), whole((1, width))],
        out_specs=[pl.BlockSpec((1, rows, inner), lambda s: (s, 0, 0)), per_slot, per_slot],
        out_shape=[
            jax.ShapeDtypeStruct((seqs, rows, inner), BF),
            jax.ShapeDtypeStruct((seqs, rows, width), F4),
            jax.ShapeDtypeStruct((seqs, rows, width), BF),
        ],
        compiler_params=params(1),
        name="mix",
    )(o_msg, x, out_weight, gain)


def norm_back(values, gain, upstream):
    scale = lax.rsqrt(jnp.mean(values * values, axis=-1, keepdims=True) + EPS)
    unit = values * scale
    pulled = upstream * gain
    result = scale * (pulled - unit * jnp.mean(pulled * unit, axis=-1, keepdims=True))
    return result, jnp.sum(upstream * unit, axis=0, keepdims=True)


def unmix_kernel(members, heads, state_ref, da2_ref, cot_ref, gain_ref, w_ref, *outs):
    dstate_ref, low_ref, msg_ref, dgain_ref = outs
    s = pl.program_id(0)
    rows = state_ref.shape[1]
    chunk = rows // 2
    pulled, dgain = norm_back(state_ref[0], gain_ref[...], da2_ref[0])
    dstate = cot_ref[0].astype(F4) + pulled
    dstate_ref[0] = dstate
    low = dstate.astype(BF)
    low_ref[0] = low

    @pl.when(s == 0)
    def _():
        dgain_ref[...] = jnp.zeros_like(dgain_ref)
        if msg_ref.shape[0] * msg_ref.shape[1] > heads * pl.num_programs(0):
            msg_ref[...] = jnp.zeros_like(msg_ref)

    dgain_ref[...] += dgain
    mixed_back = dot_nt(low, w_ref[...])
    for g in range(heads // 2):
        part = mixed_back[:, g * LANES : (g + 1) * LANES]
        pair = pair_swap(part[:chunk], part[chunk:])
        for c in range(2):
            unit = s * heads + 2 * g + c
            msg_ref[unit % members, unit // members] = pair[c].astype(BF)


def unmix(state, da2, cot, gain, out_weight, members, units):
    seqs, rows, width = state.shape
    inner = out_weight.shape[0]
    msg = (members, units, rows // 2, LANES)
    per_slot = pl.BlockSpec((1, rows, width), lambda s: (s, 0, 0))
    return pl.pallas_call(
        functools.partial(unmix_kernel, members, inner // HEAD_DIM),
        grid=(seqs,),
        in_specs=[per_slot, per_slot, per_slot, whole((1, width)), whole(out_weight.shape)],
        out_specs=[per_slot, per_slot, whole(msg), whole((1, width))],
        out_shape=[
            jax.ShapeDtypeStruct((seqs, rows, width), F4),
            jax.ShapeDtypeStruct((seqs, rows, width), BF),
            jax.ShapeDtypeStruct(msg, BF),
            jax.ShapeDtypeStruct((1, width), F4),
        ],
        compiler_params=params(1),
        name="unmix",
    )(state, da2, cot, gain, out_weight)


def unproject_kernel(
    members, heads, units, msg_ref, x_ref, dstate_ref, gain_ref, w_ref, cos_ref, sin_ref, *outs
):
    dqkv_ref, dx_ref, dgain_ref = outs
    s = pl.program_id(0)
    width = heads * HEAD_DIM
    cosine, sine = cos_ref[...], sin_ref[...]

    def rope_back(grad):
        return grad * cosine - turn_halves(grad) * sine

    for g in range(heads // 2):
        pair, early, late = [], [], []
        for c in range(2):
            unit = s * heads + 2 * g + c
            chip, u = unit % members, unit // members
            pair.append(
                jnp.concatenate([msg_ref[chip, 2 * u], msg_ref[chip, 2 * u + 1]], axis=0).astype(F4)
            )
            early.append(msg_ref[chip, 2 * units + u].astype(F4))
        key, value = pair_swap(*pair)
        query = jnp.concatenate(pair_swap(*early), axis=0)
        at = g * LANES
        dqkv_ref[0, :, at : at + LANES] = rope_back(query).astype(BF)
        dqkv_ref[0, :, width + at : width + at + LANES] = rope_back(key).astype(BF)
        dqkv_ref[0, :, 2 * width + at : 2 * width + at + LANES] = value.astype(BF)
    da1 = dot_nt(dqkv_ref[0], w_ref[...])
    pulled, dgain = norm_back(x_ref[0].astype(F4), gain_ref[...], da1)
    dx_ref[0] = (dstate_ref[0] + pulled).astype(BF)

    @pl.when(s == 0)
    def _():
        dgain_ref[...] = jnp.zeros_like(dgain_ref)

    dgain_ref[...] += dgain


def unproject(msg, x, dstate, gain, weights, cosine, sine):
    members, triple, chunk, _ = msg.shape
    seqs, rows, width = x.shape
    inner = weights.shape[1]
    per_slot = pl.BlockSpec((1, rows, width), lambda s: (s, 0, 0))
    return pl.pallas_call(
        functools.partial(unproject_kernel, members, inner // 3 // HEAD_DIM, triple // 3),
        grid=(seqs,),
        in_specs=[
            whole(msg.shape),
            per_slot,
            per_slot,
            whole((1, width)),
            whole(weights.shape),
            whole(cosine.shape),
            whole(sine.shape),
        ],
        out_specs=[
            pl.BlockSpec((1, rows, inner), lambda s: (s, 0, 0)),
            per_slot,
            whole((1, width)),
        ],
        out_shape=[
            jax.ShapeDtypeStruct((seqs, rows, inner), BF),
            jax.ShapeDtypeStruct((seqs, rows, width), BF),
            jax.ShapeDtypeStruct((1, width), F4),
        ],
        compiler_params=params(1),
        name="unproject",
    )(msg, x, dstate, gain, weights, cosine, sine)


def swiglu(gate_part, up_part):
    return jax.nn.silu(gate_part) * up_part


def swiglu_back(gate_part, up_part, hidden_back):
    unused, pull = jax.vjp(swiglu, gate_part, up_part)
    dgate, dup = pull(hidden_back)
    return dgate.astype(BF), dup.astype(BF)


def per_device(
    inputs,
    cotangent,
    lengths,
    block_pairs,
    routes,
    attn_gain,
    query_weight,
    key_weight,
    value_weight,
    out_weight,
    ffn_gain,
    router_weight,
    expert_gate,
    expert_up,
    expert_down,
    dense_gate,
    dense_up,
    dense_down,
):
    pair_rows, seqs, width = inputs.shape[1:]
    members, size = lax.axis_size("ctx"), lax.axis_size("wt")
    ctx, w = lax.axis_index("ctx"), lax.axis_index("wt")
    experts = expert_gate.shape[0]
    block = pair_rows // 2
    chunk = block // size
    rows = 2 * chunk * seqs
    inner = query_weight.shape[1] * size
    heads = inner // HEAD_DIM
    units = -(-(seqs * heads) // members)

    def rows_of(array, k):
        parted = array.reshape(2, size, chunk, seqs, -1)
        mine = lax.dynamic_index_in_dim(parted, (w + k) % size, 1, False)
        return mine.transpose(2, 0, 1, 3).reshape(seqs, 2 * chunk, -1)

    def places_of(k):
        pair = lax.dynamic_index_in_dim(block_pairs, ctx, 0, False)
        blocks = jnp.stack([pair, 2 * members - 1 - pair])
        core = (w + k) % size
        return (blocks[:, None] * block + core * chunk + jnp.arange(chunk)[None, :]).reshape(-1)

    x = rows_of(inputs[0], 0)
    half = HEAD_DIM // 2
    freqs = THETA ** (-jnp.arange(half, dtype=F4) / half)
    angles = places_of(0).astype(F4)[:, None] * freqs[None, :]
    cosine = jnp.tile(jnp.cos(angles), (1, LANES // half))
    sine = jnp.tile(
        jnp.concatenate([-jnp.sin(angles), jnp.sin(angles)], axis=1), (1, LANES // HEAD_DIM)
    )

    local = inner // size
    packed = jnp.concatenate([query_weight, key_weight, value_weight, out_weight.T], axis=1)
    packed = in_order(wt_gather(packed)).reshape(size, width, 4, local)
    packed = packed.transpose(1, 2, 0, 3).reshape(width, 4 * inner)
    qkv_weight = packed[:, : 3 * inner]
    out_full = packed[:, 3 * inner :].T

    msg, a1 = project(x, attn_gain[None], qkv_weight, cosine, sine, members, units)
    got = lax.all_to_all(msg, "ctx", 0, 0, tiled=True)
    blocks = wt_gather(got)
    inv = jnp.argsort(block_pairs).astype(jnp.int32)
    unit_slots = jnp.minimum((ctx + members * jnp.arange(units)) // heads, seqs - 1)
    unit_lengths = lengths[unit_slots]
    w_arg = w.astype(jnp.int32)[None]
    o_msg, kept, lse = attend(inv, unit_lengths, w_arg, blocks, units)
    o_got = lax.all_to_all(o_msg, "ctx", 0, 0, tiled=True)
    mixed, state, second_own = mix(o_got, x, out_full, ffn_gain[None])

    total_rows = rows * size
    second = jnp.concatenate(wt_gather(second_own.reshape(rows, width)))
    cots = []
    for k in range(size):
        valid = places_of(k)[None, :] < lengths[:, None]
        cots.append(
            jnp.where(valid[:, :, None], rows_of(cotangent[0], k), jnp.zeros((), BF)).reshape(
                rows, width
            )
        )
    cot = jnp.concatenate(cots)
    cot_float = cot.astype(F4)

    parted = routes[0].reshape(2, size, chunk, seqs, 2).transpose(1, 3, 0, 2, 4)
    chosen_all = parted.reshape(total_rows, 2)
    names = jnp.arange(experts, dtype=jnp.int32)
    picks_all = chosen_all[:, :, None] == names
    marks = jnp.any(picks_all, axis=1).astype(BF)
    index = jnp.arange(total_rows)
    before = dot((index[None, :] < index[:, None]).astype(BF), marks)
    order_all = jnp.sum(jnp.where(picks_all, before[:, None, :], 0.0), axis=-1).astype(jnp.int32)
    share = -(-CAPACITY // size)
    held = -(-share // 16) * 16
    inside = (order_all >= w * held) & (order_all < (w + 1) * held)
    target_all = jnp.where(inside, chosen_all * held + order_all - w * held, -1)

    def own_first(array):
        parts = array.reshape(size, rows, 2)
        parts = jnp.concatenate([parts, parts[:-1]]) if size > 1 else parts
        return lax.dynamic_slice_in_dim(parts, w, size, 0).reshape(total_rows, 2)

    chosen, target = own_first(chosen_all), own_first(target_all)
    picks = chosen[:, :, None] == names

    logits = dot(second, router_weight)
    selected = jnp.sum(jnp.where(picks, logits[:, None, :], 0.0), axis=-1)
    raised = jnp.exp(selected - jnp.max(selected, axis=-1, keepdims=True))
    gates = raised / jnp.sum(raised, axis=-1, keepdims=True)

    slot_ids = jnp.arange(experts * held, dtype=jnp.int32)
    hit_one = slot_ids[:, None] == target[None, :, 0]
    hit_two = slot_ids[:, None] == target[None, :, 1]
    spread = (hit_one | hit_two).astype(BF)
    slot_gate = jnp.sum(
        jnp.where(hit_one, gates[None, :, 0], 0.0) + jnp.where(hit_two, gates[None, :, 1], 0.0),
        axis=1,
    )
    routed = dot(spread, second).astype(BF)
    routed_cot = (dot(spread, cot) * slot_gate[:, None]).astype(BF)
    sent = jnp.concatenate([routed, routed_cot], axis=1).reshape(experts, held, 2 * width)
    groups = None
    if members != experts:
        groups = [[g * experts + e for e in range(experts)] for g in range(members // experts)]
    swap = functools.partial(
        lax.all_to_all,
        axis_name="ctx",
        split_axis=0,
        concat_axis=0,
        axis_index_groups=groups,
        tiled=True,
    )
    arrived = swap(sent).reshape(experts * held, 2 * width)
    xe, dye = arrived[:, :width], arrived[:, width:]

    expert = ctx % experts

    def whole_expert(weights):
        return wt_gather(lax.dynamic_index_in_dim(weights, expert, 0, False))

    gate_parts, up_parts, down_parts = (
        whole_expert(expert_gate),
        whole_expert(expert_up),
        whole_expert(expert_down),
    )
    ye, dxe = 0.0, 0.0
    expert_grads = []
    for k in range(size):
        ge, ue = dot(xe, gate_parts[k]), dot(xe, up_parts[k])
        he = swiglu(ge, ue).astype(BF)
        ye = ye + dot(he, down_parts[k])
        dhe = dot_nt(dye, down_parts[k])
        dge, due = swiglu_back(ge, ue, dhe)
        dxe = dxe + dot_nt(dge, gate_parts[k]) + dot_nt(due, up_parts[k])
        expert_grads.append((dge, due, he))
    returned = jnp.concatenate([ye.astype(BF), dxe.astype(BF)], axis=1)
    home = swap(returned.reshape(experts, held, 2 * width)).reshape(experts * held, 2 * width)

    gd, ud = dot(second, dense_gate), dot(second, dense_up)
    hd = swiglu(gd, ud).astype(BF)
    dense = dot(hd, dense_down)
    dgd, dud = swiglu_back(gd, ud, dot_nt(cot, dense_down))
    dense_back = dot_nt(dgd, dense_gate) + dot_nt(dud, dense_up)
    dense_grads = jnp.concatenate(
        [dot_tn(second, dgd), dot_tn(second, dud), dot_tn(cot, hd)], axis=1
    )
    dense_sum = lax.psum_scatter(dense_grads, "ctx", scatter_dimension=0, tiled=True)

    hits = target[:, :, None] == slot_ids
    picked = [dot(hits[:, c].astype(BF), home[:, :width]) for c in range(2)]
    moe = picked[0] * gates[:, :1] + picked[1] * gates[:, 1:]
    routed_back = dot(jnp.any(hits, axis=1).astype(BF), home[:, width:])
    gate_back = jnp.stack([jnp.sum(p * cot_float, axis=-1) for p in picked], axis=1)
    select_back = gates * (gate_back - jnp.sum(gates * gate_back, axis=-1, keepdims=True))
    logit_back = jnp.sum(jnp.where(picks, select_back[:, :, None], 0.0), axis=1)
    logit_high = logit_back.astype(BF)
    logit_low = (logit_back - logit_high.astype(F4)).astype(BF)
    logit_both = jnp.concatenate([logit_high, logit_low], axis=1)
    router_both = jnp.concatenate([router_weight, router_weight], axis=1)
    part_back = dense_back + routed_back + dot_nt(logit_both, router_both)
    router_grad = dot_tn(second, logit_both)
    router_grad = router_grad[:, :experts] + router_grad[:, experts:]
    both = jnp.stack([moe + dense, part_back], axis=1).reshape(size, rows, 2, width)
    both = wt_scatter([both[k] for k in range(size)])
    output = (state.reshape(rows, width) + both[:, 0]).astype(BF)
    da2 = both[:, 1].reshape(seqs, 2 * chunk, width)

    dstate, dstate_low, do_msg, ffn_grad = unmix(
        state, da2, cots[0].reshape(seqs, 2 * chunk, width), ffn_gain[None], out_full, members, units
    )
    do_got = lax.all_to_all(do_msg, "ctx", 0, 0, tiled=True)
    dq, *dkv = attend_back(inv, unit_lengths, w_arg, blocks, do_got, kept, lse, units)
    dkv = wt_scatter(dkv).astype(BF)
    grad_msg = jnp.concatenate([dkv, dq], axis=1)
    grad_got = lax.all_to_all(grad_msg, "ctx", 0, 0, tiled=True)
    dqkv, dx, attn_grad = unproject(grad_got, x, dstate, attn_gain[None], qkv_weight, cosine, sine)

    def split_wt(left, right, parts):
        cols = right.reshape(rows, parts, size, -1)
        pieces = []
        for k in range(size):
            mine = lax.dynamic_index_in_dim(cols, (w + k) % size, 2, False).reshape(rows, -1)
            made = dot_tn(left.reshape(rows, -1), mine)
            pieces.append(made if k == 0 else made.astype(BF))
        return wt_scatter(pieces)

    qkv_grad = split_wt(a1, dqkv, 3)
    out_grad = split_wt(dstate_low, mixed, 1)
    small = jnp.concatenate([attn_grad.T, ffn_grad.T, router_grad], axis=1)
    small = wt_sum(small)
    small_high = small.astype(BF)
    small_low = (small - small_high.astype(F4)).astype(BF)
    small = jnp.concatenate([small_high, small_low], axis=1)
    few = experts + 2
    small = jnp.pad(small, ((0, 0), (0, -(2 * few) % LANES)))
    mine_msg = jnp.concatenate([qkv_grad.astype(BF), out_grad.astype(BF), small], axis=1)
    mine_msg = mine_msg.reshape(members, width // members, -1)
    mine_got = lax.all_to_all(mine_msg, "ctx", 0, 0, tiled=True).astype(F4)
    mine_sum = jnp.sum(mine_got, axis=0)
    tail = mine_sum[:, 4 * local :]
    tail = tail[:, :few] + tail[:, few : 2 * few]

    expert_pieces = []
    for k in range(size):
        dge, due, he = expert_grads[k]
        made = jnp.stack([dot_tn(xe, dge), dot_tn(xe, due), dot_tn(dye, he)], axis=1)
        expert_pieces.append(made if k == 0 else made.astype(BF))
    expert_sum = wt_scatter(expert_pieces).astype(BF)
    hidden = expert_gate.shape[2]
    expert_msg = expert_sum.reshape(members, width // members, 3 * hidden)
    expert_got = lax.all_to_all(expert_msg, "ctx", 0, 0, tiled=True).astype(F4)
    expert_got = expert_got.reshape(members // experts, experts, width // members, 3, hidden)
    expert_got = jnp.sum(expert_got, axis=0)

    def to_tokens(own):
        array = in_order(wt_gather(own)).reshape(size, seqs, 2, chunk, width)
        return array.transpose(2, 0, 3, 1, 4).reshape(inputs.shape)

    dense_hidden = dense_gate.shape[1]
    return (
        to_tokens(output),
        to_tokens(dx),
        tail[:, 0],
        mine_sum[:, :local],
        mine_sum[:, local : 2 * local],
        mine_sum[:, 2 * local : 3 * local],
        mine_sum[:, 3 * local : 4 * local].T,
        tail[:, 1],
        tail[:, 2:],
        expert_got[:, :, 0],
        expert_got[:, :, 1],
        expert_got[:, :, 2].transpose(0, 2, 1),
        dense_sum[:, :dense_hidden],
        dense_sum[:, dense_hidden : 2 * dense_hidden],
        dense_sum[:, 2 * dense_hidden :].T,
    )


def solution(mesh):
    placed = (
        P("ctx", None, None, None),
        P("ctx", None, None, None),
        P(),
        P(),
        P("ctx", None, None, None),
        P(),
        P(None, "wt"),
        P(None, "wt"),
        P(None, "wt"),
        P("wt", None),
        P(),
        P(),
        P(None, None, "wt"),
        P(None, None, "wt"),
        P(None, "wt", None),
        P(None, "wt"),
        P(None, "wt"),
        P("wt", None),
    )
    return jax.shard_map(
        per_device,
        mesh=mesh,
        in_specs=placed,
        out_specs=(
            P("ctx", None, None, None),
            P("ctx", None, None, None),
            P("ctx"),
            P("ctx", "wt"),
            P("ctx", "wt"),
            P("ctx", "wt"),
            P("wt", "ctx"),
            P("ctx"),
            P("ctx", None),
            P(None, "ctx", "wt"),
            P(None, "ctx", "wt"),
            P(None, "wt", "ctx"),
            P("ctx", "wt"),
            P("ctx", "wt"),
            P("wt", "ctx"),
        ),
        check_vma=False,
    )
```

time: 5250 us -> 985 us (0.19)
  waiting for transfers between devices: 3840 us -> 272 us
  matrix products: 810 us -> 144 us
  other arithmetic: 206 us -> 52.8 us
  local copies, waits for them, and re-layouts: 309 us -> 167 us
  starting transfers between devices: 1.42 us -> 139 us
  Pallas kernels: 0 us -> 128 us
    reduce_scatter x11 -> x1, waiting for transfers between devices: 3480 us -> 36.7 us  [per_device(): lax.psum_scatter(dense_grads, 'ctx', scatter_dimension=0, tiled=True)]
    dot_general x105 -> x40, matrix products: 808 us -> 144 us  [the longest x16 61.5 us: dot(): return jnp.dot(a, b, preferred_element_type=F4)]
    all_gather x2 -> x0, waiting for transfers between devices: 344 us -> none  [the longest x1 176 us: per_device(): lax.all_gather(values_local, 'ctx', axis=0, tiled=True)]
    all_to_all x0 -> x7, waiting for transfers between devices: none -> 225 us  [the longest x1 68.1 us: per_device(): arrived = swap(sent).reshape(experts * held, 2 * width)]
    all_to_all x0 -> x7, starting transfers between devices: none -> 137 us  [the longest x1 46.9 us: per_device(): mine_got = lax.all_to_all(mine_msg, 'ctx', 0, 0, tiled=True).astype(F4)]
    pallas_call x0 -> x6, Pallas kernels: none -> 128 us  [the longest x1 54.9 us: attend(): pl.pallas_call(functools.partial(attend_kernel, members, size), grid_spec...]
    dynamic_update_slice x16 -> x0, local copies, waits for them, and re-layouts: 103 us -> none  [per_device(): lax.map(single, parts).reshape(rows_count, -1)]
    reduce_sum x17 -> x5, other arithmetic: 89.3 us -> 3.33 us  [the longest x1 2.13 us: per_device(): mine_sum = jnp.sum(mine_got, axis=0)]
  transfers between devices with their start and end apart: 18 -> 22, of which waited for: 15 -> 12; matrix products, arithmetic and copies ran while one was open for 9% -> 26% of each run, Pallas kernels for 0% -> 1%
where the time goes in v1:
time: 985 us; the launch traced here: 983 us
  waiting for transfers between devices  272 us (28%)
  local copies, waits for them, and re-layouts  167 us (17%)
  matrix products  144 us (15%)
  starting transfers between devices  139 us (14%)
  Pallas kernels  128 us (13%)
  blocking collectives  63.1 us (6%)
  other arithmetic  52.8 us (5%)
  between operations  16.3 us (2%)
    all_to_all x1, waiting for transfers between devices, per_device(): arrived = swap(sent).reshape(experts * held, 2 * width)  68.1 us
    all_to_all x1, blocking collectives, per_device(): got = lax.all_to_all(msg, 'ctx', 0, 0, tiled=True)  63.1 us
    dot_general x16, matrix products, dot(): return jnp.dot(a, b, preferred_element_type=F4)  61.5 us
    pallas_call x1, Pallas kernels, attend(): pl.pallas_call(functools.partial(attend_kernel, members, size), grid_spec...  54.9 us
    all_to_all x1, waiting for transfers between devices, per_device(): swap(returned.reshape(experts, held, 2 * width))  52 us
    all_to_all x1, starting transfers between devices, per_device(): mine_got = lax.all_to_all(mine_msg, 'ctx', 0, 0, tiled=True).astype(F4)  46.9 us
    dot_general x14, matrix products, dot_tn(): lax.dot_general(a, b, (((0,), (0,)), ((), ())), preferred_element_type=F4)  45.3 us
    pallas_call x1, Pallas kernels, attend_back(): pl.pallas_call(functools.partial(attend_back_kernel, members, size), grid...  42.6 us
  transfers between devices with their start and end apart: 22, of which 12 were waited for; matrix products, arithmetic and copies ran while one was open for 26% of the time, Pallas kernels for 1%

profile of v1, /device:TPU:0, one launch (start us, length us, event | category | flops | bytes accessed | tf_op | source)
XLA Modules:
  0.0 982.7 jit_solution(10518855449260764609)
XLA Ops:
  23.7 6.5 fusion.14
  30.2 12.6 %copy.209 = bf16[768,4,2,384]{3,2,1,0:T(2,128)(2,1)} copy(bf16[768,4,2,384]{0,3,1,2:T(8,128)(2,1)} %bitcast.200) | data formatting | bytes 9437184 | tf_op jit(solution)/shard_map/transpose | solution.py:636
  42.8 11.2 %reshape.453 = bf16[768,3072]{1,0:T(8,128)(2,1)} reshape(bf16[768,4,2,384]{3,2,1,0:T(2,128)(2,1)} %copy.209) | data formatting | bytes 9437184 | tf_op jit(solution)/shard_map/reshape | solution.py:636
  58.0 7.6 project.1
  65.7 63.1 %all_to_all.40.refs_0_ = bf16[16,9,64,128]{3,2,1,0:T(8,128)(2,1)} all-to-all(bf16[16,9,64,128]{3,2,1,0:T(8,128)(2,1)} %get-tuple-element.35), channel_id=1, replica_groups=mesh['ctx'=16,'wt'=2] {'ctx'}, dimensions={0} | all-to-all | bytes 4718592 | tf_op jit(solution)/shard_map/all_to_all | solution.py:641
  133.6 54.9 %attend.1 = (bf16[16,3,64,128]{3,2,1,0:T(8,128)(2,1)}, f32[3,8,64,256]{3,2,1,0:T(8,128)}, f32[3,8,1,256]{3,2,1,0:T(1,128)}) custom-call(s32[16]{0:T(128)} %get-tuple-element.34.inv_ref, s32[3]{0:T(128)} %gather_fusion, s32[1]{0:T(128)} %bitcast.1.w_ref, bf16[16,9,64,128]{3,2,1,0:T(8,128)(2,1)} %all_to_all.40.refs_0_, ...), custom_call_target="tpu_custom_call" | custom-call | tf_op jit(solution)/shard_map/attend/pallas_call | solution.py:256
  188.5 13.2 %all-to-all-start.1 = ((bf16[16,3,64,128]{3,2,1,0:T(8,128)(2,1)}), bf16[16,3,64,128]{3,2,1,0:T(8,128)(2,1)}, u32[]{:S(2)}, u32[]{:S(2)}) async-start(bf16[16,3,64,128]{3,2,1,0:T(8,128)(2,1)} %get-tuple-element.36), calls=%async_computation.1 | async-start | bytes 1572864 | tf_op jit(solution)/shard_map/all_to_all | solution.py:648
  207.7 14.1 %all-to-all-done.1.o_ref = bf16[16,3,64,128]{3,2,1,0:T(8,128)(2,1)} async-done(((bf16[16,3,64,128]{3,2,1,0:T(8,128)(2,1)}), bf16[16,3,64,128]{3,2,1,0:T(8,128)(2,1)}, u32[]{:S(2)}, u32[]{:S(2)}) %all-to-all-start.1) | async-done | bytes 786464 | tf_op jit(solution)/shard_map/all_to_all | solution.py:648
  221.8 5.1 mix.1
  238.8 6.4 copy.220
  245.2 5.0 all-to-all-start.2
  257.6 68.1 %all-to-all-done.2 = bf16[16,80,1536]{2,1,0:T(8,128)(2,1)} async-done(((bf16[16,80,1536]{2,1,0:T(8,128)(2,1)}), bf16[16,80,1536]{2,1,0:T(8,128)(2,1)}, u32[]{:S(2)}, u32[]{:S(2)}) %all-to-all-start.2) | async-done | bytes 3932192 | tf_op jit(solution)/shard_map/all_to_all | solution.py:712
  325.8 4.2 fusion.72
  333.8 6.5 multiply_convert_fusion.3
  340.4 6.8 fusion.68
  351.0 6.6 fusion.57
  361.2 4.3 fusion.103
  365.5 7.3 multiply_convert_fusion.2
  372.9 5.0 fusion.106
  388.2 6.3 copy.221
  394.5 19.3 %all-to-all-start.3 = ((bf16[16,80,1536]{2,1,0:T(8,128)(2,1)}), bf16[16,80,1536]{2,1,0:T(8,128)(2,1)}, u32[]{:S(2)}, u32[]{:S(2)}) async-start(bf16[16,80,1536]{2,1,0:T(8,128)(2,1)} %bitcast.202), calls=%async_computation.3 | async-start | bytes 7864320 | tf_op jit(solution)/shard_map/all_to_all | solution.py:736
  422.9 5.9 multiply_convert_fusion.5
  435.8 52.0 %all-to-all-done.3 = bf16[16,80,1536]{2,1,0:T(8,128)(2,1)} async-done(((bf16[16,80,1536]{2,1,0:T(8,128)(2,1)}), bf16[16,80,1536]{2,1,0:T(8,128)(2,1)}, u32[]{:S(2)}, u32[]{:S(2)}) %all-to-all-start.3) | async-done | bytes 3932192 | tf_op jit(solution)/shard_map/all_to_all | solution.py:736
  491.8 4.2 fusion.10
  496.0 4.7 fusion.33
  514.0 6.5 unmix.1
  520.6 18.1 %all-to-all-start.4 = ((bf16[16,3,64,128]{3,2,1,0:T(8,128)(2,1)}), bf16[16,3,64,128]{3,2,1,0:T(8,128)(2,1)S(1)}, u32[]{:S(2)}, u32[]{:S(2)}) async-start(bf16[16,3,64,128]{3,2,1,0:T(8,128)(2,1)} %get-tuple-element.39), calls=%async_computation.4 | async-start | bytes 1572864 | tf_op jit(solution)/shard_map/all_to_all | solution.py:770
  538.8 5.2 fusion.91
  547.6 11.1 %all-to-all-done.4.refs_2_ = bf16[16,3,64,128]{3,2,1,0:T(8,128)(2,1)S(1)} async-done(((bf16[16,3,64,128]{3,2,1,0:T(8,128)(2,1)}), bf16[16,3,64,128]{3,2,1,0:T(8,128)(2,1)S(1)}, u32[]{:S(2)}, u32[]{:S(2)}) %all-to-all-start.4) | async-done | bytes 786464 | tf_op jit(solution)/shard_map/all_to_all | solution.py:770
  559.6 42.6 %attend_back.1 = (bf16[16,3,64,128]{3,2,1,0:T(8,128)(2,1)}, f32[16,6,64,128]{3,2,1,0:T(8,128)}, f32[16,6,64,128]{3,2,1,0:T(8,128)}) custom-call(s32[16]{0:T(128)} %get-tuple-element.34.inv_ref, s32[3]{0:T(128)} %gather_fusion, s32[1]{0:T(128)} %bitcast.1.w_ref, bf16[16,9,64,128]{3,2,1,0:T(8,128)(2,1)} %all_to_all.40.refs_0_, ...), custom_call_target="tpu_custom_call" | custom-call | tf_op jit(solution)/shard_map/attend_back/pallas_call | solution.py:381
  605.7 8.6 pad_maximum_fusion
  614.3 4.7 fusion.54
  634.6 20.8 %all-to-all-start.5 = ((bf16[16,9,64,128]{3,2,1,0:T(8,128)(2,1)}), bf16[16,9,64,128]{3,2,1,0:T(8,128)(2,1)}, u32[]{:S(2)}, u32[]{:S(2)}) async-start(bf16[16,9,64,128]{3,2,1,0:T(8,128)(2,1)} %pad_maximum_fusion.6), calls=%async_computation.5 | async-start | bytes 4718592 | tf_op jit(solution)/shard_map/all_to_all | solution.py:774
  655.5 4.8 convolution_bitcast_fusion
  671.8 6.7 copy.233
  678.5 13.6 %reshape.478 = bf16[16,48,3072]{2,1,0:T(8,128)(2,1)} reshape(bf16[768,3,1024]{2,1,0:T(4,128)(2,1)} %copy.233) | data formatting | bytes 9437184 | tf_op jit(solution)/shard_map/reshape | solution.py:809
  692.1 41.6 %all-to-all-done.5.msg_ref = bf16[16,9,64,128]{3,2,1,0:T(8,128)(2,1)} async-done(((bf16[16,9,64,128]{3,2,1,0:T(8,128)(2,1)}), bf16[16,9,64,128]{3,2,1,0:T(8,128)(2,1)}, u32[]{:S(2)}, u32[]{:S(2)}) %all-to-all-start.5) | async-done | bytes 2359328 | tf_op jit(solution)/shard_map/all_to_all | solution.py:774
  733.7 13.5 %all-to-all-start.7 = ((bf16[16,48,3072]{2,1,0:T(8,128)(2,1)}), bf16[16,48,3072]{2,1,0:T(8,128)(2,1)}, u32[]{:S(2)}, u32[]{:S(2)}) async-start(bf16[16,48,3072]{2,1,0:T(8,128)(2,1)} %reshape.478), calls=%async_computation.7 | async-start | bytes 9437184 | tf_op jit(solution)/shard_map/all_to_all | solution.py:810
  747.3 11.0 %unproject.1 = (bf16[4,128,2304]{2,1,0:T(8,128)(2,1)}, bf16[4,128,768]{2,1,0:T(8,128)(2,1)}, f32[1,768]{1,0:T(1,128)}) custom-call(bf16[16,9,64,128]{3,2,1,0:T(8,128)(2,1)} %all-to-all-done.5.msg_ref, bf16[4,128,768]{2,1,0:T(8,128)(2,1)} %bitcast.206, f32[4,128,768]{2,1,0:T(8,128)} %get-tuple-element.45.dstate_ref, f32[1,768]{1,0:T(1,128)} %broadcast_in_dim.117.gain_ref, ...), custom_call_target="tpu_custom_call" | custom-call | tf_op jit(solution)/shard_map/unproject/pallas_call | solution.py:545
  758.3 5.6 reshape.470
  763.8 9.5 constant_dynamic-slice_fusion.2
  773.4 5.5 copy.243
  787.9 5.7 copy.242
  798.3 37.6 %all-to-all-done.7 = bf16[16,48,3072]{2,1,0:T(8,128)(2,1)} async-done(((bf16[16,48,3072]{2,1,0:T(8,128)(2,1)}), bf16[16,48,3072]{2,1,0:T(8,128)(2,1)}, u32[]{:S(2)}, u32[]{:S(2)}) %all-to-all-start.7) | async-done | bytes 4718624 | tf_op jit(solution)/shard_map/all_to_all | solution.py:810
  835.9 46.9 %all-to-all-start.6 = ((bf16[16,48,1664]{2,1,0:T(8,128)(2,1)}), bf16[16,48,1664]{2,1,0:T(8,128)(2,1)}, u32[]{:S(2)}, u32[]{:S(2)}) async-start(bf16[16,48,1664]{2,1,0:T(8,128)(2,1)} %bitcast.207), calls=%async_computation.6 | async-start | bytes 5111808 | tf_op jit(solution)/shard_map/all_to_all | solution.py:797
  890.4 36.7 %reduce-scatter.2.cloned.1.call-done = f32[48,3072]{1,0:T(8,128)} async-done(((f32[768,3072]{1,0:T(8,128)}), f32[48,3072]{1,0:T(8,128)}) %reduce-scatter.2.cloned.1.call-update) | async-done | bytes 589840 | tf_op jit(solution)/shard_map/reduce_scatter | solution.py:746
  929.0 15.3 %reshape.479 = f32[16,48,3,1024]{3,2,1,0:T(4,128)} reshape(bf16[16,48,3072]{2,1,0:T(8,128)(2,1)} %all-to-all-done.7) | data formatting | bytes 14155776 | tf_op jit(solution)/shard_map/reduce_sum | solution.py:812
  944.4 16.2 %fusion.99 = (f32[16,48,1,1024]{3,2,1,0:T(1,128)S(1)}, f32[16,48,1,1024]{3,2,1,0:T(1,128)S(1)}, f32[16,48,1,1024]{3,2,1,0:T(1,128)S(1)}) fusion(f32[16,48,3,1024]{3,2,1,0:T(4,128)} %reshape.479), kind=kLoop, calls=%fused_computation.216 | loop fusion | bytes 18874368 | tf_op jit(solution)/shard_map/slice | solution.py:831
  (302 shorter events, 177.2 us)
Async XLA Ops:
  7.2 415.7 %copy-start = (bf16[768,1024]{1,0:T(8,128)(2,1)S(1)}, bf16[768,1024]{1,0:T(8,128)(2,1)}, u32[]{:S(2)}) copy-start(bf16[768,1024]{1,0:T(8,128)(2,1)} %param.34) | copy-start | bytes 4718596
  14.6 9.1 collective-permute-start
  22.1 181.0 %copy-start.40 = (s32[128]{0:T(128)}, s32[128]{0:T(128)S(1)}, u32[]{:S(2)}) copy-start(s32[128]{0:T(128)S(1)} %add.278) | copy-start | bytes 1540
  65.7 63.1 %copy-start.35 = (s32[1,256,4,2]{1,3,2,0:T(2,128)S(1)}, s32[1,256,4,2]{1,3,2,0:T(2,128)}, u32[]{:S(2)}) copy-start(s32[1,256,4,2]{1,3,2,0:T(2,128)} %param.22) | copy-start | bytes 24580
  65.7 64.7 %copy-start.2 = (s32[4]{0:T(128)S(1)}, s32[4]{0:T(128)}, u32[]{:S(2)}) copy-start(s32[4]{0:T(128)} %param.20) | copy-start | bytes 52
  128.7 4.9 collective-permute-start.1
  133.6 68.7 %copy-start.37 = (f32[768]{0:T(1024)S(1)}, f32[768]{0:T(1024)}, u32[]{:S(2)}) copy-start(f32[768]{0:T(1024)} %param.28) | copy-start | bytes 9220
  188.5 33.3 %all-to-all-start.1 = ((bf16[16,3,64,128]{3,2,1,0:T(8,128)(2,1)}), bf16[16,3,64,128]{3,2,1,0:T(8,128)(2,1)}, u32[]{:S(2)}, u32[]{:S(2)}) async-start(bf16[16,3,64,128]{3,2,1,0:T(8,128)(2,1)} %get-tuple-element.36), calls=%async_computation.1 | async-start | bytes 1572864 | tf_op jit(solution)/shard_map/all_to_all | solution.py:648
  207.7 19.2 %copy-start.29 = (s32[2,512,2]{1,2,0:T(2,128)S(1)}, s32[2,512,2]{1,2,0:T(2,128)}, u32[]{:S(2)}) copy-start(s32[2,512,2]{1,2,0:T(2,128)} %get-tuple-element.183) | copy-start | bytes 24580
  207.7 19.2 %copy-start.32 = (s32[1,512,2]{1,2,0:T(2,128)S(1)}, s32[1,512,2]{1,2,0:T(2,128)}, u32[]{:S(2)}) copy-start(s32[1,512,2]{1,2,0:T(2,128)} %fusion.85) | copy-start | bytes 12292
  207.7 19.3 %copy-start.9 = (bf16[2,1,64,4,768]{4,3,2,1,0:T(4,128)(2,1)S(1)}, bf16[2,1,64,4,768]{4,3,2,1,0:T(4,128)(2,1)}, u32[]{:S(2)}) copy-start(bf16[2,1,64,4,768]{4,3,2,1,0:T(4,128)(2,1)} %get-tuple-element.164) | copy-start | bytes 2359300
  207.7 19.5 %copy-start.39 = (pred[512]{0:T(512)(128)(4,1)S(1)}, pred[512]{0:T(512)(128)(4,1)}, u32[]{:S(2)}) copy-start(pred[512]{0:T(512)(128)(4,1)} %get-tuple-element.190) | copy-start | bytes 1540
  226.9 2.5 collective-permute-start.2
  227.3 6.7 copy-start.22
  227.7 6.3 copy-start.25
  245.2 80.6 %all-to-all-start.2 = ((bf16[16,80,1536]{2,1,0:T(8,128)(2,1)}), bf16[16,80,1536]{2,1,0:T(8,128)(2,1)}, u32[]{:S(2)}, u32[]{:S(2)}) async-start(bf16[16,80,1536]{2,1,0:T(8,128)(2,1)} %bitcast.201), calls=%async_computation.2 | async-start | bytes 7864320 | tf_op jit(solution)/shard_map/all_to_all | solution.py:712
  252.9 87.6 %collective-permute-start.3 = (bf16[768,1024]{1,0:T(8,128)(2,1)}, bf16[768,1024]{1,0:T(8,128)(2,1)}, u32[]{:S(2)}, u32[]{:S(2)}) collective-permute-start(bf16[768,1024]{1,0:T(8,128)(2,1)} %dynamic-slice_bitcast_fusion.2), channel_id=1, source_target_pairs={{0,1},{1,0},{2,3},{3,2},{4,5},{5,4},{6,7},{7,6},{8,9},{9,8},{10,11... | collective-permute-start | bytes 4718600 | tf_op jit(solution)/shard_map/ppermute | solution.py:37
  254.4 96.6 %collective-permute-start.5 = (bf16[1024,768]{1,0:T(8,128)(2,1)S(1)}, bf16[1024,768]{1,0:T(8,128)(2,1)}, u32[]{:S(2)}, u32[]{:S(2)}) collective-permute-start(bf16[1024,768]{1,0:T(8,128)(2,1)S(1)} %dynamic-slice_bitcast_fusion), channel_id=1, source_target_pairs={{0,1},{1,0},{2,3},{3,2},{4,5},{5,4},{6,7},{7,6},{8,9},{9,8},{10,11... | collective-permute-start | bytes 4718600 | tf_op jit(solution)/shard_map/ppermute | solution.py:37
  257.6 107.9 %collective-permute-start.4 = (bf16[768,1024]{1,0:T(8,128)(2,1)}, bf16[768,1024]{1,0:T(8,128)(2,1)}, u32[]{:S(2)}, u32[]{:S(2)}) collective-permute-start(bf16[768,1024]{1,0:T(8,128)(2,1)} %dynamic-slice_bitcast_fusion.1), channel_id=1, source_target_pairs={{0,1},{1,0},{2,3},{3,2},{4,5},{5,4},{6,7},{7,6},{8,9},{9,8},{10,11... | collective-permute-start | bytes 4718600 | tf_op jit(solution)/shard_map/ppermute | solution.py:37
  340.4 6.9 copy-start.15
  340.4 17.2 %copy-start.17 = (bf16[1280,1024]{1,0:T(8,128)(2,1)}, bf16[1280,1024]{1,0:T(8,128)(2,1)S(1)}, u32[]{:S(2)}) copy-start(bf16[1280,1024]{1,0:T(8,128)(2,1)S(1)} %get-tuple-element.155) | copy-start | bytes 7864324
  340.4 20.8 %copy-start.19 = (bf16[1280,1024]{1,0:T(8,128)(2,1)}, bf16[1280,1024]{1,0:T(8,128)(2,1)S(1)}, u32[]{:S(2)}) copy-start(bf16[1280,1024]{1,0:T(8,128)(2,1)S(1)} %get-tuple-element.153) | copy-start | bytes 7864324
  372.9 9.2 copy-start.59
  372.9 5.3 copy-start.70
  394.5 19.3 %copy-start.23 = (bf16[512,768]{1,0:T(8,128)(2,1)S(1)}, bf16[512,768]{1,0:T(8,128)(2,1)}, u32[]{:S(2)}) copy-start(bf16[512,768]{1,0:T(8,128)(2,1)} %copy-done.22) | copy-start | bytes 2359300
  394.5 19.4 %copy-start.26 = (bf16[512,768]{1,0:T(8,128)(2,1)S(1)}, bf16[512,768]{1,0:T(8,128)(2,1)}, u32[]{:S(2)}) copy-start(bf16[512,768]{1,0:T(8,128)(2,1)} %copy-done.25) | copy-start | bytes 2359300
  394.5 93.4 %all-to-all-start.3 = ((bf16[16,80,1536]{2,1,0:T(8,128)(2,1)}), bf16[16,80,1536]{2,1,0:T(8,128)(2,1)}, u32[]{:S(2)}, u32[]{:S(2)}) async-start(bf16[16,80,1536]{2,1,0:T(8,128)(2,1)} %bitcast.202), calls=%async_computation.3 | async-start | bytes 7864320 | tf_op jit(solution)/shard_map/all_to_all | solution.py:736
  505.0 5.7 collective-permute-start.6
  520.6 38.1 %all-to-all-start.4 = ((bf16[16,3,64,128]{3,2,1,0:T(8,128)(2,1)}), bf16[16,3,64,128]{3,2,1,0:T(8,128)(2,1)S(1)}, u32[]{:S(2)}, u32[]{:S(2)}) async-start(bf16[16,3,64,128]{3,2,1,0:T(8,128)(2,1)} %get-tuple-element.39), calls=%async_computation.4 | async-start | bytes 1572864 | tf_op jit(solution)/shard_map/all_to_all | solution.py:770
  538.7 5.3 copy-start.49
  538.7 388.4 %reduce-scatter.2.cloned.1.call-start = ((), (), s32[]{:S(2)}) async-start(), calls=%async_computation.9 | async-start | bytes 10027008 | tf_op jit(solution)/shard_map/reduce_scatter | solution.py:746
  559.6 42.6 %copy-start.55 = (bf16[512,768]{1,0:T(8,128)(2,1)S(1)}, bf16[512,768]{1,0:T(8,128)(2,1)}, u32[]{:S(2)}) copy-start(bf16[512,768]{1,0:T(8,128)(2,1)} %copy-done.51) | copy-start | bytes 2359300
  559.6 42.6 %copy-start.63 = (bf16[1024,1024]{1,0:T(8,128)(2,1)S(1)}, bf16[1024,1024]{1,0:T(8,128)(2,1)}, u32[]{:S(2)}) copy-start(bf16[1024,1024]{1,0:T(8,128)(2,1)} %copy-done.62) | copy-start | bytes 6291460
  602.2 27.8 %collective-permute-start.8 = (f32[16,6,64,128]{3,2,1,0:T(8,128)}, f32[16,6,64,128]{3,2,1,0:T(8,128)}, u32[]{:S(2)}, u32[]{:S(2)}) collective-permute-start(f32[16,6,64,128]{3,2,1,0:T(8,128)} %get-tuple-element.43), channel_id=1, source_target_pairs={{0,1},{1,0},{2,3},{3,2},{4,5},{5,4},{6,7},{7,6},{8,9},{9,8},{10,11... | collective-permute-start | bytes 9437192 | tf_op jit(solution)/shard_map/ppermute | solution.py:45
  629.5 38.6 %collective-permute-start.13 = (bf16[768,3,1024]{2,0,1:T(8,128)(2,1)}, bf16[768,3,1024]{2,0,1:T(8,128)(2,1)}, u32[]{:S(2)}, u32[]{:S(2)}) collective-permute-start(bf16[768,3,1024]{2,0,1:T(8,128)(2,1)} %pad_maximum_fusion.1), channel_id=1, source_target_pairs={{0,1},{1,0},{2,3},{3,2},{4,5},{5,4},{6,7},{7,6},{8,9},{9,8},{10,11... | collective-permute-start | bytes 14155784 | tf_op jit(solution)/shard_map/ppermute | solution.py:45
  634.6 99.1 %all-to-all-start.5 = ((bf16[16,9,64,128]{3,2,1,0:T(8,128)(2,1)}), bf16[16,9,64,128]{3,2,1,0:T(8,128)(2,1)}, u32[]{:S(2)}, u32[]{:S(2)}) async-start(bf16[16,9,64,128]{3,2,1,0:T(8,128)(2,1)} %pad_maximum_fusion.6), calls=%async_computation.5 | async-start | bytes 4718592 | tf_op jit(solution)/shard_map/all_to_all | solution.py:774
  733.7 102.2 %all-to-all-start.7 = ((bf16[16,48,3072]{2,1,0:T(8,128)(2,1)}), bf16[16,48,3072]{2,1,0:T(8,128)(2,1)}, u32[]{:S(2)}, u32[]{:S(2)}) async-start(bf16[16,48,3072]{2,1,0:T(8,128)(2,1)} %reshape.478), calls=%async_computation.7 | async-start | bytes 9437184 | tf_op jit(solution)/shard_map/all_to_all | solution.py:810
  773.4 5.6 copy-start.44
  781.4 12.5 %collective-permute-start.10 = (bf16[768,1152]{1,0:T(8,128)(2,1)}, bf16[768,1152]{1,0:T(8,128)(2,1)}, u32[]{:S(2)}, u32[]{:S(2)}) collective-permute-start(bf16[768,1152]{1,0:T(8,128)(2,1)} %convolution_convert_fusion), channel_id=1, source_target_pairs={{0,1},{1,0},{2,3},{3,2},{4,5},{5,4},{6,7},{7,6},{8,9},{9,8},{10,11... | collective-permute-start | bytes 5308424 | tf_op jit(solution)/shard_map/ppermute | solution.py:45
  785.1 2.2 collective-permute-start.11
  786.1 7.5 collective-permute-start.12
  787.9 6.0 copy-start.45
  798.3 84.5 %copy-start.6 = (f32[4,128,768]{2,1,0:T(8,128)S(1)}, f32[4,128,768]{2,1,0:T(8,128)}, u32[]{:S(2)}) copy-start(f32[4,128,768]{2,1,0:T(8,128)} %get-tuple-element.37.state_ref) | copy-start | bytes 4718596
  835.9 135.3 %all-to-all-start.6 = ((bf16[16,48,1664]{2,1,0:T(8,128)(2,1)}), bf16[16,48,1664]{2,1,0:T(8,128)(2,1)}, u32[]{:S(2)}, u32[]{:S(2)}) async-start(bf16[16,48,1664]{2,1,0:T(8,128)(2,1)} %bitcast.207), calls=%async_computation.6 | async-start | bytes 5111808 | tf_op jit(solution)/shard_map/all_to_all | solution.py:797
  884.7 2.4 collective-permute-start.7
  929.0 15.3 %copy-start.28 = (bf16[4,128,768]{2,1,0:T(8,128)(2,1)S(1)}, bf16[4,128,768]{2,1,0:T(8,128)(2,1)}, u32[]{:S(2)}) copy-start(bf16[4,128,768]{2,1,0:T(8,128)(2,1)} %get-tuple-element.46) | copy-start | bytes 2359300
  944.4 23.5 %collective-permute-start.9 = (bf16[4,128,768]{2,1,0:T(8,128)(2,1)S(1)}, bf16[4,128,768]{2,1,0:T(8,128)(2,1)S(1)}, u32[]{:S(2)}, u32[]{:S(2)}) collective-permute-start(bf16[4,128,768]{2,1,0:T(8,128)(2,1)S(1)} %copy-done.28), channel_id=1, source_target_pairs={{0,1},{1,0},{2,3},{3,2},{4,5},{5,4},{6,7},{7,6},{8,9},{9,8},{10,11... | collective-permute-start | bytes 2359304 | tf_op jit(solution)/shard_map/ppermute | solution.py:37
  968.8 6.7 copy-start.1
  (45 other events, 148.0 us)
Sparse Core Ops, SparseCore 0:
  614.4 312.6 reduce-scatter.1

commit v2 on v1

--- a/solution.py
+++ b/solution.py
@@ -90,63 +90,67 @@
     return pl.BlockSpec(shape, lambda *i: (0,) * len(shape))
 
 
-def project_kernel(members, heads, units, x_ref, gain_ref, w_ref, cos_ref, sin_ref, msg_ref, a1_ref):
-    s = pl.program_id(0)
-    rows = x_ref.shape[1]
+def head_units(seqs, heads, members, shift, s, rel):
+    unit = s * heads + lax.rem(rel + shift, heads)
+    return lax.rem(unit, members), lax.div(unit, members)
+
+
+def project_kernel(heads, units, members, count, shift_ref, x_ref, gain_ref, cos_ref, sin_ref, *refs):
+    w_refs = refs[: 3 * count]
+    msg_ref, a1_ref = refs[3 * count :]
+    seqs, rows, width = x_ref.shape
     chunk = rows // 2
-    width = heads * HEAD_DIM
-    x = x_ref[0].astype(F4)
-    scale = lax.rsqrt(jnp.mean(x * x, axis=-1, keepdims=True) + EPS)
-    a1 = (x * scale * gain_ref[...]).astype(BF)
-    a1_ref[0] = a1
+    for s in range(seqs):
+        x = x_ref[s].astype(F4)
+        scale = lax.rsqrt(jnp.mean(x * x, axis=-1, keepdims=True) + EPS)
+        a1_ref[s] = (x * scale * gain_ref[...]).astype(BF)
+    if units * members > heads * seqs:
+        msg_ref[...] = jnp.zeros_like(msg_ref)
+    a1 = a1_ref[...].reshape(seqs * rows, width)
     cosine, sine = cos_ref[...], sin_ref[...]
-    query = dot(a1, w_ref[:, :width])
-    key = dot(a1, w_ref[:, width : 2 * width])
-    value = dot(a1, w_ref[:, 2 * width :])
-    if units * members > (heads * pl.num_programs(0)):
-
-        @pl.when(s == 0)
-        def _():
-            msg_ref[...] = jnp.zeros_like(msg_ref)
 
     def rope(t):
         return t * cosine + turn_halves(t) * sine
 
-    for g in range(heads // 2):
-        part = slice(g * LANES, (g + 1) * LANES)
-        pairs = pair_swap(rope(key[:, part]), value[:, part])
-        turned = rope(query[:, part])
-        asked = pair_swap(turned[:chunk], turned[chunk:])
-        for c in range(2):
-            unit = s * heads + 2 * g + c
-            chip, u = unit % members, unit // members
-            msg_ref[chip, 3 * u] = pairs[c][:chunk].astype(BF)
-            msg_ref[chip, 3 * u + 1] = pairs[c][chunk:].astype(BF)
-            msg_ref[chip, 3 * u + 2] = asked[c].astype(BF)
-
-
-def project(x, gain, weights, cosine, sine, members, units):
+    per = heads // count
+    for k in range(count):
+        query, key, value = (dot(a1, ref[...]) for ref in w_refs[3 * k : 3 * k + 3])
+        for s in range(seqs):
+            mine = slice(s * rows, (s + 1) * rows)
+            for g in range(per // 2):
+                part = slice(g * LANES, (g + 1) * LANES)
+                pairs = pair_swap(rope(key[mine, part]), value[mine, part])
+                turned = rope(query[mine, part])
+                asked = pair_swap(turned[:chunk], turned[chunk:])
+                for c in range(2):
+                    chip, u = head_units(
+                        seqs, heads, members, shift_ref[0], s, k * per + 2 * g + c
+                    )
+                    msg_ref[chip, 3 * u] = pairs[c][:chunk].astype(BF)
+                    msg_ref[chip, 3 * u + 1] = pairs[c][chunk:].astype(BF)
+                    msg_ref[chip, 3 * u + 2] = asked[c].astype(BF)
+
+
+SMEM = pl.BlockSpec(memory_space=pltpu.SMEM)
+VMEM = pl.BlockSpec(memory_space=pltpu.VMEM)
+
+
+def project(shift, x, gain, cosine, sine, parts, members, units):
     seqs, rows, width = x.shape
-    heads = weights.shape[1] // 3 // HEAD_DIM
-    msg = (members, 3 * units, rows // 2, LANES)
+    count = len(parts)
+    heads = sum(part[0].shape[1] for part in parts) // HEAD_DIM
+    flat = [w for part in parts for w in part]
     return pl.pallas_call(
-        functools.partial(project_kernel, members, heads, units),
-        grid=(seqs,),
-        in_specs=[
-            pl.BlockSpec((1, rows, width), lambda s: (s, 0, 0)),
-            whole((1, width)),
-            whole(weights.shape),
-            whole(cosine.shape),
-            whole(sine.shape),
-        ],
-        out_specs=[whole(msg), pl.BlockSpec((1, rows, width), lambda s: (s, 0, 0))],
+        functools.partial(project_kernel, heads, units, members, count),
+        in_specs=[SMEM] + [VMEM] * (4 + len(flat)),
+        out_specs=[VMEM, VMEM],
         out_shape=[
-            jax.ShapeDtypeStruct(msg, BF),
+            jax.ShapeDtypeStruct((members, 3 * units, rows // 2, LANES), BF),
             jax.ShapeDtypeStruct((seqs, rows, width), BF),
         ],
-        compiler_params=params(1),
+        compiler_params=params(0),
         name="project",
-    )(x, gain, weights, cosine, sine)
+    )(shift, x, gain, cosine, sine, *flat)
 
 
 def gather_keys(inv_ref, w, kv_refs, kv_s, members, chunk):
@@ -406,42 +410,48 @@
     )(inv, lengths, w, *blocks, do_msg, kept, lse)
 
 
-def mix_kernel(members, heads, o_ref, x_ref, w_ref, gain_ref, mixed_ref, state_ref, a2_ref):
-    s = pl.program_id(0)
-    chunk = o_ref.shape[2]
-    for g in range(heads // 2):
-        pair = []
-        for c in range(2):
-            unit = s * heads + 2 * g + c
-            pair.append(o_ref[unit % members, unit // members].astype(F4))
-        early, late = pair_swap(*pair)
-        part = slice(g * LANES, (g + 1) * LANES)
-        mixed_ref[0, :chunk, part] = early.astype(BF)
-        mixed_ref[0, chunk:, part] = late.astype(BF)
-    state = x_ref[0].astype(F4) + dot(mixed_ref[0], w_ref[...])
-    state_ref[0] = state
-    scale = lax.rsqrt(jnp.mean(state * state, axis=-1, keepdims=True) + EPS)
-    a2_ref[0] = (state * scale * gain_ref[...]).astype(BF)
-
-
-def mix(o_msg, x, out_weight, gain):
-    members, units, chunk, _ = o_msg.shape
+def mix_kernel(heads, count, shift_ref, o_ref, x_ref, gain_ref, *refs):
+    w_refs = refs[:count]
+    mixed_ref, state_ref, a2_ref = refs[count:]
+    members, _, chunk, _ = o_ref.shape
+    seqs, rows, width = x_ref.shape
+    for s in range(seqs):
+        for g in range(heads // 2):
+            pair = []
+            for c in range(2):
+                chip, u = head_units(seqs, heads, members, shift_ref[0], s, 2 * g + c)
+                pair.append(o_ref[chip, u].astype(F4))
+            early, late = pair_swap(*pair)
+            part = slice(g * LANES, (g + 1) * LANES)
+            mixed_ref[s, :chunk, part] = early.astype(BF)
+            mixed_ref[s, chunk:, part] = late.astype(BF)
+    inner = heads * HEAD_DIM // count
+    made = 0.0
+    for k in range(count):
+        mixed = mixed_ref[:, :, k * inner : (k + 1) * inner].reshape(seqs * rows, inner)
+        made = made + dot(mixed, w_refs[k][...])
+    for s in range(seqs):
+        state = x_ref[s].astype(F4) + made[s * rows : (s + 1) * rows]
+        state_ref[s] = state
+        scale = lax.rsqrt(jnp.mean(state * state, axis=-1, keepdims=True) + EPS)
+        a2_ref[s] = (state * scale * gain_ref[...]).astype(BF)
+
+
+def mix(shift, o_msg, x, gain, parts):
     seqs, rows, width = x.shape
-    inner = out_weight.shape[0]
-    per_slot = pl.BlockSpec((1, rows, width), lambda s: (s, 0, 0))
+    inner = sum(part.shape[0] for part in parts)
     return pl.pallas_call(
-        functools.partial(mix_kernel, members, inner // HEAD_DIM),
-        grid=(seqs,),
-        in_specs=[whole(o_msg.shape), per_slot, whole(out_weight.shape), whole((1, width))],
-        out_specs=[pl.BlockSpec((1, rows, inner), lambda s: (s, 0, 0)), per_slot, per_slot],
+        functools.partial(mix_kernel, inner // HEAD_DIM, len(parts)),
+        in_specs=[SMEM] + [VMEM] * (3 + len(parts)),
+        out_specs=[VMEM] * 3,
         out_shape=[
             jax.ShapeDtypeStruct((seqs, rows, inner), BF),
             jax.ShapeDtypeStruct((seqs, rows, width), F4),
             jax.ShapeDtypeStruct((seqs, rows, width), BF),
         ],
-        compiler_params=params(1),
+        compiler_params=params(0),
         name="mix",
-    )(o_msg, x, out_weight, gain)
+    )(shift, o_msg, x, gain, *parts)
 
 
 def norm_back(values, gain, upstream):
@@ -452,131 +462,360 @@
     return result, jnp.sum(upstream * unit, axis=0, keepdims=True)
 
 
-def unmix_kernel(members, heads, state_ref, da2_ref, cot_ref, gain_ref, w_ref, *outs):
-    dstate_ref, low_ref, msg_ref, dgain_ref = outs
-    s = pl.program_id(0)
-    rows = state_ref.shape[1]
-    chunk = rows // 2
-    pulled, dgain = norm_back(state_ref[0], gain_ref[...], da2_ref[0])
-    dstate = cot_ref[0].astype(F4) + pulled
-    dstate_ref[0] = dstate
+def unrotate_kernel(heads, count, shift_ref, msg_ref, cos_ref, sin_ref, dqkv_ref):
+    members, triple, chunk, _ = msg_ref.shape
+    units = triple // 3
+    seqs = dqkv_ref.shape[0]
+    cosine, sine = cos_ref[...], sin_ref[...]
+    per = heads // count
+    inner = per * HEAD_DIM
+
+    def rope_back(grad):
+        return grad * cosine - turn_halves(grad) * sine
+
+    for k in range(count):
+        for s in range(seqs):
+            for g in range(per // 2):
+                pair, asked = [], []
+                for c in range(2):
+                    chip, u = head_units(
+                        seqs, heads, members, shift_ref[0], s, k * per + 2 * g + c
+                    )
+                    both = [msg_ref[chip, 2 * u], msg_ref[chip, 2 * u + 1]]
+                    pair.append(jnp.concatenate(both, axis=0).astype(F4))
+                    asked.append(msg_ref[chip, 2 * units + u].astype(F4))
+                key, value = pair_swap(*pair)
+                query = jnp.concatenate(pair_swap(*asked), axis=0)
+                at = 3 * k * inner + g * LANES
+                dqkv_ref[s, :, at : at + LANES] = rope_back(query).astype(BF)
+                at = at + inner
+                dqkv_ref[s, :, at : at + LANES] = rope_back(key).astype(BF)
+                at = at + inner
+                dqkv_ref[s, :, at : at + LANES] = value.astype(BF)
+
+
+def unrotate(shift, msg, cosine, sine, seqs, heads, count):
+    rows = 2 * msg.shape[2]
+    return pl.pallas_call(
+        functools.partial(unrotate_kernel, heads, count),
+        in_specs=[SMEM] + [VMEM] * 3,
+        out_specs=VMEM,
+        out_shape=jax.ShapeDtypeStruct((seqs, rows, 3 * heads * HEAD_DIM), BF),
+        compiler_params=params(0),
+        name="unrotate",
+    )(shift, msg, cosine, sine)
+
+
+def unproject_kernel(count, dqkv_ref, x_ref, dstate_ref, gain_ref, *refs):
+    w_refs = refs[:count]
+    dx_ref, dgain_ref = refs[count:]
+    seqs, rows, width = x_ref.shape
+    inner = dqkv_ref.shape[2] // count
+    made = 0.0
+    for k in range(count):
+        cols = dqkv_ref[:, :, k * inner : (k + 1) * inner].reshape(seqs * rows, inner)
+        made = made + dot(cols, w_refs[k][...])
+    total = jnp.zeros((1, width), F4)
+    for s in range(seqs):
+        pulled, dgain = norm_back(
+            x_ref[s].astype(F4), gain_ref[...], made[s * rows : (s + 1) * rows]
+        )
+        total = total + dgain
+        dx_ref[s] = (dstate_ref[s] + pulled).astype(BF)
+    dgain_ref[...] = total
+
+
+def unproject(dqkv, x, dstate, gain, parts):
+    seqs, rows, width = x.shape
+    return pl.pallas_call(
+        functools.partial(unproject_kernel, len(parts)),
+        in_specs=[VMEM] * (4 + len(parts)),
+        out_specs=[VMEM] * 2,
+        out_shape=[
+            jax.ShapeDtypeStruct((seqs, rows, width), BF),
+            jax.ShapeDtypeStruct((1, width), F4),
+        ],
+        compiler_params=params(0),
+        name="unproject",
+    )(dqkv, x, dstate, gain, *parts)
+
+
+def dispatch_kernel(info_ref, second_ref, cot_ref, out_ref):
+    step = pl.program_id(0)
+    count, held, double = out_ref.shape
+    width = double // 2
+    shape = (count * held, info_ref.shape[1])
+    ids = lax.broadcasted_iota(jnp.int32, shape, 0) + step * (count * held)
+    target = info_ref[0:2, :].astype(jnp.int32)
+    one, two = ids == target[0:1], ids == target[1:2]
+    hits = (one | two).astype(BF)
+    gate = jnp.where(one, info_ref[2:3, :], 0.0) + jnp.where(two, info_ref[3:4, :], 0.0)
+    gate = jnp.sum(gate, axis=1, keepdims=True)
+    out_ref[:, :, :width] = dot(hits, second_ref[...]).astype(BF).reshape(count, held, width)
+    out_ref[:, :, width:] = (
+        (dot(hits, cot_ref[...]) * gate).astype(BF).reshape(count, held, width)
+    )
+
+
+def dispatch(info, second, cot, experts, held):
+    total, width = second.shape
+    count = 4 if experts % 4 == 0 else 1
+    return pl.pallas_call(
+        dispatch_kernel,
+        grid=(experts // count,),
+        in_specs=[whole(info.shape), whole(second.shape), whole(cot.shape)],
+        out_specs=pl.BlockSpec((count, held, 2 * width), lambda e: (e, 0, 0)),
+        out_shape=jax.ShapeDtypeStruct((experts, held, 2 * width), BF),
+        compiler_params=params(1),
+        name="dispatch",
+    )(info, second, cot)
+
+
+def finish_kernel(heads, size, count, shift_ref, info_ref, state_ref, cot_ref, gain_ref, router_ref, *refs):
+    home_refs, refs = refs[:size], refs[size:]
+    dense_refs, refs = refs[:size], refs[size:]
+    w_refs = refs[:count]
+    out_ref, dstate_ref, low_ref, logit_ref, msg_ref, dgain_ref = refs[count:]
+    step = pl.program_id(0)
+    take, rows, width = state_ref.shape
+    lines = take * rows
+    members, units, chunk, _ = msg_ref.shape
+    slots = home_refs[0].shape[0]
+    experts = router_ref.shape[0]
+    info = info_ref[...].reshape(lines, info_ref.shape[2])
+    target = info[:, : 2 * size].astype(jnp.int32)
+    gates = [info[:, 2 * size + c : 2 * size + c + 1] for c in range(2)]
+    chosen = info[:, 2 * size + 2 : 2 * size + 4].astype(jnp.int32)
+    ids = lax.broadcasted_iota(jnp.int32, (lines, slots), 1)
+    made, back = [0.0, 0.0], 0.0
+    for k in range(size):
+        hits = [ids == target[:, 2 * k + c : 2 * k + c + 1] for c in range(2)]
+        for c in range(2):
+            made[c] = made[c] + dot(hits[c].astype(BF), home_refs[k][:, :width])
+        back = back + dot((hits[0] | hits[1]).astype(BF), home_refs[k][:, width:])
+    cot = cot_ref[...].reshape(lines, width).astype(F4)
+    pulled = [jnp.sum(y * cot, axis=-1, keepdims=True) for y in made]
+    middle = gates[0] * pulled[0] + gates[1] * pulled[1]
+    names = lax.broadcasted_iota(jnp.int32, (lines, experts), 1)
+    logit = 0.0
+    for c in range(2):
+        logit = logit + jnp.where(
+            names == chosen[:, c : c + 1], gates[c] * (pulled[c] - middle), 0.0
+        )
+    logit = logit.astype(BF)
+    logit_ref[...] = logit.reshape(take, rows, experts)
+    back = back + dot(logit, router_ref[...])
+    branch = gates[0] * made[0] + gates[1] * made[1]
+    for ref in dense_refs:
+        dense = ref[...].reshape(lines, 2 * width)
+        branch = branch + dense[:, :width]
+        back = back + dense[:, width:]
+    state = state_ref[...].reshape(lines, width)
+    out_ref[...] = (state + branch).astype(BF).reshape(take, rows, width)
+    pulled, dgain = norm_back(state, gain_ref[...], back)
+    dstate = cot + pulled
+    dstate_ref[...] = dstate.reshape(take, rows, width)
     low = dstate.astype(BF)
-    low_ref[0] = low
-
-    @pl.when(s == 0)
+    low_ref[...] = low.reshape(take, rows, width)
+    seqs = take * pl.num_programs(0)
+
+    @pl.when(step == 0)
     def _():
         dgain_ref[...] = jnp.zeros_like(dgain_ref)
-        if msg_ref.shape[0] * msg_ref.shape[1] > heads * pl.num_programs(0):
+        if members * units > heads * seqs:
             msg_ref[...] = jnp.zeros_like(msg_ref)
 
     dgain_ref[...] += dgain
-    mixed_back = dot_nt(low, w_ref[...])
-    for g in range(heads // 2):
-        part = mixed_back[:, g * LANES : (g + 1) * LANES]
-        pair = pair_swap(part[:chunk], part[chunk:])
-        for c in range(2):
-            unit = s * heads + 2 * g + c
-            msg_ref[unit % members, unit // members] = pair[c].astype(BF)
-
-
-def unmix(state, da2, cot, gain, out_weight, members, units):
+    per = heads // count
+    for k in range(count):
+        mixed_back = dot(low, w_refs[k][...])
+        for s in range(take):
+            for g in range(per // 2):
+                part = mixed_back[s * rows : (s + 1) * rows, g * LANES : (g + 1) * LANES]
+                pair = pair_swap(part[:chunk], part[chunk:])
+                for c in range(2):
+                    chip, u = head_units(
+                        seqs, heads, members, shift_ref[0], step * take + s, k * per + 2 * g + c
+                    )
+                    msg_ref[chip, u] = pair[c].astype(BF)
+
+
+def finish(shift, info, state, cot, gain, router, homes, denses, parts, members, units):
     seqs, rows, width = state.shape
-    inner = out_weight.shape[0]
+    inner = sum(part.shape[1] for part in parts)
+    experts = router.shape[0]
+    take = max(1, min(seqs, 256 // rows))
     msg = (members, units, rows // 2, LANES)
-    per_slot = pl.BlockSpec((1, rows, width), lambda s: (s, 0, 0))
+    some = lambda cols: pl.BlockSpec((take, rows, cols), lambda s: (s, 0, 0))
     return pl.pallas_call(
-        functools.partial(unmix_kernel, members, inner // HEAD_DIM),
-        grid=(seqs,),
-        in_specs=[per_slot, per_slot, per_slot, whole((1, width)), whole(out_weight.shape)],
-        out_specs=[per_slot, per_slot, whole(msg), whole((1, width))],
+        functools.partial(finish_kernel, inner // HEAD_DIM, len(homes), len(parts)),
+        grid=(seqs // take,),
+        in_specs=[SMEM, some(info.shape[2]), some(width), some(width), whole((1, width))]
+        + [whole(router.shape)]
+        + [whole(home.shape) for home in homes]
+        + [some(2 * width)] * len(denses)
+        + [whole(part.shape) for part in parts],
+        out_specs=[some(width)] * 3 + [some(experts), whole(msg), whole((1, width))],
         out_shape=[
+            jax.ShapeDtypeStruct((seqs, rows, width), BF),
             jax.ShapeDtypeStruct((seqs, rows, width), F4),
             jax.ShapeDtypeStruct((seqs, rows, width), BF),
+            jax.ShapeDtypeStruct((seqs, rows, experts), BF),
             jax.ShapeDtypeStruct(msg, BF),
             jax.ShapeDtypeStruct((1, width), F4),
         ],
         compiler_params=params(1),
-        name="unmix",
-    )(state, da2, cot, gain, out_weight)
-
-
-def unproject_kernel(
-    members, heads, units, msg_ref, x_ref, dstate_ref, gain_ref, w_ref, cos_ref, sin_ref, *outs
-):
-    dqkv_ref, dx_ref, dgain_ref = outs
-    s = pl.program_id(0)
-    width = heads * HEAD_DIM
-    cosine, sine = cos_ref[...], sin_ref[...]
-
-    def rope_back(grad):
-        return grad * cosine - turn_halves(grad) * sine
-
-    for g in range(heads // 2):
-        pair, early, late = [], [], []
-        for c in range(2):
-            unit = s * heads + 2 * g + c
-            chip, u = unit % members, unit // members
-            pair.append(
-                jnp.concatenate([msg_ref[chip, 2 * u], msg_ref[chip, 2 * u + 1]], axis=0).astype(F4)
-            )
-            early.append(msg_ref[chip, 2 * units + u].astype(F4))
-        key, value = pair_swap(*pair)
-        query = jnp.concatenate(pair_swap(*early), axis=0)
-        at = g * LANES
-        dqkv_ref[0, :, at : at + LANES] = rope_back(query).astype(BF)
-        dqkv_ref[0, :, width + at : width + at + LANES] = rope_back(key).astype(BF)
-        dqkv_ref[0, :, 2 * width + at : 2 * width + at + LANES] = value.astype(BF)
-    da1 = dot_nt(dqkv_ref[0], w_ref[...])
-    pulled, dgain = norm_back(x_ref[0].astype(F4), gain_ref[...], da1)
-    dx_ref[0] = (dstate_ref[0] + pulled).astype(BF)
-
-    @pl.when(s == 0)
+        name="finish",
+    )(shift, info, state, cot, gain, router, *homes, *denses, *parts)
+
+
+def place_kernel(copies, *refs):
+    total = refs[0][...].astype(F4)
+    for ref in refs[1:copies]:
+        total = total + ref[...].astype(F4)
+    for n, out in enumerate(refs[copies:]):
+        out[...] = untile(total, n)
+
+
+def place(blocks, experts):
+    members, rows, triple = blocks.shape
+    hidden = triple // 3
+    copies = members // experts
+    take = 2 if experts % 2 == 0 else 1
+    return pl.pallas_call(
+        functools.partial(place_kernel, copies),
+        grid=(experts // take,),
+        in_specs=[
+            pl.BlockSpec((take, rows, triple), lambda e, n=n: (n * experts // take + e, 0, 0))
+            for n in range(copies)
+        ],
+        out_specs=[pl.BlockSpec((take, rows, hidden), lambda e: (e, 0, 0))] * 3,
+        out_shape=[jax.ShapeDtypeStruct((experts, rows, hidden), F4)] * 3,
+        compiler_params=params(1),
+        name="place",
+    )(*[blocks] * copies)
+
+
+def gated_kernel(count, tiles, x_ref, d_ref, *refs):
+    w_refs = refs[: 3 * count]
+    out_ref, hid_ref, acc_ref = refs[3 * count :]
+    step = pl.program_id(0)
+    rows, width = x_ref.shape
+    tile = hid_ref.shape[1] // 3
+    take = min(256, rows)
+
+    @pl.when(step == 0)
     def _():
-        dgain_ref[...] = jnp.zeros_like(dgain_ref)
-
-    dgain_ref[...] += dgain
-
-
-def unproject(msg, x, dstate, gain, weights, cosine, sine):
-    members, triple, chunk, _ = msg.shape
-    seqs, rows, width = x.shape
-    inner = weights.shape[1]
-    per_slot = pl.BlockSpec((1, rows, width), lambda s: (s, 0, 0))
+        acc_ref[...] = jnp.zeros_like(acc_ref)
+
+    for k in range(count):
+
+        @pl.when(step // tiles == k)
+        def _(k=k):
+            gate_w, up_w, down_w = w_refs[3 * k : 3 * k + 3]
+            gate_t, up_t, down_t = gate_w[...].T, up_w[...].T, down_w[...].T
+            for r in range(0, rows, take):
+                mine = slice(r, r + take)
+                x, d = x_ref[mine, :], d_ref[mine, :]
+                gate, up, back = dot(x, gate_w[...]), dot(x, up_w[...]), dot(d, down_t)
+                share = 1.0 / (1.0 + jnp.exp(-gate))
+                silu = gate * share
+                hidden = (silu * up).astype(BF)
+                dup = (back * silu).astype(BF)
+                dgate = (back * up * (share * (1.0 + gate * (1.0 - share)))).astype(BF)
+                hid_ref[mine, :tile] = dgate
+                hid_ref[mine, tile : 2 * tile] = dup
+                hid_ref[mine, 2 * tile :] = hidden
+                acc_ref[mine, :width] += dot(hidden, down_w[...])
+                acc_ref[mine, width:] += dot(dgate, gate_t) + dot(dup, up_t)
+
+    @pl.when(step == pl.num_programs(0) - 1)
+    def _():
+        out_ref[...] = acc_ref[...].astype(out_ref.dtype)
+
+
+def tile_of(hidden):
+    return min(512, hidden)
+
+
+def gated(x, d, parts, kind, name, both=False):
+    rows = x.shape[0]
+    width, hidden = parts[0][0].shape
+    tile = tile_of(hidden)
+    tiles = hidden // tile
+    count = len(parts)
+    flat, specs = [], []
+    for k, part in enumerate(parts):
+        at = lambda f, k=k: jnp.clip(f - k * tiles, 0, tiles - 1)
+        cols = pl.BlockSpec((width, tile), lambda f, at=at: (0, at(f)))
+        lines = pl.BlockSpec((tile, width), lambda f, at=at: (at(f), 0))
+        flat += list(part)
+        specs += [cols, cols, lines]
     return pl.pallas_call(
-        functools.partial(unproject_kernel, members, inner // 3 // HEAD_DIM, triple // 3),
-        grid=(seqs,),
+        functools.partial(gated_kernel, count, tiles),
+        grid=(count * tiles,),
         in_specs=[
-            whole(msg.shape),
-            per_slot,
-            per_slot,
-            whole((1, width)),
-            whole(weights.shape),
-            whole(cosine.shape),
-            whole(sine.shape),
+            pl.BlockSpec((rows, width), lambda f: (0, 0)),
+            pl.BlockSpec((rows, width), lambda f: (0, 1 if both else 0)),
+        ]
+        + specs,
+        out_specs=[whole((rows, 2 * width)), pl.BlockSpec((rows, 3 * tile), lambda f: (0, f))],
+        out_shape=[
+            jax.ShapeDtypeStruct((rows, 2 * width), kind),
+            jax.ShapeDtypeStruct((rows, 3 * count * hidden), BF),
         ],
-        out_specs=[
-            pl.BlockSpec((1, rows, inner), lambda s: (s, 0, 0)),
-            per_slot,
-            whole((1, width)),
+        scratch_shapes=[pltpu.VMEM((rows, 2 * width), F4)],
+        compiler_params=params(1),
+        name=name,
+    )(x, d, *flat)
+
+
+def gated_grads_kernel(x_ref, d_ref, hid_ref, out_ref, xt_ref, dt_ref):
+    tile = hid_ref.shape[1] // 3
+
+    @pl.when(pl.program_id(0) == 0)
+    def _():
+        xt_ref[...] = x_ref[...].T
+        dt_ref[...] = d_ref[...].T
+
+    out_ref[:, : 2 * tile] = dot(xt_ref[...], hid_ref[:, : 2 * tile]).astype(BF)
+    out_ref[:, 2 * tile :] = dot(dt_ref[...], hid_ref[:, 2 * tile :]).astype(BF)
+
+
+def gated_grads(x, d, hid, k, count, name, both=False):
+    rows = x.shape[0]
+    width = x.shape[1] // 2 if both else x.shape[1]
+    hidden = hid.shape[1] // 3 // count
+    tile = tile_of(hidden)
+    tiles = hidden // tile
+    return pl.pallas_call(
+        gated_grads_kernel,
+        grid=(tiles,),
+        in_specs=[
+            pl.BlockSpec((rows, width), lambda f: (0, 0)),
+            pl.BlockSpec((rows, width), lambda f: (0, 1 if both else 0)),
+            pl.BlockSpec((rows, 3 * tile), lambda f: (0, k * tiles + f)),
         ],
-        out_shape=[
-            jax.ShapeDtypeStruct((seqs, rows, inner), BF),
-            jax.ShapeDtypeStruct((seqs, rows, width), BF),
-            jax.ShapeDtypeStruct((1, width), F4),
-        ],
+        out_specs=pl.BlockSpec((width, 3 * tile), lambda f: (0, f)),
+        out_shape=jax.ShapeDtypeStruct((width, 3 * hidden), BF),
+        scratch_shapes=[pltpu.VMEM((width, rows), BF)] * 2,
         compiler_params=params(1),
-        name="unproject",
-    )(msg, x, dstate, gain, weights, cosine, sine)
-
-
-def swiglu(gate_part, up_part):
-    return jax.nn.silu(gate_part) * up_part
-
-
-def swiglu_back(gate_part, up_part, hidden_back):
-    unused, pull = jax.vjp(swiglu, gate_part, up_part)
-    dgate, dup = pull(hidden_back)
-    return dgate.astype(BF), dup.astype(BF)
+        cost_estimate=pl.CostEstimate(
+            flops=6 * rows * width * hidden,
+            bytes_accessed=2 * (2 * rows * width + 3 * hidden * (rows + width)),
+            transcendentals=0,
+        ),
+        name=name,
+    )(x, d, hid)
+
+
+def untile(array, n):
+    hidden = array.shape[-1] // 3
+    tile = tile_of(hidden)
+    parts = [
+        array[..., (3 * j + n) * tile : (3 * j + n + 1) * tile] for j in range(hidden // tile)
+    ]
+    return jnp.concatenate(parts, axis=-1)
 
 
 def per_device(
@@ -631,25 +870,30 @@
     )
 
     local = inner // size
-    packed = jnp.concatenate([query_weight, key_weight, value_weight, out_weight.T], axis=1)
-    packed = in_order(wt_gather(packed)).reshape(size, width, 4, local)
-    packed = packed.transpose(1, 2, 0, 3).reshape(width, 4 * inner)
-    qkv_weight = packed[:, : 3 * inner]
-    out_full = packed[:, 3 * inner :].T
-
-    msg, a1 = project(x, attn_gain[None], qkv_weight, cosine, sine, members, units)
+    split = size == 2 and local % LANES == 0
+    shift = (w * (heads // size) if split else jnp.zeros_like(w)).astype(jnp.int32)[None]
+    own_qkv = [query_weight, key_weight, value_weight]
+    if split:
+        parts = list(zip(*[wt_gather(weight) for weight in own_qkv]))
+        out_parts = wt_gather(out_weight)
+    else:
+        parts = [[lax.all_gather(weight, "wt", axis=1, tiled=True) for weight in own_qkv]]
+        out_parts = [lax.all_gather(out_weight, "wt", axis=0, tiled=True)]
+    msg, a1 = project(shift, x, attn_gain[None], cosine, sine, parts, members, units)
     got = lax.all_to_all(msg, "ctx", 0, 0, tiled=True)
-    blocks = wt_gather(got)
-    inv = jnp.argsort(block_pairs).astype(jnp.int32)
-    unit_slots = jnp.minimum((ctx + members * jnp.arange(units)) // heads, seqs - 1)
-    unit_lengths = lengths[unit_slots]
-    w_arg = w.astype(jnp.int32)[None]
-    o_msg, kept, lse = attend(inv, unit_lengths, w_arg, blocks, units)
-    o_got = lax.all_to_all(o_msg, "ctx", 0, 0, tiled=True)
-    mixed, state, second_own = mix(o_got, x, out_full, ffn_gain[None])
-
+
+    back_parts = [jnp.concatenate([weight.T for weight in part]) for part in parts]
+    out_back = [part.T for part in out_parts]
+    expert = ctx % experts
+    expert_parts = list(
+        zip(
+            *[
+                wt_gather(lax.dynamic_index_in_dim(weights, expert, 0, False))
+                for weights in (expert_gate, expert_up, expert_down)
+            ]
+        )
+    )
     total_rows = rows * size
-    second = jnp.concatenate(wt_gather(second_own.reshape(rows, width)))
     cots = []
     for k in range(size):
         valid = places_of(k)[None, :] < lengths[:, None]
@@ -659,7 +903,6 @@
             )
         )
     cot = jnp.concatenate(cots)
-    cot_float = cot.astype(F4)
 
     parted = routes[0].reshape(2, size, chunk, seqs, 2).transpose(1, 3, 0, 2, 4)
     chosen_all = parted.reshape(total_rows, 2)
@@ -671,33 +914,58 @@
     order_all = jnp.sum(jnp.where(picks_all, before[:, None, :], 0.0), axis=-1).astype(jnp.int32)
     share = -(-CAPACITY // size)
     held = -(-share // 16) * 16
-    inside = (order_all >= w * held) & (order_all < (w + 1) * held)
-    target_all = jnp.where(inside, chosen_all * held + order_all - w * held, -1)
+
+    def targets(chosen, order, core):
+        inside = (order >= core * held) & (order < (core + 1) * held)
+        return jnp.where(inside, chosen * held + order - core * held, -1)
 
     def own_first(array):
-        parts = array.reshape(size, rows, 2)
-        parts = jnp.concatenate([parts, parts[:-1]]) if size > 1 else parts
-        return lax.dynamic_slice_in_dim(parts, w, size, 0).reshape(total_rows, 2)
-
-    chosen, target = own_first(chosen_all), own_first(target_all)
+        pieces = array.reshape(size, rows, 2)
+        pieces = jnp.concatenate([pieces, pieces[:-1]])
+        return lax.dynamic_slice_in_dim(pieces, w, size, 0).reshape(total_rows, 2)
+
+    chosen, order_here = own_first(chosen_all), own_first(order_all)
+    target = targets(chosen, order_here, w)
+    own_targets = [
+        targets(chosen[:rows], order_here[:rows], (w + k) % size).astype(F4) for k in range(size)
+    ]
+    inv = jnp.argsort(block_pairs).astype(jnp.int32)
+    unit_slots = jnp.minimum((ctx + members * jnp.arange(units)) // heads, seqs - 1)
+    unit_lengths = lengths[unit_slots]
+    w_arg = w.astype(jnp.int32)[None]
+    got, back_parts, out_back, expert_parts, cots, cot, chosen, target, own_targets, inv, unit_lengths = (
+        lax.optimization_barrier(
+            (
+                got,
+                back_parts,
+                out_back,
+                expert_parts,
+                cots,
+                cot,
+                chosen,
+                target,
+                own_targets,
+                inv,
+                unit_lengths,
+            )
+        )
+    )
+
+    blocks = wt_gather(got)
+    o_msg, kept, lse = attend(inv, unit_lengths, w_arg, blocks, units)
+    o_got = lax.all_to_all(o_msg, "ctx", 0, 0, tiled=True)
+    mixed, state, second_own = mix(shift, o_got, x, ffn_gain[None], out_parts)
+
+    second = jnp.concatenate(wt_gather(second_own.reshape(rows, width)))
     picks = chosen[:, :, None] == names
-
     logits = dot(second, router_weight)
     selected = jnp.sum(jnp.where(picks, logits[:, None, :], 0.0), axis=-1)
     raised = jnp.exp(selected - jnp.max(selected, axis=-1, keepdims=True))
     gates = raised / jnp.sum(raised, axis=-1, keepdims=True)
-
-    slot_ids = jnp.arange(experts * held, dtype=jnp.int32)
-    hit_one = slot_ids[:, None] == target[None, :, 0]
-    hit_two = slot_ids[:, None] == target[None, :, 1]
-    spread = (hit_one | hit_two).astype(BF)
-    slot_gate = jnp.sum(
-        jnp.where(hit_one, gates[None, :, 0], 0.0) + jnp.where(hit_two, gates[None, :, 1], 0.0),
-        axis=1,
-    )
-    routed = dot(spread, second).astype(BF)
-    routed_cot = (dot(spread, cot) * slot_gate[:, None]).astype(BF)
-    sent = jnp.concatenate([routed, routed_cot], axis=1).reshape(experts, held, 2 * width)
+    info = jnp.concatenate([target.astype(F4), gates, jnp.zeros((total_rows, 4), F4)], axis=1)
+    sent = dispatch(info.T, second, cot, experts, held)
+    info = jnp.concatenate(own_targets + [gates[:rows], chosen[:rows].astype(F4)], axis=1)
+    info = info.reshape(seqs, 2 * chunk, -1)
     groups = None
     if members != experts:
         groups = [[g * experts + e for e in range(experts)] for g in range(members // experts)]
@@ -709,129 +977,124 @@
         axis_index_groups=groups,
         tiled=True,
     )
-    arrived = swap(sent).reshape(experts * held, 2 * width)
-    xe, dye = arrived[:, :width], arrived[:, width:]
-
-    expert = ctx % experts
-
-    def whole_expert(weights):
-        return wt_gather(lax.dynamic_index_in_dim(weights, expert, 0, False))
-
-    gate_parts, up_parts, down_parts = (
-        whole_expert(expert_gate),
-        whole_expert(expert_up),
-        whole_expert(expert_down),
-    )
-    ye, dxe = 0.0, 0.0
-    expert_grads = []
-    for k in range(size):
-        ge, ue = dot(xe, gate_parts[k]), dot(xe, up_parts[k])
-        he = swiglu(ge, ue).astype(BF)
-        ye = ye + dot(he, down_parts[k])
-        dhe = dot_nt(dye, down_parts[k])
-        dge, due = swiglu_back(ge, ue, dhe)
-        dxe = dxe + dot_nt(dge, gate_parts[k]) + dot_nt(due, up_parts[k])
-        expert_grads.append((dge, due, he))
-    returned = jnp.concatenate([ye.astype(BF), dxe.astype(BF)], axis=1)
-    home = swap(returned.reshape(experts, held, 2 * width)).reshape(experts * held, 2 * width)
-
-    gd, ud = dot(second, dense_gate), dot(second, dense_up)
-    hd = swiglu(gd, ud).astype(BF)
-    dense = dot(hd, dense_down)
-    dgd, dud = swiglu_back(gd, ud, dot_nt(cot, dense_down))
-    dense_back = dot_nt(dgd, dense_gate) + dot_nt(dud, dense_up)
-    dense_grads = jnp.concatenate(
-        [dot_tn(second, dgd), dot_tn(second, dud), dot_tn(cot, hd)], axis=1
-    )
-    dense_sum = lax.psum_scatter(dense_grads, "ctx", scatter_dimension=0, tiled=True)
-
-    hits = target[:, :, None] == slot_ids
-    picked = [dot(hits[:, c].astype(BF), home[:, :width]) for c in range(2)]
-    moe = picked[0] * gates[:, :1] + picked[1] * gates[:, 1:]
-    routed_back = dot(jnp.any(hits, axis=1).astype(BF), home[:, width:])
-    gate_back = jnp.stack([jnp.sum(p * cot_float, axis=-1) for p in picked], axis=1)
-    select_back = gates * (gate_back - jnp.sum(gates * gate_back, axis=-1, keepdims=True))
-    logit_back = jnp.sum(jnp.where(picks, select_back[:, :, None], 0.0), axis=1)
-    logit_high = logit_back.astype(BF)
-    logit_low = (logit_back - logit_high.astype(F4)).astype(BF)
-    logit_both = jnp.concatenate([logit_high, logit_low], axis=1)
-    router_both = jnp.concatenate([router_weight, router_weight], axis=1)
-    part_back = dense_back + routed_back + dot_nt(logit_both, router_both)
-    router_grad = dot_tn(second, logit_both)
-    router_grad = router_grad[:, :experts] + router_grad[:, experts:]
-    both = jnp.stack([moe + dense, part_back], axis=1).reshape(size, rows, 2, width)
-    both = wt_scatter([both[k] for k in range(size)])
-    output = (state.reshape(rows, width) + both[:, 0]).astype(BF)
-    da2 = both[:, 1].reshape(seqs, 2 * chunk, width)
-
-    dstate, dstate_low, do_msg, ffn_grad = unmix(
-        state, da2, cots[0].reshape(seqs, 2 * chunk, width), ffn_gain[None], out_full, members, units
+
+    sent, second = lax.optimization_barrier((sent, second))
+    arrived = swap(sent)
+    dense, dense_hid = gated(second, cot, [[dense_gate, dense_up, dense_down]], F4, "dense_branch")
+    dense_grads = gated_grads(second, cot, dense_hid, 0, 1, "dense_grads")
+    near = 4 if members % 4 == 0 else 1
+    outer = members // near
+    near_groups = [[o * near + i for i in range(near)] for o in range(outer)]
+    far_groups = [[o * near + i for o in range(outer)] for i in range(near)]
+    dense_grads = dense_grads.reshape(outer, near, width // members, -1).swapaxes(0, 1)
+    dense_grads = dense_grads.reshape(width, -1)
+    denses = [dense[:rows]]
+    for k in range(1, size):
+        perm = [(i, (i + k) % size) for i in range(size)]
+        denses.append(lax.ppermute(dense[k * rows : (k + 1) * rows], "wt", perm))
+    arrived, denses, dense_grads = lax.optimization_barrier((arrived, denses, dense_grads))
+    dense_near = lax.psum_scatter(
+        dense_grads,
+        "ctx",
+        scatter_dimension=0,
+        tiled=True,
+        axis_index_groups=near_groups,
+    )
+
+    arrived = arrived.reshape(experts * held, 2 * width)
+    returned, hid = gated(
+        arrived, arrived, [list(part) for part in expert_parts], BF, "expert_branch", True
+    )
+    home = swap(returned.reshape(experts, held, 2 * width))
+    hidden = expert_gate.shape[2]
+    expert_sum = None
+    for k in list(range(1, size)) + [0]:
+        made = gated_grads(arrived, arrived, hid, k, size, "expert_grads", True)
+        if k:
+            made = lax.ppermute(made, "wt", [(i, (i + k) % size) for i in range(size)])
+        expert_sum = made.astype(F4) if expert_sum is None else expert_sum + made.astype(F4)
+    expert_sum = expert_sum.astype(BF).reshape(members, width // members, 3 * hidden)
+    home, expert_sum, dense_near = lax.optimization_barrier((home, expert_sum, dense_near))
+    dense_sum = lax.psum_scatter(
+        dense_near, "ctx", scatter_dimension=0, tiled=True, axis_index_groups=far_groups
+    )
+    homes = wt_gather(home.reshape(experts * held, 2 * width))
+
+    own_cot = cots[0].reshape(seqs, 2 * chunk, width)
+    denses = [part.reshape(seqs, 2 * chunk, 2 * width) for part in denses]
+    output, dstate, dstate_low, logit_back, do_msg, ffn_grad = finish(
+        shift,
+        info,
+        state,
+        own_cot,
+        ffn_gain[None],
+        router_weight.T,
+        homes,
+        denses,
+        out_back,
+        members,
+        units,
     )
     do_got = lax.all_to_all(do_msg, "ctx", 0, 0, tiled=True)
+
+    def share_of(array, kinds, k):
+        if split:
+            return array[..., k * kinds * local : (k + 1) * kinds * local].reshape(rows, -1)
+        cols = array.reshape(rows, kinds, size, local)
+        return lax.dynamic_index_in_dim(cols, (w + k) % size, 2, False).reshape(rows, -1)
+
+    def split_wt(left, right, kinds):
+        pieces = []
+        for k in range(size):
+            made = dot_tn(left.reshape(rows, -1), share_of(right, kinds, k))
+            pieces.append(made if k == 0 else made.astype(BF))
+        return wt_scatter(pieces).astype(BF)
+
+    def by_owner(blocks):
+        return jnp.concatenate(blocks, axis=1).reshape(members, width // members, -1)
+
+    router_grad = dot_tn(second_own.reshape(rows, width), logit_back.reshape(rows, experts))
+    small = wt_sum(jnp.concatenate([ffn_grad.T, router_grad], axis=1))
+    out_grad = split_wt(dstate_low, mixed, 1)
+    do_got, out_grad, small, output, expert_sum, dense_sum = lax.optimization_barrier(
+        (do_got, out_grad, small, output, expert_sum, dense_sum)
+    )
+    expert_got = lax.all_to_all(expert_sum, "ctx", 0, 0, tiled=True)
     dq, *dkv = attend_back(inv, unit_lengths, w_arg, blocks, do_got, kept, lse, units)
+    dq, dkv, expert_got = lax.optimization_barrier((dq, dkv, expert_got))
     dkv = wt_scatter(dkv).astype(BF)
     grad_msg = jnp.concatenate([dkv, dq], axis=1)
     grad_got = lax.all_to_all(grad_msg, "ctx", 0, 0, tiled=True)
-    dqkv, dx, attn_grad = unproject(grad_got, x, dstate, attn_gain[None], qkv_weight, cosine, sine)
-
-    def split_wt(left, right, parts):
-        cols = right.reshape(rows, parts, size, -1)
-        pieces = []
-        for k in range(size):
-            mine = lax.dynamic_index_in_dim(cols, (w + k) % size, 2, False).reshape(rows, -1)
-            made = dot_tn(left.reshape(rows, -1), mine)
-            pieces.append(made if k == 0 else made.astype(BF))
-        return wt_scatter(pieces)
-
-    qkv_grad = split_wt(a1, dqkv, 3)
-    out_grad = split_wt(dstate_low, mixed, 1)
-    small = jnp.concatenate([attn_grad.T, ffn_grad.T, router_grad], axis=1)
-    small = wt_sum(small)
+    expert_grads = place(expert_got, experts)
+    dqkv = unrotate(shift, grad_got, cosine, sine, seqs, heads, len(parts))
+    dx, attn_grad = unproject(dqkv, x, dstate, attn_gain[None], back_parts)
+    small = jnp.concatenate([wt_sum(attn_grad).T, small], axis=1)
     small_high = small.astype(BF)
     small_low = (small - small_high.astype(F4)).astype(BF)
-    small = jnp.concatenate([small_high, small_low], axis=1)
     few = experts + 2
-    small = jnp.pad(small, ((0, 0), (0, -(2 * few) % LANES)))
-    mine_msg = jnp.concatenate([qkv_grad.astype(BF), out_grad.astype(BF), small], axis=1)
-    mine_msg = mine_msg.reshape(members, width // members, -1)
-    mine_got = lax.all_to_all(mine_msg, "ctx", 0, 0, tiled=True).astype(F4)
-    mine_sum = jnp.sum(mine_got, axis=0)
-    tail = mine_sum[:, 4 * local :]
+    blank = jnp.zeros((width, -(2 * few) % LANES), BF)
+    last_msg = by_owner([split_wt(a1, dqkv, 3), out_grad, small_high, small_low, blank])
+    last_got = lax.all_to_all(last_msg, "ctx", 0, 0, tiled=True)
+    last_sum = jnp.sum(last_got.astype(F4), axis=0)
+    tail = last_sum[:, 4 * local :]
     tail = tail[:, :few] + tail[:, few : 2 * few]
-
-    expert_pieces = []
-    for k in range(size):
-        dge, due, he = expert_grads[k]
-        made = jnp.stack([dot_tn(xe, dge), dot_tn(xe, due), dot_tn(dye, he)], axis=1)
-        expert_pieces.append(made if k == 0 else made.astype(BF))
-    expert_sum = wt_scatter(expert_pieces).astype(BF)
-    hidden = expert_gate.shape[2]
-    expert_msg = expert_sum.reshape(members, width // members, 3 * hidden)
-    expert_got = lax.all_to_all(expert_msg, "ctx", 0, 0, tiled=True).astype(F4)
-    expert_got = expert_got.reshape(members // experts, experts, width // members, 3, hidden)
-    expert_got = jnp.sum(expert_got, axis=0)
 
     def to_tokens(own):
         array = in_order(wt_gather(own)).reshape(size, seqs, 2, chunk, width)
         return array.transpose(2, 0, 3, 1, 4).reshape(inputs.shape)
 
-    dense_hidden = dense_gate.shape[1]
     return (
         to_tokens(output),
         to_tokens(dx),
         tail[:, 0],
-        mine_sum[:, :local],
-        mine_sum[:, local : 2 * local],
-        mine_sum[:, 2 * local : 3 * local],
-        mine_sum[:, 3 * local : 4 * local].T,
+        *[last_sum[:, n * local : (n + 1) * local] for n in range(3)],
+        last_sum[:, 3 * local : 4 * local].T,
         tail[:, 1],
         tail[:, 2:],
-        expert_got[:, :, 0],
-        expert_got[:, :, 1],
-        expert_got[:, :, 2].transpose(0, 2, 1),
-        dense_sum[:, :dense_hidden],
-        dense_sum[:, dense_hidden : 2 * dense_hidden],
-        dense_sum[:, 2 * dense_hidden :].T,
+        *expert_grads[:2],
+        expert_grads[2].transpose(0, 2, 1),
+        *[untile(dense_sum, n).astype(F4) for n in range(2)],
+        untile(dense_sum, 2).astype(F4).T,
     )
 
 

time: 985 us -> 769 us (0.78)
  matrix products: 144 us -> 11.4 us
  Pallas kernels: 128 us -> 239 us
  local copies, waits for them, and re-layouts: 167 us -> 60.2 us
  starting transfers between devices: 139 us -> 85.3 us
  waiting for transfers between devices: 272 us -> 241 us
  other arithmetic: 52.8 us -> 28.6 us
  blocking collectives: 63.1 us -> 76.6 us
    pallas_call x4 -> x12, Pallas kernels: 30.3 us -> 155 us  [the longest x2 62.9 us: gated(): pl.pallas_call(functools.partial(gated_kernel, count, tiles), grid=(count...]
    all_to_all x5, starting transfers between devices: 106 us -> 41.5 us  [the longest x1 19.4 us: per_device(): home = swap(returned.reshape(experts, held, 2 * width))]
    dot_general x16 -> x2, matrix products: 61.5 us -> 0.98 us  [dot(): return jnp.dot(a, b, preferred_element_type=F4)]
    dot_general x10 -> x0, matrix products: 37.7 us -> none  [dot_nt(): lax.dot_general(a, b, (((1,), (1,)), ((), ())), preferred_element_type=F4)]
    reduce_scatter x1 -> x2, waiting for transfers between devices: 36.7 us -> 0.02 us  [the longest x1 0.02 us: per_device(): lax.psum_scatter(dense_near, 'ctx', scatter_dimension=0, tiled=True, axis...]
    dot_general x14 -> x5, matrix products: 45.3 us -> 10.5 us  [dot_tn(): lax.dot_general(a, b, (((0,), (0,)), ((), ())), preferred_element_type=F4)]
    reshape x5 -> x0, local copies, waits for them, and re-layouts: 30.7 us -> none  [the longest x1 13.6 us: per_device(): expert_msg = expert_sum.reshape(members, width // members, 3 * hidden)]
    unnamed x153 -> x73, local copies, waits for them, and re-layouts: 33.9 us -> 14.7 us
  transfers between devices with their start and end apart: 22 -> 28, of which waited for: 12 -> 13; matrix products, arithmetic and copies ran while one was open for 26% -> 10% of each run, Pallas kernels for 1% -> 22%
where the time goes in v2:
time: 769 us; the launch traced here: 758 us
  waiting for transfers between devices  241 us (31%)
  Pallas kernels  239 us (31%)
  starting transfers between devices  85.3 us (11%)
  blocking collectives  76.6 us (10%)
  local copies, waits for them, and re-layouts  60.2 us (8%)
  other arithmetic  28.6 us (4%)
  between operations  15.6 us (2%)
  matrix products  11.4 us (1%)
    all_to_all x1, blocking collectives, per_device(): grad_got = lax.all_to_all(grad_msg, 'ctx', 0, 0, tiled=True)  76.6 us
    pallas_call x2, Pallas kernels, gated(): pl.pallas_call(functools.partial(gated_kernel, count, tiles), grid=(count...  62.9 us
    all_to_all x1, waiting for transfers between devices, per_device(): expert_got = lax.all_to_all(expert_sum, 'ctx', 0, 0, tiled=True)  53.7 us
    pallas_call x1, Pallas kernels, attend(): pl.pallas_call(functools.partial(attend_kernel, members, size), grid_spec...  50.4 us
    all_to_all x1, waiting for transfers between devices, per_device(): home = swap(returned.reshape(experts, held, 2 * width))  43.5 us
    all_to_all x1, waiting for transfers between devices, per_device(): arrived = swap(sent)  36.9 us
    pallas_call x3, Pallas kernels, gated_grads(): pl.pallas_call(gated_grads_kernel, grid=(tiles,), in_specs=[pl.BlockSpec(...  35.2 us
    pallas_call x1, Pallas kernels, attend_back(): pl.pallas_call(functools.partial(attend_back_kernel, members, size), grid...  33.7 us
  transfers between devices with their start and end apart: 28, of which 13 were waited for; matrix products, arithmetic and copies ran while one was open for 10% of the time, Pallas kernels for 22%

profile of v2, /device:TPU:0, one launch (start us, length us, event | category | flops | bytes accessed | tf_op | source)
XLA Modules:
  0.0 757.9 jit_solution(10454459595560996909)
XLA Ops:
  16.4 3.3 constant_dynamic-slice_fusion
  25.0 7.2 project.1
  32.1 8.0 %all-to-all-start = ((bf16[16,9,64,128]{3,2,1,0:T(8,128)(2,1)}), bf16[16,9,64,128]{3,2,1,0:T(8,128)(2,1)S(1)}, u32[]{:S(2)}, u32[]{:S(2)}) async-start(bf16[16,9,64,128]{3,2,1,0:T(8,128)(2,1)} %get-tuple-element.80), calls=%async_computation | async-start | bytes 4718592 | tf_op jit(solution)/shard_map/all_to_all | solution.py:883
  42.4 2.7 dynamic-slice_bitcast_fusion.refs_2_
  45.5 2.7 dynamic-slice_bitcast_fusion.1.refs_1_
  48.2 2.7 dynamic-slice_bitcast_fusion.2.refs_0_
  61.0 2.5 pad_maximum_fusion.1.refs_0_
  63.5 2.4 pad_maximum_fusion.2.refs_1_
  65.9 21.9 %all-to-all-done.refs_0_ = bf16[16,9,64,128]{3,2,1,0:T(8,128)(2,1)S(1)} async-done(((bf16[16,9,64,128]{3,2,1,0:T(8,128)(2,1)}), bf16[16,9,64,128]{3,2,1,0:T(8,128)(2,1)S(1)}, u32[]{:S(2)}, u32[]{:S(2)}) %all-to-all-start) | async-done | bytes 2359328 | tf_op jit(solution)/shard_map/all_to_all | solution.py:883
  87.8 4.5 collective-permute-done.7.refs_1_
  93.8 50.4 %attend.1 = (bf16[16,3,64,128]{3,2,1,0:T(8,128)(2,1)}, f32[3,8,64,256]{3,2,1,0:T(8,128)}, f32[3,8,1,256]{3,2,1,0:T(1,128)}) custom-call(s32[16]{0:T(128)} %get-tuple-element.85.inv_ref, s32[3]{0:T(128)} %gather_fusion, s32[1]{0:T(128)} %bitcast.37.w_ref, bf16[16,9,64,128]{3,2,1,0:T(8,128)(2,1)} %copy-done.2, bf16[16,9,64,128]{3,2,1,0:T(8,128)(2,1)} %copy-done.4), custom_call_target="tpu_custom_call" | custom-call | tf_op jit(solution)/shard_map/attend/pallas_call | solution.py:260
  144.2 22.3 %all-to-all-start.1 = ((bf16[16,3,64,128]{3,2,1,0:T(8,128)(2,1)}), bf16[16,3,64,128]{3,2,1,0:T(8,128)(2,1)S(1)}, u32[]{:S(2)}, u32[]{:S(2)}) async-start(bf16[16,3,64,128]{3,2,1,0:T(8,128)(2,1)} %get-tuple-element.88), calls=%async_computation.1 | async-start | bytes 1572864 | tf_op jit(solution)/shard_map/all_to_all | solution.py:956
  169.2 17.3 %all-to-all-done.1.o_ref = bf16[16,3,64,128]{3,2,1,0:T(8,128)(2,1)S(1)} async-done(((bf16[16,3,64,128]{3,2,1,0:T(8,128)(2,1)}), bf16[16,3,64,128]{3,2,1,0:T(8,128)(2,1)S(1)}, u32[]{:S(2)}, u32[]{:S(2)}) %all-to-all-start.1) | async-done | bytes 786464 | tf_op jit(solution)/shard_map/all_to_all | solution.py:956
  187.4 4.2 mix.1
  191.7 2.4 collective-permute-done.8
  196.7 8.0 %dispatch.1 = bf16[16,80,1536]{2,1,0:T(8,128)(2,1)} custom-call(f32[8,1024]{1,0:T(8,128)} %maximum_bitcast_fusion.info_ref, bf16[1024,768]{1,0:T(8,128)(2,1)} %copy-done.1, bf16[1024,768]{1,0:T(8,128)(2,1)} %pad_maximum_fusion.3.cot_ref.d_ref), custom_call_target="tpu_custom_call" | custom-call | tf_op jit(solution)/shard_map/dispatch/pallas_call | solution.py:563
  204.6 5.0 all-to-all-start.2
  209.7 18.2 %dense_branch.1 = (f32[1024,1536]{1,0:T(8,128)}, bf16[1024,3072]{1,0:T(8,128)(2,1)}) custom-call(bf16[1024,768]{1,0:T(8,128)(2,1)} %copy-done.1, bf16[1024,768]{1,0:T(8,128)(2,1)} %pad_maximum_fusion.3.cot_ref.d_ref, bf16[768,1024]{1,0:T(8,128)(2,1)} %refs_0_.5, bf16[768,1024]{1,0:T(8,128)(2,1)} %refs_1_.3, bf16[1024,768]{1,0:T(8,128)(2,1)} %refs_2_.3), custom_call_target="tpu_custom_call" | custom-call | tf_op jit(solution)/shard_map/dense_branch/pallas_call | solution.py:754
  227.9 5.0 fusion.29
  232.8 10.5 %dense_grads.1 = bf16[768,3072]{1,0:T(8,128)(2,1)} custom-call(bf16[1024,768]{1,0:T(8,128)(2,1)} %copy-done.1, bf16[1024,768]{1,0:T(8,128)(2,1)} %pad_maximum_fusion.3.cot_ref.d_ref, bf16[1024,3072]{1,0:T(8,128)(2,1)} %get-tuple-element.97.hid_ref), custom_call_target="tpu_custom_call" | custom-call | flops 4831838208 | bytes 14155776 | tf_op jit(solution)/shard_map/dense_grads/pallas_call | solution.py:791
  243.3 5.0 copy.249
  248.3 36.9 %all-to-all-done.2 = bf16[16,80,1536]{2,1,0:T(8,128)(2,1)} async-done(((bf16[16,80,1536]{2,1,0:T(8,128)(2,1)}), bf16[16,80,1536]{2,1,0:T(8,128)(2,1)}, u32[]{:S(2)}, u32[]{:S(2)}) %all-to-all-start.2) | async-done | bytes 3932192 | tf_op jit(solution)/shard_map/all_to_all | solution.py:982
  285.3 44.8 %expert_branch.1 = (bf16[1280,1536]{1,0:T(8,128)(2,1)}, bf16[1280,6144]{1,0:T(8,128)(2,1)}) custom-call(bf16[1280,1536]{1,0:T(8,128)(2,1)} %bitcast.48.x_ref.d_ref, bf16[1280,1536]{1,0:T(8,128)(2,1)} %bitcast.48.x_ref.d_ref, bf16[768,1024]{1,0:T(8,128)(2,1)} %dynamic-slice_bitcast_fusion.2.refs_0_, bf16[768,1024]{1,0:T(8,128)(2,1)} %dynamic-slice_bitcast_fusion.1.refs_1_, ...), custom_call_target="tpu_custom_call" | custom-call | tf_op jit(solution)/shard_map/expert_branch/pallas_call | solution.py:754
  330.1 19.4 %all-to-all-start.3 = ((bf16[16,80,1536]{2,1,0:T(8,128)(2,1)}), bf16[16,80,1536]{2,1,0:T(8,128)(2,1)}, u32[]{:S(2)}, u32[]{:S(2)}) async-start(bf16[16,80,1536]{2,1,0:T(8,128)(2,1)} %bitcast.145), calls=%async_computation.3 | async-start | bytes 7864320 | tf_op jit(solution)/shard_map/all_to_all | solution.py:1008
  349.5 12.4 %expert_grads.2 = bf16[768,3072]{1,0:T(8,128)(2,1)} custom-call(bf16[1280,1536]{1,0:T(8,128)(2,1)} %bitcast.48.x_ref.d_ref, bf16[1280,1536]{1,0:T(8,128)(2,1)} %bitcast.48.x_ref.d_ref, bf16[1280,6144]{1,0:T(8,128)(2,1)} %get-tuple-element.106.hid_ref), custom_call_target="tpu_custom_call" | custom-call | flops 6039797760 | bytes 16515072 | tf_op jit(solution)/shard_map/expert_grads/pallas_call | solution.py:791
  361.9 12.3 %expert_grads.3 = bf16[768,3072]{1,0:T(8,128)(2,1)} custom-call(bf16[1280,1536]{1,0:T(8,128)(2,1)} %bitcast.48.x_ref.d_ref, bf16[1280,1536]{1,0:T(8,128)(2,1)} %bitcast.48.x_ref.d_ref, bf16[1280,6144]{1,0:T(8,128)(2,1)} %get-tuple-element.106.hid_ref), custom_call_target="tpu_custom_call" | custom-call | flops 6039797760 | bytes 16515072 | tf_op jit(solution)/shard_map/expert_grads/pallas_call | solution.py:791
  374.2 6.4 add_convert_fusion
  380.6 43.5 %all-to-all-done.3 = bf16[16,80,1536]{2,1,0:T(8,128)(2,1)} async-done(((bf16[16,80,1536]{2,1,0:T(8,128)(2,1)}), bf16[16,80,1536]{2,1,0:T(8,128)(2,1)}, u32[]{:S(2)}, u32[]{:S(2)}) %all-to-all-start.3) | async-done | bytes 3932192 | tf_op jit(solution)/shard_map/all_to_all | solution.py:1008
  425.1 6.2 collective-permute-done.11.refs_1_
  431.3 17.3 %finish.1 = (bf16[4,128,768]{2,1,0:T(8,128)(2,1)}, f32[4,128,768]{2,1,0:T(8,128)}, bf16[4,128,768]{2,1,0:T(8,128)(2,1)}, bf16[4,128,16]{2,1,0:T(8,128)(2,1)}, bf...) custom-call(s32[1]{0:T(128)} %bitcast.shift_ref, f32[4,128,8]{2,1,0:T(8,128)} %bitcast.155, ...), custom_call_target="tpu_custom_call" | custom-call | tf_op jit(solution)/shard_map/finish/pallas_call | solution.py:650
  448.6 17.6 %all-to-all-start.4 = ((bf16[16,3,64,128]{3,2,1,0:T(8,128)(2,1)}), bf16[16,3,64,128]{3,2,1,0:T(8,128)(2,1)S(1)}, u32[]{:S(2)}, u32[]{:S(2)}) async-start(bf16[16,3,64,128]{3,2,1,0:T(8,128)(2,1)} %get-tuple-element.113), calls=%async_computation.5 | async-start | bytes 1572864 | tf_op jit(solution)/shard_map/all_to_all | solution.py:1038
  470.9 15.4 %all-to-all-done.4.refs_2_ = bf16[16,3,64,128]{3,2,1,0:T(8,128)(2,1)S(1)} async-done(((bf16[16,3,64,128]{3,2,1,0:T(8,128)(2,1)}), bf16[16,3,64,128]{3,2,1,0:T(8,128)(2,1)S(1)}, u32[]{:S(2)}, u32[]{:S(2)}) %all-to-all-start.4) | async-done | bytes 786464 | tf_op jit(solution)/shard_map/all_to_all | solution.py:1038
  487.1 5.0 all-to-all-start.5
  492.1 33.7 %attend_back.1 = (bf16[16,3,64,128]{3,2,1,0:T(8,128)(2,1)}, f32[16,6,64,128]{3,2,1,0:T(8,128)}, f32[16,6,64,128]{3,2,1,0:T(8,128)}) custom-call(s32[16]{0:T(128)} %get-tuple-element.85.inv_ref, s32[3]{0:T(128)} %gather_fusion, s32[1]{0:T(128)} %bitcast.37.w_ref, bf16[16,9,64,128]{3,2,1,0:T(8,128)(2,1)} %copy-done.2, bf16[16,9,64,128]{3,2,1,0:T(8,128)(2,1)} %copy-done.4, ...), custom_call_target="tpu_custom_call" | custom-call | tf_op jit(solution)/shard_map/attend_back/pallas_call | solution.py:385
  525.8 53.7 %all-to-all-done.5.refs_0_ = bf16[16,48,3072]{2,1,0:T(8,128)(2,1)} async-done(((bf16[16,48,3072]{2,1,0:T(8,128)(2,1)}), bf16[16,48,3072]{2,1,0:T(8,128)(2,1)}, u32[]{:S(2)}, u32[]{:S(2)}) %all-to-all-start.5) | async-done | bytes 4718624 | tf_op jit(solution)/shard_map/all_to_all | solution.py:1062
  579.5 5.9 collective-permute-done.15
  585.3 2.6 add_convert_fusion.1
  588.2 76.6 %all_to_all.40.msg_ref = bf16[16,9,64,128]{3,2,1,0:T(8,128)(2,1)} all-to-all(bf16[16,9,64,128]{3,2,1,0:T(8,128)(2,1)S(1)} %pad_maximum_fusion), channel_id=1, replica_groups=mesh['ctx'=16,'wt'=2] {'ctx'}, dimensions={0} | all-to-all | bytes 4718592 | tf_op jit(solution)/shard_map/all_to_all | solution.py:1067
  664.7 6.1 unrotate.1.dqkv_ref
  670.8 3.7 fusion.3
  674.5 7.0 unproject.1
  684.1 4.1 fusion.2
  688.3 5.0 concatenate.67
  693.2 4.1 all-to-all-start.7
  703.0 2.4 copy.261
  705.4 7.6 %place.1 = (f32[16,48,1024]{2,1,0:T(8,128)}, f32[16,48,1024]{2,1,0:T(8,128)}, f32[16,48,1024]{2,1,0:T(8,128)}) custom-call(bf16[16,48,3072]{2,1,0:T(8,128)(2,1)} %all-to-all-done.5.refs_0_), custom_call_target="tpu_custom_call" | custom-call | tf_op jit(solution)/shard_map/place/pallas_call | solution.py:685
  715.1 2.4 copy.262
  717.5 30.8 %all-to-all-done.7 = bf16[16,48,1664]{2,1,0:T(8,128)(2,1)S(1)} async-done(((bf16[16,48,1664]{2,1,0:T(8,128)(2,1)}), bf16[16,48,1664]{2,1,0:T(8,128)(2,1)S(1)}, u32[]{:S(2)}, u32[]{:S(2)}) %all-to-all-start.7) | async-done | bytes 2555936 | tf_op jit(solution)/shard_map/all_to_all | solution.py:1077
  (200 shorter events, 53.9 us)
Async XLA Ops:
  7.2 4.9 copy-start.32
  7.2 7.0 copy-start.27
  8.6 11.2 %copy-start.12 = (bf16[768,384]{0,1:T(8,128)(2,1)}, bf16[768,384]{0,1:T(8,128)(2,1)S(1)}, u32[]{:S(2)}) copy-start(bf16[768,384]{0,1:T(8,128)(2,1)S(1)} %copy.231) | copy-start | bytes 1769476
  8.6 12.1 %collective-permute-start.2 = (bf16[768,384]{0,1:T(8,128)(2,1)S(1)}, bf16[768,384]{0,1:T(8,128)(2,1)S(1)}, u32[]{:S(2)}, u32[]{:S(2)}) collective-permute-start(bf16[768,384]{0,1:T(8,128)(2,1)S(1)} %copy.231), channel_id=1, source_target_pairs={{0,1},{1,0},{2,3},{3,2},{4,5},{5,4},{6,7},{7,6},{8,9},{9,8},{10,11... | collective-permute-start | bytes 1769480 | tf_op jit(solution)/shard_map/ppermute | solution.py:37
  10.4 9.3 %copy-start.16 = (bf16[768,384]{0,1:T(8,128)(2,1)}, bf16[768,384]{0,1:T(8,128)(2,1)S(1)}, u32[]{:S(2)}) copy-start(bf16[768,384]{0,1:T(8,128)(2,1)S(1)} %copy.230) | copy-start | bytes 1769476
  10.4 11.4 %collective-permute-start.1 = (bf16[768,384]{0,1:T(8,128)(2,1)S(1)}, bf16[768,384]{0,1:T(8,128)(2,1)}, u32[]{:S(2)}, u32[]{:S(2)}) collective-permute-start(bf16[768,384]{0,1:T(8,128)(2,1)S(1)} %copy.230), channel_id=1, source_target_pairs={{0,1},{1,0},{2,3},{3,2},{4,5},{5,4},{6,7},{7,6},{8,9},{9,8},{10,11... | collective-permute-start | bytes 1769480 | tf_op jit(solution)/shard_map/ppermute | solution.py:37
  11.7 12.2 %collective-permute-start = (bf16[768,384]{0,1:T(8,128)(2,1)}, bf16[768,384]{0,1:T(8,128)(2,1)S(1)}, u32[]{:S(2)}, u32[]{:S(2)}) collective-permute-start(bf16[768,384]{0,1:T(8,128)(2,1)} %copy.229), channel_id=1, source_target_pairs={{0,1},{1,0},{2,3},{3,2},{4,5},{5,4},{6,7},{7,6},{8,9},{9,8},{10,11... | collective-permute-start | bytes 1769480 | tf_op jit(solution)/shard_map/ppermute | solution.py:37
  20.7 11.4 %copy-start.14 = (bf16[768,384]{0,1:T(8,128)(2,1)}, bf16[768,384]{0,1:T(8,128)(2,1)S(1)}, u32[]{:S(2)}) copy-start(bf16[768,384]{0,1:T(8,128)(2,1)S(1)} %collective-permute-done.2) | copy-start | bytes 1769476
  23.9 8.2 %copy-start.18 = (bf16[768,384]{0,1:T(8,128)(2,1)}, bf16[768,384]{0,1:T(8,128)(2,1)S(1)}, u32[]{:S(2)}) copy-start(bf16[768,384]{0,1:T(8,128)(2,1)S(1)} %collective-permute-done) | copy-start | bytes 1769476
  32.1 55.7 %all-to-all-start = ((bf16[16,9,64,128]{3,2,1,0:T(8,128)(2,1)}), bf16[16,9,64,128]{3,2,1,0:T(8,128)(2,1)S(1)}, u32[]{:S(2)}, u32[]{:S(2)}) async-start(bf16[16,9,64,128]{3,2,1,0:T(8,128)(2,1)} %get-tuple-element.80), calls=%async_computation | async-start | bytes 4718592 | tf_op jit(solution)/shard_map/all_to_all | solution.py:883
  42.3 23.6 %collective-permute-start.3 = (bf16[384,768]{0,1:T(8,128)(2,1)}, bf16[384,768]{0,1:T(8,128)(2,1)}, u32[]{:S(2)}, u32[]{:S(2)}) collective-permute-start(bf16[384,768]{0,1:T(8,128)(2,1)} %copy.240), channel_id=1, source_target_pairs={{0,1},{1,0},{2,3},{3,2},{4,5},{5,4},{6,7},{7,6},{8,9},{9,8},{10,11... | collective-permute-start | bytes 1769480 | tf_op jit(solution)/shard_map/ppermute | solution.py:37
  45.0 20.9 %collective-permute-start.6 = (bf16[1024,768]{1,0:T(8,128)(2,1)}, bf16[1024,768]{1,0:T(8,128)(2,1)}, u32[]{:S(2)}, u32[]{:S(2)}) collective-permute-start(bf16[1024,768]{1,0:T(8,128)(2,1)} %dynamic-slice_bitcast_fusion.refs_2_), channel_id=1, source_target_pairs={{0,1},{1,0},{2,3},{3,2},{4,5},{5,4},{6,7},{7,6},{8,9},{9,8},{10,11... | collective-permute-start | bytes 4718600 | tf_op jit(solution)/shard_map/ppermute | solution.py:37
  48.2 17.8 %collective-permute-start.5 = (bf16[768,1024]{1,0:T(8,128)(2,1)}, bf16[768,1024]{1,0:T(8,128)(2,1)}, u32[]{:S(2)}, u32[]{:S(2)}) collective-permute-start(bf16[768,1024]{1,0:T(8,128)(2,1)} %dynamic-slice_bitcast_fusion.1.refs_1_), channel_id=1, source_target_pairs={{0,1},{1,0},{2,3},{3,2},{4,5},{5,4},{6,7},{7,6},{8,9},{9,8},{10,11... | collective-permute-start | bytes 4718600 | tf_op jit(solution)/shard_map/ppermute | solution.py:37
  50.9 5.9 copy-start
  50.9 15.0 %collective-permute-start.4 = (bf16[768,1024]{1,0:T(8,128)(2,1)}, bf16[768,1024]{1,0:T(8,128)(2,1)}, u32[]{:S(2)}, u32[]{:S(2)}) collective-permute-start(bf16[768,1024]{1,0:T(8,128)(2,1)} %dynamic-slice_bitcast_fusion.2.refs_0_), channel_id=1, source_target_pairs={{0,1},{1,0},{2,3},{3,2},{4,5},{5,4},{6,7},{7,6},{8,9},{9,8},{10,11... | collective-permute-start | bytes 4718600 | tf_op jit(solution)/shard_map/ppermute | solution.py:37
  87.8 4.5 copy-start.2
  87.8 4.5 collective-permute-start.7
  93.8 72.7 %copy-start.28 = (f32[768]{0:T(1024)S(1)}, f32[768]{0:T(1024)}, u32[]{:S(2)}) copy-start(f32[768]{0:T(1024)} %param.28) | copy-start | bytes 9220
  144.2 42.3 %all-to-all-start.1 = ((bf16[16,3,64,128]{3,2,1,0:T(8,128)(2,1)}), bf16[16,3,64,128]{3,2,1,0:T(8,128)(2,1)S(1)}, u32[]{:S(2)}, u32[]{:S(2)}) async-start(bf16[16,3,64,128]{3,2,1,0:T(8,128)(2,1)} %get-tuple-element.88), calls=%async_computation.1 | async-start | bytes 1572864 | tf_op jit(solution)/shard_map/all_to_all | solution.py:956
  169.2 26.1 %copy-start.24 = (bf16[768,16]{0,1:T(8,128)(2,1)S(1)}, bf16[768,16]{0,1:T(8,128)(2,1)}, u32[]{:S(2)}) copy-start(bf16[768,16]{0,1:T(8,128)(2,1)} %param.29) | copy-start | bytes 73732
  191.6 2.5 collective-permute-start.8
  204.6 80.6 %all-to-all-start.2 = ((bf16[16,80,1536]{2,1,0:T(8,128)(2,1)}), bf16[16,80,1536]{2,1,0:T(8,128)(2,1)}, u32[]{:S(2)}, u32[]{:S(2)}) async-start(bf16[16,80,1536]{2,1,0:T(8,128)(2,1)} %dispatch.1), calls=%async_computation.2 | async-start | bytes 7864320 | tf_op jit(solution)/shard_map/all_to_all | solution.py:982
  209.7 214.5 %reduce-scatter.3.cloned.1.call-start = ((), (), s32[]{:S(2)}) async-start(), calls=%async_computation.10 | async-start | bytes 5898240 | tf_op jit(solution)/shard_map/reduce_scatter | solution.py:996
  232.8 15.5 %collective-permute-start.9 = (f32[512,1536]{1,0:T(8,128)S(1)}, f32[512,1536]{1,0:T(8,128)S(1)}, u32[]{:S(2)}, u32[]{:S(2)}) collective-permute-start(f32[512,1536]{1,0:T(8,128)S(1)} %get-tuple-element.237), channel_id=1, source_target_pairs={{0,1},{1,0},{2,3},{3,2},{4,5},{5,4},{6,7},{7,6},{8,9},{9,8},{10,11... | collective-permute-start | bytes 9437192 | tf_op jit(solution)/shard_map/ppermute | solution.py:994
  248.3 36.9 %copy-start.6 = (f32[512,1536]{1,0:T(8,128)}, f32[512,1536]{1,0:T(8,128)S(1)}, u32[]{:S(2)}) copy-start(f32[512,1536]{1,0:T(8,128)S(1)} %collective-permute-done.9) | copy-start | bytes 9437188
  330.1 94.1 %all-to-all-start.3 = ((bf16[16,80,1536]{2,1,0:T(8,128)(2,1)}), bf16[16,80,1536]{2,1,0:T(8,128)(2,1)}, u32[]{:S(2)}, u32[]{:S(2)}) async-start(bf16[16,80,1536]{2,1,0:T(8,128)(2,1)} %bitcast.145), calls=%async_computation.3 | async-start | bytes 7864320 | tf_op jit(solution)/shard_map/all_to_all | solution.py:1008
  349.5 121.4 %reduce-scatter.5.cloned.1.call-start = ((), (), s32[]{:S(2)}) async-start(), calls=%async_computation.11 | async-start | bytes 1474560 | tf_op jit(solution)/shard_map/reduce_scatter | solution.py:1018
  361.9 12.3 %collective-permute-start.10 = (bf16[768,3072]{1,0:T(8,128)(2,1)}, bf16[768,3072]{1,0:T(8,128)(2,1)S(1)}, u32[]{:S(2)}, u32[]{:S(2)}) collective-permute-start(bf16[768,3072]{1,0:T(8,128)(2,1)} %expert_grads.2), channel_id=1, source_target_pairs={{0,1},{1,0},{2,3},{3,2},{4,5},{5,4},{6,7},{7,6},{8,9},{9,8},{10,11... | collective-permute-start | bytes 14155784 | tf_op jit(solution)/shard_map/ppermute | solution.py:1014
  424.1 7.1 collective-permute-start.11
  431.3 35.0 %copy-start.30 = (bf16[4,128,768]{2,1,0:T(8,128)(2,1)S(1)}, bf16[4,128,768]{2,1,0:T(8,128)(2,1)}, u32[]{:S(2)}) copy-start(bf16[4,128,768]{2,1,0:T(8,128)(2,1)} %get-tuple-element.115) | copy-start | bytes 2359300
  448.6 19.6 %copy-start.10 = (bf16[4,128,768]{2,1,0:T(8,128)(2,1)S(1)}, bf16[4,128,768]{2,1,0:T(8,128)(2,1)}, u32[]{:S(2)}) copy-start(bf16[4,128,768]{2,1,0:T(8,128)(2,1)} %get-tuple-element.89) | copy-start | bytes 2359300
  448.6 19.6 %copy-start.23 = (bf16[4,128,16]{2,1,0:T(8,128)(2,1)S(1)}, bf16[4,128,16]{2,1,0:T(8,128)(2,1)}, u32[]{:S(2)}) copy-start(bf16[4,128,16]{2,1,0:T(8,128)(2,1)} %get-tuple-element.117) | copy-start | bytes 49156
  448.6 19.8 %copy-start.25 = (f32[1,768]{1,0:T(1,128)S(1)}, f32[1,768]{1,0:T(1,128)}, u32[]{:S(2)}) copy-start(f32[1,768]{1,0:T(1,128)} %get-tuple-element.116) | copy-start | bytes 9220
  448.6 37.6 %all-to-all-start.4 = ((bf16[16,3,64,128]{3,2,1,0:T(8,128)(2,1)}), bf16[16,3,64,128]{3,2,1,0:T(8,128)(2,1)S(1)}, u32[]{:S(2)}, u32[]{:S(2)}) async-start(bf16[16,3,64,128]{3,2,1,0:T(8,128)(2,1)} %get-tuple-element.113), calls=%async_computation.5 | async-start | bytes 1572864 | tf_op jit(solution)/shard_map/all_to_all | solution.py:1038
  468.0 2.2 collective-permute-start.12
  468.4 1.8 collective-permute-start.13
  487.1 92.3 %all-to-all-start.5 = ((bf16[16,48,3072]{2,1,0:T(8,128)(2,1)}), bf16[16,48,3072]{2,1,0:T(8,128)(2,1)}, u32[]{:S(2)}, u32[]{:S(2)}) async-start(bf16[16,48,3072]{2,1,0:T(8,128)(2,1)} %bitcast.133), calls=%async_computation.7 | async-start | bytes 9437184 | tf_op jit(solution)/shard_map/all_to_all | solution.py:1062
  579.5 8.5 %copy-start.20 = (bf16[16,3,64,128]{3,2,1,0:T(8,128)(2,1)S(1)}, bf16[16,3,64,128]{3,2,1,0:T(8,128)(2,1)}, u32[]{:S(2)}) copy-start(bf16[16,3,64,128]{3,2,1,0:T(8,128)(2,1)} %get-tuple-element.131) | copy-start | bytes 2359300
  579.5 5.9 collective-permute-start.15
  664.7 6.1 copy-start.29
  674.5 9.6 %collective-permute-start.17 = (bf16[768,1152]{1,0:T(8,128)(2,1)}, bf16[768,1152]{1,0:T(8,128)(2,1)}, u32[]{:S(2)}, u32[]{:S(2)}) collective-permute-start(bf16[768,1152]{1,0:T(8,128)(2,1)} %fusion.3), channel_id=1, source_target_pairs={{0,1},{1,0},{2,3},{3,2},{4,5},{5,4},{6,7},{7,6},{8,9},{9,8},{10,11... | collective-permute-start | bytes 5308424 | tf_op jit(solution)/shard_map/ppermute | solution.py:45
  674.5 9.6 %copy-start.3 = (bf16[4,128,2304]{2,1,0:T(8,128)(2,1)S(1)}, bf16[4,128,2304]{2,1,0:T(8,128)(2,1)}, u32[]{:S(2)}) copy-start(bf16[4,128,2304]{2,1,0:T(8,128)(2,1)} %unrotate.1.dqkv_ref) | copy-start | bytes 7077892
  681.5 1.5 collective-permute-start.18
  693.2 4.1 copy-start.21
  693.2 55.0 %all-to-all-start.7 = ((bf16[16,48,1664]{2,1,0:T(8,128)(2,1)}), bf16[16,48,1664]{2,1,0:T(8,128)(2,1)S(1)}, u32[]{:S(2)}, u32[]{:S(2)}) async-start(bf16[16,48,1664]{2,1,0:T(8,128)(2,1)} %bitcast.71), calls=%async_computation.9 | async-start | bytes 5111808 | tf_op jit(solution)/shard_map/all_to_all | solution.py:1077
  697.3 3.6 collective-permute-start.14
  697.7 15.3 %collective-permute-start.16 = (bf16[4,128,768]{2,1,0:T(8,128)(2,1)}, bf16[4,128,768]{2,1,0:T(8,128)(2,1)}, u32[]{:S(2)}, u32[]{:S(2)}) collective-permute-start(bf16[4,128,768]{2,1,0:T(8,128)(2,1)} %get-tuple-element.135), channel_id=1, source_target_pairs={{0,1},{1,0},{2,3},{3,2},{4,5},{5,4},{6,7},{7,6},{8,9},{9,8},{10,11... | collective-permute-start | bytes 2359304 | tf_op jit(solution)/shard_map/ppermute | solution.py:37
  705.4 7.6 %copy-start.22 = (bf16[4,128,768]{2,1,0:T(8,128)(2,1)S(1)}, bf16[4,128,768]{2,1,0:T(8,128)(2,1)}, u32[]{:S(2)}) copy-start(bf16[4,128,768]{2,1,0:T(8,128)(2,1)} %get-tuple-element.135) | copy-start | bytes 2359300
  (13 other events, 30.2 us)
Sparse Core Ops, SparseCore 0:
  285.4 87.2 reduce-scatter.2
  424.3 40.9 reduce-scatter.4

commit v3 on v2

--- a/solution.py
+++ b/solution.py
@@ -14,8 +14,8 @@
 LANES = 128
 BF = jnp.bfloat16
 F4 = jnp.float32
-TQ = 256
-TK = 512
+TQ = 512
+TK = 1024
 VMEM_LIMIT = 56 * 1024 * 1024
 
 
@@ -51,6 +51,17 @@
     if lax.axis_size("wt") == 2:
         return x + lax.ppermute(x, "wt", [(0, 1), (1, 0)])
     return lax.psum(x, "wt")
+
+
+def ctx_sum(x):
+    size = lax.axis_size("ctx")
+    if size & (size - 1):
+        return lax.psum(x, "ctx")
+    by = 1
+    while by < size:
+        x = x + lax.ppermute(x, "ctx", [(i, i ^ by) for i in range(size)])
+        by *= 2
+    return x
 
 
 def in_order(parts):
@@ -132,7 +143,18 @@
 
 
 SMEM = pl.BlockSpec(memory_space=pltpu.SMEM)
-VMEM = pl.BlockSpec(memory_space=pltpu.VMEM)
+
+
+def one_step(kernel, name, shift, arrays, shapes):
+    return pl.pallas_call(
+        kernel,
+        grid=(1,),
+        in_specs=[SMEM] + [whole(array.shape) for array in arrays],
+        out_specs=[whole(shape.shape) for shape in shapes],
+        out_shape=shapes,
+        compiler_params=params(1),
+        name=name,
+    )(shift, *arrays)
 
 
 def project(shift, x, gain, cosine, sine, parts, members, units):
@@ -140,17 +162,16 @@
     count = len(parts)
     heads = sum(part[0].shape[1] for part in parts) // HEAD_DIM
     flat = [w for part in parts for w in part]
-    return pl.pallas_call(
+    return one_step(
         functools.partial(project_kernel, heads, units, members, count),
-        in_specs=[SMEM] + [VMEM] * (4 + len(flat)),
-        out_specs=[VMEM, VMEM],
-        out_shape=[
+        "project",
+        shift,
+        [x, gain, cosine, sine, *flat],
+        [
             jax.ShapeDtypeStruct((members, 3 * units, rows // 2, LANES), BF),
             jax.ShapeDtypeStruct((seqs, rows, width), BF),
         ],
-        compiler_params=params(0),
-        name="project",
-    )(shift, x, gain, cosine, sine, *flat)
+    )
 
 
 def gather_keys(inv_ref, w, kv_refs, kv_s, members, chunk):
@@ -179,7 +200,7 @@
 def attend_kernel(members, size, inv_ref, len_ref, w_ref, *refs):
     kv_refs = refs[:size]
     o_ref, of_ref, lse_ref = refs[size : size + 3]
-    kv_s, vt_s, q_s, o_s = refs[size + 3 :]
+    kv_s, vt_s, q_s, o_s, s_s = refs[size + 3 :]
     u = pl.program_id(0)
     chunk = kv_refs[0].shape[2]
     own_rows = q_s.shape[0]
@@ -208,29 +229,30 @@
         place = t * span + (index // chunk) * (size * chunk) + w * chunk + index % chunk
         limit = jnp.minimum(place, length - 1)
 
-        def step(masked, kt, state):
-            top, total, acc = state
+        def first_step(masked, kt, top):
             start = pl.multiple_of(kt * TK, TK)
             scores = dot(kv_s[pl.ds(start, TK), :], qt)
             if masked:
                 keys = kt * TK + lax.broadcasted_iota(jnp.int32, (TK, 1), 0)
                 scores = jnp.where(keys <= limit, scores, -1e30)
-            new_top = jnp.maximum(top, jnp.max(scores, axis=0, keepdims=True))
-            weights = jnp.exp(scores - new_top)
-            fade = jnp.exp(top - new_top)
-            total = total * fade + jnp.sum(weights, axis=0, keepdims=True)
-            acc = acc * fade + dot(vt_s[kt], weights.astype(BF))
-            return new_top, total, acc
+            s_s[kt] = scores
+            return jnp.maximum(top, jnp.max(scores.reshape(TK // 8, 8, TQ), axis=0))
+
+        def second_step(kt, state):
+            total, acc = state
+            weights = jnp.exp(s_s[kt] - top)
+            total = total + jnp.sum(weights.reshape(TK // 8, 8, TQ), axis=0)
+            return total, acc + dot(vt_s[kt], weights.astype(BF))
 
         clear = jnp.minimum(t * span, length) // TK
         last = jnp.minimum(pl.cdiv((t + 1) * span, TK), pl.cdiv(length, TK))
-        state = (
-            jnp.full((1, TQ), -1e30, F4),
-            jnp.zeros((1, TQ), F4),
-            jnp.zeros((HEAD_DIM, TQ), F4),
-        )
-        state = lax.fori_loop(0, clear, functools.partial(step, False), state)
-        top, total, acc = lax.fori_loop(clear, last, functools.partial(step, True), state)
+        top = jnp.full((8, TQ), -1e30, F4)
+        top = lax.fori_loop(0, clear, functools.partial(first_step, False), top)
+        top = lax.fori_loop(clear, last, functools.partial(first_step, True), top)
+        top = jnp.max(top, axis=0, keepdims=True)
+        state = (jnp.zeros((8, TQ), F4), jnp.zeros((HEAD_DIM, TQ), F4))
+        total, acc = lax.fori_loop(0, last, second_step, state)
+        total = jnp.sum(total, axis=0, keepdims=True)
         result = acc / total
         of_ref[0, t] = result
         lse_ref[0, t] = top + jnp.log(total)
@@ -273,6 +295,7 @@
                 pltpu.VMEM((slot // TK, HEAD_DIM, TK), BF),
                 pltpu.VMEM((rows, LANES), F4),
                 pltpu.VMEM((rows, LANES), F4),
+                pltpu.VMEM((slot // TK, TK, TQ), F4),
             ],
         ),
         out_shape=[
@@ -371,7 +394,7 @@
             for k, ref in enumerate(dkv_refs):
                 core = lax.rem(w + k, size)
                 start = pl.multiple_of(block * size * chunk + core * chunk, chunk)
-                ref[chip, half] = dkv_s[pl.ds(start, chunk), :]
+                ref[chip, half] = dkv_s[pl.ds(start, chunk), :].astype(ref.dtype)
 
 
 def attend_back(inv, lengths, w, blocks, do_msg, kept, lse, units):
@@ -404,7 +427,10 @@
             ],
         ),
         out_shape=[jax.ShapeDtypeStruct((members, units, chunk, LANES), BF)]
-        + [jax.ShapeDtypeStruct((members, 2 * units, chunk, LANES), F4)] * size,
+        + [
+            jax.ShapeDtypeStruct((members, 2 * units, chunk, LANES), BF if k else F4)
+            for k in range(size)
+        ],
         compiler_params=params(1),
         name="attend_back",
     )(inv, lengths, w, *blocks, do_msg, kept, lse)
@@ -440,18 +466,17 @@
 def mix(shift, o_msg, x, gain, parts):
     seqs, rows, width = x.shape
     inner = sum(part.shape[0] for part in parts)
-    return pl.pallas_call(
+    return one_step(
         functools.partial(mix_kernel, inner // HEAD_DIM, len(parts)),
-        in_specs=[SMEM] + [VMEM] * (3 + len(parts)),
-        out_specs=[VMEM] * 3,
-        out_shape=[
+        "mix",
+        shift,
+        [o_msg, x, gain, *parts],
+        [
             jax.ShapeDtypeStruct((seqs, rows, inner), BF),
             jax.ShapeDtypeStruct((seqs, rows, width), F4),
             jax.ShapeDtypeStruct((seqs, rows, width), BF),
         ],
-        compiler_params=params(0),
-        name="mix",
-    )(shift, o_msg, x, gain, *parts)
+    )
 
 
 def norm_back(values, gain, upstream):
@@ -462,10 +487,11 @@
     return result, jnp.sum(upstream * unit, axis=0, keepdims=True)
 
 
-def unrotate_kernel(heads, count, shift_ref, msg_ref, cos_ref, sin_ref, dqkv_ref):
+def unrotate_kernel(heads, count, shift_ref, msg_ref, cos_ref, sin_ref, at_ref, *outs):
+    dqkv_ref, *grad_refs = outs
     members, triple, chunk, _ = msg_ref.shape
     units = triple // 3
-    seqs = dqkv_ref.shape[0]
+    seqs, rows, _ = dqkv_ref.shape
     cosine, sine = cos_ref[...], sin_ref[...]
     per = heads // count
     inner = per * HEAD_DIM
@@ -473,7 +499,7 @@
     def rope_back(grad):
         return grad * cosine - turn_halves(grad) * sine
 
-    for k in range(count):
+    for k in list(range(1, count)) + [0]:
         for s in range(seqs):
             for g in range(per // 2):
                 pair, asked = [], []
@@ -492,21 +518,26 @@
                 dqkv_ref[s, :, at : at + LANES] = rope_back(key).astype(BF)
                 at = at + inner
                 dqkv_ref[s, :, at : at + LANES] = value.astype(BF)
-
-
-def unrotate(shift, msg, cosine, sine, seqs, heads, count):
+        cols = dqkv_ref[:, :, 3 * k * inner : 3 * (k + 1) * inner]
+        made = dot(at_ref[...], cols.reshape(seqs * rows, 3 * inner))
+        grad_refs[k][...] = made.astype(grad_refs[k].dtype)
+
+
+def unrotate(shift, msg, cosine, sine, a1_turned, seqs, heads, count):
     rows = 2 * msg.shape[2]
-    return pl.pallas_call(
+    width = a1_turned.shape[0]
+    inner = heads * HEAD_DIM
+    return one_step(
         functools.partial(unrotate_kernel, heads, count),
-        in_specs=[SMEM] + [VMEM] * 3,
-        out_specs=VMEM,
-        out_shape=jax.ShapeDtypeStruct((seqs, rows, 3 * heads * HEAD_DIM), BF),
-        compiler_params=params(0),
-        name="unrotate",
-    )(shift, msg, cosine, sine)
-
-
-def unproject_kernel(count, dqkv_ref, x_ref, dstate_ref, gain_ref, *refs):
+        "unrotate",
+        shift,
+        [msg, cosine, sine, a1_turned],
+        [jax.ShapeDtypeStruct((seqs, rows, 3 * inner), BF)]
+        + [jax.ShapeDtypeStruct((width, 3 * inner // count), BF if k else F4) for k in range(count)],
+    )
+
+
+def unproject_kernel(count, shift_ref, dqkv_ref, x_ref, dstate_ref, gain_ref, *refs):
     w_refs = refs[:count]
     dx_ref, dgain_ref = refs[count:]
     seqs, rows, width = x_ref.shape
@@ -525,53 +556,81 @@
     dgain_ref[...] = total
 
 
-def unproject(dqkv, x, dstate, gain, parts):
+def unproject(shift, dqkv, x, dstate, gain, parts):
     seqs, rows, width = x.shape
-    return pl.pallas_call(
+    return one_step(
         functools.partial(unproject_kernel, len(parts)),
-        in_specs=[VMEM] * (4 + len(parts)),
-        out_specs=[VMEM] * 2,
-        out_shape=[
+        "unproject",
+        shift,
+        [dqkv, x, dstate, gain, *parts],
+        [
             jax.ShapeDtypeStruct((seqs, rows, width), BF),
             jax.ShapeDtypeStruct((1, width), F4),
         ],
-        compiler_params=params(0),
-        name="unproject",
-    )(dqkv, x, dstate, gain, *parts)
-
-
-def dispatch_kernel(info_ref, second_ref, cot_ref, out_ref):
-    step = pl.program_id(0)
-    count, held, double = out_ref.shape
-    width = double // 2
-    shape = (count * held, info_ref.shape[1])
-    ids = lax.broadcasted_iota(jnp.int32, shape, 0) + step * (count * held)
-    target = info_ref[0:2, :].astype(jnp.int32)
-    one, two = ids == target[0:1], ids == target[1:2]
+    )
+
+
+def two_gates(picked):
+    top = jnp.maximum(*picked)
+    raised = [jnp.exp(value - top) for value in picked]
+    total = raised[0] + raised[1]
+    return [value / total for value in raised]
+
+
+def slot_hits(info_ref, count):
+    shape = (count, info_ref.shape[1])
+    ids = lax.broadcasted_iota(jnp.int32, shape, 0) + pl.program_id(0) * count
+    return ids == info_ref[0:1, :], ids == info_ref[1:2, :]
+
+
+def dispatch_kernel(info_ref, *refs):
+    *second_refs, out_ref = refs
+    count, held, width = out_ref.shape
+    part = second_refs[0].shape[0]
+    one, two = slot_hits(info_ref, count * held)
     hits = (one | two).astype(BF)
-    gate = jnp.where(one, info_ref[2:3, :], 0.0) + jnp.where(two, info_ref[3:4, :], 0.0)
-    gate = jnp.sum(gate, axis=1, keepdims=True)
-    out_ref[:, :, :width] = dot(hits, second_ref[...]).astype(BF).reshape(count, held, width)
-    out_ref[:, :, width:] = (
-        (dot(hits, cot_ref[...]) * gate).astype(BF).reshape(count, held, width)
-    )
-
-
-def dispatch(info, second, cot, experts, held):
-    total, width = second.shape
+    routed = 0.0
+    for k, ref in enumerate(second_refs):
+        routed = routed + dot(hits[:, k * part : (k + 1) * part], ref[...])
+    out_ref[...] = routed.astype(BF).reshape(count, held, width)
+
+
+def dispatch_early_kernel(info_ref, cot_ref, out_ref):
+    count, held, wide = out_ref.shape
+    width = cot_ref.shape[1]
+    one, two = slot_hits(info_ref, count * held)
+    hits = (one | two).astype(BF)
+    out_ref[:, :, :width] = dot(hits, cot_ref[...]).astype(BF).reshape(count, held, width)
+    other = jnp.where(one, info_ref[3:4, :], 0) + jnp.where(two, info_ref[2:3, :], 0)
+    other = jnp.sum(other.astype(F4), axis=1, keepdims=True)
+    other = jnp.broadcast_to(other, (count * held, wide - width)).astype(BF)
+    out_ref[:, :, width:] = other.reshape(count, held, wide - width)
+
+
+def dispatch(kernel, info, arrays, wide, experts, held, name):
     count = 4 if experts % 4 == 0 else 1
     return pl.pallas_call(
-        dispatch_kernel,
+        kernel,
         grid=(experts // count,),
-        in_specs=[whole(info.shape), whole(second.shape), whole(cot.shape)],
-        out_specs=pl.BlockSpec((count, held, 2 * width), lambda e: (e, 0, 0)),
-        out_shape=jax.ShapeDtypeStruct((experts, held, 2 * width), BF),
+        in_specs=[whole(array.shape) for array in (info, *arrays)],
+        out_specs=pl.BlockSpec((count, held, wide), lambda e: (e, 0, 0)),
+        out_shape=jax.ShapeDtypeStruct((experts, held, wide), BF),
         compiler_params=params(1),
-        name="dispatch",
-    )(info, second, cot)
-
-
-def finish_kernel(heads, size, count, shift_ref, info_ref, state_ref, cot_ref, gain_ref, router_ref, *refs):
+        name=name,
+    )(info, *arrays)
+
+
+def two_gates(picked):
+    top = jnp.maximum(*picked)
+    raised = [jnp.exp(value - top) for value in picked]
+    total = raised[0] + raised[1]
+    return [value / total for value in raised]
+
+
+def finish_kernel(
+    heads, size, count, shift_ref, info_ref, second_ref, state_ref, cot_ref, gain_ref, *refs
+):
+    router_ref, turned_ref, *refs = refs
     home_refs, refs = refs[:size], refs[size:]
     dense_refs, refs = refs[:size], refs[size:]
     w_refs = refs[:count]
@@ -581,11 +640,15 @@
     lines = take * rows
     members, units, chunk, _ = msg_ref.shape
     slots = home_refs[0].shape[0]
-    experts = router_ref.shape[0]
+    experts = turned_ref.shape[0]
     info = info_ref[...].reshape(lines, info_ref.shape[2])
-    target = info[:, : 2 * size].astype(jnp.int32)
-    gates = [info[:, 2 * size + c : 2 * size + c + 1] for c in range(2)]
-    chosen = info[:, 2 * size + 2 : 2 * size + 4].astype(jnp.int32)
+    target = info[:, : 2 * size]
+    chosen = [info[:, 2 * size + c : 2 * size + c + 1] for c in range(2)]
+    logits = dot(second_ref[...].reshape(lines, width), router_ref[...])[:, :experts]
+    names = lax.broadcasted_iota(jnp.int32, (lines, experts), 1)
+    gates = two_gates(
+        [jnp.sum(jnp.where(names == pick, logits, 0.0), axis=1, keepdims=True) for pick in chosen]
+    )
     ids = lax.broadcasted_iota(jnp.int32, (lines, slots), 1)
     made, back = [0.0, 0.0], 0.0
     for k in range(size):
@@ -596,15 +659,12 @@
     cot = cot_ref[...].reshape(lines, width).astype(F4)
     pulled = [jnp.sum(y * cot, axis=-1, keepdims=True) for y in made]
     middle = gates[0] * pulled[0] + gates[1] * pulled[1]
-    names = lax.broadcasted_iota(jnp.int32, (lines, experts), 1)
     logit = 0.0
     for c in range(2):
-        logit = logit + jnp.where(
-            names == chosen[:, c : c + 1], gates[c] * (pulled[c] - middle), 0.0
-        )
+        logit = logit + jnp.where(names == chosen[c], gates[c] * (pulled[c] - middle), 0.0)
     logit = logit.astype(BF)
     logit_ref[...] = logit.reshape(take, rows, experts)
-    back = back + dot(logit, router_ref[...])
+    back = back + dot(logit, turned_ref[...])
     branch = gates[0] * made[0] + gates[1] * made[1]
     for ref in dense_refs:
         dense = ref[...].reshape(lines, 2 * width)
@@ -640,18 +700,18 @@
                     msg_ref[chip, u] = pair[c].astype(BF)
 
 
-def finish(shift, info, state, cot, gain, router, homes, denses, parts, members, units):
+def finish(shift, info, second, state, cot, gain, router, turned, homes, denses, parts, members, units):
     seqs, rows, width = state.shape
     inner = sum(part.shape[1] for part in parts)
-    experts = router.shape[0]
+    experts = turned.shape[0]
     take = max(1, min(seqs, 256 // rows))
     msg = (members, units, rows // 2, LANES)
     some = lambda cols: pl.BlockSpec((take, rows, cols), lambda s: (s, 0, 0))
     return pl.pallas_call(
         functools.partial(finish_kernel, inner // HEAD_DIM, len(homes), len(parts)),
         grid=(seqs // take,),
-        in_specs=[SMEM, some(info.shape[2]), some(width), some(width), whole((1, width))]
-        + [whole(router.shape)]
+        in_specs=[SMEM, some(info.shape[2]), some(width), some(width), some(width)]
+        + [whole((1, width)), whole(router.shape), whole(turned.shape)]
         + [whole(home.shape) for home in homes]
         + [some(2 * width)] * len(denses)
         + [whole(part.shape) for part in parts],
@@ -666,39 +726,51 @@
         ],
         compiler_params=params(1),
         name="finish",
-    )(shift, info, state, cot, gain, router, *homes, *denses, *parts)
-
-
-def place_kernel(copies, *refs):
-    total = refs[0][...].astype(F4)
-    for ref in refs[1:copies]:
-        total = total + ref[...].astype(F4)
-    for n, out in enumerate(refs[copies:]):
+    )(shift, info, second, state, cot, gain, router, turned, *homes, *denses, *parts)
+
+
+def place_kernel(copies, cuts, *refs):
+    whole_refs = refs[cuts * copies :]
+    blocks = []
+    for n in range(cuts):
+        total = refs[n * copies][...].astype(F4)
+        for ref in refs[n * copies + 1 : (n + 1) * copies]:
+            total = total + ref[...].astype(F4)
+        blocks.append(total)
+    total = jnp.concatenate(blocks, axis=-1)
+    for n, out in enumerate(whole_refs):
         out[...] = untile(total, n)
 
 
 def place(blocks, experts):
-    members, rows, triple = blocks.shape
-    hidden = triple // 3
+    members, rows, _ = blocks[0].shape
+    hidden = sum(block.shape[2] for block in blocks) // 3
     copies = members // experts
     take = 2 if experts % 2 == 0 else 1
     return pl.pallas_call(
-        functools.partial(place_kernel, copies),
+        functools.partial(place_kernel, copies, len(blocks)),
         grid=(experts // take,),
         in_specs=[
-            pl.BlockSpec((take, rows, triple), lambda e, n=n: (n * experts // take + e, 0, 0))
+            pl.BlockSpec(
+                (take, rows, block.shape[2]), lambda e, n=n: (n * experts // take + e, 0, 0)
+            )
+            for block in blocks
             for n in range(copies)
         ],
         out_specs=[pl.BlockSpec((take, rows, hidden), lambda e: (e, 0, 0))] * 3,
         out_shape=[jax.ShapeDtypeStruct((experts, rows, hidden), F4)] * 3,
         compiler_params=params(1),
         name="place",
-    )(*[blocks] * copies)
-
-
-def gated_kernel(count, tiles, x_ref, d_ref, *refs):
-    w_refs = refs[: 3 * count]
-    out_ref, hid_ref, acc_ref = refs[3 * count :]
+    )(*[block for block in blocks for n in range(copies)])
+
+
+def gated_kernel(count, tiles, routed, *refs):
+    if routed:
+        expert_ref, router_ref, early_ref, x_ref, *refs = refs
+        d_ref = refs[3 * count]
+    else:
+        d_ref, x_ref, *refs = refs
+    w_refs, (out_ref, hid_ref, acc_ref) = refs[: 3 * count], refs[-3:]
     step = pl.program_id(0)
     rows, width = x_ref.shape
     tile = hid_ref.shape[1] // 3
@@ -707,6 +779,16 @@
     @pl.when(step == 0)
     def _():
         acc_ref[...] = jnp.zeros_like(acc_ref)
+        if routed:
+            logits = dot(x_ref[...], router_ref[...])
+            names = lane_of(logits.shape)
+            other = early_ref[:, width : width + 1].astype(F4).astype(jnp.int32)
+            picked = [
+                jnp.sum(jnp.where(names == name, logits, 0.0), axis=1, keepdims=True)
+                for name in (expert_ref[0], other)
+            ]
+            gate = two_gates(picked)[0]
+            d_ref[...] = (early_ref[:, :width].astype(F4) * gate).astype(BF)
 
     for k in range(count):
 
@@ -738,7 +820,7 @@
     return min(512, hidden)
 
 
-def gated(x, d, parts, kind, name, both=False):
+def gated(x, d, parts, kind, name, routed=()):
     rows = x.shape[0]
     width, hidden = parts[0][0].shape
     tile = tile_of(hidden)
@@ -751,23 +833,23 @@
         lines = pl.BlockSpec((tile, width), lambda f, at=at: (at(f), 0))
         flat += list(part)
         specs += [cols, cols, lines]
+    ahead = [SMEM, whole(routed[1].shape)] if routed else []
+    gated_out = [(whole((rows, width)), jax.ShapeDtypeStruct((rows, width), BF))] if routed else []
     return pl.pallas_call(
-        functools.partial(gated_kernel, count, tiles),
+        functools.partial(gated_kernel, count, tiles, bool(routed)),
         grid=(count * tiles,),
-        in_specs=[
-            pl.BlockSpec((rows, width), lambda f: (0, 0)),
-            pl.BlockSpec((rows, width), lambda f: (0, 1 if both else 0)),
-        ]
-        + specs,
-        out_specs=[whole((rows, 2 * width)), pl.BlockSpec((rows, 3 * tile), lambda f: (0, f))],
-        out_shape=[
+        in_specs=ahead + [whole(d.shape), whole(x.shape)] + specs,
+        out_specs=[spec for spec, _ in gated_out]
+        + [whole((rows, 2 * width)), pl.BlockSpec((rows, 3 * tile), lambda f: (0, f))],
+        out_shape=[shape for _, shape in gated_out]
+        + [
             jax.ShapeDtypeStruct((rows, 2 * width), kind),
             jax.ShapeDtypeStruct((rows, 3 * count * hidden), BF),
         ],
         scratch_shapes=[pltpu.VMEM((rows, 2 * width), F4)],
         compiler_params=params(1),
         name=name,
-    )(x, d, *flat)
+    )(*routed, d, x, *flat)
 
 
 def gated_grads_kernel(x_ref, d_ref, hid_ref, out_ref, xt_ref, dt_ref):
@@ -782,9 +864,8 @@
     out_ref[:, 2 * tile :] = dot(dt_ref[...], hid_ref[:, 2 * tile :]).astype(BF)
 
 
-def gated_grads(x, d, hid, k, count, name, both=False):
-    rows = x.shape[0]
-    width = x.shape[1] // 2 if both else x.shape[1]
+def gated_grads(x, d, hid, k, count, name):
+    rows, width = x.shape
     hidden = hid.shape[1] // 3 // count
     tile = tile_of(hidden)
     tiles = hidden // tile
@@ -792,8 +873,8 @@
         gated_grads_kernel,
         grid=(tiles,),
         in_specs=[
-            pl.BlockSpec((rows, width), lambda f: (0, 0)),
-            pl.BlockSpec((rows, width), lambda f: (0, 1 if both else 0)),
+            whole(x.shape),
+            whole(d.shape),
             pl.BlockSpec((rows, 3 * tile), lambda f: (0, k * tiles + f)),
         ],
         out_specs=pl.BlockSpec((width, 3 * tile), lambda f: (0, f)),
@@ -882,6 +963,26 @@
     msg, a1 = project(shift, x, attn_gain[None], cosine, sine, parts, members, units)
     got = lax.all_to_all(msg, "ctx", 0, 0, tiled=True)
 
+    near = 4 if members % 4 == 0 else 1
+    outer = members // near
+    near_groups = [[o * near + i for i in range(near)] for o in range(outer)]
+    far_groups = [[o * near + i for o in range(outer)] for i in range(near)]
+
+    def by_steps(array):
+        array = array.reshape(outer, near, width // members, -1).swapaxes(0, 1)
+        return array.reshape(width, -1)
+
+    def near_scatter(array):
+        return lax.psum_scatter(
+            array, "ctx", scatter_dimension=0, tiled=True, axis_index_groups=near_groups
+        )
+
+    def far_scatter(array):
+        return lax.psum_scatter(
+            array, "ctx", scatter_dimension=0, tiled=True, axis_index_groups=far_groups
+        )
+
+    a1_turned = by_steps(a1.reshape(rows, width).T)
     back_parts = [jnp.concatenate([weight.T for weight in part]) for part in parts]
     out_back = [part.T for part in out_parts]
     expert = ctx % experts
@@ -927,45 +1028,17 @@
     chosen, order_here = own_first(chosen_all), own_first(order_all)
     target = targets(chosen, order_here, w)
     own_targets = [
-        targets(chosen[:rows], order_here[:rows], (w + k) % size).astype(F4) for k in range(size)
+        targets(chosen[:rows], order_here[:rows], (w + k) % size) for k in range(size)
     ]
+    own_info = jnp.concatenate(own_targets + [chosen[:rows]], axis=1)
+    own_info = own_info.reshape(seqs, 2 * chunk, -1)
+    info = jnp.concatenate([target, chosen, jnp.zeros((total_rows, 4), jnp.int32)], axis=1).T
+    router_wide = jnp.pad(router_weight, ((0, 0), (0, LANES - experts)))
+    router_turned = router_weight.T
     inv = jnp.argsort(block_pairs).astype(jnp.int32)
     unit_slots = jnp.minimum((ctx + members * jnp.arange(units)) // heads, seqs - 1)
     unit_lengths = lengths[unit_slots]
     w_arg = w.astype(jnp.int32)[None]
-    got, back_parts, out_back, expert_parts, cots, cot, chosen, target, own_targets, inv, unit_lengths = (
-        lax.optimization_barrier(
-            (
-                got,
-                back_parts,
-                out_back,
-                expert_parts,
-                cots,
-                cot,
-                chosen,
-                target,
-                own_targets,
-                inv,
-                unit_lengths,
-            )
-        )
-    )
-
-    blocks = wt_gather(got)
-    o_msg, kept, lse = attend(inv, unit_lengths, w_arg, blocks, units)
-    o_got = lax.all_to_all(o_msg, "ctx", 0, 0, tiled=True)
-    mixed, state, second_own = mix(shift, o_got, x, ffn_gain[None], out_parts)
-
-    second = jnp.concatenate(wt_gather(second_own.reshape(rows, width)))
-    picks = chosen[:, :, None] == names
-    logits = dot(second, router_weight)
-    selected = jnp.sum(jnp.where(picks, logits[:, None, :], 0.0), axis=-1)
-    raised = jnp.exp(selected - jnp.max(selected, axis=-1, keepdims=True))
-    gates = raised / jnp.sum(raised, axis=-1, keepdims=True)
-    info = jnp.concatenate([target.astype(F4), gates, jnp.zeros((total_rows, 4), F4)], axis=1)
-    sent = dispatch(info.T, second, cot, experts, held)
-    info = jnp.concatenate(own_targets + [gates[:rows], chosen[:rows].astype(F4)], axis=1)
-    info = info.reshape(seqs, 2 * chunk, -1)
     groups = None
     if members != experts:
         groups = [[g * experts + e for e in range(experts)] for g in range(members // experts)]
@@ -978,57 +1051,103 @@
         tiled=True,
     )
 
-    sent, second = lax.optimization_barrier((sent, second))
+    early = dispatch(
+        dispatch_early_kernel, info, [cot], width + LANES, experts, held, "dispatch_early"
+    )
+    (
+        got,
+        early,
+        a1_turned,
+        back_parts,
+        out_back,
+        expert_parts,
+        cots,
+        cot,
+        own_info,
+        info,
+        router_wide,
+        router_turned,
+        inv,
+        unit_lengths,
+    ) = (
+        lax.optimization_barrier(
+            (
+                got,
+                early,
+                a1_turned,
+                back_parts,
+                out_back,
+                expert_parts,
+                cots,
+                cot,
+                own_info,
+                info,
+                router_wide,
+                router_turned,
+                inv,
+                unit_lengths,
+            )
+        )
+    )
+
+    blocks = wt_gather(got)
+    early = swap(early)
+    o_msg, kept, lse = attend(inv, unit_lengths, w_arg, blocks, units)
+    o_msg, early = lax.optimization_barrier((o_msg, early))
+    o_got = lax.all_to_all(o_msg, "ctx", 0, 0, tiled=True)
+    mixed, state, second_own = mix(shift, o_got, x, ffn_gain[None], out_parts)
+
+    seconds = wt_gather(second_own.reshape(rows, width))
+    sent = dispatch(dispatch_kernel, info, seconds, width, experts, held, "dispatch")
+
+    sent, seconds = lax.optimization_barrier((sent, seconds))
+    second = jnp.concatenate(seconds)
     arrived = swap(sent)
     dense, dense_hid = gated(second, cot, [[dense_gate, dense_up, dense_down]], F4, "dense_branch")
     dense_grads = gated_grads(second, cot, dense_hid, 0, 1, "dense_grads")
-    near = 4 if members % 4 == 0 else 1
-    outer = members // near
-    near_groups = [[o * near + i for i in range(near)] for o in range(outer)]
-    far_groups = [[o * near + i for o in range(outer)] for i in range(near)]
-    dense_grads = dense_grads.reshape(outer, near, width // members, -1).swapaxes(0, 1)
-    dense_grads = dense_grads.reshape(width, -1)
+    dense_grads = by_steps(dense_grads)
     denses = [dense[:rows]]
     for k in range(1, size):
         perm = [(i, (i + k) % size) for i in range(size)]
         denses.append(lax.ppermute(dense[k * rows : (k + 1) * rows], "wt", perm))
     arrived, denses, dense_grads = lax.optimization_barrier((arrived, denses, dense_grads))
-    dense_near = lax.psum_scatter(
-        dense_grads,
-        "ctx",
-        scatter_dimension=0,
-        tiled=True,
-        axis_index_groups=near_groups,
-    )
-
-    arrived = arrived.reshape(experts * held, 2 * width)
-    returned, hid = gated(
-        arrived, arrived, [list(part) for part in expert_parts], BF, "expert_branch", True
+    dense_near = near_scatter(dense_grads)
+
+    arrived = arrived.reshape(experts * held, width)
+    dye, returned, hid = gated(
+        arrived,
+        early.reshape(experts * held, -1),
+        expert_parts,
+        BF,
+        "expert_branch",
+        (expert.astype(jnp.int32)[None], router_wide),
     )
     home = swap(returned.reshape(experts, held, 2 * width))
     hidden = expert_gate.shape[2]
     expert_sum = None
     for k in list(range(1, size)) + [0]:
-        made = gated_grads(arrived, arrived, hid, k, size, "expert_grads", True)
+        made = gated_grads(arrived, dye, hid, k, size, "expert_grads")
         if k:
             made = lax.ppermute(made, "wt", [(i, (i + k) % size) for i in range(size)])
         expert_sum = made.astype(F4) if expert_sum is None else expert_sum + made.astype(F4)
     expert_sum = expert_sum.astype(BF).reshape(members, width // members, 3 * hidden)
+    cut = 3 * hidden // 2
+    expert_sum = [expert_sum[:, :, :cut], expert_sum[:, :, cut:]]
     home, expert_sum, dense_near = lax.optimization_barrier((home, expert_sum, dense_near))
-    dense_sum = lax.psum_scatter(
-        dense_near, "ctx", scatter_dimension=0, tiled=True, axis_index_groups=far_groups
-    )
+    dense_sum = far_scatter(dense_near)
     homes = wt_gather(home.reshape(experts * held, 2 * width))
 
     own_cot = cots[0].reshape(seqs, 2 * chunk, width)
     denses = [part.reshape(seqs, 2 * chunk, 2 * width) for part in denses]
     output, dstate, dstate_low, logit_back, do_msg, ffn_grad = finish(
         shift,
-        info,
+        own_info,
+        second_own,
         state,
         own_cot,
         ffn_gain[None],
-        router_weight.T,
+        router_wide,
+        router_turned,
         homes,
         denses,
         out_back,
@@ -1050,33 +1169,41 @@
             pieces.append(made if k == 0 else made.astype(BF))
         return wt_scatter(pieces).astype(BF)
 
-    def by_owner(blocks):
-        return jnp.concatenate(blocks, axis=1).reshape(members, width // members, -1)
-
     router_grad = dot_tn(second_own.reshape(rows, width), logit_back.reshape(rows, experts))
     small = wt_sum(jnp.concatenate([ffn_grad.T, router_grad], axis=1))
-    out_grad = split_wt(dstate_low, mixed, 1)
-    do_got, out_grad, small, output, expert_sum, dense_sum = lax.optimization_barrier(
-        (do_got, out_grad, small, output, expert_sum, dense_sum)
-    )
-    expert_got = lax.all_to_all(expert_sum, "ctx", 0, 0, tiled=True)
+    small_high = small.astype(BF)
+    small_low = (small - small_high.astype(F4)).astype(BF)
+    few = experts + 1
+    blank = jnp.zeros((width, -(2 * few) % LANES), BF)
+    out_msg = [split_wt(dstate_low, mixed, 1), small_high, small_low, blank]
+    out_msg = by_steps(jnp.concatenate(out_msg, axis=1))
+    do_got, out_msg, output, dense_sum, expert_sum = lax.optimization_barrier(
+        (do_got, out_msg, output, dense_sum, expert_sum)
+    )
+    expert_got = [lax.all_to_all(expert_sum[0], "ctx", 0, 0, tiled=True)]
+    out_near = near_scatter(out_msg)
     dq, *dkv = attend_back(inv, unit_lengths, w_arg, blocks, do_got, kept, lse, units)
-    dq, dkv, expert_got = lax.optimization_barrier((dq, dkv, expert_got))
+    dq, dkv, expert_got, out_near = lax.optimization_barrier((dq, dkv, expert_got, out_near))
+    out_sum = far_scatter(out_near)
     dkv = wt_scatter(dkv).astype(BF)
     grad_msg = jnp.concatenate([dkv, dq], axis=1)
     grad_got = lax.all_to_all(grad_msg, "ctx", 0, 0, tiled=True)
+    grad_got, out_sum, expert_sum = lax.optimization_barrier((grad_got, out_sum, expert_sum))
+    expert_got.append(lax.all_to_all(expert_sum[1], "ctx", 0, 0, tiled=True))
+    dqkv, *pieces = unrotate(shift, grad_got, cosine, sine, a1_turned, seqs, heads, len(parts))
+    if split:
+        last_msg = wt_scatter(pieces).astype(BF)
+    else:
+        last_msg = by_steps(split_wt(a1, dqkv, 3))
+    last_sum = far_scatter(near_scatter(last_msg))
+    dqkv, last_msg = lax.optimization_barrier((dqkv, last_msg))
+    dx, attn_grad = unproject(shift, dqkv, x, dstate, attn_gain[None], back_parts)
+    attn_grad = ctx_sum(wt_sum(attn_grad)).reshape(members, -1)
+    attn_grad = lax.dynamic_index_in_dim(attn_grad, ctx, 0, False)
     expert_grads = place(expert_got, experts)
-    dqkv = unrotate(shift, grad_got, cosine, sine, seqs, heads, len(parts))
-    dx, attn_grad = unproject(dqkv, x, dstate, attn_gain[None], back_parts)
-    small = jnp.concatenate([wt_sum(attn_grad).T, small], axis=1)
-    small_high = small.astype(BF)
-    small_low = (small - small_high.astype(F4)).astype(BF)
-    few = experts + 2
-    blank = jnp.zeros((width, -(2 * few) % LANES), BF)
-    last_msg = by_owner([split_wt(a1, dqkv, 3), out_grad, small_high, small_low, blank])
-    last_got = lax.all_to_all(last_msg, "ctx", 0, 0, tiled=True)
-    last_sum = jnp.sum(last_got.astype(F4), axis=0)
-    tail = last_sum[:, 4 * local :]
+    last_sum = last_sum.astype(F4)
+    out_sum = out_sum.astype(F4)
+    tail = out_sum[:, local:]
     tail = tail[:, :few] + tail[:, few : 2 * few]
 
     def to_tokens(own):
@@ -1086,11 +1213,11 @@
     return (
         to_tokens(output),
         to_tokens(dx),
+        attn_grad,
+        *[last_sum[:, n * local : (n + 1) * local] for n in range(3)],
+        out_sum[:, :local].T,
         tail[:, 0],
-        *[last_sum[:, n * local : (n + 1) * local] for n in range(3)],
-        last_sum[:, 3 * local : 4 * local].T,
-        tail[:, 1],
-        tail[:, 2:],
+        tail[:, 1:],
         *expert_grads[:2],
         expert_grads[2].transpose(0, 2, 1),
         *[untile(dense_sum, n).astype(F4) for n in range(2)],

time: 769 us -> 671 us (0.87); the launches traced: 758 us -> 670 us
  blocking collectives: 76.6 us -> 0 us
  waiting for transfers between devices: 241 us -> 215 us
  starting transfers between devices: 85.3 us -> 106 us
  matrix products: 11.4 us -> 2.94 us
  local copies, waits for them, and re-layouts: 60.2 us -> 68 us
    all_to_all x1 -> x0, blocking collectives: 76.6 us -> none  [per_device(): grad_got = lax.all_to_all(grad_msg, 'ctx', 0, 0, tiled=True)]
    reduce_scatter x2 -> x6, waiting for transfers between devices: 0.02 us -> 67.3 us  [the longest x3 34.6 us: near_scatter(): lax.psum_scatter(array, 'ctx', scatter_dimension=0, tiled=True, axis_inde...]
    all_to_all x2 -> x4, waiting for transfers between devices: 84.5 us -> 32.9 us  [the longest x1 17.9 us: per_device(): grad_got = lax.all_to_all(grad_msg, 'ctx', 0, 0, tiled=True)]
    all_to_all x2 -> x4, starting transfers between devices: 9.06 us -> 44.6 us  [the longest x1 15.6 us: per_device(): grad_got = lax.all_to_all(grad_msg, 'ctx', 0, 0, tiled=True)]
    all_to_all x1, waiting for transfers between devices: 36.9 us -> 1.39 us  [per_device(): arrived = swap(sent)]
    pallas_call x1, Pallas kernels: 50.4 us -> 30.4 us  [attend(): pl.pallas_call(functools.partial(attend_kernel, members, size), grid_spec...]
    all_to_all x1, starting transfers between devices: 22.3 us -> 10.5 us  [per_device(): o_got = lax.all_to_all(o_msg, 'ctx', 0, 0, tiled=True)]
    all_to_all x1, starting transfers between devices: 19.4 us -> 9.75 us  [per_device(): home = swap(returned.reshape(experts, held, 2 * width))]
  transfers between devices with their start and end apart: 28 -> 38, of which waited for: 13 -> 20; matrix products, arithmetic and copies ran while one was open for 10% -> 12% of each run, Pallas kernels for 22% -> 31%
where the time goes in v3:
time: 671 us; the launch traced here: 670 us
  Pallas kernels  232 us (35%)
  waiting for transfers between devices  215 us (32%)
  starting transfers between devices  106 us (16%)
  local copies, waits for them, and re-layouts  68 us (10%)
  other arithmetic  30.8 us (5%)
  between operations  15.8 us (2%)
    pallas_call x2, Pallas kernels, gated(): pl.pallas_call(functools.partial(gated_kernel, count, tiles, bool(routed)...  64.9 us
    all_to_all x1, waiting for transfers between devices, per_device(): home = swap(returned.reshape(experts, held, 2 * width))  42.1 us
    pallas_call x1, Pallas kernels, attend_back(): pl.pallas_call(functools.partial(attend_back_kernel, members, size), grid...  40.7 us
    pallas_call x3, Pallas kernels, gated_grads(): pl.pallas_call(gated_grads_kernel, grid=(tiles,), in_specs=[whole(x.shape...  35.2 us
    reduce_scatter x3, waiting for transfers between devices, near_scatter(): lax.psum_scatter(array, 'ctx', scatter_dimension=0, tiled=True, axis_inde...  34.6 us
    reduce_scatter x3, waiting for transfers between devices, far_scatter(): lax.psum_scatter(array, 'ctx', scatter_dimension=0, tiled=True, axis_inde...  32.8 us
    pallas_call x1, Pallas kernels, attend(): pl.pallas_call(functools.partial(attend_kernel, members, size), grid_spec...  30.4 us
    pallas_call x4, Pallas kernels, one_step(): pl.pallas_call(kernel, grid=(1,), in_specs=[SMEM] + [whole(array.shape) f...  25.8 us
  transfers between devices with their start and end apart: 38, of which 20 were waited for; matrix products, arithmetic and copies ran while one was open for 12% of the time, Pallas kernels for 31%

profile of v3, /device:TPU:0, one launch (start us, length us, event | category | flops | bytes accessed | tf_op | source)
XLA Modules:
  0.0 669.7 jit_solution(5593410856587865990)
XLA Ops:
  17.2 3.3 constant_dynamic-slice_fusion.2
  24.7 7.2 %project.1 = (bf16[16,9,64,128]{3,2,1,0:T(8,128)(2,1)}, bf16[4,128,768]{2,1,0:T(8,128)(2,1)}) custom-call(s32[1]{0:T(128)} %bitcast.shift_ref, bf16[4,128,768]{2,1,0:T(8,128)(2,1)} %bitcast.139, f32[1,768]{1,0:T(1,128)} %broadcast_in_dim.80.gain_ref, f32[128,128]{1,0:T(8,128)} %copy.183.cos_ref, f32[128,128]{1,0:T(8,128)} %copy.184.sin_ref, ...), custom_call_target="tpu_custom_call" | custom-call | tf_op jit(solution)/shard_map/project/pallas_call | solution.py:149
  31.8 8.0 %all-to-all-start = ((bf16[16,9,64,128]{3,2,1,0:T(8,128)(2,1)}), bf16[16,9,64,128]{3,2,1,0:T(8,128)(2,1)S(1)}, u32[]{:S(2)}, u32[]{:S(2)}) async-start(bf16[16,9,64,128]{3,2,1,0:T(8,128)(2,1)} %get-tuple-element.95), calls=%async_computation | async-start | bytes 4718592 | tf_op jit(solution)/shard_map/all_to_all | solution.py:964
  42.1 2.7 dynamic-slice_bitcast_fusion.refs_6_
  45.2 2.7 dynamic-slice_bitcast_fusion.1.refs_5_
  48.0 2.8 dynamic-slice_bitcast_fusion.2.refs_4_
  61.6 5.6 dispatch_early.1
  67.3 2.6 pad_maximum_fusion.1.refs_0_
  75.2 12.3 %all-to-all-done.refs_0_ = bf16[16,9,64,128]{3,2,1,0:T(8,128)(2,1)S(1)} async-done(((bf16[16,9,64,128]{3,2,1,0:T(8,128)(2,1)}), bf16[16,9,64,128]{3,2,1,0:T(8,128)(2,1)S(1)}, u32[]{:S(2)}, u32[]{:S(2)}) %all-to-all-start) | async-done | bytes 2359328 | tf_op jit(solution)/shard_map/all_to_all | solution.py:964
  87.5 12.3 %all-to-all-start.1 = ((bf16[16,80,896]{2,1,0:T(8,128)(2,1)}), bf16[16,80,896]{2,1,0:T(8,128)(2,1)}, u32[]{:S(2)}, u32[]{:S(2)}) async-start(bf16[16,80,896]{2,1,0:T(8,128)(2,1)} %dispatch_early.1), calls=%async_computation.1 | async-start | bytes 4587520 | tf_op jit(solution)/shard_map/all_to_all | solution.py:1094
  99.9 4.5 collective-permute-done.7.refs_1_
  105.8 30.4 %attend.1 = (bf16[16,3,64,128]{3,2,1,0:T(8,128)(2,1)}, f32[3,4,64,512]{3,2,1,0:T(8,128)}, f32[3,4,1,512]{3,2,1,0:T(1,128)}) custom-call(s32[16]{0:T(128)} %get-tuple-element.99.inv_ref, s32[3]{0:T(128)} %gather_fusion, s32[1]{0:T(128)} %bitcast.42.w_ref, bf16[16,9,64,128]{3,2,1,0:T(8,128)(2,1)} %copy-done.2, bf16[16,9,64,128]{3,2,1,0:T(8,128)(2,1)} %copy-done.5), custom_call_target="tpu_custom_call" | custom-call | tf_op jit(solution)/shard_map/attend/pallas_call | solution.py:282
  136.2 9.6 %all-to-all-done.1 = bf16[16,80,896]{2,1,0:T(8,128)(2,1)} async-done(((bf16[16,80,896]{2,1,0:T(8,128)(2,1)}), bf16[16,80,896]{2,1,0:T(8,128)(2,1)}, u32[]{:S(2)}, u32[]{:S(2)}) %all-to-all-start.1) | async-done | bytes 2293792 | tf_op jit(solution)/shard_map/all_to_all | solution.py:1094
  145.8 10.5 %all-to-all-start.2 = ((bf16[16,3,64,128]{3,2,1,0:T(8,128)(2,1)}), bf16[16,3,64,128]{3,2,1,0:T(8,128)(2,1)S(1)}, u32[]{:S(2)}, u32[]{:S(2)}) async-start(bf16[16,3,64,128]{3,2,1,0:T(8,128)(2,1)} %get-tuple-element.104), calls=%async_computation.2 | async-start | bytes 1572864 | tf_op jit(solution)/shard_map/all_to_all | solution.py:1097
  159.1 16.2 %all-to-all-done.2.o_ref = bf16[16,3,64,128]{3,2,1,0:T(8,128)(2,1)S(1)} async-done(((bf16[16,3,64,128]{3,2,1,0:T(8,128)(2,1)}), bf16[16,3,64,128]{3,2,1,0:T(8,128)(2,1)S(1)}, u32[]{:S(2)}, u32[]{:S(2)}) %all-to-all-start.2) | async-done | bytes 786464 | tf_op jit(solution)/shard_map/all_to_all | solution.py:1097
  176.2 4.3 mix.1
  183.9 5.0 dispatch.1
  188.9 5.0 all-to-all-start.3
  195.3 18.1 %dense_branch.1 = (f32[1024,1536]{1,0:T(8,128)}, bf16[1024,3072]{1,0:T(8,128)(2,1)}) custom-call(bf16[1024,768]{1,0:T(8,128)(2,1)} %pad_maximum_fusion.3.cot_ref.refs_0_.d_ref, bf16[1024,768]{1,0:T(8,128)(2,1)} %copy-done.10, bf16[768,1024]{1,0:T(8,128)(2,1)} %refs_2_.3, bf16[768,1024]{1,0:T(8,128)(2,1)} %refs_3_.1, bf16[1024,768]{1,0:T(8,128)(2,1)} %refs_4_.1), custom_call_target="tpu_custom_call" | custom-call | tf_op jit(solution)/shard_map/dense_branch/pallas_call | solution.py:838
  213.3 5.0 fusion.16
  218.3 10.5 %dense_grads.1 = bf16[768,3072]{1,0:T(8,128)(2,1)} custom-call(bf16[1024,768]{1,0:T(8,128)(2,1)} %copy-done.10, bf16[1024,768]{1,0:T(8,128)(2,1)} %pad_maximum_fusion.3.cot_ref.refs_0_.d_ref, bf16[1024,3072]{1,0:T(8,128)(2,1)} %get-tuple-element.117.hid_ref), custom_call_target="tpu_custom_call" | custom-call | flops 4831838208 | bytes 14155776 | tf_op jit(solution)/shard_map/dense_grads/pallas_call | solution.py:872
  228.8 4.9 copy.202
  236.4 46.8 %expert_branch.1 = (bf16[1280,768]{1,0:T(8,128)(2,1)}, bf16[1280,1536]{1,0:T(8,128)(2,1)}, bf16[1280,6144]{1,0:T(8,128)(2,1)}) custom-call(s32[1]{0:T(128)} %bitcast.46.refs_0_, bf16[768,128]{1,0:T(8,128)(2,1)} %pad.4.refs_1_.refs_0_, bf16[1280,896]{1,0:T(8,128)(2,1)} %bitcast.47.refs_2_, bf16[1280,768]{1,0:T(8,128)(2,1)} %bitcast.130, ...), custom_call_target="tpu_custom_call" | custom-call | tf_op jit(solution)/shard_map/expert_branch/pallas_call | solution.py:838
  283.2 9.7 %all-to-all-start.4 = ((bf16[16,80,1536]{2,1,0:T(8,128)(2,1)}), bf16[16,80,1536]{2,1,0:T(8,128)(2,1)}, u32[]{:S(2)}, u32[]{:S(2)}) async-start(bf16[16,80,1536]{2,1,0:T(8,128)(2,1)} %bitcast.148), calls=%async_computation.4 | async-start | bytes 7864320 | tf_op jit(solution)/shard_map/all_to_all | solution.py:1125
  293.0 12.4 %expert_grads.2 = bf16[768,3072]{1,0:T(8,128)(2,1)} custom-call(bf16[1280,768]{1,0:T(8,128)(2,1)} %bitcast.131, bf16[1280,768]{1,0:T(8,128)(2,1)} %get-tuple-element.126.d_ref, bf16[1280,6144]{1,0:T(8,128)(2,1)} %get-tuple-element.127.hid_ref), custom_call_target="tpu_custom_call" | custom-call | flops 6039797760 | bytes 16515072 | tf_op jit(solution)/shard_map/expert_grads/pallas_call | solution.py:872
  305.4 12.3 %expert_grads.3 = bf16[768,3072]{1,0:T(8,128)(2,1)} custom-call(bf16[1280,768]{1,0:T(8,128)(2,1)} %bitcast.132, bf16[1280,768]{1,0:T(8,128)(2,1)} %get-tuple-element.126.d_ref, bf16[1280,6144]{1,0:T(8,128)(2,1)} %get-tuple-element.127.hid_ref), custom_call_target="tpu_custom_call" | custom-call | flops 6039797760 | bytes 16515072 | tf_op jit(solution)/shard_map/expert_grads/pallas_call | solution.py:872
  317.7 4.3 add_convert_fusion
  322.0 2.8 fusion.17
  324.8 42.1 %all-to-all-done.4 = bf16[16,80,1536]{2,1,0:T(8,128)(2,1)} async-done(((bf16[16,80,1536]{2,1,0:T(8,128)(2,1)}), bf16[16,80,1536]{2,1,0:T(8,128)(2,1)}, u32[]{:S(2)}, u32[]{:S(2)}) %all-to-all-start.4) | async-done | bytes 3932192 | tf_op jit(solution)/shard_map/all_to_all | solution.py:1125
  367.8 6.2 collective-permute-done.11.refs_3_
  374.1 16.9 %finish.1 = (bf16[4,128,768]{2,1,0:T(8,128)(2,1)}, f32[4,128,768]{2,1,0:T(8,128)}, bf16[4,128,768]{2,1,0:T(8,128)(2,1)}, bf16[4,128,16]{2,1,0:T(8,128)(2,1)}, bf...) custom-call(s32[1]{0:T(128)} %bitcast.shift_ref, s32[4,128,6]{2,1,0:T(8,128)} %copy.203.info_ref, ...), custom_call_target="tpu_custom_call" | custom-call | tf_op jit(solution)/shard_map/finish/pallas_call | solution.py:710
  391.1 18.3 %all-to-all-start.5 = ((bf16[16,3,64,128]{3,2,1,0:T(8,128)(2,1)}), bf16[16,3,64,128]{3,2,1,0:T(8,128)(2,1)S(1)}, u32[]{:S(2)}, u32[]{:S(2)}) async-start(bf16[16,3,64,128]{3,2,1,0:T(8,128)(2,1)} %get-tuple-element.134), calls=%async_computation.6 | async-start | bytes 1572864 | tf_op jit(solution)/shard_map/all_to_all | solution.py:1157
  415.3 14.1 %all-to-all-done.5.refs_2_ = bf16[16,3,64,128]{3,2,1,0:T(8,128)(2,1)S(1)} async-done(((bf16[16,3,64,128]{3,2,1,0:T(8,128)(2,1)}), bf16[16,3,64,128]{3,2,1,0:T(8,128)(2,1)S(1)}, u32[]{:S(2)}, u32[]{:S(2)}) %all-to-all-start.5) | async-done | bytes 786464 | tf_op jit(solution)/shard_map/all_to_all | solution.py:1157
  430.3 4.9 all-to-all-start.6
  436.0 40.7 %attend_back.1 = (bf16[16,3,64,128]{3,2,1,0:T(8,128)(2,1)}, f32[16,6,64,128]{3,2,1,0:T(8,128)}, bf16[16,6,64,128]{3,2,1,0:T(8,128)(2,1)}) custom-call(s32[16]{0:T(128)} %get-tuple-element.99.inv_ref, s32[3]{0:T(128)} %gather_fusion, s32[1]{0:T(128)} %bitcast.42.w_ref, bf16[16,9,64,128]{3,2,1,0:T(8,128)(2,1)} %copy-done.2, ...), custom_call_target="tpu_custom_call" | custom-call | tf_op jit(solution)/shard_map/attend_back/pallas_call | solution.py:408
  476.6 5.3 all-to-all-done.6.refs_0_
  481.9 3.6 collective-permute-done.15
  489.6 15.6 %all-to-all-start.7 = ((bf16[16,9,64,128]{3,2,1,0:T(8,128)(2,1)}), bf16[16,9,64,128]{3,2,1,0:T(8,128)(2,1)S(1)}, u32[]{:S(2)}, u32[]{:S(2)}) async-start(bf16[16,9,64,128]{3,2,1,0:T(8,128)(2,1)} %pad_maximum_fusion), calls=%async_computation.10 | async-start | bytes 4718592 | tf_op jit(solution)/shard_map/all_to_all | solution.py:1190
  505.9 32.1 %reduce-scatter.13.cloned.1.call-done = bf16[48,512]{1,0:T(8,128)(2,1)} async-done(((bf16[192,512]{1,0:T(8,128)(2,1)}), bf16[48,512]{1,0:T(8,128)(2,1)}) %reduce-scatter.13.cloned.1.call-update) | async-done | bytes 49168 | tf_op jit(solution)/shard_map/reduce_scatter | solution.py:981
  538.0 17.9 %all-to-all-done.7.msg_ref = bf16[16,9,64,128]{3,2,1,0:T(8,128)(2,1)S(1)} async-done(((bf16[16,9,64,128]{3,2,1,0:T(8,128)(2,1)}), bf16[16,9,64,128]{3,2,1,0:T(8,128)(2,1)S(1)}, u32[]{:S(2)}, u32[]{:S(2)}) %all-to-all-start.7) | async-done | bytes 2359328 | tf_op jit(solution)/shard_map/all_to_all | solution.py:1190
  557.4 7.6 %unrotate.1 = (bf16[4,128,2304]{2,1,0:T(8,128)(2,1)}, f32[768,1152]{1,0:T(8,128)}, bf16[768,1152]{1,0:T(8,128)(2,1)}) custom-call(s32[1]{0:T(128)} %bitcast.shift_ref, bf16[16,9,64,128]{3,2,1,0:T(8,128)(2,1)} %copy-done.8, f32[128,128]{1,0:T(8,128)} %copy.183.cos_ref, f32[128,128]{1,0:T(8,128)} %copy.184.sin_ref, bf16[768,512]{1,0:T(8,128)(2,1)} %bitcast.152), custom_call_target="tpu_custom_call" | custom-call | tf_op jit(solution)/shard_map/unrotate/pallas_call | solution.py:149
  564.9 3.9 collective-permute-done.16
  568.8 3.5 add_convert_fusion.1
  572.4 11.7 %all-to-all-start.8 = ((bf16[16,48,1536]{2,1,0:T(8,128)(2,1)}), bf16[16,48,1536]{2,1,0:T(8,128)(2,1)S(1)}, u32[]{:S(2)}, u32[]{:S(2)}) async-start(bf16[16,48,1536]{2,1,0:T(8,128)(2,1)} %get-tuple-element.170), calls=%async_computation.14 | async-start | bytes 4718592 | tf_op jit(solution)/shard_map/all_to_all | solution.py:1192
  585.9 6.8 %unproject.1 = (bf16[4,128,768]{2,1,0:T(8,128)(2,1)}, f32[1,768]{1,0:T(1,128)}) custom-call(s32[1]{0:T(128)} %bitcast.shift_ref, bf16[4,128,2304]{2,1,0:T(8,128)(2,1)} %get-tuple-element.162.dqkv_ref, bf16[4,128,768]{2,1,0:T(8,128)(2,1)} %bitcast.141, f32[4,128,768]{2,1,0:T(8,128)} %get-tuple-element.163.dstate_ref, f32[1,768]{1,0:T(1,128)} %broadcast_in_dim.80.gain_ref, ...), custom_call_target="tpu_custom_call" | custom-call | tf_op jit(solution)/shard_map/unproject/pallas_call | solution.py:149
  603.2 34.5 %reduce-scatter.15.cloned.1.call-done = bf16[192,1152]{1,0:T(8,128)(2,1)} async-done(((bf16[768,1152]{1,0:T(8,128)(2,1)}), bf16[192,1152]{1,0:T(8,128)(2,1)}) %reduce-scatter.15.cloned.1.call-update) | async-done | bytes 442384 | tf_op jit(solution)/shard_map/reduce_scatter | solution.py:976
  638.6 3.5 collective-permute-done.21
  653.0 7.5 %place.1 = (f32[16,48,1024]{2,1,0:T(8,128)}, f32[16,48,1024]{2,1,0:T(8,128)}, f32[16,48,1024]{2,1,0:T(8,128)}) custom-call(bf16[16,48,1536]{2,1,0:T(8,128)(2,1)} %copy-done.6, bf16[16,48,1536]{2,1,0:T(8,128)(2,1)} %copy-done.7), custom_call_target="tpu_custom_call" | custom-call | tf_op jit(solution)/shard_map/place/pallas_call | solution.py:750
  (238 shorter events, 85.2 us)
Async XLA Ops:
  8.6 11.9 %copy-start.20 = (bf16[768,384]{0,1:T(8,128)(2,1)}, bf16[768,384]{0,1:T(8,128)(2,1)S(1)}, u32[]{:S(2)}) copy-start(bf16[768,384]{0,1:T(8,128)(2,1)S(1)} %copy.182) | copy-start | bytes 1769476
  8.6 12.9 %collective-permute-start.2 = (bf16[768,384]{0,1:T(8,128)(2,1)S(1)}, bf16[768,384]{0,1:T(8,128)(2,1)S(1)}, u32[]{:S(2)}, u32[]{:S(2)}) collective-permute-start(bf16[768,384]{0,1:T(8,128)(2,1)S(1)} %copy.182), channel_id=1, source_target_pairs={{0,1},{1,0},{2,3},{3,2},{4,5},{5,4},{6,7},{7,6},{8,9},{9,8},{10,11... | collective-permute-start | bytes 1769480 | tf_op jit(solution)/shard_map/ppermute | solution.py:37
  11.2 11.3 %collective-permute-start.1 = (bf16[768,384]{0,1:T(8,128)(2,1)}, bf16[768,384]{0,1:T(8,128)(2,1)S(1)}, u32[]{:S(2)}, u32[]{:S(2)}) collective-permute-start(bf16[768,384]{0,1:T(8,128)(2,1)} %copy.181), channel_id=1, source_target_pairs={{0,1},{1,0},{2,3},{3,2},{4,5},{5,4},{6,7},{7,6},{8,9},{9,8},{10,11... | collective-permute-start | bytes 1769480 | tf_op jit(solution)/shard_map/ppermute | solution.py:37
  12.5 11.2 %collective-permute-start = (bf16[768,384]{0,1:T(8,128)(2,1)}, bf16[768,384]{0,1:T(8,128)(2,1)S(1)}, u32[]{:S(2)}, u32[]{:S(2)}) collective-permute-start(bf16[768,384]{0,1:T(8,128)(2,1)} %copy.180), channel_id=1, source_target_pairs={{0,1},{1,0},{2,3},{3,2},{4,5},{5,4},{6,7},{7,6},{8,9},{9,8},{10,11... | collective-permute-start | bytes 1769480 | tf_op jit(solution)/shard_map/ppermute | solution.py:37
  21.5 10.3 %copy-start.16 = (bf16[768,384]{0,1:T(8,128)(2,1)}, bf16[768,384]{0,1:T(8,128)(2,1)S(1)}, u32[]{:S(2)}) copy-start(bf16[768,384]{0,1:T(8,128)(2,1)S(1)} %collective-permute-done.2) | copy-start | bytes 1769476
  31.8 55.7 %all-to-all-start = ((bf16[16,9,64,128]{3,2,1,0:T(8,128)(2,1)}), bf16[16,9,64,128]{3,2,1,0:T(8,128)(2,1)S(1)}, u32[]{:S(2)}, u32[]{:S(2)}) async-start(bf16[16,9,64,128]{3,2,1,0:T(8,128)(2,1)} %get-tuple-element.95), calls=%async_computation | async-start | bytes 4718592 | tf_op jit(solution)/shard_map/all_to_all | solution.py:964
  42.0 33.2 %collective-permute-start.3 = (bf16[384,768]{0,1:T(8,128)(2,1)}, bf16[384,768]{0,1:T(8,128)(2,1)}, u32[]{:S(2)}, u32[]{:S(2)}) collective-permute-start(bf16[384,768]{0,1:T(8,128)(2,1)} %copy.198), channel_id=1, source_target_pairs={{0,1},{1,0},{2,3},{3,2},{4,5},{5,4},{6,7},{7,6},{8,9},{9,8},{10,11... | collective-permute-start | bytes 1769480 | tf_op jit(solution)/shard_map/ppermute | solution.py:37
  44.7 30.5 %collective-permute-start.6 = (bf16[1024,768]{1,0:T(8,128)(2,1)}, bf16[1024,768]{1,0:T(8,128)(2,1)}, u32[]{:S(2)}, u32[]{:S(2)}) collective-permute-start(bf16[1024,768]{1,0:T(8,128)(2,1)} %dynamic-slice_bitcast_fusion.refs_6_), channel_id=1, source_target_pairs={{0,1},{1,0},{2,3},{3,2},{4,5},{5,4},{6,7},{7,6},{8,9},{9,8},{10,11... | collective-permute-start | bytes 4718600 | tf_op jit(solution)/shard_map/ppermute | solution.py:37
  47.9 27.3 %collective-permute-start.5 = (bf16[768,1024]{1,0:T(8,128)(2,1)}, bf16[768,1024]{1,0:T(8,128)(2,1)}, u32[]{:S(2)}, u32[]{:S(2)}) collective-permute-start(bf16[768,1024]{1,0:T(8,128)(2,1)} %dynamic-slice_bitcast_fusion.1.refs_5_), channel_id=1, source_target_pairs={{0,1},{1,0},{2,3},{3,2},{4,5},{5,4},{6,7},{7,6},{8,9},{9,8},{10,11... | collective-permute-start | bytes 4718600 | tf_op jit(solution)/shard_map/ppermute | solution.py:37
  50.7 24.5 %collective-permute-start.4 = (bf16[768,1024]{1,0:T(8,128)(2,1)}, bf16[768,1024]{1,0:T(8,128)(2,1)}, u32[]{:S(2)}, u32[]{:S(2)}) collective-permute-start(bf16[768,1024]{1,0:T(8,128)(2,1)} %dynamic-slice_bitcast_fusion.2.refs_4_), channel_id=1, source_target_pairs={{0,1},{1,0},{2,3},{3,2},{4,5},{5,4},{6,7},{7,6},{8,9},{9,8},{10,11... | collective-permute-start | bytes 4718600 | tf_op jit(solution)/shard_map/ppermute | solution.py:37
  87.5 12.3 %copy-start.2 = (bf16[16,9,64,128]{3,2,1,0:T(8,128)(2,1)}, bf16[16,9,64,128]{3,2,1,0:T(8,128)(2,1)S(1)}, u32[]{:S(2)}) copy-start(bf16[16,9,64,128]{3,2,1,0:T(8,128)(2,1)S(1)} %all-to-all-done.refs_0_) | copy-start | bytes 7077892
  87.5 58.3 %all-to-all-start.1 = ((bf16[16,80,896]{2,1,0:T(8,128)(2,1)}), bf16[16,80,896]{2,1,0:T(8,128)(2,1)}, u32[]{:S(2)}, u32[]{:S(2)}) async-start(bf16[16,80,896]{2,1,0:T(8,128)(2,1)} %dispatch_early.1), calls=%async_computation.1 | async-start | bytes 4587520 | tf_op jit(solution)/shard_map/all_to_all | solution.py:1094
  99.8 4.6 collective-permute-start.7
  105.8 50.5 %copy-start.33 = (f32[768]{0:T(1024)S(1)}, f32[768]{0:T(1024)}, u32[]{:S(2)}) copy-start(f32[768]{0:T(1024)} %param.28) | copy-start | bytes 9220
  145.8 29.5 %all-to-all-start.2 = ((bf16[16,3,64,128]{3,2,1,0:T(8,128)(2,1)}), bf16[16,3,64,128]{3,2,1,0:T(8,128)(2,1)S(1)}, u32[]{:S(2)}, u32[]{:S(2)}) async-start(bf16[16,3,64,128]{3,2,1,0:T(8,128)(2,1)} %get-tuple-element.104), calls=%async_computation.2 | async-start | bytes 1572864 | tf_op jit(solution)/shard_map/all_to_all | solution.py:1097
  180.5 2.5 collective-permute-start.8
  188.9 46.2 %all-to-all-start.3 = ((bf16[16,80,768]{2,1,0:T(8,128)(2,1)}), bf16[16,80,768]{2,1,0:T(8,128)(2,1)S(1)}, u32[]{:S(2)}, u32[]{:S(2)}) async-start(bf16[16,80,768]{2,1,0:T(8,128)(2,1)} %dispatch.1), calls=%async_computation.3 | async-start | bytes 3932160 | tf_op jit(solution)/shard_map/all_to_all | solution.py:1105
  194.0 173.0 %reduce-scatter.7.cloned.1.call-start = ((), (), s32[]{:S(2)}) async-start(), calls=%async_computation.15 | async-start | bytes 5898240 | tf_op jit(solution)/shard_map/reduce_scatter | solution.py:976
  218.3 15.4 %collective-permute-start.9 = (f32[512,1536]{1,0:T(8,128)S(1)}, f32[512,1536]{1,0:T(8,128)}, u32[]{:S(2)}, u32[]{:S(2)}) collective-permute-start(f32[512,1536]{1,0:T(8,128)S(1)} %get-tuple-element.250), channel_id=1, source_target_pairs={{0,1},{1,0},{2,3},{3,2},{4,5},{5,4},{6,7},{7,6},{8,9},{9,8},{10,11... | collective-permute-start | bytes 9437192 | tf_op jit(solution)/shard_map/ppermute | solution.py:1112
  283.2 83.8 %all-to-all-start.4 = ((bf16[16,80,1536]{2,1,0:T(8,128)(2,1)}), bf16[16,80,1536]{2,1,0:T(8,128)(2,1)}, u32[]{:S(2)}, u32[]{:S(2)}) async-start(bf16[16,80,1536]{2,1,0:T(8,128)(2,1)} %bitcast.148), calls=%async_computation.4 | async-start | bytes 7864320 | tf_op jit(solution)/shard_map/all_to_all | solution.py:1125
  293.0 122.4 %reduce-scatter.9.cloned.1.call-start = ((), (), s32[]{:S(2)}) async-start(), calls=%async_computation.16 | async-start | bytes 1474560 | tf_op jit(solution)/shard_map/reduce_scatter | solution.py:981
  305.4 12.3 %collective-permute-start.10 = (bf16[768,3072]{1,0:T(8,128)(2,1)}, bf16[768,3072]{1,0:T(8,128)(2,1)S(1)}, u32[]{:S(2)}, u32[]{:S(2)}) collective-permute-start(bf16[768,3072]{1,0:T(8,128)(2,1)} %expert_grads.2), channel_id=1, source_target_pairs={{0,1},{1,0},{2,3},{3,2},{4,5},{5,4},{6,7},{7,6},{8,9},{9,8},{10,11... | collective-permute-start | bytes 14155784 | tf_op jit(solution)/shard_map/ppermute | solution.py:1131
  367.0 7.1 %collective-permute-start.11 = (bf16[1280,1536]{1,0:T(8,128)(2,1)}, bf16[1280,1536]{1,0:T(8,128)(2,1)}, u32[]{:S(2)}, u32[]{:S(2)}) collective-permute-start(bf16[1280,1536]{1,0:T(8,128)(2,1)} %bitcast.55.refs_2_), channel_id=1, source_target_pairs={{0,1},{1,0},{2,3},{3,2},{4,5},{5,4},{6,7},{7,6},{8,9},{9,8},{10,11... | collective-permute-start | bytes 11796488 | tf_op jit(solution)/shard_map/ppermute | solution.py:37
  374.1 35.3 %copy-start.34 = (bf16[4,128,768]{2,1,0:T(8,128)(2,1)S(1)}, bf16[4,128,768]{2,1,0:T(8,128)(2,1)}, u32[]{:S(2)}) copy-start(bf16[4,128,768]{2,1,0:T(8,128)(2,1)} %get-tuple-element.136) | copy-start | bytes 2359300
  391.0 20.2 %copy-start.4 = (bf16[4,128,768]{2,1,0:T(8,128)(2,1)S(1)}, bf16[4,128,768]{2,1,0:T(8,128)(2,1)}, u32[]{:S(2)}) copy-start(bf16[4,128,768]{2,1,0:T(8,128)(2,1)} %get-tuple-element.105.second_ref) | copy-start | bytes 2359300
  391.0 20.2 %copy-start.27 = (bf16[4,128,16]{2,1,0:T(8,128)(2,1)S(1)}, bf16[4,128,16]{2,1,0:T(8,128)(2,1)}, u32[]{:S(2)}) copy-start(bf16[4,128,16]{2,1,0:T(8,128)(2,1)} %get-tuple-element.138) | copy-start | bytes 49156
  391.0 20.4 %copy-start.30 = (f32[1,768]{1,0:T(1,128)S(1)}, f32[1,768]{1,0:T(1,128)}, u32[]{:S(2)}) copy-start(f32[1,768]{1,0:T(1,128)} %get-tuple-element.137) | copy-start | bytes 9220
  391.1 38.3 %all-to-all-start.5 = ((bf16[16,3,64,128]{3,2,1,0:T(8,128)(2,1)}), bf16[16,3,64,128]{3,2,1,0:T(8,128)(2,1)S(1)}, u32[]{:S(2)}, u32[]{:S(2)}) async-start(bf16[16,3,64,128]{3,2,1,0:T(8,128)(2,1)} %get-tuple-element.134), calls=%async_computation.6 | async-start | bytes 1572864 | tf_op jit(solution)/shard_map/all_to_all | solution.py:1157
  411.1 2.2 collective-permute-start.12
  411.5 1.8 collective-permute-start.13
  430.3 51.6 %all-to-all-start.6 = ((bf16[16,48,1536]{2,1,0:T(8,128)(2,1)}), bf16[16,48,1536]{2,1,0:T(8,128)(2,1)S(1)}, u32[]{:S(2)}, u32[]{:S(2)}) async-start(bf16[16,48,1536]{2,1,0:T(8,128)(2,1)} %get-tuple-element.150), calls=%async_computation.8 | async-start | bytes 4718592 | tf_op jit(solution)/shard_map/all_to_all | solution.py:1183
  435.2 41.4 %reduce-scatter.11.cloned.1.call-start = ((), (), s32[]{:S(2)}) async-start(), calls=%async_computation.17 | async-start | bytes 983040 | tf_op jit(solution)/shard_map/reduce_scatter | solution.py:976
  481.9 3.6 collective-permute-start.15
  489.6 66.3 %all-to-all-start.7 = ((bf16[16,9,64,128]{3,2,1,0:T(8,128)(2,1)}), bf16[16,9,64,128]{3,2,1,0:T(8,128)(2,1)S(1)}, u32[]{:S(2)}, u32[]{:S(2)}) async-start(bf16[16,9,64,128]{3,2,1,0:T(8,128)(2,1)} %pad_maximum_fusion), calls=%async_computation.10 | async-start | bytes 4718592 | tf_op jit(solution)/shard_map/all_to_all | solution.py:1190
  505.3 32.8 %reduce-scatter.13.cloned.1.call-start = ((), (), s32[]{:S(2)}) async-start(), calls=%async_computation.18 | async-start | bytes 245760 | tf_op jit(solution)/shard_map/reduce_scatter | solution.py:981
  505.8 131.9 %reduce-scatter.15.cloned.1.call-start = ((), (), s32[]{:S(2)}) async-start(), calls=%async_computation.19 | async-start | bytes 2211840 | tf_op jit(solution)/shard_map/reduce_scatter | solution.py:976
  564.9 3.9 collective-permute-start.16
  572.4 12.0 %copy-start.24 = (bf16[4,128,768]{2,1,0:T(8,128)(2,1)S(1)}, bf16[4,128,768]{2,1,0:T(8,128)(2,1)}, u32[]{:S(2)}) copy-start(bf16[4,128,768]{2,1,0:T(8,128)(2,1)} %get-tuple-element.143) | copy-start | bytes 2359300
  572.4 12.1 %copy-start.26 = (bf16[48,3072]{1,0:T(8,128)(2,1)S(1)}, bf16[48,3072]{1,0:T(8,128)(2,1)}, u32[]{:S(2)}) copy-start(bf16[48,3072]{1,0:T(8,128)(2,1)} %reduce-scatter.9.cloned.1.call-done) | copy-start | bytes 884740
  572.4 79.3 %all-to-all-start.8 = ((bf16[16,48,1536]{2,1,0:T(8,128)(2,1)}), bf16[16,48,1536]{2,1,0:T(8,128)(2,1)S(1)}, u32[]{:S(2)}, u32[]{:S(2)}) async-start(bf16[16,48,1536]{2,1,0:T(8,128)(2,1)} %get-tuple-element.170), calls=%async_computation.14 | async-start | bytes 4718592 | tf_op jit(solution)/shard_map/all_to_all | solution.py:1192
  584.1 77.0 %reduce-scatter.17.cloned.1.call-start = ((), (), s32[]{:S(2)}) async-start(), calls=%async_computation.20 | async-start | bytes 552960 | tf_op jit(solution)/shard_map/reduce_scatter | solution.py:981
  584.4 12.5 %collective-permute-start.14 = (bf16[4,128,768]{2,1,0:T(8,128)(2,1)S(1)}, bf16[4,128,768]{2,1,0:T(8,128)(2,1)}, u32[]{:S(2)}, u32[]{:S(2)}) collective-permute-start(bf16[4,128,768]{2,1,0:T(8,128)(2,1)S(1)} %copy-done.24), channel_id=1, source_target_pairs={{0,1},{1,0},{2,3},{3,2},{4,5},{5,4},{6,7},{7,6},{8,9},{9,8},{10,11... | collective-permute-start | bytes 2359304 | tf_op jit(solution)/shard_map/ppermute | solution.py:37
  592.8 1.5 collective-permute-start.18
  594.9 6.6 collective-permute-start.19
  601.4 45.8 %collective-permute-start.17 = (bf16[4,128,768]{2,1,0:T(8,128)(2,1)S(1)}, bf16[4,128,768]{2,1,0:T(8,128)(2,1)}, u32[]{:S(2)}, u32[]{:S(2)}) collective-permute-start(bf16[4,128,768]{2,1,0:T(8,128)(2,1)S(1)} %copy-done.25), channel_id=1, source_target_pairs={{0,1},{1,0},{2,3},{3,2},{4,5},{5,4},{6,7},{7,6},{8,9},{9,8},{10,11... | collective-permute-start | bytes 2359304 | tf_op jit(solution)/shard_map/ppermute | solution.py:37
  601.6 36.8 %collective-permute-start.20 = (f32[1,768]{1,0:T(1,128)S(1)}, f32[1,768]{1,0:T(1,128)S(1)}, u32[]{:S(2)}, u32[]{:S(2)}) collective-permute-start(f32[1,768]{1,0:T(1,128)S(1)} %add.262), channel_id=1, source_target_pairs={{0,4},{2,6},{4,0},{6,2},{8,12},{10,14},{12,8},{14,10},{16,20},{18,... | collective-permute-start | bytes 9224 | tf_op jit(solution)/shard_map/ppermute | solution.py:62
  638.4 3.7 collective-permute-start.21
  642.1 4.5 collective-permute-start.22
  (27 other events, 100.2 us)
Sparse Core Ops, SparseCore 0:
  235.2 61.0 reduce-scatter.6
  367.1 41.8 reduce-scatter.8
  439.0 37.4 reduce-scatter.10
  508.0 29.9 reduce-scatter.12
  572.5 65.1 reduce-scatter.14
  640.0 21.1 reduce-scatter.16

commit v4 on v3

--- a/solution.py
+++ b/solution.py
@@ -172,6 +172,33 @@
             jax.ShapeDtypeStruct((seqs, rows, width), BF),
         ],
     )
+
+
+def turn_kernel(count, shift_ref, *refs):
+    (a1_ref, *ins), (a1t_ref, *outs) = refs[: 1 + 4 * count], refs[1 + 4 * count :]
+    a1t_ref[...] = a1_ref[...].T
+    for k in range(count):
+        inner = ins[4 * k].shape[1]
+        for n in range(3):
+            outs[2 * k][n * inner : (n + 1) * inner, :] = ins[4 * k + n][...].T
+        outs[2 * k + 1][...] = ins[4 * k + 3][...].T
+
+
+def turn(a1, parts, out_parts):
+    rows, width = a1.shape
+    ins = [a1]
+    shapes = [jax.ShapeDtypeStruct((width, rows), BF)]
+    for part, out_part in zip(parts, out_parts):
+        ins += [*part, out_part]
+        inner = out_part.shape[0]
+        shapes += [
+            jax.ShapeDtypeStruct((3 * inner, width), BF),
+            jax.ShapeDtypeStruct((width, inner), BF),
+        ]
+    made = one_step(
+        functools.partial(turn_kernel, len(parts)), "turn", jnp.zeros((1,), jnp.int32), ins, shapes
+    )
+    return made[0], list(made[1::2]), list(made[2::2])
 
 
 def gather_keys(inv_ref, w, kv_refs, kv_s, members, chunk):
@@ -632,7 +659,7 @@
 ):
     router_ref, turned_ref, *refs = refs
     home_refs, refs = refs[:size], refs[size:]
-    dense_refs, refs = refs[:size], refs[size:]
+    dense_ref, *refs = refs
     w_refs = refs[:count]
     out_ref, dstate_ref, low_ref, logit_ref, msg_ref, dgain_ref = refs[count:]
     step = pl.program_id(0)
@@ -666,10 +693,9 @@
     logit_ref[...] = logit.reshape(take, rows, experts)
     back = back + dot(logit, turned_ref[...])
     branch = gates[0] * made[0] + gates[1] * made[1]
-    for ref in dense_refs:
-        dense = ref[...].reshape(lines, 2 * width)
-        branch = branch + dense[:, :width]
-        back = back + dense[:, width:]
+    dense = dense_ref[...].reshape(lines, 2 * width)
+    branch = branch + dense[:, :width]
+    back = back + dense[:, width:]
     state = state_ref[...].reshape(lines, width)
     out_ref[...] = (state + branch).astype(BF).reshape(take, rows, width)
     pulled, dgain = norm_back(state, gain_ref[...], back)
@@ -700,7 +726,7 @@
                     msg_ref[chip, u] = pair[c].astype(BF)
 
 
-def finish(shift, info, second, state, cot, gain, router, turned, homes, denses, parts, members, units):
+def finish(shift, info, second, state, cot, gain, router, turned, homes, dense, parts, members, units):
     seqs, rows, width = state.shape
     inner = sum(part.shape[1] for part in parts)
     experts = turned.shape[0]
@@ -713,7 +739,7 @@
         in_specs=[SMEM, some(info.shape[2]), some(width), some(width), some(width)]
         + [whole((1, width)), whole(router.shape), whole(turned.shape)]
         + [whole(home.shape) for home in homes]
-        + [some(2 * width)] * len(denses)
+        + [some(2 * width)]
         + [whole(part.shape) for part in parts],
         out_specs=[some(width)] * 3 + [some(experts), whole(msg), whole((1, width))],
         out_shape=[
@@ -726,7 +752,7 @@
         ],
         compiler_params=params(1),
         name="finish",
-    )(shift, info, second, state, cot, gain, router, turned, *homes, *denses, *parts)
+    )(shift, info, second, state, cot, gain, router, turned, *homes, dense, *parts)
 
 
 def place_kernel(copies, cuts, *refs):
@@ -943,12 +969,11 @@
 
     x = rows_of(inputs[0], 0)
     half = HEAD_DIM // 2
-    freqs = THETA ** (-jnp.arange(half, dtype=F4) / half)
+    lane = jnp.arange(LANES)
+    freqs = THETA ** (-(lane % half).astype(F4) / half)
     angles = places_of(0).astype(F4)[:, None] * freqs[None, :]
-    cosine = jnp.tile(jnp.cos(angles), (1, LANES // half))
-    sine = jnp.tile(
-        jnp.concatenate([-jnp.sin(angles), jnp.sin(angles)], axis=1), (1, LANES // HEAD_DIM)
-    )
+    cosine = jnp.cos(angles)
+    sine = jnp.sin(angles) * jnp.where(lane % HEAD_DIM < half, -1.0, 1.0)[None, :]
 
     local = inner // size
     split = size == 2 and local % LANES == 0
@@ -960,7 +985,9 @@
     else:
         parts = [[lax.all_gather(weight, "wt", axis=1, tiled=True) for weight in own_qkv]]
         out_parts = [lax.all_gather(out_weight, "wt", axis=0, tiled=True)]
+    x, cosine, sine = lax.optimization_barrier((x, cosine, sine))
     msg, a1 = project(shift, x, attn_gain[None], cosine, sine, parts, members, units)
+    msg, cotangent, routes = lax.optimization_barrier((msg, cotangent, routes))
     got = lax.all_to_all(msg, "ctx", 0, 0, tiled=True)
 
     near = 4 if members % 4 == 0 else 1
@@ -982,9 +1009,8 @@
             array, "ctx", scatter_dimension=0, tiled=True, axis_index_groups=far_groups
         )
 
-    a1_turned = by_steps(a1.reshape(rows, width).T)
-    back_parts = [jnp.concatenate([weight.T for weight in part]) for part in parts]
-    out_back = [part.T for part in out_parts]
+    a1_turned, back_parts, out_back = turn(a1.reshape(rows, width), parts, out_parts)
+    a1_turned = by_steps(a1_turned)
     expert = ctx % experts
     expert_parts = list(
         zip(
@@ -1111,6 +1137,9 @@
         perm = [(i, (i + k) % size) for i in range(size)]
         denses.append(lax.ppermute(dense[k * rows : (k + 1) * rows], "wt", perm))
     arrived, denses, dense_grads = lax.optimization_barrier((arrived, denses, dense_grads))
+    dense = denses[0]
+    for part in denses[1:]:
+        dense = dense + part
     dense_near = near_scatter(dense_grads)
 
     arrived = arrived.reshape(experts * held, width)
@@ -1133,12 +1162,14 @@
     expert_sum = expert_sum.astype(BF).reshape(members, width // members, 3 * hidden)
     cut = 3 * hidden // 2
     expert_sum = [expert_sum[:, :, :cut], expert_sum[:, :, cut:]]
-    home, expert_sum, dense_near = lax.optimization_barrier((home, expert_sum, dense_near))
+    home, expert_sum, dense_near, dense = lax.optimization_barrier(
+        (home, expert_sum, dense_near, dense)
+    )
     dense_sum = far_scatter(dense_near)
     homes = wt_gather(home.reshape(experts * held, 2 * width))
 
     own_cot = cots[0].reshape(seqs, 2 * chunk, width)
-    denses = [part.reshape(seqs, 2 * chunk, 2 * width) for part in denses]
+    dense = dense.reshape(seqs, 2 * chunk, 2 * width)
     output, dstate, dstate_low, logit_back, do_msg, ffn_grad = finish(
         shift,
         own_info,
@@ -1149,7 +1180,7 @@
         router_wide,
         router_turned,
         homes,
-        denses,
+        dense,
         out_back,
         members,
         units,
@@ -1196,7 +1227,6 @@
     else:
         last_msg = by_steps(split_wt(a1, dqkv, 3))
     last_sum = far_scatter(near_scatter(last_msg))
-    dqkv, last_msg = lax.optimization_barrier((dqkv, last_msg))
     dx, attn_grad = unproject(shift, dqkv, x, dstate, attn_gain[None], back_parts)
     attn_grad = ctx_sum(wt_sum(attn_grad)).reshape(members, -1)
     attn_grad = lax.dynamic_index_in_dim(attn_grad, ctx, 0, False)

time: 671 us -> 656 us (0.978); the launches traced: 670 us -> 645 us
  Pallas kernels: 232 us -> 221 us
  starting transfers between devices: 106 us -> 98.3 us
    all_to_all x1, waiting for transfers between devices: 12.3 us -> 0.01 us  [per_device(): got = lax.all_to_all(msg, 'ctx', 0, 0, tiled=True)]
    pallas_call x2, Pallas kernels: 64.9 us -> 54.8 us  [gated(): pl.pallas_call(functools.partial(gated_kernel, count, tiles, bool(routed)...]
    reduce_scatter x3, waiting for transfers between devices: 34.6 us -> 41.5 us  [near_scatter(): lax.psum_scatter(array, 'ctx', scatter_dimension=0, tiled=True, axis_inde...]
    pallas_call x4 -> x5, Pallas kernels: 25.8 us -> 31.5 us  [one_step(): pl.pallas_call(kernel, grid=(1,), in_specs=[SMEM] + [whole(array.shape) f...]
    unnamed x83 -> x85, local copies, waits for them, and re-layouts: 22.2 us -> 17.6 us
  transfers between devices with their start and end apart: 38 -> 38, of which waited for: 20 -> 20; matrix products, arithmetic and copies ran while one was open for 12% -> 12% of each run, Pallas kernels for 31% -> 30%
where the time goes in v4:
time: 656 us; the launch traced here: 645 us
  Pallas kernels  221 us (34%)
  waiting for transfers between devices  211 us (32%)
  starting transfers between devices  98.3 us (15%)
  local copies, waits for them, and re-layouts  66.4 us (10%)
  other arithmetic  30.3 us (5%)
  between operations  15.8 us (2%)
    pallas_call x2, Pallas kernels, gated(): pl.pallas_call(functools.partial(gated_kernel, count, tiles, bool(routed)...  54.8 us
    reduce_scatter x3, waiting for transfers between devices, near_scatter(): lax.psum_scatter(array, 'ctx', scatter_dimension=0, tiled=True, axis_inde...  41.5 us
    all_to_all x1, waiting for transfers between devices, per_device(): home = swap(returned.reshape(experts, held, 2 * width))  38.4 us
    pallas_call x3, Pallas kernels, gated_grads(): pl.pallas_call(gated_grads_kernel, grid=(tiles,), in_specs=[whole(x.shape...  35.3 us
    reduce_scatter x3, waiting for transfers between devices, far_scatter(): lax.psum_scatter(array, 'ctx', scatter_dimension=0, tiled=True, axis_inde...  35.1 us
    pallas_call x1, Pallas kernels, attend_back(): pl.pallas_call(functools.partial(attend_back_kernel, members, size), grid...  34.6 us
    pallas_call x5, Pallas kernels, one_step(): pl.pallas_call(kernel, grid=(1,), in_specs=[SMEM] + [whole(array.shape) f...  31.5 us
    pallas_call x1, Pallas kernels, attend(): pl.pallas_call(functools.partial(attend_kernel, members, size), grid_spec...  29.5 us
  transfers between devices with their start and end apart: 38, of which 20 were waited for; matrix products, arithmetic and copies ran while one was open for 12% of the time, Pallas kernels for 30%

profile of v4, /device:TPU:0, one launch (start us, length us, event | category | flops | bytes accessed | tf_op | source)
XLA Modules:
  0.0 645.5 jit_solution(2540493176695370837)
XLA Ops:
  15.7 7.2 %project.1 = (bf16[16,9,64,128]{3,2,1,0:T(8,128)(2,1)}, bf16[4,128,768]{2,1,0:T(8,128)(2,1)}) custom-call(s32[1]{0:T(128)} %bitcast.shift_ref, bf16[4,128,768]{2,1,0:T(8,128)(2,1)} %bitcast.126, f32[1,768]{1,0:T(1,128)} %broadcast_in_dim.91.gain_ref, f32[128,128]{1,0:T(8,128)} %get-tuple-element.107.cos_ref, f32[128,128]{1,0:T(8,128)} %get-tuple-element.108.sin_ref, ...), custom_call_target="tpu_custom_call" | custom-call | tf_op jit(solution)/shard_map/project/pallas_call | solution.py:149
  22.9 8.1 %all-to-all-start = ((bf16[16,9,64,128]{3,2,1,0:T(8,128)(2,1)}), bf16[16,9,64,128]{3,2,1,0:T(8,128)(2,1)S(1)}, u32[]{:S(2)}, u32[]{:S(2)}) async-start(bf16[16,9,64,128]{3,2,1,0:T(8,128)(2,1)} %get-tuple-element.110), calls=%async_computation | async-start | bytes 4718592 | tf_op jit(solution)/shard_map/all_to_all | solution.py:991
  31.2 2.7 dynamic-slice_bitcast_fusion.refs_6_
  37.1 2.7 dynamic-slice_bitcast_fusion.2.refs_4_
  64.8 5.7 turn.1
  75.0 5.5 dispatch_early.1
  80.6 10.3 %all-to-all-start.1 = ((bf16[16,80,896]{2,1,0:T(8,128)(2,1)}), bf16[16,80,896]{2,1,0:T(8,128)(2,1)}, u32[]{:S(2)}, u32[]{:S(2)}) async-start(bf16[16,80,896]{2,1,0:T(8,128)(2,1)} %dispatch_early.1), calls=%async_computation.1 | async-start | bytes 4587520 | tf_op jit(solution)/shard_map/all_to_all | solution.py:1120
  91.0 4.5 collective-permute-done.7.refs_1_
  96.9 29.5 %attend.1 = (bf16[16,3,64,128]{3,2,1,0:T(8,128)(2,1)}, f32[3,4,64,512]{3,2,1,0:T(8,128)}, f32[3,4,1,512]{3,2,1,0:T(1,128)}) custom-call(s32[16]{0:T(128)} %get-tuple-element.121.inv_ref, s32[3]{0:T(128)} %gather_fusion, s32[1]{0:T(128)} %bitcast.31.w_ref, bf16[16,9,64,128]{3,2,1,0:T(8,128)(2,1)} %copy-done.4, bf16[16,9,64,128]{3,2,1,0:T(8,128)(2,1)} %copy-done.8), custom_call_target="tpu_custom_call" | custom-call | tf_op jit(solution)/shard_map/attend/pallas_call | solution.py:309
  126.4 10.8 %all-to-all-done.1 = bf16[16,80,896]{2,1,0:T(8,128)(2,1)} async-done(((bf16[16,80,896]{2,1,0:T(8,128)(2,1)}), bf16[16,80,896]{2,1,0:T(8,128)(2,1)}, u32[]{:S(2)}, u32[]{:S(2)}) %all-to-all-start.1) | async-done | bytes 2293792 | tf_op jit(solution)/shard_map/all_to_all | solution.py:1120
  137.2 11.0 %all-to-all-start.2 = ((bf16[16,3,64,128]{3,2,1,0:T(8,128)(2,1)}), bf16[16,3,64,128]{3,2,1,0:T(8,128)(2,1)S(1)}, u32[]{:S(2)}, u32[]{:S(2)}) async-start(bf16[16,3,64,128]{3,2,1,0:T(8,128)(2,1)} %get-tuple-element.126), calls=%async_computation.2 | async-start | bytes 1572864 | tf_op jit(solution)/shard_map/all_to_all | solution.py:1123
  148.8 18.4 %all-to-all-done.2.o_ref = bf16[16,3,64,128]{3,2,1,0:T(8,128)(2,1)S(1)} async-done(((bf16[16,3,64,128]{3,2,1,0:T(8,128)(2,1)}), bf16[16,3,64,128]{3,2,1,0:T(8,128)(2,1)S(1)}, u32[]{:S(2)}, u32[]{:S(2)}) %all-to-all-start.2) | async-done | bytes 786464 | tf_op jit(solution)/shard_map/all_to_all | solution.py:1123
  168.0 4.2 mix.1
  175.6 5.1 dispatch.1
  180.7 5.0 all-to-all-start.3
  187.1 18.0 %dense_branch.1 = (f32[1024,1536]{1,0:T(8,128)}, bf16[1024,3072]{1,0:T(8,128)(2,1)}) custom-call(bf16[1024,768]{1,0:T(8,128)(2,1)} %pad_maximum_fusion.1.cot_ref.refs_0_.d_ref, bf16[1024,768]{1,0:T(8,128)(2,1)} %copy-done.12, bf16[768,1024]{1,0:T(8,128)(2,1)} %refs_2_.5, bf16[768,1024]{1,0:T(8,128)(2,1)} %refs_3_.3, bf16[1024,768]{1,0:T(8,128)(2,1)} %refs_4_.3), custom_call_target="tpu_custom_call" | custom-call | tf_op jit(solution)/shard_map/dense_branch/pallas_call | solution.py:864
  205.1 5.0 fusion.20
  210.1 10.5 %dense_grads.1 = bf16[768,3072]{1,0:T(8,128)(2,1)} custom-call(bf16[1024,768]{1,0:T(8,128)(2,1)} %copy-done.12, bf16[1024,768]{1,0:T(8,128)(2,1)} %pad_maximum_fusion.1.cot_ref.refs_0_.d_ref, bf16[1024,3072]{1,0:T(8,128)(2,1)} %get-tuple-element.139.hid_ref), custom_call_target="tpu_custom_call" | custom-call | flops 4831838208 | bytes 14155776 | tf_op jit(solution)/shard_map/dense_grads/pallas_call | solution.py:898
  220.5 4.9 copy.125
  228.1 36.8 %expert_branch.1 = (bf16[1280,768]{1,0:T(8,128)(2,1)}, bf16[1280,1536]{1,0:T(8,128)(2,1)}, bf16[1280,6144]{1,0:T(8,128)(2,1)}) custom-call(s32[1]{0:T(128)} %bitcast.33.refs_0_, bf16[768,128]{1,0:T(8,128)(2,1)} %pad.4.refs_1_.refs_0_, bf16[1280,896]{1,0:T(8,128)(2,1)} %bitcast.34.refs_2_, bf16[1280,768]{1,0:T(8,128)(2,1)} %bitcast.118, ...), custom_call_target="tpu_custom_call" | custom-call | tf_op jit(solution)/shard_map/expert_branch/pallas_call | solution.py:864
  264.9 9.5 %all-to-all-start.4 = ((bf16[16,80,1536]{2,1,0:T(8,128)(2,1)}), bf16[16,80,1536]{2,1,0:T(8,128)(2,1)}, u32[]{:S(2)}, u32[]{:S(2)}) async-start(bf16[16,80,1536]{2,1,0:T(8,128)(2,1)} %bitcast.136), calls=%async_computation.4 | async-start | bytes 7864320 | tf_op jit(solution)/shard_map/all_to_all | solution.py:1154
  274.5 12.5 %expert_grads.2 = bf16[768,3072]{1,0:T(8,128)(2,1)} custom-call(bf16[1280,768]{1,0:T(8,128)(2,1)} %bitcast.119, bf16[1280,768]{1,0:T(8,128)(2,1)} %get-tuple-element.148.d_ref, bf16[1280,6144]{1,0:T(8,128)(2,1)} %get-tuple-element.149.hid_ref), custom_call_target="tpu_custom_call" | custom-call | flops 6039797760 | bytes 16515072 | tf_op jit(solution)/shard_map/expert_grads/pallas_call | solution.py:898
  287.0 4.1 add.278
  291.2 12.3 %expert_grads.3 = bf16[768,3072]{1,0:T(8,128)(2,1)} custom-call(bf16[1280,768]{1,0:T(8,128)(2,1)} %bitcast.120, bf16[1280,768]{1,0:T(8,128)(2,1)} %get-tuple-element.148.d_ref, bf16[1280,6144]{1,0:T(8,128)(2,1)} %get-tuple-element.149.hid_ref), custom_call_target="tpu_custom_call" | custom-call | flops 6039797760 | bytes 16515072 | tf_op jit(solution)/shard_map/expert_grads/pallas_call | solution.py:898
  303.5 4.3 add_convert_fusion
  307.7 2.8 fusion.21
  310.6 38.4 %all-to-all-done.4 = bf16[16,80,1536]{2,1,0:T(8,128)(2,1)} async-done(((bf16[16,80,1536]{2,1,0:T(8,128)(2,1)}), bf16[16,80,1536]{2,1,0:T(8,128)(2,1)}, u32[]{:S(2)}, u32[]{:S(2)}) %all-to-all-start.4) | async-done | bytes 3932192 | tf_op jit(solution)/shard_map/all_to_all | solution.py:1154
  349.8 6.2 collective-permute-done.11.refs_3_
  356.1 16.8 %finish.1 = (bf16[4,128,768]{2,1,0:T(8,128)(2,1)}, f32[4,128,768]{2,1,0:T(8,128)}, bf16[4,128,768]{2,1,0:T(8,128)(2,1)}, bf16[4,128,16]{2,1,0:T(8,128)(2,1)}, bf...) custom-call(s32[1]{0:T(128)} %bitcast.shift_ref, s32[4,128,6]{2,1,0:T(8,128)} %copy.126.info_ref, ...), custom_call_target="tpu_custom_call" | custom-call | tf_op jit(solution)/shard_map/finish/pallas_call | solution.py:736
  372.9 17.0 %all-to-all-start.5 = ((bf16[16,3,64,128]{3,2,1,0:T(8,128)(2,1)}), bf16[16,3,64,128]{3,2,1,0:T(8,128)(2,1)S(1)}, u32[]{:S(2)}, u32[]{:S(2)}) async-start(bf16[16,3,64,128]{3,2,1,0:T(8,128)(2,1)} %get-tuple-element.157), calls=%async_computation.6 | async-start | bytes 1572864 | tf_op jit(solution)/shard_map/all_to_all | solution.py:1188
  395.9 14.1 %all-to-all-done.5.refs_2_ = bf16[16,3,64,128]{3,2,1,0:T(8,128)(2,1)S(1)} async-done(((bf16[16,3,64,128]{3,2,1,0:T(8,128)(2,1)}), bf16[16,3,64,128]{3,2,1,0:T(8,128)(2,1)S(1)}, u32[]{:S(2)}, u32[]{:S(2)}) %all-to-all-start.5) | async-done | bytes 786464 | tf_op jit(solution)/shard_map/all_to_all | solution.py:1188
  410.9 4.9 all-to-all-start.6
  416.6 34.6 %attend_back.1 = (bf16[16,3,64,128]{3,2,1,0:T(8,128)(2,1)}, f32[16,6,64,128]{3,2,1,0:T(8,128)}, bf16[16,6,64,128]{3,2,1,0:T(8,128)(2,1)}) custom-call(s32[16]{0:T(128)} %get-tuple-element.121.inv_ref, s32[3]{0:T(128)} %gather_fusion, s32[1]{0:T(128)} %bitcast.31.w_ref, bf16[16,9,64,128]{3,2,1,0:T(8,128)(2,1)} %copy-done.4, ...), custom_call_target="tpu_custom_call" | custom-call | tf_op jit(solution)/shard_map/attend_back/pallas_call | solution.py:435
  451.2 5.9 reduce-scatter.11.cloned.1.call-done
  457.1 5.4 all-to-all-done.6.refs_0_
  462.5 3.6 collective-permute-done.15
  470.2 10.8 %all-to-all-start.7 = ((bf16[16,9,64,128]{3,2,1,0:T(8,128)(2,1)}), bf16[16,9,64,128]{3,2,1,0:T(8,128)(2,1)S(1)}, u32[]{:S(2)}, u32[]{:S(2)}) async-start(bf16[16,9,64,128]{3,2,1,0:T(8,128)(2,1)} %pad_maximum_fusion), calls=%async_computation.10 | async-start | bytes 4718592 | tf_op jit(solution)/shard_map/all_to_all | solution.py:1221
  481.9 32.0 %reduce-scatter.13.cloned.1.call-done = bf16[48,512]{1,0:T(8,128)(2,1)} async-done(((bf16[192,512]{1,0:T(8,128)(2,1)}), bf16[48,512]{1,0:T(8,128)(2,1)}) %reduce-scatter.13.cloned.1.call-update) | async-done | bytes 49168 | tf_op jit(solution)/shard_map/reduce_scatter | solution.py:1008
  513.8 17.9 %all-to-all-done.7.msg_ref = bf16[16,9,64,128]{3,2,1,0:T(8,128)(2,1)S(1)} async-done(((bf16[16,9,64,128]{3,2,1,0:T(8,128)(2,1)}), bf16[16,9,64,128]{3,2,1,0:T(8,128)(2,1)S(1)}, u32[]{:S(2)}, u32[]{:S(2)}) %all-to-all-start.7) | async-done | bytes 2359328 | tf_op jit(solution)/shard_map/all_to_all | solution.py:1221
  533.2 7.6 %unrotate.1 = (bf16[4,128,2304]{2,1,0:T(8,128)(2,1)}, f32[768,1152]{1,0:T(8,128)}, bf16[768,1152]{1,0:T(8,128)(2,1)}) custom-call(s32[1]{0:T(128)} %bitcast.shift_ref, bf16[16,9,64,128]{3,2,1,0:T(8,128)(2,1)} %copy-done.10, f32[128,128]{1,0:T(8,128)} %get-tuple-element.107.cos_ref, f32[128,128]{1,0:T(8,128)} %get-tuple-element.108.sin_ref, ...), custom_call_target="tpu_custom_call" | custom-call | tf_op jit(solution)/shard_map/unrotate/pallas_call | solution.py:149
  540.7 3.9 collective-permute-done.22
  544.6 3.5 add_convert_fusion.1
  548.2 11.8 %all-to-all-start.8 = ((bf16[16,48,1536]{2,1,0:T(8,128)(2,1)}), bf16[16,48,1536]{2,1,0:T(8,128)(2,1)}, u32[]{:S(2)}, u32[]{:S(2)}) async-start(bf16[16,48,1536]{2,1,0:T(8,128)(2,1)} %get-tuple-element.192), calls=%async_computation.14 | async-start | bytes 4718592 | tf_op jit(solution)/shard_map/all_to_all | solution.py:1223
  561.6 6.8 %unproject.1 = (bf16[4,128,768]{2,1,0:T(8,128)(2,1)}, f32[1,768]{1,0:T(1,128)}) custom-call(s32[1]{0:T(128)} %bitcast.shift_ref, bf16[4,128,2304]{2,1,0:T(8,128)(2,1)} %get-tuple-element.182.dqkv_ref, bf16[4,128,768]{2,1,0:T(8,128)(2,1)} %bitcast.128, f32[4,128,768]{2,1,0:T(8,128)} %get-tuple-element.183.dstate_ref, f32[1,768]{1,0:T(1,128)} %broadcast_in_dim.91.gain_ref, ...), custom_call_target="tpu_custom_call" | custom-call | tf_op jit(solution)/shard_map/unproject/pallas_call | solution.py:149
  578.0 35.5 %reduce-scatter.15.cloned.1.call-done = bf16[192,1152]{1,0:T(8,128)(2,1)} async-done(((bf16[768,1152]{1,0:T(8,128)(2,1)}), bf16[192,1152]{1,0:T(8,128)(2,1)}) %reduce-scatter.15.cloned.1.call-update) | async-done | bytes 442384 | tf_op jit(solution)/shard_map/reduce_scatter | solution.py:1003
  614.4 3.5 collective-permute-done.20
  626.3 7.5 %place.1 = (f32[16,48,1024]{2,1,0:T(8,128)}, f32[16,48,1024]{2,1,0:T(8,128)}, f32[16,48,1024]{2,1,0:T(8,128)}) custom-call(bf16[16,48,1536]{2,1,0:T(8,128)(2,1)} %copy-done.9, bf16[16,48,1536]{2,1,0:T(8,128)(2,1)} %all-to-all-done.8.refs_1_), custom_call_target="tpu_custom_call" | custom-call | tf_op jit(solution)/shard_map/place/pallas_call | solution.py:776
  633.8 3.1 reduce-scatter.17.cloned.1.call-done
  (232 shorter events, 87.4 us)
Async XLA Ops:
  7.2 7.3 %collective-permute-start = (bf16[768,384]{1,0:T(8,128)(2,1)}, bf16[768,384]{1,0:T(8,128)(2,1)S(1)}, u32[]{:S(2)}, u32[]{:S(2)}) collective-permute-start(bf16[768,384]{1,0:T(8,128)(2,1)} %refs_1_.3), channel_id=1, source_target_pairs={{0,1},{1,0},{2,3},{3,2},{4,5},{5,4},{6,7},{7,6},{8,9},{9,8},{10,11... | collective-permute-start | bytes 1769480 | tf_op jit(solution)/shard_map/ppermute | solution.py:37
  7.7 6.8 %collective-permute-start.1 = (bf16[768,384]{1,0:T(8,128)(2,1)}, bf16[768,384]{1,0:T(8,128)(2,1)S(1)}, u32[]{:S(2)}, u32[]{:S(2)}) collective-permute-start(bf16[768,384]{1,0:T(8,128)(2,1)} %refs_2_.4), channel_id=1, source_target_pairs={{0,1},{1,0},{2,3},{3,2},{4,5},{5,4},{6,7},{7,6},{8,9},{9,8},{10,11... | collective-permute-start | bytes 1769480 | tf_op jit(solution)/shard_map/ppermute | solution.py:37
  7.8 6.7 %collective-permute-start.2 = (bf16[768,384]{1,0:T(8,128)(2,1)}, bf16[768,384]{1,0:T(8,128)(2,1)S(1)}, u32[]{:S(2)}, u32[]{:S(2)}) collective-permute-start(bf16[768,384]{1,0:T(8,128)(2,1)} %refs_3_.2), channel_id=1, source_target_pairs={{0,1},{1,0},{2,3},{3,2},{4,5},{5,4},{6,7},{7,6},{8,9},{9,8},{10,11... | collective-permute-start | bytes 1769480 | tf_op jit(solution)/shard_map/ppermute | solution.py:37
  22.9 57.7 %all-to-all-start = ((bf16[16,9,64,128]{3,2,1,0:T(8,128)(2,1)}), bf16[16,9,64,128]{3,2,1,0:T(8,128)(2,1)S(1)}, u32[]{:S(2)}, u32[]{:S(2)}) async-start(bf16[16,9,64,128]{3,2,1,0:T(8,128)(2,1)} %get-tuple-element.110), calls=%async_computation | async-start | bytes 4718592 | tf_op jit(solution)/shard_map/all_to_all | solution.py:991
  31.0 33.0 %collective-permute-start.3 = (bf16[384,768]{1,0:T(8,128)(2,1)S(1)}, bf16[384,768]{1,0:T(8,128)(2,1)S(1)}, u32[]{:S(2)}, u32[]{:S(2)}) collective-permute-start(bf16[384,768]{1,0:T(8,128)(2,1)S(1)} %copy-done.20), channel_id=1, source_target_pairs={{0,1},{1,0},{2,3},{3,2},{4,5},{5,4},{6,7},{7,6},{8,9},{9,8},{10,11... | collective-permute-start | bytes 1769480 | tf_op jit(solution)/shard_map/ppermute | solution.py:37
  33.9 46.7 %collective-permute-start.6 = (bf16[1024,768]{1,0:T(8,128)(2,1)}, bf16[1024,768]{1,0:T(8,128)(2,1)}, u32[]{:S(2)}, u32[]{:S(2)}) collective-permute-start(bf16[1024,768]{1,0:T(8,128)(2,1)} %dynamic-slice_bitcast_fusion.refs_6_), channel_id=1, source_target_pairs={{0,1},{1,0},{2,3},{3,2},{4,5},{5,4},{6,7},{7,6},{8,9},{9,8},{10,11... | collective-permute-start | bytes 4718600 | tf_op jit(solution)/shard_map/ppermute | solution.py:37
  36.9 14.1 %copy-start.32 = (s32[1,256,4,2]{1,3,2,0:T(2,128)S(1)}, s32[1,256,4,2]{1,3,2,0:T(2,128)}, u32[]{:S(2)}) copy-start(s32[1,256,4,2]{1,3,2,0:T(2,128)} %param.22) | copy-start | bytes 24580
  36.9 43.6 %collective-permute-start.5 = (bf16[768,1024]{1,0:T(8,128)(2,1)}, bf16[768,1024]{1,0:T(8,128)(2,1)}, u32[]{:S(2)}, u32[]{:S(2)}) collective-permute-start(bf16[768,1024]{1,0:T(8,128)(2,1)} %dynamic-slice_bitcast_fusion.1.refs_5_), channel_id=1, source_target_pairs={{0,1},{1,0},{2,3},{3,2},{4,5},{5,4},{6,7},{7,6},{8,9},{9,8},{10,11... | collective-permute-start | bytes 4718600 | tf_op jit(solution)/shard_map/ppermute | solution.py:37
  39.8 40.8 %collective-permute-start.4 = (bf16[768,1024]{1,0:T(8,128)(2,1)}, bf16[768,1024]{1,0:T(8,128)(2,1)}, u32[]{:S(2)}, u32[]{:S(2)}) collective-permute-start(bf16[768,1024]{1,0:T(8,128)(2,1)} %dynamic-slice_bitcast_fusion.2.refs_4_), channel_id=1, source_target_pairs={{0,1},{1,0},{2,3},{3,2},{4,5},{5,4},{6,7},{7,6},{8,9},{9,8},{10,11... | collective-permute-start | bytes 4718600 | tf_op jit(solution)/shard_map/ppermute | solution.py:37
  80.6 56.6 %all-to-all-start.1 = ((bf16[16,80,896]{2,1,0:T(8,128)(2,1)}), bf16[16,80,896]{2,1,0:T(8,128)(2,1)}, u32[]{:S(2)}, u32[]{:S(2)}) async-start(bf16[16,80,896]{2,1,0:T(8,128)(2,1)} %dispatch_early.1), calls=%async_computation.1 | async-start | bytes 4587520 | tf_op jit(solution)/shard_map/all_to_all | solution.py:1120
  90.9 4.6 collective-permute-start.7
  96.9 51.3 %copy-start.33 = (f32[768]{0:T(1024)S(1)}, f32[768]{0:T(1024)}, u32[]{:S(2)}) copy-start(f32[768]{0:T(1024)} %param.28) | copy-start | bytes 9220
  137.2 30.0 %all-to-all-start.2 = ((bf16[16,3,64,128]{3,2,1,0:T(8,128)(2,1)}), bf16[16,3,64,128]{3,2,1,0:T(8,128)(2,1)S(1)}, u32[]{:S(2)}, u32[]{:S(2)}) async-start(bf16[16,3,64,128]{3,2,1,0:T(8,128)(2,1)} %get-tuple-element.126), calls=%async_computation.2 | async-start | bytes 1572864 | tf_op jit(solution)/shard_map/all_to_all | solution.py:1123
  172.3 2.5 collective-permute-start.8
  180.7 46.1 %all-to-all-start.3 = ((bf16[16,80,768]{2,1,0:T(8,128)(2,1)}), bf16[16,80,768]{2,1,0:T(8,128)(2,1)S(1)}, u32[]{:S(2)}, u32[]{:S(2)}) async-start(bf16[16,80,768]{2,1,0:T(8,128)(2,1)} %dispatch.1), calls=%async_computation.3 | async-start | bytes 3932160 | tf_op jit(solution)/shard_map/all_to_all | solution.py:1131
  185.7 163.2 %reduce-scatter.7.cloned.1.call-start = ((), (), s32[]{:S(2)}) async-start(), calls=%async_computation.15 | async-start | bytes 5898240 | tf_op jit(solution)/shard_map/reduce_scatter | solution.py:1003
  210.1 15.4 %collective-permute-start.9 = (f32[512,1536]{1,0:T(8,128)S(1)}, f32[512,1536]{1,0:T(8,128)}, u32[]{:S(2)}, u32[]{:S(2)}) collective-permute-start(f32[512,1536]{1,0:T(8,128)S(1)} %get-tuple-element.272), channel_id=1, source_target_pairs={{0,1},{1,0},{2,3},{3,2},{4,5},{5,4},{6,7},{7,6},{8,9},{9,8},{10,11... | collective-permute-start | bytes 9437192 | tf_op jit(solution)/shard_map/ppermute | solution.py:1138
  264.9 84.0 %all-to-all-start.4 = ((bf16[16,80,1536]{2,1,0:T(8,128)(2,1)}), bf16[16,80,1536]{2,1,0:T(8,128)(2,1)}, u32[]{:S(2)}, u32[]{:S(2)}) async-start(bf16[16,80,1536]{2,1,0:T(8,128)(2,1)} %bitcast.136), calls=%async_computation.4 | async-start | bytes 7864320 | tf_op jit(solution)/shard_map/all_to_all | solution.py:1154
  274.5 121.5 %reduce-scatter.9.cloned.1.call-start = ((), (), s32[]{:S(2)}) async-start(), calls=%async_computation.16 | async-start | bytes 1474560 | tf_op jit(solution)/shard_map/reduce_scatter | solution.py:1008
  274.5 12.5 %copy-start.7 = (f32[512,1536]{1,0:T(8,128)S(1)}, f32[512,1536]{1,0:T(8,128)}, u32[]{:S(2)}) copy-start(f32[512,1536]{1,0:T(8,128)} %get-tuple-element.151) | copy-start | bytes 9437188
  287.0 16.4 %collective-permute-start.10 = (bf16[768,3072]{1,0:T(8,128)(2,1)}, bf16[768,3072]{1,0:T(8,128)(2,1)S(1)}, u32[]{:S(2)}, u32[]{:S(2)}) collective-permute-start(bf16[768,3072]{1,0:T(8,128)(2,1)} %expert_grads.2), channel_id=1, source_target_pairs={{0,1},{1,0},{2,3},{3,2},{4,5},{5,4},{6,7},{7,6},{8,9},{9,8},{10,11... | collective-permute-start | bytes 14155784 | tf_op jit(solution)/shard_map/ppermute | solution.py:1160
  348.9 7.1 %collective-permute-start.11 = (bf16[1280,1536]{1,0:T(8,128)(2,1)}, bf16[1280,1536]{1,0:T(8,128)(2,1)}, u32[]{:S(2)}, u32[]{:S(2)}) collective-permute-start(bf16[1280,1536]{1,0:T(8,128)(2,1)} %bitcast.42.refs_2_), channel_id=1, source_target_pairs={{0,1},{1,0},{2,3},{3,2},{4,5},{5,4},{6,7},{7,6},{8,9},{9,8},{10,11... | collective-permute-start | bytes 11796488 | tf_op jit(solution)/shard_map/ppermute | solution.py:37
  356.1 33.9 %copy-start.38 = (bf16[4,128,768]{2,1,0:T(8,128)(2,1)S(1)}, bf16[4,128,768]{2,1,0:T(8,128)(2,1)}, u32[]{:S(2)}) copy-start(bf16[4,128,768]{2,1,0:T(8,128)(2,1)} %get-tuple-element.159) | copy-start | bytes 2359300
  372.9 18.9 %copy-start.6 = (bf16[4,128,768]{2,1,0:T(8,128)(2,1)S(1)}, bf16[4,128,768]{2,1,0:T(8,128)(2,1)}, u32[]{:S(2)}) copy-start(bf16[4,128,768]{2,1,0:T(8,128)(2,1)} %get-tuple-element.127.second_ref) | copy-start | bytes 2359300
  372.9 18.9 %copy-start.26 = (bf16[4,128,16]{2,1,0:T(8,128)(2,1)S(1)}, bf16[4,128,16]{2,1,0:T(8,128)(2,1)}, u32[]{:S(2)}) copy-start(bf16[4,128,16]{2,1,0:T(8,128)(2,1)} %get-tuple-element.161) | copy-start | bytes 49156
  372.9 19.1 %copy-start.31 = (f32[1,768]{1,0:T(1,128)S(1)}, f32[1,768]{1,0:T(1,128)}, u32[]{:S(2)}) copy-start(f32[1,768]{1,0:T(1,128)} %get-tuple-element.160) | copy-start | bytes 9220
  372.9 37.0 %all-to-all-start.5 = ((bf16[16,3,64,128]{3,2,1,0:T(8,128)(2,1)}), bf16[16,3,64,128]{3,2,1,0:T(8,128)(2,1)S(1)}, u32[]{:S(2)}, u32[]{:S(2)}) async-start(bf16[16,3,64,128]{3,2,1,0:T(8,128)(2,1)} %get-tuple-element.157), calls=%async_computation.6 | async-start | bytes 1572864 | tf_op jit(solution)/shard_map/all_to_all | solution.py:1188
  391.7 2.2 collective-permute-start.12
  392.1 1.8 collective-permute-start.13
  410.9 51.6 %all-to-all-start.6 = ((bf16[16,48,1536]{2,1,0:T(8,128)(2,1)}), bf16[16,48,1536]{2,1,0:T(8,128)(2,1)S(1)}, u32[]{:S(2)}, u32[]{:S(2)}) async-start(bf16[16,48,1536]{2,1,0:T(8,128)(2,1)} %get-tuple-element.173), calls=%async_computation.8 | async-start | bytes 4718592 | tf_op jit(solution)/shard_map/all_to_all | solution.py:1214
  415.9 41.3 %reduce-scatter.11.cloned.1.call-start = ((), (), s32[]{:S(2)}) async-start(), calls=%async_computation.17 | async-start | bytes 983040 | tf_op jit(solution)/shard_map/reduce_scatter | solution.py:1003
  462.5 3.6 collective-permute-start.15
  470.2 61.5 %all-to-all-start.7 = ((bf16[16,9,64,128]{3,2,1,0:T(8,128)(2,1)}), bf16[16,9,64,128]{3,2,1,0:T(8,128)(2,1)S(1)}, u32[]{:S(2)}, u32[]{:S(2)}) async-start(bf16[16,9,64,128]{3,2,1,0:T(8,128)(2,1)} %pad_maximum_fusion), calls=%async_computation.10 | async-start | bytes 4718592 | tf_op jit(solution)/shard_map/all_to_all | solution.py:1221
  481.1 32.8 %reduce-scatter.13.cloned.1.call-start = ((), (), s32[]{:S(2)}) async-start(), calls=%async_computation.18 | async-start | bytes 245760 | tf_op jit(solution)/shard_map/reduce_scatter | solution.py:1008
  481.6 131.9 %reduce-scatter.15.cloned.1.call-start = ((), (), s32[]{:S(2)}) async-start(), calls=%async_computation.19 | async-start | bytes 2211840 | tf_op jit(solution)/shard_map/reduce_scatter | solution.py:1003
  540.7 3.9 collective-permute-start.22
  548.2 11.9 %copy-start.23 = (bf16[4,128,768]{2,1,0:T(8,128)(2,1)S(1)}, bf16[4,128,768]{2,1,0:T(8,128)(2,1)}, u32[]{:S(2)}) copy-start(bf16[4,128,768]{2,1,0:T(8,128)(2,1)} %get-tuple-element.166) | copy-start | bytes 2359300
  548.2 11.9 %copy-start.25 = (bf16[48,3072]{1,0:T(8,128)(2,1)S(1)}, bf16[48,3072]{1,0:T(8,128)(2,1)}, u32[]{:S(2)}) copy-start(bf16[48,3072]{1,0:T(8,128)(2,1)} %reduce-scatter.9.cloned.1.call-done) | copy-start | bytes 884740
  548.2 78.1 %all-to-all-start.8 = ((bf16[16,48,1536]{2,1,0:T(8,128)(2,1)}), bf16[16,48,1536]{2,1,0:T(8,128)(2,1)}, u32[]{:S(2)}, u32[]{:S(2)}) async-start(bf16[16,48,1536]{2,1,0:T(8,128)(2,1)} %get-tuple-element.192), calls=%async_computation.14 | async-start | bytes 4718592 | tf_op jit(solution)/shard_map/all_to_all | solution.py:1223
  560.0 76.9 %reduce-scatter.17.cloned.1.call-start = ((), (), s32[]{:S(2)}) async-start(), calls=%async_computation.20 | async-start | bytes 552960 | tf_op jit(solution)/shard_map/reduce_scatter | solution.py:1008
  560.1 12.4 %collective-permute-start.14 = (bf16[4,128,768]{2,1,0:T(8,128)(2,1)S(1)}, bf16[4,128,768]{2,1,0:T(8,128)(2,1)S(1)}, u32[]{:S(2)}, u32[]{:S(2)}) collective-permute-start(bf16[4,128,768]{2,1,0:T(8,128)(2,1)S(1)} %copy-done.23), channel_id=1, source_target_pairs={{0,1},{1,0},{2,3},{3,2},{4,5},{5,4},{6,7},{7,6},{8,9},{9,8},{10,11... | collective-permute-start | bytes 2359304 | tf_op jit(solution)/shard_map/ppermute | solution.py:37
  568.4 1.5 collective-permute-start.17
  570.6 5.4 collective-permute-start.18
  575.8 47.2 %collective-permute-start.16 = (bf16[4,128,768]{2,1,0:T(8,128)(2,1)S(1)}, bf16[4,128,768]{2,1,0:T(8,128)(2,1)S(1)}, u32[]{:S(2)}, u32[]{:S(2)}) collective-permute-start(bf16[4,128,768]{2,1,0:T(8,128)(2,1)S(1)} %copy-done.24), channel_id=1, source_target_pairs={{0,1},{1,0},{2,3},{3,2},{4,5},{5,4},{6,7},{7,6},{8,9},{9,8},{10,11... | collective-permute-start | bytes 2359304 | tf_op jit(solution)/shard_map/ppermute | solution.py:37
  576.0 38.2 %collective-permute-start.19 = (f32[1,768]{1,0:T(1,128)S(1)}, f32[1,768]{1,0:T(1,128)S(1)}, u32[]{:S(2)}, u32[]{:S(2)}) collective-permute-start(f32[1,768]{1,0:T(1,128)S(1)} %add.285), channel_id=1, source_target_pairs={{0,4},{2,6},{4,0},{6,2},{8,12},{10,14},{12,8},{14,10},{16,20},{18,... | collective-permute-start | bytes 9224 | tf_op jit(solution)/shard_map/ppermute | solution.py:62
  614.2 3.7 collective-permute-start.20
  617.9 4.5 collective-permute-start.21
  624.0 14.5 %copy-start.1 = (bf16[1,256,4,768]{3,2,1,0:T(4,128)(2,1)S(1)}, bf16[1,256,4,768]{3,2,1,0:T(4,128)(2,1)}, u32[]{:S(2)}) copy-start(bf16[1,256,4,768]{3,2,1,0:T(4,128)(2,1)} %param.18) | copy-start | bytes 4718596
  (30 other events, 98.1 us)
Sparse Core Ops, SparseCore 0:
  227.0 89.8 reduce-scatter.6
  349.1 40.5 reduce-scatter.8
  419.6 37.5 reduce-scatter.10
  483.9 29.9 reduce-scatter.12
  548.3 65.1 reduce-scatter.14
  615.8 21.1 reduce-scatter.16

commit v5 on v4

--- a/solution.py
+++ b/solution.py
@@ -226,7 +226,7 @@
 
 def attend_kernel(members, size, inv_ref, len_ref, w_ref, *refs):
     kv_refs = refs[:size]
-    o_ref, of_ref, lse_ref = refs[size : size + 3]
+    o_ref, of_ref, stat_ref = refs[size : size + 3]
     kv_s, vt_s, q_s, o_s, s_s = refs[size + 3 :]
     u = pl.program_id(0)
     chunk = kv_refs[0].shape[2]
@@ -282,7 +282,8 @@
         total = jnp.sum(total, axis=0, keepdims=True)
         result = acc / total
         of_ref[0, t] = result
-        lse_ref[0, t] = top + jnp.log(total)
+        stat_ref[0, t, 0:1] = top
+        stat_ref[0, t, 1:2] = 1.0 / total
         blank = jnp.zeros_like(result)
         first = 2 * t * TQ < own_rows
         both = jnp.concatenate(
@@ -315,7 +316,7 @@
             out_specs=[
                 pl.BlockSpec((members, 1, chunk, LANES), lambda u, *_: (0, u, 0, 0)),
                 pl.BlockSpec((1, rows // TQ, HEAD_DIM, TQ), lambda u, *_: (u, 0, 0, 0)),
-                pl.BlockSpec((1, rows // TQ, 1, TQ), lambda u, *_: (u, 0, 0, 0)),
+                pl.BlockSpec((1, rows // TQ, 2, TQ), lambda u, *_: (u, 0, 0, 0)),
             ],
             scratch_shapes=[
                 pltpu.VMEM((slot, LANES), BF),
@@ -328,7 +329,7 @@
         out_shape=[
             jax.ShapeDtypeStruct((members, units, chunk, LANES), BF),
             jax.ShapeDtypeStruct((units, rows // TQ, HEAD_DIM, TQ), F4),
-            jax.ShapeDtypeStruct((units, rows // TQ, 1, TQ), F4),
+            jax.ShapeDtypeStruct((units, rows // TQ, 2, TQ), F4),
         ],
         compiler_params=params(1),
         name="attend",
@@ -337,7 +338,7 @@
 
 def attend_back_kernel(members, size, inv_ref, len_ref, w_ref, *refs):
     kv_refs = refs[:size]
-    do_ref, of_ref, lse_ref = refs[size : size + 3]
+    do_ref, of_ref, stat_ref = refs[size : size + 3]
     dq_ref = refs[size + 3]
     dkv_refs = refs[size + 4 : 2 * size + 4]
     kv_s, kt_s, q_s, do_s, dq_s, dkv_s = refs[2 * size + 4 :]
@@ -376,7 +377,7 @@
         delta = jnp.sum(dot_[HEAD_DIM:] * of_ref[0, t], axis=0, keepdims=True)
         qt, dot_ = qt.astype(BF), dot_.astype(BF)
         stacked = jnp.concatenate([do_rows.astype(BF), q_rows.astype(BF)], axis=0)
-        lse = lse_ref[0, t]
+        top, share = stat_ref[0, t, 0:1], stat_ref[0, t, 1:2]
         index = lax.broadcasted_iota(jnp.int32, (1, TQ), 1)
         place = t * span + (index // chunk) * (size * chunk) + w * chunk + index % chunk
         limit = jnp.minimum(place, length - 1)
@@ -384,7 +385,7 @@
         def step(masked, kt, dqt):
             start = pl.multiple_of(kt * TK, TK)
             kv = kv_s[pl.ds(start, TK), :]
-            weights = jnp.exp(dot(kv, qt) - lse)
+            weights = jnp.exp(dot(kv, qt) - top) * share
             if masked:
                 keys = kt * TK + lax.broadcasted_iota(jnp.int32, (TK, 1), 0)
                 weights = jnp.where(keys <= limit, weights, 0.0)
@@ -424,7 +425,7 @@
                 ref[chip, half] = dkv_s[pl.ds(start, chunk), :].astype(ref.dtype)
 
 
-def attend_back(inv, lengths, w, blocks, do_msg, kept, lse, units):
+def attend_back(inv, lengths, w, blocks, do_msg, kept, stats, units):
     members, _, chunk, _ = blocks[0].shape
     size = len(blocks)
     slot = 2 * members * chunk * size
@@ -441,7 +442,7 @@
             + [
                 one,
                 pl.BlockSpec((1, rows // TQ, HEAD_DIM, TQ), lambda u, *_: (u, 0, 0, 0)),
-                pl.BlockSpec((1, rows // TQ, 1, TQ), lambda u, *_: (u, 0, 0, 0)),
+                pl.BlockSpec((1, rows // TQ, 2, TQ), lambda u, *_: (u, 0, 0, 0)),
             ],
             out_specs=[one] + [two] * size,
             scratch_shapes=[
@@ -460,7 +461,7 @@
         ],
         compiler_params=params(1),
         name="attend_back",
-    )(inv, lengths, w, *blocks, do_msg, kept, lse)
+    )(inv, lengths, w, *blocks, do_msg, kept, stats)
 
 
 def mix_kernel(heads, count, shift_ref, o_ref, x_ref, gain_ref, *refs):
@@ -514,65 +515,60 @@
     return result, jnp.sum(upstream * unit, axis=0, keepdims=True)
 
 
-def unrotate_kernel(heads, count, shift_ref, msg_ref, cos_ref, sin_ref, at_ref, *outs):
-    dqkv_ref, *grad_refs = outs
+def unrotate_kernel(heads, per, k, shift_ref, msg_ref, cos_ref, sin_ref, at_ref, dqkv_ref, grad_ref):
     members, triple, chunk, _ = msg_ref.shape
     units = triple // 3
     seqs, rows, _ = dqkv_ref.shape
     cosine, sine = cos_ref[...], sin_ref[...]
+    inner = per * HEAD_DIM
+
+    def rope_back(grad):
+        return grad * cosine - turn_halves(grad) * sine
+
+    for s in range(seqs):
+        for g in range(per // 2):
+            pair, asked = [], []
+            for c in range(2):
+                chip, u = head_units(seqs, heads, members, shift_ref[0], s, k * per + 2 * g + c)
+                both = [msg_ref[chip, 2 * u], msg_ref[chip, 2 * u + 1]]
+                pair.append(jnp.concatenate(both, axis=0).astype(F4))
+                asked.append(msg_ref[chip, 2 * units + u].astype(F4))
+            key, value = pair_swap(*pair)
+            query = jnp.concatenate(pair_swap(*asked), axis=0)
+            at = g * LANES
+            dqkv_ref[s, :, at : at + LANES] = rope_back(query).astype(BF)
+            at = at + inner
+            dqkv_ref[s, :, at : at + LANES] = rope_back(key).astype(BF)
+            at = at + inner
+            dqkv_ref[s, :, at : at + LANES] = value.astype(BF)
+    made = dot(at_ref[...], dqkv_ref[...].reshape(seqs * rows, 3 * inner))
+    grad_ref[...] = made.astype(grad_ref.dtype)
+
+
+def unrotate(shift, msg, cosine, sine, a1_turned, seqs, heads, k, count):
+    rows = 2 * msg.shape[2]
+    width = a1_turned.shape[0]
     per = heads // count
     inner = per * HEAD_DIM
-
-    def rope_back(grad):
-        return grad * cosine - turn_halves(grad) * sine
-
-    for k in list(range(1, count)) + [0]:
-        for s in range(seqs):
-            for g in range(per // 2):
-                pair, asked = [], []
-                for c in range(2):
-                    chip, u = head_units(
-                        seqs, heads, members, shift_ref[0], s, k * per + 2 * g + c
-                    )
-                    both = [msg_ref[chip, 2 * u], msg_ref[chip, 2 * u + 1]]
-                    pair.append(jnp.concatenate(both, axis=0).astype(F4))
-                    asked.append(msg_ref[chip, 2 * units + u].astype(F4))
-                key, value = pair_swap(*pair)
-                query = jnp.concatenate(pair_swap(*asked), axis=0)
-                at = 3 * k * inner + g * LANES
-                dqkv_ref[s, :, at : at + LANES] = rope_back(query).astype(BF)
-                at = at + inner
-                dqkv_ref[s, :, at : at + LANES] = rope_back(key).astype(BF)
-                at = at + inner
-                dqkv_ref[s, :, at : at + LANES] = value.astype(BF)
-        cols = dqkv_ref[:, :, 3 * k * inner : 3 * (k + 1) * inner]
-        made = dot(at_ref[...], cols.reshape(seqs * rows, 3 * inner))
-        grad_refs[k][...] = made.astype(grad_refs[k].dtype)
-
-
-def unrotate(shift, msg, cosine, sine, a1_turned, seqs, heads, count):
-    rows = 2 * msg.shape[2]
-    width = a1_turned.shape[0]
-    inner = heads * HEAD_DIM
     return one_step(
-        functools.partial(unrotate_kernel, heads, count),
+        functools.partial(unrotate_kernel, heads, per, k),
         "unrotate",
         shift,
         [msg, cosine, sine, a1_turned],
-        [jax.ShapeDtypeStruct((seqs, rows, 3 * inner), BF)]
-        + [jax.ShapeDtypeStruct((width, 3 * inner // count), BF if k else F4) for k in range(count)],
-    )
-
-
-def unproject_kernel(count, shift_ref, dqkv_ref, x_ref, dstate_ref, gain_ref, *refs):
-    w_refs = refs[:count]
-    dx_ref, dgain_ref = refs[count:]
+        [
+            jax.ShapeDtypeStruct((seqs, rows, 3 * inner), BF),
+            jax.ShapeDtypeStruct((width, 3 * inner), BF if k else F4),
+        ],
+    )
+
+
+def unproject_kernel(count, shift_ref, x_ref, dstate_ref, gain_ref, *refs):
+    dqkv_refs, w_refs = refs[:count], refs[count : 2 * count]
+    dx_ref, dgain_ref = refs[2 * count :]
     seqs, rows, width = x_ref.shape
-    inner = dqkv_ref.shape[2] // count
     made = 0.0
-    for k in range(count):
-        cols = dqkv_ref[:, :, k * inner : (k + 1) * inner].reshape(seqs * rows, inner)
-        made = made + dot(cols, w_refs[k][...])
+    for dqkv_ref, w_ref in zip(dqkv_refs, w_refs):
+        made = made + dot(dqkv_ref[...].reshape(seqs * rows, -1), w_ref[...])
     total = jnp.zeros((1, width), F4)
     for s in range(seqs):
         pulled, dgain = norm_back(
@@ -589,7 +585,7 @@
         functools.partial(unproject_kernel, len(parts)),
         "unproject",
         shift,
-        [dqkv, x, dstate, gain, *parts],
+        [x, dstate, gain, *dqkv, *parts],
         [
             jax.ShapeDtypeStruct((seqs, rows, width), BF),
             jax.ShapeDtypeStruct((1, width), F4),
@@ -654,35 +650,63 @@
     return [value / total for value in raised]
 
 
+def take_back(info, home_ref, k, width):
+    target = info[:, 2 * k : 2 * k + 2]
+    ids = lax.broadcasted_iota(jnp.int32, (info.shape[0], home_ref.shape[0]), 1)
+    hits = [ids == target[:, c : c + 1] for c in range(2)]
+    made = [dot(hit.astype(BF), home_ref[:, :width]) for hit in hits]
+    return [*made, dot((hits[0] | hits[1]).astype(BF), home_ref[:, width:])]
+
+
+def first_part_kernel(info_ref, home_ref, out_ref):
+    take, rows, triple = out_ref.shape
+    width = triple // 3
+    info = info_ref[...].reshape(take * rows, info_ref.shape[2])
+    for n, part in enumerate(take_back(info, home_ref, 0, width)):
+        out_ref[:, :, n * width : (n + 1) * width] = part.reshape(take, rows, width)
+
+
+def first_part(info, home):
+    seqs, rows, cols = info.shape
+    width = home.shape[1] // 2
+    take = max(1, min(seqs, 256 // rows))
+    return pl.pallas_call(
+        first_part_kernel,
+        grid=(seqs // take,),
+        in_specs=[pl.BlockSpec((take, rows, cols), lambda s: (s, 0, 0)), whole(home.shape)],
+        out_specs=pl.BlockSpec((take, rows, 3 * width), lambda s: (s, 0, 0)),
+        out_shape=jax.ShapeDtypeStruct((seqs, rows, 3 * width), F4),
+        compiler_params=params(1),
+        name="first_part",
+    )(info, home)
+
+
 def finish_kernel(
     heads, size, count, shift_ref, info_ref, second_ref, state_ref, cot_ref, gain_ref, *refs
 ):
     router_ref, turned_ref, *refs = refs
-    home_refs, refs = refs[:size], refs[size:]
-    dense_ref, *refs = refs
+    home_refs, refs = refs[: size - 1], refs[size - 1 :]
+    first_ref, dense_ref, *refs = refs
     w_refs = refs[:count]
     out_ref, dstate_ref, low_ref, logit_ref, msg_ref, dgain_ref = refs[count:]
     step = pl.program_id(0)
     take, rows, width = state_ref.shape
     lines = take * rows
     members, units, chunk, _ = msg_ref.shape
-    slots = home_refs[0].shape[0]
     experts = turned_ref.shape[0]
     info = info_ref[...].reshape(lines, info_ref.shape[2])
-    target = info[:, : 2 * size]
     chosen = [info[:, 2 * size + c : 2 * size + c + 1] for c in range(2)]
     logits = dot(second_ref[...].reshape(lines, width), router_ref[...])[:, :experts]
     names = lax.broadcasted_iota(jnp.int32, (lines, experts), 1)
     gates = two_gates(
         [jnp.sum(jnp.where(names == pick, logits, 0.0), axis=1, keepdims=True) for pick in chosen]
     )
-    ids = lax.broadcasted_iota(jnp.int32, (lines, slots), 1)
-    made, back = [0.0, 0.0], 0.0
-    for k in range(size):
-        hits = [ids == target[:, 2 * k + c : 2 * k + c + 1] for c in range(2)]
-        for c in range(2):
-            made[c] = made[c] + dot(hits[c].astype(BF), home_refs[k][:, :width])
-        back = back + dot((hits[0] | hits[1]).astype(BF), home_refs[k][:, width:])
+    first = first_ref[...].reshape(lines, 3 * width)
+    *made, back = [first[:, n * width : (n + 1) * width] for n in range(3)]
+    for k, home_ref in enumerate(home_refs):
+        more = take_back(info, home_ref, k + 1, width)
+        made = [a + b for a, b in zip(made, more)]
+        back = back + more[2]
     cot = cot_ref[...].reshape(lines, width).astype(F4)
     pulled = [jnp.sum(y * cot, axis=-1, keepdims=True) for y in made]
     middle = gates[0] * pulled[0] + gates[1] * pulled[1]
@@ -726,7 +750,7 @@
                     msg_ref[chip, u] = pair[c].astype(BF)
 
 
-def finish(shift, info, second, state, cot, gain, router, turned, homes, dense, parts, members, units):
+def finish(shift, info, second, state, cot, gain, router, turned, homes, first, dense, parts, members, units):
     seqs, rows, width = state.shape
     inner = sum(part.shape[1] for part in parts)
     experts = turned.shape[0]
@@ -734,12 +758,12 @@
     msg = (members, units, rows // 2, LANES)
     some = lambda cols: pl.BlockSpec((take, rows, cols), lambda s: (s, 0, 0))
     return pl.pallas_call(
-        functools.partial(finish_kernel, inner // HEAD_DIM, len(homes), len(parts)),
+        functools.partial(finish_kernel, inner // HEAD_DIM, len(homes) + 1, len(parts)),
         grid=(seqs // take,),
         in_specs=[SMEM, some(info.shape[2]), some(width), some(width), some(width)]
         + [whole((1, width)), whole(router.shape), whole(turned.shape)]
         + [whole(home.shape) for home in homes]
-        + [some(2 * width)]
+        + [some(3 * width), some(2 * width)]
         + [whole(part.shape) for part in parts],
         out_specs=[some(width)] * 3 + [some(experts), whole(msg), whole((1, width))],
         out_shape=[
@@ -752,7 +776,7 @@
         ],
         compiler_params=params(1),
         name="finish",
-    )(shift, info, second, state, cot, gain, router, turned, *homes, dense, *parts)
+    )(shift, info, second, state, cot, gain, router, turned, *homes, first, dense, *parts)
 
 
 def place_kernel(copies, cuts, *refs):
@@ -1118,7 +1142,7 @@
 
     blocks = wt_gather(got)
     early = swap(early)
-    o_msg, kept, lse = attend(inv, unit_lengths, w_arg, blocks, units)
+    o_msg, kept, stats = attend(inv, unit_lengths, w_arg, blocks, units)
     o_msg, early = lax.optimization_barrier((o_msg, early))
     o_got = lax.all_to_all(o_msg, "ctx", 0, 0, tiled=True)
     mixed, state, second_own = mix(shift, o_got, x, ffn_gain[None], out_parts)
@@ -1167,6 +1191,7 @@
     )
     dense_sum = far_scatter(dense_near)
     homes = wt_gather(home.reshape(experts * held, 2 * width))
+    first = first_part(own_info, homes[0])
 
     own_cot = cots[0].reshape(seqs, 2 * chunk, width)
     dense = dense.reshape(seqs, 2 * chunk, 2 * width)
@@ -1179,7 +1204,8 @@
         ffn_gain[None],
         router_wide,
         router_turned,
-        homes,
+        homes[1:],
+        first,
         dense,
         out_back,
         members,
@@ -1213,7 +1239,7 @@
     )
     expert_got = [lax.all_to_all(expert_sum[0], "ctx", 0, 0, tiled=True)]
     out_near = near_scatter(out_msg)
-    dq, *dkv = attend_back(inv, unit_lengths, w_arg, blocks, do_got, kept, lse, units)
+    dq, *dkv = attend_back(inv, unit_lengths, w_arg, blocks, do_got, kept, stats, units)
     dq, dkv, expert_got, out_near = lax.optimization_barrier((dq, dkv, expert_got, out_near))
     out_sum = far_scatter(out_near)
     dkv = wt_scatter(dkv).astype(BF)
@@ -1221,11 +1247,17 @@
     grad_got = lax.all_to_all(grad_msg, "ctx", 0, 0, tiled=True)
     grad_got, out_sum, expert_sum = lax.optimization_barrier((grad_got, out_sum, expert_sum))
     expert_got.append(lax.all_to_all(expert_sum[1], "ctx", 0, 0, tiled=True))
-    dqkv, *pieces = unrotate(shift, grad_got, cosine, sine, a1_turned, seqs, heads, len(parts))
+    count = len(parts)
+    dqkv, last_msg = [None] * count, None
+    for k in list(range(1, count)) + [0]:
+        dqkv[k], made = unrotate(shift, grad_got, cosine, sine, a1_turned, seqs, heads, k, count)
+        if k:
+            made = lax.ppermute(made, "wt", [(i, (i + k) % size) for i in range(size)])
+        last_msg = made.astype(F4) if last_msg is None else last_msg + made.astype(F4)
     if split:
-        last_msg = wt_scatter(pieces).astype(BF)
+        last_msg = last_msg.astype(BF)
     else:
-        last_msg = by_steps(split_wt(a1, dqkv, 3))
+        last_msg = by_steps(split_wt(a1, dqkv[0], 3))
     last_sum = far_scatter(near_scatter(last_msg))
     dx, attn_grad = unproject(shift, dqkv, x, dstate, attn_gain[None], back_parts)
     attn_grad = ctx_sum(wt_sum(attn_grad)).reshape(members, -1)

time: 656 us -> 653 us (level)
  waiting for transfers between devices: 211 us -> 189 us
  Pallas kernels: 221 us -> 240 us
    pallas_call x1, Pallas kernels: 34.6 us -> 43.2 us  [attend_back(): pl.pallas_call(functools.partial(attend_back_kernel, members, size), grid...]
    pallas_call x0 -> x1, Pallas kernels: none -> 7.18 us  [first_part(): pl.pallas_call(first_part_kernel, grid=(seqs // take,), in_specs=[pl.Bloc...]
    pallas_call x5 -> x6, Pallas kernels: 31.5 us -> 34.3 us  [one_step(): pl.pallas_call(kernel, grid=(1,), in_specs=[SMEM] + [whole(array.shape) f...]
  transfers between devices with their start and end apart: 38 -> 38, of which waited for: 20 -> 17; matrix products, arithmetic and copies ran while one was open for 12% -> 12% of each run, Pallas kernels for 30% -> 34%
where the time goes in v5:
time: 653 us; the launch traced here: 643 us
  Pallas kernels  240 us (37%)
  waiting for transfers between devices  189 us (29%)
  starting transfers between devices  98.6 us (15%)
  local copies, waits for them, and re-layouts  66.4 us (10%)
  other arithmetic  30.3 us (5%)
  between operations  15.7 us (2%)
    pallas_call x2, Pallas kernels, gated(): pl.pallas_call(functools.partial(gated_kernel, count, tiles, bool(routed)...  55 us
    pallas_call x1, Pallas kernels, attend_back(): pl.pallas_call(functools.partial(attend_back_kernel, members, size), grid...  43.2 us
    all_to_all x1, waiting for transfers between devices, per_device(): home = swap(returned.reshape(experts, held, 2 * width))  38.4 us
    reduce_scatter x3, waiting for transfers between devices, near_scatter(): lax.psum_scatter(array, 'ctx', scatter_dimension=0, tiled=True, axis_inde...  35.9 us
    pallas_call x3, Pallas kernels, gated_grads(): pl.pallas_call(gated_grads_kernel, grid=(tiles,), in_specs=[whole(x.shape...  35.2 us
    reduce_scatter x3, waiting for transfers between devices, far_scatter(): lax.psum_scatter(array, 'ctx', scatter_dimension=0, tiled=True, axis_inde...  35 us
    pallas_call x6, Pallas kernels, one_step(): pl.pallas_call(kernel, grid=(1,), in_specs=[SMEM] + [whole(array.shape) f...  34.3 us
    pallas_call x1, Pallas kernels, attend(): pl.pallas_call(functools.partial(attend_kernel, members, size), grid_spec...  33.9 us
  transfers between devices with their start and end apart: 38, of which 17 were waited for; matrix products, arithmetic and copies ran while one was open for 12% of the time, Pallas kernels for 34%

profile of v5, /device:TPU:0, one launch (start us, length us, event | category | flops | bytes accessed | tf_op | source)
XLA Modules:
  0.0 642.6 jit_solution(8424922187636056186)
XLA Ops:
  15.7 7.2 %project.1 = (bf16[16,9,64,128]{3,2,1,0:T(8,128)(2,1)}, bf16[4,128,768]{2,1,0:T(8,128)(2,1)}) custom-call(s32[1]{0:T(128)} %bitcast.shift_ref, bf16[4,128,768]{2,1,0:T(8,128)(2,1)} %bitcast.127, f32[1,768]{1,0:T(1,128)} %broadcast_in_dim.91.gain_ref, f32[128,128]{1,0:T(8,128)} %get-tuple-element.108.cos_ref, f32[128,128]{1,0:T(8,128)} %get-tuple-element.109.sin_ref, ...), custom_call_target="tpu_custom_call" | custom-call | tf_op jit(solution)/shard_map/project/pallas_call | solution.py:149
  22.9 8.1 %all-to-all-start = ((bf16[16,9,64,128]{3,2,1,0:T(8,128)(2,1)}), bf16[16,9,64,128]{3,2,1,0:T(8,128)(2,1)S(1)}, u32[]{:S(2)}, u32[]{:S(2)}) async-start(bf16[16,9,64,128]{3,2,1,0:T(8,128)(2,1)} %get-tuple-element.111), calls=%async_computation | async-start | bytes 4718592 | tf_op jit(solution)/shard_map/all_to_all | solution.py:1015
  31.2 2.7 dynamic-slice_bitcast_fusion.refs_6_
  34.2 2.7 dynamic-slice_bitcast_fusion.1.refs_5_
  37.0 2.7 dynamic-slice_bitcast_fusion.2.refs_4_
  64.8 5.7 turn.1
  74.9 5.5 dispatch_early.1
  80.5 10.3 %all-to-all-start.1 = ((bf16[16,80,896]{2,1,0:T(8,128)(2,1)}), bf16[16,80,896]{2,1,0:T(8,128)(2,1)}, u32[]{:S(2)}, u32[]{:S(2)}) async-start(bf16[16,80,896]{2,1,0:T(8,128)(2,1)} %dispatch_early.1), calls=%async_computation.1 | async-start | bytes 4587520 | tf_op jit(solution)/shard_map/all_to_all | solution.py:1144
  90.9 4.5 collective-permute-done.7.refs_1_
  96.9 33.9 %attend.1 = (bf16[16,3,64,128]{3,2,1,0:T(8,128)(2,1)}, f32[3,4,64,512]{3,2,1,0:T(8,128)}, f32[3,4,2,512]{3,2,1,0:T(2,128)}) custom-call(s32[16]{0:T(128)} %get-tuple-element.122.inv_ref, s32[3]{0:T(128)} %gather_fusion, s32[1]{0:T(128)} %bitcast.31.w_ref, bf16[16,9,64,128]{3,2,1,0:T(8,128)(2,1)} %copy-done.5, bf16[16,9,64,128]{3,2,1,0:T(8,128)(2,1)} %copy-done.10), custom_call_target="tpu_custom_call" | custom-call | tf_op jit(solution)/shard_map/attend/pallas_call | solution.py:310
  130.7 6.4 all-to-all-done.1
  137.1 10.5 %all-to-all-start.2 = ((bf16[16,3,64,128]{3,2,1,0:T(8,128)(2,1)}), bf16[16,3,64,128]{3,2,1,0:T(8,128)(2,1)S(1)}, u32[]{:S(2)}, u32[]{:S(2)}) async-start(bf16[16,3,64,128]{3,2,1,0:T(8,128)(2,1)} %get-tuple-element.127), calls=%async_computation.2 | async-start | bytes 1572864 | tf_op jit(solution)/shard_map/all_to_all | solution.py:1147
  148.2 18.4 %all-to-all-done.2.o_ref = bf16[16,3,64,128]{3,2,1,0:T(8,128)(2,1)S(1)} async-done(((bf16[16,3,64,128]{3,2,1,0:T(8,128)(2,1)}), bf16[16,3,64,128]{3,2,1,0:T(8,128)(2,1)S(1)}, u32[]{:S(2)}, u32[]{:S(2)}) %all-to-all-start.2) | async-done | bytes 786464 | tf_op jit(solution)/shard_map/all_to_all | solution.py:1147
  167.5 4.2 mix.1
  175.1 5.1 dispatch.1
  180.2 5.0 all-to-all-start.3
  186.6 18.1 %dense_branch.1 = (f32[1024,1536]{1,0:T(8,128)}, bf16[1024,3072]{1,0:T(8,128)(2,1)}) custom-call(bf16[1024,768]{1,0:T(8,128)(2,1)} %pad_maximum_fusion.1.cot_ref.refs_0_.d_ref, bf16[1024,768]{1,0:T(8,128)(2,1)} %copy-done.12, bf16[768,1024]{1,0:T(8,128)(2,1)} %refs_2_.5, bf16[768,1024]{1,0:T(8,128)(2,1)} %refs_3_.3, bf16[1024,768]{1,0:T(8,128)(2,1)} %refs_4_.3), custom_call_target="tpu_custom_call" | custom-call | tf_op jit(solution)/shard_map/dense_branch/pallas_call | solution.py:888
  204.7 5.0 fusion.20
  209.7 10.4 %dense_grads.1 = bf16[768,3072]{1,0:T(8,128)(2,1)} custom-call(bf16[1024,768]{1,0:T(8,128)(2,1)} %copy-done.12, bf16[1024,768]{1,0:T(8,128)(2,1)} %pad_maximum_fusion.1.cot_ref.refs_0_.d_ref, bf16[1024,3072]{1,0:T(8,128)(2,1)} %get-tuple-element.140.hid_ref), custom_call_target="tpu_custom_call" | custom-call | flops 4831838208 | bytes 14155776 | tf_op jit(solution)/shard_map/dense_grads/pallas_call | solution.py:922
  220.1 4.9 copy.126
  227.6 36.8 %expert_branch.1 = (bf16[1280,768]{1,0:T(8,128)(2,1)}, bf16[1280,1536]{1,0:T(8,128)(2,1)}, bf16[1280,6144]{1,0:T(8,128)(2,1)}) custom-call(s32[1]{0:T(128)} %bitcast.33.refs_0_, bf16[768,128]{1,0:T(8,128)(2,1)} %pad.4.refs_1_.refs_0_, bf16[1280,896]{1,0:T(8,128)(2,1)} %bitcast.34.refs_2_, bf16[1280,768]{1,0:T(8,128)(2,1)} %bitcast.118, ...), custom_call_target="tpu_custom_call" | custom-call | tf_op jit(solution)/shard_map/expert_branch/pallas_call | solution.py:888
  264.5 9.5 %all-to-all-start.4 = ((bf16[16,80,1536]{2,1,0:T(8,128)(2,1)}), bf16[16,80,1536]{2,1,0:T(8,128)(2,1)}, u32[]{:S(2)}, u32[]{:S(2)}) async-start(bf16[16,80,1536]{2,1,0:T(8,128)(2,1)} %bitcast.138), calls=%async_computation.4 | async-start | bytes 7864320 | tf_op jit(solution)/shard_map/all_to_all | solution.py:1178
  274.1 12.4 %expert_grads.2 = bf16[768,3072]{1,0:T(8,128)(2,1)} custom-call(bf16[1280,768]{1,0:T(8,128)(2,1)} %bitcast.119, bf16[1280,768]{1,0:T(8,128)(2,1)} %get-tuple-element.149.d_ref, bf16[1280,6144]{1,0:T(8,128)(2,1)} %get-tuple-element.150.hid_ref), custom_call_target="tpu_custom_call" | custom-call | flops 6039797760 | bytes 16515072 | tf_op jit(solution)/shard_map/expert_grads/pallas_call | solution.py:922
  286.5 4.1 add.278
  290.7 12.3 %expert_grads.3 = bf16[768,3072]{1,0:T(8,128)(2,1)} custom-call(bf16[1280,768]{1,0:T(8,128)(2,1)} %bitcast.120, bf16[1280,768]{1,0:T(8,128)(2,1)} %get-tuple-element.149.d_ref, bf16[1280,6144]{1,0:T(8,128)(2,1)} %get-tuple-element.150.hid_ref), custom_call_target="tpu_custom_call" | custom-call | flops 6039797760 | bytes 16515072 | tf_op jit(solution)/shard_map/expert_grads/pallas_call | solution.py:922
  303.0 4.3 add_convert_fusion
  307.2 2.9 fusion.21
  310.1 38.4 %all-to-all-done.4 = bf16[16,80,1536]{2,1,0:T(8,128)(2,1)} async-done(((bf16[16,80,1536]{2,1,0:T(8,128)(2,1)}), bf16[16,80,1536]{2,1,0:T(8,128)(2,1)}, u32[]{:S(2)}, u32[]{:S(2)}) %all-to-all-start.4) | async-done | bytes 3932192 | tf_op jit(solution)/shard_map/all_to_all | solution.py:1178
  349.4 7.2 %first_part.1.refs_3_ = f32[4,128,2304]{2,1,0:T(8,128)} custom-call(s32[4,128,6]{2,1,0:T(8,128)} %copy.128.info_ref, bf16[1280,1536]{1,0:T(8,128)(2,1)} %bitcast.42.home_ref), custom_call_target="tpu_custom_call" | custom-call | tf_op jit(solution)/shard_map/first_part/pallas_call | solution.py:673
  356.6 13.0 %finish.1 = (bf16[4,128,768]{2,1,0:T(8,128)(2,1)}, f32[4,128,768]{2,1,0:T(8,128)}, bf16[4,128,768]{2,1,0:T(8,128)(2,1)}, bf16[4,128,16]{2,1,0:T(8,128)(2,1)}, bf...) custom-call(s32[1]{0:T(128)} %bitcast.shift_ref, s32[4,128,6]{2,1,0:T(8,128)} %copy.128.info_ref, ...), custom_call_target="tpu_custom_call" | custom-call | tf_op jit(solution)/shard_map/finish/pallas_call | solution.py:760
  369.6 17.0 %all-to-all-start.5 = ((bf16[16,3,64,128]{3,2,1,0:T(8,128)(2,1)}), bf16[16,3,64,128]{3,2,1,0:T(8,128)(2,1)S(1)}, u32[]{:S(2)}, u32[]{:S(2)}) async-start(bf16[16,3,64,128]{3,2,1,0:T(8,128)(2,1)} %get-tuple-element.158), calls=%async_computation.6 | async-start | bytes 1572864 | tf_op jit(solution)/shard_map/all_to_all | solution.py:1214
  392.6 14.1 %all-to-all-done.5.refs_2_ = bf16[16,3,64,128]{3,2,1,0:T(8,128)(2,1)S(1)} async-done(((bf16[16,3,64,128]{3,2,1,0:T(8,128)(2,1)}), bf16[16,3,64,128]{3,2,1,0:T(8,128)(2,1)S(1)}, u32[]{:S(2)}, u32[]{:S(2)}) %all-to-all-start.5) | async-done | bytes 786464 | tf_op jit(solution)/shard_map/all_to_all | solution.py:1214
  407.6 5.5 all-to-all-start.6
  413.9 43.2 %attend_back.1 = (bf16[16,3,64,128]{3,2,1,0:T(8,128)(2,1)}, f32[16,6,64,128]{3,2,1,0:T(8,128)}, bf16[16,6,64,128]{3,2,1,0:T(8,128)(2,1)}) custom-call(s32[16]{0:T(128)} %get-tuple-element.122.inv_ref, s32[3]{0:T(128)} %gather_fusion, s32[1]{0:T(128)} %bitcast.31.w_ref, bf16[16,9,64,128]{3,2,1,0:T(8,128)(2,1)} %copy-done.5, ...), custom_call_target="tpu_custom_call" | custom-call | tf_op jit(solution)/shard_map/attend_back/pallas_call | solution.py:436
  457.1 3.2 all-to-all-done.6.refs_0_
  460.3 3.6 collective-permute-done.15
  468.0 10.8 %all-to-all-start.7 = ((bf16[16,9,64,128]{3,2,1,0:T(8,128)(2,1)}), bf16[16,9,64,128]{3,2,1,0:T(8,128)(2,1)S(1)}, u32[]{:S(2)}, u32[]{:S(2)}) async-start(bf16[16,9,64,128]{3,2,1,0:T(8,128)(2,1)} %pad_maximum_fusion), calls=%async_computation.10 | async-start | bytes 4718592 | tf_op jit(solution)/shard_map/all_to_all | solution.py:1247
  479.6 32.0 %reduce-scatter.13.cloned.1.call-done = bf16[48,512]{1,0:T(8,128)(2,1)} async-done(((bf16[192,512]{1,0:T(8,128)(2,1)}), bf16[48,512]{1,0:T(8,128)(2,1)}) %reduce-scatter.13.cloned.1.call-update) | async-done | bytes 49168 | tf_op jit(solution)/shard_map/reduce_scatter | solution.py:1032
  511.5 17.9 %all-to-all-done.7.msg_ref = bf16[16,9,64,128]{3,2,1,0:T(8,128)(2,1)S(1)} async-done(((bf16[16,9,64,128]{3,2,1,0:T(8,128)(2,1)}), bf16[16,9,64,128]{3,2,1,0:T(8,128)(2,1)S(1)}, u32[]{:S(2)}, u32[]{:S(2)}) %all-to-all-start.7) | async-done | bytes 2359328 | tf_op jit(solution)/shard_map/all_to_all | solution.py:1247
  530.9 4.9 unrotate.3
  535.8 5.5 unrotate.2
  541.2 3.5 add_convert_fusion.1
  544.8 11.8 %all-to-all-start.8 = ((bf16[16,48,1536]{2,1,0:T(8,128)(2,1)}), bf16[16,48,1536]{2,1,0:T(8,128)(2,1)}, u32[]{:S(2)}, u32[]{:S(2)}) async-start(bf16[16,48,1536]{2,1,0:T(8,128)(2,1)} %get-tuple-element.194), calls=%async_computation.14 | async-start | bytes 4718592 | tf_op jit(solution)/shard_map/all_to_all | solution.py:1249
  558.3 6.8 %unproject.1 = (bf16[4,128,768]{2,1,0:T(8,128)(2,1)}, f32[1,768]{1,0:T(1,128)}) custom-call(s32[1]{0:T(128)} %bitcast.shift_ref, bf16[4,128,768]{2,1,0:T(8,128)(2,1)} %bitcast.129, f32[4,128,768]{2,1,0:T(8,128)} %get-tuple-element.168.dstate_ref, f32[1,768]{1,0:T(1,128)} %broadcast_in_dim.91.gain_ref, bf16[4,128,1152]{2,1,0:T(8,128)(2,1)} %get-tuple-element.184.refs_0_, ...), custom_call_target="tpu_custom_call" | custom-call | tf_op jit(solution)/shard_map/unproject/pallas_call | solution.py:149
  574.8 35.9 %reduce-scatter.15.cloned.1.call-done = bf16[192,1152]{1,0:T(8,128)(2,1)} async-done(((bf16[768,1152]{1,0:T(8,128)(2,1)}), bf16[192,1152]{1,0:T(8,128)(2,1)}) %reduce-scatter.15.cloned.1.call-update) | async-done | bytes 442384 | tf_op jit(solution)/shard_map/reduce_scatter | solution.py:1027
  611.5 3.5 collective-permute-done.20
  623.5 7.5 %place.1 = (f32[16,48,1024]{2,1,0:T(8,128)}, f32[16,48,1024]{2,1,0:T(8,128)}, f32[16,48,1024]{2,1,0:T(8,128)}) custom-call(bf16[16,48,1536]{2,1,0:T(8,128)(2,1)} %copy-done.9, bf16[16,48,1536]{2,1,0:T(8,128)(2,1)} %all-to-all-done.8.refs_1_), custom_call_target="tpu_custom_call" | custom-call | tf_op jit(solution)/shard_map/place/pallas_call | solution.py:800
  631.0 3.1 reduce-scatter.17.cloned.1.call-done
  (234 shorter events, 84.9 us)
Async XLA Ops:
  7.2 7.3 %collective-permute-start = (bf16[768,384]{1,0:T(8,128)(2,1)}, bf16[768,384]{1,0:T(8,128)(2,1)S(1)}, u32[]{:S(2)}, u32[]{:S(2)}) collective-permute-start(bf16[768,384]{1,0:T(8,128)(2,1)} %refs_1_.3), channel_id=1, source_target_pairs={{0,1},{1,0},{2,3},{3,2},{4,5},{5,4},{6,7},{7,6},{8,9},{9,8},{10,11... | collective-permute-start | bytes 1769480 | tf_op jit(solution)/shard_map/ppermute | solution.py:37
  7.7 6.8 %collective-permute-start.1 = (bf16[768,384]{1,0:T(8,128)(2,1)}, bf16[768,384]{1,0:T(8,128)(2,1)S(1)}, u32[]{:S(2)}, u32[]{:S(2)}) collective-permute-start(bf16[768,384]{1,0:T(8,128)(2,1)} %refs_2_.4), channel_id=1, source_target_pairs={{0,1},{1,0},{2,3},{3,2},{4,5},{5,4},{6,7},{7,6},{8,9},{9,8},{10,11... | collective-permute-start | bytes 1769480 | tf_op jit(solution)/shard_map/ppermute | solution.py:37
  7.8 6.7 %collective-permute-start.2 = (bf16[768,384]{1,0:T(8,128)(2,1)}, bf16[768,384]{1,0:T(8,128)(2,1)S(1)}, u32[]{:S(2)}, u32[]{:S(2)}) collective-permute-start(bf16[768,384]{1,0:T(8,128)(2,1)} %refs_3_.2), channel_id=1, source_target_pairs={{0,1},{1,0},{2,3},{3,2},{4,5},{5,4},{6,7},{7,6},{8,9},{9,8},{10,11... | collective-permute-start | bytes 1769480 | tf_op jit(solution)/shard_map/ppermute | solution.py:37
  22.9 57.6 %all-to-all-start = ((bf16[16,9,64,128]{3,2,1,0:T(8,128)(2,1)}), bf16[16,9,64,128]{3,2,1,0:T(8,128)(2,1)S(1)}, u32[]{:S(2)}, u32[]{:S(2)}) async-start(bf16[16,9,64,128]{3,2,1,0:T(8,128)(2,1)} %get-tuple-element.111), calls=%async_computation | async-start | bytes 4718592 | tf_op jit(solution)/shard_map/all_to_all | solution.py:1015
  31.0 33.0 %collective-permute-start.3 = (bf16[384,768]{1,0:T(8,128)(2,1)S(1)}, bf16[384,768]{1,0:T(8,128)(2,1)S(1)}, u32[]{:S(2)}, u32[]{:S(2)}) collective-permute-start(bf16[384,768]{1,0:T(8,128)(2,1)S(1)} %copy-done.20), channel_id=1, source_target_pairs={{0,1},{1,0},{2,3},{3,2},{4,5},{5,4},{6,7},{7,6},{8,9},{9,8},{10,11... | collective-permute-start | bytes 1769480 | tf_op jit(solution)/shard_map/ppermute | solution.py:37
  33.9 46.6 %collective-permute-start.6 = (bf16[1024,768]{1,0:T(8,128)(2,1)}, bf16[1024,768]{1,0:T(8,128)(2,1)}, u32[]{:S(2)}, u32[]{:S(2)}) collective-permute-start(bf16[1024,768]{1,0:T(8,128)(2,1)} %dynamic-slice_bitcast_fusion.refs_6_), channel_id=1, source_target_pairs={{0,1},{1,0},{2,3},{3,2},{4,5},{5,4},{6,7},{7,6},{8,9},{9,8},{10,11... | collective-permute-start | bytes 4718600 | tf_op jit(solution)/shard_map/ppermute | solution.py:37
  36.9 14.1 %copy-start.32 = (s32[1,256,4,2]{1,3,2,0:T(2,128)S(1)}, s32[1,256,4,2]{1,3,2,0:T(2,128)}, u32[]{:S(2)}) copy-start(s32[1,256,4,2]{1,3,2,0:T(2,128)} %param.22) | copy-start | bytes 24580
  36.9 43.6 %collective-permute-start.5 = (bf16[768,1024]{1,0:T(8,128)(2,1)}, bf16[768,1024]{1,0:T(8,128)(2,1)}, u32[]{:S(2)}, u32[]{:S(2)}) collective-permute-start(bf16[768,1024]{1,0:T(8,128)(2,1)} %dynamic-slice_bitcast_fusion.1.refs_5_), channel_id=1, source_target_pairs={{0,1},{1,0},{2,3},{3,2},{4,5},{5,4},{6,7},{7,6},{8,9},{9,8},{10,11... | collective-permute-start | bytes 4718600 | tf_op jit(solution)/shard_map/ppermute | solution.py:37
  39.7 40.8 %collective-permute-start.4 = (bf16[768,1024]{1,0:T(8,128)(2,1)}, bf16[768,1024]{1,0:T(8,128)(2,1)}, u32[]{:S(2)}, u32[]{:S(2)}) collective-permute-start(bf16[768,1024]{1,0:T(8,128)(2,1)} %dynamic-slice_bitcast_fusion.2.refs_4_), channel_id=1, source_target_pairs={{0,1},{1,0},{2,3},{3,2},{4,5},{5,4},{6,7},{7,6},{8,9},{9,8},{10,11... | collective-permute-start | bytes 4718600 | tf_op jit(solution)/shard_map/ppermute | solution.py:37
  80.5 56.6 %all-to-all-start.1 = ((bf16[16,80,896]{2,1,0:T(8,128)(2,1)}), bf16[16,80,896]{2,1,0:T(8,128)(2,1)}, u32[]{:S(2)}, u32[]{:S(2)}) async-start(bf16[16,80,896]{2,1,0:T(8,128)(2,1)} %dispatch_early.1), calls=%async_computation.1 | async-start | bytes 4587520 | tf_op jit(solution)/shard_map/all_to_all | solution.py:1144
  90.9 4.6 collective-permute-start.7
  96.9 50.8 %copy-start.33 = (f32[768]{0:T(1024)S(1)}, f32[768]{0:T(1024)}, u32[]{:S(2)}) copy-start(f32[768]{0:T(1024)} %param.28) | copy-start | bytes 9220
  137.1 29.5 %all-to-all-start.2 = ((bf16[16,3,64,128]{3,2,1,0:T(8,128)(2,1)}), bf16[16,3,64,128]{3,2,1,0:T(8,128)(2,1)S(1)}, u32[]{:S(2)}, u32[]{:S(2)}) async-start(bf16[16,3,64,128]{3,2,1,0:T(8,128)(2,1)} %get-tuple-element.127), calls=%async_computation.2 | async-start | bytes 1572864 | tf_op jit(solution)/shard_map/all_to_all | solution.py:1147
  171.7 2.5 collective-permute-start.8
  180.2 46.1 %all-to-all-start.3 = ((bf16[16,80,768]{2,1,0:T(8,128)(2,1)}), bf16[16,80,768]{2,1,0:T(8,128)(2,1)S(1)}, u32[]{:S(2)}, u32[]{:S(2)}) async-start(bf16[16,80,768]{2,1,0:T(8,128)(2,1)} %dispatch.1), calls=%async_computation.3 | async-start | bytes 3932160 | tf_op jit(solution)/shard_map/all_to_all | solution.py:1155
  185.2 163.3 %reduce-scatter.7.cloned.1.call-start = ((), (), s32[]{:S(2)}) async-start(), calls=%async_computation.15 | async-start | bytes 5898240 | tf_op jit(solution)/shard_map/reduce_scatter | solution.py:1027
  209.7 15.3 %collective-permute-start.9 = (f32[512,1536]{1,0:T(8,128)S(1)}, f32[512,1536]{1,0:T(8,128)}, u32[]{:S(2)}, u32[]{:S(2)}) collective-permute-start(f32[512,1536]{1,0:T(8,128)S(1)} %get-tuple-element.274), channel_id=1, source_target_pairs={{0,1},{1,0},{2,3},{3,2},{4,5},{5,4},{6,7},{7,6},{8,9},{9,8},{10,11... | collective-permute-start | bytes 9437192 | tf_op jit(solution)/shard_map/ppermute | solution.py:1162
  264.5 84.0 %all-to-all-start.4 = ((bf16[16,80,1536]{2,1,0:T(8,128)(2,1)}), bf16[16,80,1536]{2,1,0:T(8,128)(2,1)}, u32[]{:S(2)}, u32[]{:S(2)}) async-start(bf16[16,80,1536]{2,1,0:T(8,128)(2,1)} %bitcast.138), calls=%async_computation.4 | async-start | bytes 7864320 | tf_op jit(solution)/shard_map/all_to_all | solution.py:1178
  274.0 118.6 %reduce-scatter.9.cloned.1.call-start = ((), (), s32[]{:S(2)}) async-start(), calls=%async_computation.16 | async-start | bytes 1474560 | tf_op jit(solution)/shard_map/reduce_scatter | solution.py:1032
  274.1 12.5 %copy-start.8 = (f32[512,1536]{1,0:T(8,128)S(1)}, f32[512,1536]{1,0:T(8,128)}, u32[]{:S(2)}) copy-start(f32[512,1536]{1,0:T(8,128)} %get-tuple-element.152) | copy-start | bytes 9437188
  286.5 16.4 %collective-permute-start.10 = (bf16[768,3072]{1,0:T(8,128)(2,1)}, bf16[768,3072]{1,0:T(8,128)(2,1)S(1)}, u32[]{:S(2)}, u32[]{:S(2)}) collective-permute-start(bf16[768,3072]{1,0:T(8,128)(2,1)} %expert_grads.2), channel_id=1, source_target_pairs={{0,1},{1,0},{2,3},{3,2},{4,5},{5,4},{6,7},{7,6},{8,9},{9,8},{10,11... | collective-permute-start | bytes 14155784 | tf_op jit(solution)/shard_map/ppermute | solution.py:1184
  348.5 8.1 %collective-permute-start.11 = (bf16[1280,1536]{1,0:T(8,128)(2,1)}, bf16[1280,1536]{1,0:T(8,128)(2,1)}, u32[]{:S(2)}, u32[]{:S(2)}) collective-permute-start(bf16[1280,1536]{1,0:T(8,128)(2,1)} %bitcast.42.home_ref), channel_id=1, source_target_pairs={{0,1},{1,0},{2,3},{3,2},{4,5},{5,4},{6,7},{7,6},{8,9},{9,8},{10,11... | collective-permute-start | bytes 11796488 | tf_op jit(solution)/shard_map/ppermute | solution.py:37
  356.6 30.0 %copy-start.38 = (bf16[4,128,768]{2,1,0:T(8,128)(2,1)S(1)}, bf16[4,128,768]{2,1,0:T(8,128)(2,1)}, u32[]{:S(2)}) copy-start(bf16[4,128,768]{2,1,0:T(8,128)(2,1)} %get-tuple-element.160) | copy-start | bytes 2359300
  369.6 19.1 %copy-start.7 = (bf16[4,128,768]{2,1,0:T(8,128)(2,1)S(1)}, bf16[4,128,768]{2,1,0:T(8,128)(2,1)}, u32[]{:S(2)}) copy-start(bf16[4,128,768]{2,1,0:T(8,128)(2,1)} %get-tuple-element.128.second_ref) | copy-start | bytes 2359300
  369.6 19.1 %copy-start.26 = (bf16[4,128,16]{2,1,0:T(8,128)(2,1)S(1)}, bf16[4,128,16]{2,1,0:T(8,128)(2,1)}, u32[]{:S(2)}) copy-start(bf16[4,128,16]{2,1,0:T(8,128)(2,1)} %get-tuple-element.162) | copy-start | bytes 49156
  369.6 19.3 %copy-start.31 = (f32[1,768]{1,0:T(1,128)S(1)}, f32[1,768]{1,0:T(1,128)}, u32[]{:S(2)}) copy-start(f32[1,768]{1,0:T(1,128)} %get-tuple-element.161) | copy-start | bytes 9220
  369.6 37.1 %all-to-all-start.5 = ((bf16[16,3,64,128]{3,2,1,0:T(8,128)(2,1)}), bf16[16,3,64,128]{3,2,1,0:T(8,128)(2,1)S(1)}, u32[]{:S(2)}, u32[]{:S(2)}) async-start(bf16[16,3,64,128]{3,2,1,0:T(8,128)(2,1)} %get-tuple-element.158), calls=%async_computation.6 | async-start | bytes 1572864 | tf_op jit(solution)/shard_map/all_to_all | solution.py:1214
  388.4 2.2 collective-permute-start.12
  389.0 1.6 collective-permute-start.13
  407.6 52.6 %all-to-all-start.6 = ((bf16[16,48,1536]{2,1,0:T(8,128)(2,1)}), bf16[16,48,1536]{2,1,0:T(8,128)(2,1)S(1)}, u32[]{:S(2)}, u32[]{:S(2)}) async-start(bf16[16,48,1536]{2,1,0:T(8,128)(2,1)} %get-tuple-element.175), calls=%async_computation.8 | async-start | bytes 4718592 | tf_op jit(solution)/shard_map/all_to_all | solution.py:1240
  413.1 44.0 %reduce-scatter.11.cloned.1.call-start = ((), (), s32[]{:S(2)}) async-start(), calls=%async_computation.17 | async-start | bytes 983040 | tf_op jit(solution)/shard_map/reduce_scatter | solution.py:1027
  460.3 3.6 collective-permute-start.15
  468.0 61.5 %all-to-all-start.7 = ((bf16[16,9,64,128]{3,2,1,0:T(8,128)(2,1)}), bf16[16,9,64,128]{3,2,1,0:T(8,128)(2,1)S(1)}, u32[]{:S(2)}, u32[]{:S(2)}) async-start(bf16[16,9,64,128]{3,2,1,0:T(8,128)(2,1)} %pad_maximum_fusion), calls=%async_computation.10 | async-start | bytes 4718592 | tf_op jit(solution)/shard_map/all_to_all | solution.py:1247
  478.8 32.8 %reduce-scatter.13.cloned.1.call-start = ((), (), s32[]{:S(2)}) async-start(), calls=%async_computation.18 | async-start | bytes 245760 | tf_op jit(solution)/shard_map/reduce_scatter | solution.py:1032
  479.3 131.3 %reduce-scatter.15.cloned.1.call-start = ((), (), s32[]{:S(2)}) async-start(), calls=%async_computation.19 | async-start | bytes 2211840 | tf_op jit(solution)/shard_map/reduce_scatter | solution.py:1027
  535.8 5.5 collective-permute-start.22
  544.8 11.9 %copy-start.23 = (bf16[4,128,768]{2,1,0:T(8,128)(2,1)S(1)}, bf16[4,128,768]{2,1,0:T(8,128)(2,1)}, u32[]{:S(2)}) copy-start(bf16[4,128,768]{2,1,0:T(8,128)(2,1)} %get-tuple-element.167) | copy-start | bytes 2359300
  544.8 12.1 %copy-start.25 = (bf16[48,3072]{1,0:T(8,128)(2,1)S(1)}, bf16[48,3072]{1,0:T(8,128)(2,1)}, u32[]{:S(2)}) copy-start(bf16[48,3072]{1,0:T(8,128)(2,1)} %reduce-scatter.9.cloned.1.call-done) | copy-start | bytes 884740
  544.8 78.7 %all-to-all-start.8 = ((bf16[16,48,1536]{2,1,0:T(8,128)(2,1)}), bf16[16,48,1536]{2,1,0:T(8,128)(2,1)}, u32[]{:S(2)}, u32[]{:S(2)}) async-start(bf16[16,48,1536]{2,1,0:T(8,128)(2,1)} %get-tuple-element.194), calls=%async_computation.14 | async-start | bytes 4718592 | tf_op jit(solution)/shard_map/all_to_all | solution.py:1249
  556.6 77.5 %reduce-scatter.17.cloned.1.call-start = ((), (), s32[]{:S(2)}) async-start(), calls=%async_computation.20 | async-start | bytes 552960 | tf_op jit(solution)/shard_map/reduce_scatter | solution.py:1032
  556.6 12.4 %collective-permute-start.14 = (bf16[4,128,768]{2,1,0:T(8,128)(2,1)S(1)}, bf16[4,128,768]{2,1,0:T(8,128)(2,1)S(1)}, u32[]{:S(2)}, u32[]{:S(2)}) collective-permute-start(bf16[4,128,768]{2,1,0:T(8,128)(2,1)S(1)} %copy-done.23), channel_id=1, source_target_pairs={{0,1},{1,0},{2,3},{3,2},{4,5},{5,4},{6,7},{7,6},{8,9},{9,8},{10,11... | collective-permute-start | bytes 2359304 | tf_op jit(solution)/shard_map/ppermute | solution.py:37
  565.2 1.4 collective-permute-start.17
  567.2 5.3 collective-permute-start.18
  572.4 47.7 %collective-permute-start.16 = (bf16[4,128,768]{2,1,0:T(8,128)(2,1)S(1)}, bf16[4,128,768]{2,1,0:T(8,128)(2,1)S(1)}, u32[]{:S(2)}, u32[]{:S(2)}) collective-permute-start(bf16[4,128,768]{2,1,0:T(8,128)(2,1)S(1)} %copy-done.24), channel_id=1, source_target_pairs={{0,1},{1,0},{2,3},{3,2},{4,5},{5,4},{6,7},{7,6},{8,9},{9,8},{10,11... | collective-permute-start | bytes 2359304 | tf_op jit(solution)/shard_map/ppermute | solution.py:37
  572.6 38.8 %collective-permute-start.19 = (f32[1,768]{1,0:T(1,128)S(1)}, f32[1,768]{1,0:T(1,128)S(1)}, u32[]{:S(2)}, u32[]{:S(2)}) collective-permute-start(f32[1,768]{1,0:T(1,128)S(1)} %add.285), channel_id=1, source_target_pairs={{0,4},{2,6},{4,0},{6,2},{8,12},{10,14},{12,8},{14,10},{16,20},{18,... | collective-permute-start | bytes 9224 | tf_op jit(solution)/shard_map/ppermute | solution.py:62
  611.4 3.7 collective-permute-start.20
  615.0 4.5 collective-permute-start.21
  621.1 14.4 %copy-start.1 = (bf16[1,256,4,768]{3,2,1,0:T(4,128)(2,1)S(1)}, bf16[1,256,4,768]{3,2,1,0:T(4,128)(2,1)}, u32[]{:S(2)}) copy-start(bf16[1,256,4,768]{3,2,1,0:T(4,128)(2,1)} %param.18) | copy-start | bytes 4718596
  (30 other events, 98.2 us)
Sparse Core Ops, SparseCore 0:
  226.5 89.8 reduce-scatter.6
  348.7 40.5 reduce-scatter.8
  416.9 38.0 reduce-scatter.10
  481.5 29.9 reduce-scatter.12
  544.9 65.7 reduce-scatter.14
  612.9 21.0 reduce-scatter.16

commit v6 on v5

--- a/solution.py
+++ b/solution.py
@@ -456,8 +456,7 @@
         ),
         out_shape=[jax.ShapeDtypeStruct((members, units, chunk, LANES), BF)]
         + [
-            jax.ShapeDtypeStruct((members, 2 * units, chunk, LANES), BF if k else F4)
-            for k in range(size)
+            jax.ShapeDtypeStruct((members, 2 * units, chunk, LANES), BF) for k in range(size)
         ],
         compiler_params=params(1),
         name="attend_back",
@@ -557,7 +556,7 @@
         [msg, cosine, sine, a1_turned],
         [
             jax.ShapeDtypeStruct((seqs, rows, 3 * inner), BF),
-            jax.ShapeDtypeStruct((width, 3 * inner), BF if k else F4),
+            jax.ShapeDtypeStruct((width, 3 * inner), BF),
         ],
     )
 
@@ -1242,7 +1241,7 @@
     dq, *dkv = attend_back(inv, unit_lengths, w_arg, blocks, do_got, kept, stats, units)
     dq, dkv, expert_got, out_near = lax.optimization_barrier((dq, dkv, expert_got, out_near))
     out_sum = far_scatter(out_near)
-    dkv = wt_scatter(dkv).astype(BF)
+    dkv = wt_scatter([dkv[0].astype(F4), *dkv[1:]]).astype(BF)
     grad_msg = jnp.concatenate([dkv, dq], axis=1)
     grad_got = lax.all_to_all(grad_msg, "ctx", 0, 0, tiled=True)
     grad_got, out_sum, expert_sum = lax.optimization_barrier((grad_got, out_sum, expert_sum))

time: 653 us -> 653 us (level)
  Pallas kernels: 240 us -> 227 us
  waiting for transfers between devices: 189 us -> 200 us
    pallas_call x1, Pallas kernels: 43.2 us -> 34.9 us  [attend_back(): pl.pallas_call(functools.partial(attend_back_kernel, members, size), grid...]
    reduce_scatter x3, waiting for transfers between devices: 35.9 us -> 42.5 us  [near_scatter(): lax.psum_scatter(array, 'ctx', scatter_dimension=0, tiled=True, axis_inde...]
  transfers between devices with their start and end apart: 38 -> 38, of which waited for: 17 -> 18; matrix products, arithmetic and copies ran while one was open for 12% -> 12% of each run, Pallas kernels for 34% -> 32%
where the time goes in v6:
time: 653 us; the launch traced here: 641 us
  Pallas kernels  227 us (35%)
  waiting for transfers between devices  200 us (31%)
  starting transfers between devices  98.6 us (15%)
  local copies, waits for them, and re-layouts  67.4 us (10%)
  other arithmetic  29.5 us (5%)
  between operations  15.7 us (2%)
    pallas_call x2, Pallas kernels, gated(): pl.pallas_call(functools.partial(gated_kernel, count, tiles, bool(routed)...  55 us
    reduce_scatter x3, waiting for transfers between devices, near_scatter(): lax.psum_scatter(array, 'ctx', scatter_dimension=0, tiled=True, axis_inde...  42.5 us
    all_to_all x1, waiting for transfers between devices, per_device(): home = swap(returned.reshape(experts, held, 2 * width))  38.4 us
    pallas_call x3, Pallas kernels, gated_grads(): pl.pallas_call(gated_grads_kernel, grid=(tiles,), in_specs=[whole(x.shape...  35.2 us
    reduce_scatter x3, waiting for transfers between devices, far_scatter(): lax.psum_scatter(array, 'ctx', scatter_dimension=0, tiled=True, axis_inde...  35.1 us
    pallas_call x1, Pallas kernels, attend_back(): pl.pallas_call(functools.partial(attend_back_kernel, members, size), grid...  34.9 us
    pallas_call x6, Pallas kernels, one_step(): pl.pallas_call(kernel, grid=(1,), in_specs=[SMEM] + [whole(array.shape) f...  33.7 us
    pallas_call x1, Pallas kernels, attend(): pl.pallas_call(functools.partial(attend_kernel, members, size), grid_spec...  29.4 us
  transfers between devices with their start and end apart: 38, of which 18 were waited for; matrix products, arithmetic and copies ran while one was open for 12% of the time, Pallas kernels for 32%

profile of v6, /device:TPU:0, one launch (start us, length us, event | category | flops | bytes accessed | tf_op | source)
XLA Modules:
  0.0 641.1 jit_solution(16933702003493725531)
XLA Ops:
  15.7 7.2 %project.1 = (bf16[16,9,64,128]{3,2,1,0:T(8,128)(2,1)}, bf16[4,128,768]{2,1,0:T(8,128)(2,1)}) custom-call(s32[1]{0:T(128)} %bitcast.shift_ref, bf16[4,128,768]{2,1,0:T(8,128)(2,1)} %bitcast.127, f32[1,768]{1,0:T(1,128)} %broadcast_in_dim.91.gain_ref, f32[128,128]{1,0:T(8,128)} %get-tuple-element.108.cos_ref, f32[128,128]{1,0:T(8,128)} %get-tuple-element.109.sin_ref, ...), custom_call_target="tpu_custom_call" | custom-call | tf_op jit(solution)/shard_map/project/pallas_call | solution.py:149
  22.9 8.1 %all-to-all-start = ((bf16[16,9,64,128]{3,2,1,0:T(8,128)(2,1)}), bf16[16,9,64,128]{3,2,1,0:T(8,128)(2,1)S(1)}, u32[]{:S(2)}, u32[]{:S(2)}) async-start(bf16[16,9,64,128]{3,2,1,0:T(8,128)(2,1)} %get-tuple-element.111), calls=%async_computation | async-start | bytes 4718592 | tf_op jit(solution)/shard_map/all_to_all | solution.py:1014
  31.2 2.7 dynamic-slice_bitcast_fusion.refs_6_
  37.0 2.7 dynamic-slice_bitcast_fusion.2.refs_4_
  64.8 5.7 turn.1
  74.9 5.6 dispatch_early.1
  80.5 10.3 %all-to-all-start.1 = ((bf16[16,80,896]{2,1,0:T(8,128)(2,1)}), bf16[16,80,896]{2,1,0:T(8,128)(2,1)}, u32[]{:S(2)}, u32[]{:S(2)}) async-start(bf16[16,80,896]{2,1,0:T(8,128)(2,1)} %dispatch_early.1), calls=%async_computation.1 | async-start | bytes 4587520 | tf_op jit(solution)/shard_map/all_to_all | solution.py:1143
  90.9 4.5 collective-permute-done.7.refs_1_
  96.9 29.4 %attend.1 = (bf16[16,3,64,128]{3,2,1,0:T(8,128)(2,1)}, f32[3,4,64,512]{3,2,1,0:T(8,128)}, f32[3,4,2,512]{3,2,1,0:T(2,128)}) custom-call(s32[16]{0:T(128)} %get-tuple-element.122.inv_ref, s32[3]{0:T(128)} %gather_fusion, s32[1]{0:T(128)} %bitcast.31.w_ref, bf16[16,9,64,128]{3,2,1,0:T(8,128)(2,1)} %copy-done.5, bf16[16,9,64,128]{3,2,1,0:T(8,128)(2,1)} %copy-done.10), custom_call_target="tpu_custom_call" | custom-call | tf_op jit(solution)/shard_map/attend/pallas_call | solution.py:310
  126.3 10.8 %all-to-all-done.1 = bf16[16,80,896]{2,1,0:T(8,128)(2,1)} async-done(((bf16[16,80,896]{2,1,0:T(8,128)(2,1)}), bf16[16,80,896]{2,1,0:T(8,128)(2,1)}, u32[]{:S(2)}, u32[]{:S(2)}) %all-to-all-start.1) | async-done | bytes 2293792 | tf_op jit(solution)/shard_map/all_to_all | solution.py:1143
  137.1 10.5 %all-to-all-start.2 = ((bf16[16,3,64,128]{3,2,1,0:T(8,128)(2,1)}), bf16[16,3,64,128]{3,2,1,0:T(8,128)(2,1)S(1)}, u32[]{:S(2)}, u32[]{:S(2)}) async-start(bf16[16,3,64,128]{3,2,1,0:T(8,128)(2,1)} %get-tuple-element.127), calls=%async_computation.2 | async-start | bytes 1572864 | tf_op jit(solution)/shard_map/all_to_all | solution.py:1146
  148.2 18.4 %all-to-all-done.2.o_ref = bf16[16,3,64,128]{3,2,1,0:T(8,128)(2,1)S(1)} async-done(((bf16[16,3,64,128]{3,2,1,0:T(8,128)(2,1)}), bf16[16,3,64,128]{3,2,1,0:T(8,128)(2,1)S(1)}, u32[]{:S(2)}, u32[]{:S(2)}) %all-to-all-start.2) | async-done | bytes 786464 | tf_op jit(solution)/shard_map/all_to_all | solution.py:1146
  167.5 4.2 mix.1
  175.1 5.1 dispatch.1
  180.2 5.0 all-to-all-start.3
  187.6 18.1 %dense_branch.1 = (f32[1024,1536]{1,0:T(8,128)}, bf16[1024,3072]{1,0:T(8,128)(2,1)}) custom-call(bf16[1024,768]{1,0:T(8,128)(2,1)} %pad_maximum_fusion.1.cot_ref.refs_0_.d_ref, bf16[1024,768]{1,0:T(8,128)(2,1)} %copy-done.12, bf16[768,1024]{1,0:T(8,128)(2,1)} %refs_2_.5, bf16[768,1024]{1,0:T(8,128)(2,1)} %refs_3_.3, bf16[1024,768]{1,0:T(8,128)(2,1)} %refs_4_.3), custom_call_target="tpu_custom_call" | custom-call | tf_op jit(solution)/shard_map/dense_branch/pallas_call | solution.py:887
  205.7 5.0 fusion.20
  210.7 10.4 %dense_grads.1 = bf16[768,3072]{1,0:T(8,128)(2,1)} custom-call(bf16[1024,768]{1,0:T(8,128)(2,1)} %copy-done.12, bf16[1024,768]{1,0:T(8,128)(2,1)} %pad_maximum_fusion.1.cot_ref.refs_0_.d_ref, bf16[1024,3072]{1,0:T(8,128)(2,1)} %get-tuple-element.140.hid_ref), custom_call_target="tpu_custom_call" | custom-call | flops 4831838208 | bytes 14155776 | tf_op jit(solution)/shard_map/dense_grads/pallas_call | solution.py:921
  221.1 4.9 copy.126
  227.6 36.8 %expert_branch.1 = (bf16[1280,768]{1,0:T(8,128)(2,1)}, bf16[1280,1536]{1,0:T(8,128)(2,1)}, bf16[1280,6144]{1,0:T(8,128)(2,1)}) custom-call(s32[1]{0:T(128)} %bitcast.33.refs_0_, bf16[768,128]{1,0:T(8,128)(2,1)} %pad.4.refs_1_.refs_0_, bf16[1280,896]{1,0:T(8,128)(2,1)} %bitcast.34.refs_2_, bf16[1280,768]{1,0:T(8,128)(2,1)} %bitcast.118, ...), custom_call_target="tpu_custom_call" | custom-call | tf_op jit(solution)/shard_map/expert_branch/pallas_call | solution.py:887
  264.5 9.5 %all-to-all-start.4 = ((bf16[16,80,1536]{2,1,0:T(8,128)(2,1)}), bf16[16,80,1536]{2,1,0:T(8,128)(2,1)}, u32[]{:S(2)}, u32[]{:S(2)}) async-start(bf16[16,80,1536]{2,1,0:T(8,128)(2,1)} %bitcast.138), calls=%async_computation.4 | async-start | bytes 7864320 | tf_op jit(solution)/shard_map/all_to_all | solution.py:1177
  274.1 12.4 %expert_grads.2 = bf16[768,3072]{1,0:T(8,128)(2,1)} custom-call(bf16[1280,768]{1,0:T(8,128)(2,1)} %bitcast.119, bf16[1280,768]{1,0:T(8,128)(2,1)} %get-tuple-element.149.d_ref, bf16[1280,6144]{1,0:T(8,128)(2,1)} %get-tuple-element.150.hid_ref), custom_call_target="tpu_custom_call" | custom-call | flops 6039797760 | bytes 16515072 | tf_op jit(solution)/shard_map/expert_grads/pallas_call | solution.py:921
  286.5 4.1 add.278
  290.6 12.3 %expert_grads.3 = bf16[768,3072]{1,0:T(8,128)(2,1)} custom-call(bf16[1280,768]{1,0:T(8,128)(2,1)} %bitcast.120, bf16[1280,768]{1,0:T(8,128)(2,1)} %get-tuple-element.149.d_ref, bf16[1280,6144]{1,0:T(8,128)(2,1)} %get-tuple-element.150.hid_ref), custom_call_target="tpu_custom_call" | custom-call | flops 6039797760 | bytes 16515072 | tf_op jit(solution)/shard_map/expert_grads/pallas_call | solution.py:921
  303.0 4.3 add_convert_fusion
  307.2 2.9 fusion.21
  310.1 38.4 %all-to-all-done.4 = bf16[16,80,1536]{2,1,0:T(8,128)(2,1)} async-done(((bf16[16,80,1536]{2,1,0:T(8,128)(2,1)}), bf16[16,80,1536]{2,1,0:T(8,128)(2,1)}, u32[]{:S(2)}, u32[]{:S(2)}) %all-to-all-start.4) | async-done | bytes 3932192 | tf_op jit(solution)/shard_map/all_to_all | solution.py:1177
  349.4 7.2 %first_part.1.refs_3_ = f32[4,128,2304]{2,1,0:T(8,128)} custom-call(s32[4,128,6]{2,1,0:T(8,128)} %copy.128.info_ref, bf16[1280,1536]{1,0:T(8,128)(2,1)} %bitcast.42.home_ref), custom_call_target="tpu_custom_call" | custom-call | tf_op jit(solution)/shard_map/first_part/pallas_call | solution.py:672
  356.6 13.0 %finish.1 = (bf16[4,128,768]{2,1,0:T(8,128)(2,1)}, f32[4,128,768]{2,1,0:T(8,128)}, bf16[4,128,768]{2,1,0:T(8,128)(2,1)}, bf16[4,128,16]{2,1,0:T(8,128)(2,1)}, bf...) custom-call(s32[1]{0:T(128)} %bitcast.shift_ref, s32[4,128,6]{2,1,0:T(8,128)} %copy.128.info_ref, ...), custom_call_target="tpu_custom_call" | custom-call | tf_op jit(solution)/shard_map/finish/pallas_call | solution.py:759
  369.6 17.0 %all-to-all-start.5 = ((bf16[16,3,64,128]{3,2,1,0:T(8,128)(2,1)}), bf16[16,3,64,128]{3,2,1,0:T(8,128)(2,1)S(1)}, u32[]{:S(2)}, u32[]{:S(2)}) async-start(bf16[16,3,64,128]{3,2,1,0:T(8,128)(2,1)} %get-tuple-element.158), calls=%async_computation.6 | async-start | bytes 1572864 | tf_op jit(solution)/shard_map/all_to_all | solution.py:1213
  392.6 14.1 %all-to-all-done.5.refs_2_ = bf16[16,3,64,128]{3,2,1,0:T(8,128)(2,1)S(1)} async-done(((bf16[16,3,64,128]{3,2,1,0:T(8,128)(2,1)}), bf16[16,3,64,128]{3,2,1,0:T(8,128)(2,1)S(1)}, u32[]{:S(2)}, u32[]{:S(2)}) %all-to-all-start.5) | async-done | bytes 786464 | tf_op jit(solution)/shard_map/all_to_all | solution.py:1213
  407.6 5.4 all-to-all-start.6
  413.8 34.9 %attend_back.1 = (bf16[16,3,64,128]{3,2,1,0:T(8,128)(2,1)}, bf16[16,6,64,128]{3,2,1,0:T(8,128)(2,1)}, bf16[16,6,64,128]{3,2,1,0:T(8,128)(2,1)}) custom-call(s32[16]{0:T(128)} %get-tuple-element.122.inv_ref, s32[3]{0:T(128)} %gather_fusion, s32[1]{0:T(128)} %bitcast.31.w_ref, bf16[16,9,64,128]{3,2,1,0:T(8,128)(2,1)} %copy-done.5, ...), custom_call_target="tpu_custom_call" | custom-call | tf_op jit(solution)/shard_map/attend_back/pallas_call | solution.py:436
  448.7 6.7 %reduce-scatter.11.cloned.1.call-done = bf16[192,512]{1,0:T(8,128)(2,1)} async-done(((bf16[768,512]{1,0:T(8,128)(2,1)}), bf16[192,512]{1,0:T(8,128)(2,1)}) %reduce-scatter.11.cloned.1.call-update) | async-done | bytes 196624 | tf_op jit(solution)/shard_map/reduce_scatter | solution.py:1026
  455.4 4.7 all-to-all-done.6.refs_0_
  460.1 3.6 collective-permute-done.15
  467.5 10.8 %all-to-all-start.7 = ((bf16[16,9,64,128]{3,2,1,0:T(8,128)(2,1)}), bf16[16,9,64,128]{3,2,1,0:T(8,128)(2,1)S(1)}, u32[]{:S(2)}, u32[]{:S(2)}) async-start(bf16[16,9,64,128]{3,2,1,0:T(8,128)(2,1)} %pad_maximum_fusion), calls=%async_computation.10 | async-start | bytes 4718592 | tf_op jit(solution)/shard_map/all_to_all | solution.py:1246
  479.1 32.0 %reduce-scatter.13.cloned.1.call-done = bf16[48,512]{1,0:T(8,128)(2,1)} async-done(((bf16[192,512]{1,0:T(8,128)(2,1)}), bf16[48,512]{1,0:T(8,128)(2,1)}) %reduce-scatter.13.cloned.1.call-update) | async-done | bytes 49168 | tf_op jit(solution)/shard_map/reduce_scatter | solution.py:1031
  511.0 17.9 %all-to-all-done.7.msg_ref = bf16[16,9,64,128]{3,2,1,0:T(8,128)(2,1)S(1)} async-done(((bf16[16,9,64,128]{3,2,1,0:T(8,128)(2,1)}), bf16[16,9,64,128]{3,2,1,0:T(8,128)(2,1)S(1)}, u32[]{:S(2)}, u32[]{:S(2)}) %all-to-all-start.7) | async-done | bytes 2359328 | tf_op jit(solution)/shard_map/all_to_all | solution.py:1246
  530.4 4.9 unrotate.3
  535.3 4.9 unrotate.2
  540.2 3.1 add_convert_fusion.1
  543.3 11.8 %all-to-all-start.8 = ((bf16[16,48,1536]{2,1,0:T(8,128)(2,1)}), bf16[16,48,1536]{2,1,0:T(8,128)(2,1)}, u32[]{:S(2)}, u32[]{:S(2)}) async-start(bf16[16,48,1536]{2,1,0:T(8,128)(2,1)} %get-tuple-element.194), calls=%async_computation.14 | async-start | bytes 4718592 | tf_op jit(solution)/shard_map/all_to_all | solution.py:1248
  556.9 6.8 %unproject.1 = (bf16[4,128,768]{2,1,0:T(8,128)(2,1)}, f32[1,768]{1,0:T(1,128)}) custom-call(s32[1]{0:T(128)} %bitcast.shift_ref, bf16[4,128,768]{2,1,0:T(8,128)(2,1)} %bitcast.129, f32[4,128,768]{2,1,0:T(8,128)} %get-tuple-element.168.dstate_ref, f32[1,768]{1,0:T(1,128)} %broadcast_in_dim.91.gain_ref, bf16[4,128,1152]{2,1,0:T(8,128)(2,1)} %get-tuple-element.184.refs_0_, ...), custom_call_target="tpu_custom_call" | custom-call | tf_op jit(solution)/shard_map/unproject/pallas_call | solution.py:149
  573.3 35.9 %reduce-scatter.15.cloned.1.call-done = bf16[192,1152]{1,0:T(8,128)(2,1)} async-done(((bf16[768,1152]{1,0:T(8,128)(2,1)}), bf16[192,1152]{1,0:T(8,128)(2,1)}) %reduce-scatter.15.cloned.1.call-update) | async-done | bytes 442384 | tf_op jit(solution)/shard_map/reduce_scatter | solution.py:1026
  610.0 3.5 collective-permute-done.20
  622.0 7.5 %place.1 = (f32[16,48,1024]{2,1,0:T(8,128)}, f32[16,48,1024]{2,1,0:T(8,128)}, f32[16,48,1024]{2,1,0:T(8,128)}) custom-call(bf16[16,48,1536]{2,1,0:T(8,128)(2,1)} %copy-done.9, bf16[16,48,1536]{2,1,0:T(8,128)(2,1)} %all-to-all-done.8.refs_1_), custom_call_target="tpu_custom_call" | custom-call | tf_op jit(solution)/shard_map/place/pallas_call | solution.py:799
  629.5 3.1 reduce-scatter.17.cloned.1.call-done
  (234 shorter events, 87.2 us)
Async XLA Ops:
  7.2 7.3 %collective-permute-start = (bf16[768,384]{1,0:T(8,128)(2,1)}, bf16[768,384]{1,0:T(8,128)(2,1)S(1)}, u32[]{:S(2)}, u32[]{:S(2)}) collective-permute-start(bf16[768,384]{1,0:T(8,128)(2,1)} %refs_1_.3), channel_id=1, source_target_pairs={{0,1},{1,0},{2,3},{3,2},{4,5},{5,4},{6,7},{7,6},{8,9},{9,8},{10,11... | collective-permute-start | bytes 1769480 | tf_op jit(solution)/shard_map/ppermute | solution.py:37
  7.7 6.8 %collective-permute-start.1 = (bf16[768,384]{1,0:T(8,128)(2,1)}, bf16[768,384]{1,0:T(8,128)(2,1)S(1)}, u32[]{:S(2)}, u32[]{:S(2)}) collective-permute-start(bf16[768,384]{1,0:T(8,128)(2,1)} %refs_2_.4), channel_id=1, source_target_pairs={{0,1},{1,0},{2,3},{3,2},{4,5},{5,4},{6,7},{7,6},{8,9},{9,8},{10,11... | collective-permute-start | bytes 1769480 | tf_op jit(solution)/shard_map/ppermute | solution.py:37
  7.8 6.7 %collective-permute-start.2 = (bf16[768,384]{1,0:T(8,128)(2,1)}, bf16[768,384]{1,0:T(8,128)(2,1)S(1)}, u32[]{:S(2)}, u32[]{:S(2)}) collective-permute-start(bf16[768,384]{1,0:T(8,128)(2,1)} %refs_3_.2), channel_id=1, source_target_pairs={{0,1},{1,0},{2,3},{3,2},{4,5},{5,4},{6,7},{7,6},{8,9},{9,8},{10,11... | collective-permute-start | bytes 1769480 | tf_op jit(solution)/shard_map/ppermute | solution.py:37
  22.9 57.6 %all-to-all-start = ((bf16[16,9,64,128]{3,2,1,0:T(8,128)(2,1)}), bf16[16,9,64,128]{3,2,1,0:T(8,128)(2,1)S(1)}, u32[]{:S(2)}, u32[]{:S(2)}) async-start(bf16[16,9,64,128]{3,2,1,0:T(8,128)(2,1)} %get-tuple-element.111), calls=%async_computation | async-start | bytes 4718592 | tf_op jit(solution)/shard_map/all_to_all | solution.py:1014
  31.0 33.0 %collective-permute-start.3 = (bf16[384,768]{1,0:T(8,128)(2,1)S(1)}, bf16[384,768]{1,0:T(8,128)(2,1)S(1)}, u32[]{:S(2)}, u32[]{:S(2)}) collective-permute-start(bf16[384,768]{1,0:T(8,128)(2,1)S(1)} %copy-done.20), channel_id=1, source_target_pairs={{0,1},{1,0},{2,3},{3,2},{4,5},{5,4},{6,7},{7,6},{8,9},{9,8},{10,11... | collective-permute-start | bytes 1769480 | tf_op jit(solution)/shard_map/ppermute | solution.py:37
  33.9 46.6 %collective-permute-start.6 = (bf16[1024,768]{1,0:T(8,128)(2,1)}, bf16[1024,768]{1,0:T(8,128)(2,1)}, u32[]{:S(2)}, u32[]{:S(2)}) collective-permute-start(bf16[1024,768]{1,0:T(8,128)(2,1)} %dynamic-slice_bitcast_fusion.refs_6_), channel_id=1, source_target_pairs={{0,1},{1,0},{2,3},{3,2},{4,5},{5,4},{6,7},{7,6},{8,9},{9,8},{10,11... | collective-permute-start | bytes 4718600 | tf_op jit(solution)/shard_map/ppermute | solution.py:37
  36.9 14.1 %copy-start.32 = (s32[1,256,4,2]{1,3,2,0:T(2,128)S(1)}, s32[1,256,4,2]{1,3,2,0:T(2,128)}, u32[]{:S(2)}) copy-start(s32[1,256,4,2]{1,3,2,0:T(2,128)} %param.22) | copy-start | bytes 24580
  36.9 43.6 %collective-permute-start.5 = (bf16[768,1024]{1,0:T(8,128)(2,1)}, bf16[768,1024]{1,0:T(8,128)(2,1)}, u32[]{:S(2)}, u32[]{:S(2)}) collective-permute-start(bf16[768,1024]{1,0:T(8,128)(2,1)} %dynamic-slice_bitcast_fusion.1.refs_5_), channel_id=1, source_target_pairs={{0,1},{1,0},{2,3},{3,2},{4,5},{5,4},{6,7},{7,6},{8,9},{9,8},{10,11... | collective-permute-start | bytes 4718600 | tf_op jit(solution)/shard_map/ppermute | solution.py:37
  39.7 40.8 %collective-permute-start.4 = (bf16[768,1024]{1,0:T(8,128)(2,1)}, bf16[768,1024]{1,0:T(8,128)(2,1)}, u32[]{:S(2)}, u32[]{:S(2)}) collective-permute-start(bf16[768,1024]{1,0:T(8,128)(2,1)} %dynamic-slice_bitcast_fusion.2.refs_4_), channel_id=1, source_target_pairs={{0,1},{1,0},{2,3},{3,2},{4,5},{5,4},{6,7},{7,6},{8,9},{9,8},{10,11... | collective-permute-start | bytes 4718600 | tf_op jit(solution)/shard_map/ppermute | solution.py:37
  80.5 10.3 %copy-start.5 = (bf16[16,9,64,128]{3,2,1,0:T(8,128)(2,1)}, bf16[16,9,64,128]{3,2,1,0:T(8,128)(2,1)S(1)}, u32[]{:S(2)}) copy-start(bf16[16,9,64,128]{3,2,1,0:T(8,128)(2,1)S(1)} %all-to-all-done.refs_0_) | copy-start | bytes 7077892
  80.5 56.6 %all-to-all-start.1 = ((bf16[16,80,896]{2,1,0:T(8,128)(2,1)}), bf16[16,80,896]{2,1,0:T(8,128)(2,1)}, u32[]{:S(2)}, u32[]{:S(2)}) async-start(bf16[16,80,896]{2,1,0:T(8,128)(2,1)} %dispatch_early.1), calls=%async_computation.1 | async-start | bytes 4587520 | tf_op jit(solution)/shard_map/all_to_all | solution.py:1143
  90.9 4.6 collective-permute-start.7
  96.9 50.8 %copy-start.33 = (f32[768]{0:T(1024)S(1)}, f32[768]{0:T(1024)}, u32[]{:S(2)}) copy-start(f32[768]{0:T(1024)} %param.28) | copy-start | bytes 9220
  137.1 29.5 %all-to-all-start.2 = ((bf16[16,3,64,128]{3,2,1,0:T(8,128)(2,1)}), bf16[16,3,64,128]{3,2,1,0:T(8,128)(2,1)S(1)}, u32[]{:S(2)}, u32[]{:S(2)}) async-start(bf16[16,3,64,128]{3,2,1,0:T(8,128)(2,1)} %get-tuple-element.127), calls=%async_computation.2 | async-start | bytes 1572864 | tf_op jit(solution)/shard_map/all_to_all | solution.py:1146
  171.7 2.5 collective-permute-start.8
  180.2 46.1 %all-to-all-start.3 = ((bf16[16,80,768]{2,1,0:T(8,128)(2,1)}), bf16[16,80,768]{2,1,0:T(8,128)(2,1)S(1)}, u32[]{:S(2)}, u32[]{:S(2)}) async-start(bf16[16,80,768]{2,1,0:T(8,128)(2,1)} %dispatch.1), calls=%async_computation.3 | async-start | bytes 3932160 | tf_op jit(solution)/shard_map/all_to_all | solution.py:1154
  185.2 163.3 %reduce-scatter.7.cloned.1.call-start = ((), (), s32[]{:S(2)}) async-start(), calls=%async_computation.15 | async-start | bytes 5898240 | tf_op jit(solution)/shard_map/reduce_scatter | solution.py:1026
  210.7 15.3 %collective-permute-start.9 = (f32[512,1536]{1,0:T(8,128)S(1)}, f32[512,1536]{1,0:T(8,128)}, u32[]{:S(2)}, u32[]{:S(2)}) collective-permute-start(f32[512,1536]{1,0:T(8,128)S(1)} %get-tuple-element.274), channel_id=1, source_target_pairs={{0,1},{1,0},{2,3},{3,2},{4,5},{5,4},{6,7},{7,6},{8,9},{9,8},{10,11... | collective-permute-start | bytes 9437192 | tf_op jit(solution)/shard_map/ppermute | solution.py:1161
  264.5 84.1 %all-to-all-start.4 = ((bf16[16,80,1536]{2,1,0:T(8,128)(2,1)}), bf16[16,80,1536]{2,1,0:T(8,128)(2,1)}, u32[]{:S(2)}, u32[]{:S(2)}) async-start(bf16[16,80,1536]{2,1,0:T(8,128)(2,1)} %bitcast.138), calls=%async_computation.4 | async-start | bytes 7864320 | tf_op jit(solution)/shard_map/all_to_all | solution.py:1177
  274.0 118.6 %reduce-scatter.9.cloned.1.call-start = ((), (), s32[]{:S(2)}) async-start(), calls=%async_computation.16 | async-start | bytes 1474560 | tf_op jit(solution)/shard_map/reduce_scatter | solution.py:1031
  274.1 12.5 %copy-start.8 = (f32[512,1536]{1,0:T(8,128)S(1)}, f32[512,1536]{1,0:T(8,128)}, u32[]{:S(2)}) copy-start(f32[512,1536]{1,0:T(8,128)} %get-tuple-element.152) | copy-start | bytes 9437188
  286.5 16.4 %collective-permute-start.10 = (bf16[768,3072]{1,0:T(8,128)(2,1)}, bf16[768,3072]{1,0:T(8,128)(2,1)S(1)}, u32[]{:S(2)}, u32[]{:S(2)}) collective-permute-start(bf16[768,3072]{1,0:T(8,128)(2,1)} %expert_grads.2), channel_id=1, source_target_pairs={{0,1},{1,0},{2,3},{3,2},{4,5},{5,4},{6,7},{7,6},{8,9},{9,8},{10,11... | collective-permute-start | bytes 14155784 | tf_op jit(solution)/shard_map/ppermute | solution.py:1183
  348.5 8.1 %collective-permute-start.11 = (bf16[1280,1536]{1,0:T(8,128)(2,1)}, bf16[1280,1536]{1,0:T(8,128)(2,1)}, u32[]{:S(2)}, u32[]{:S(2)}) collective-permute-start(bf16[1280,1536]{1,0:T(8,128)(2,1)} %bitcast.42.home_ref), channel_id=1, source_target_pairs={{0,1},{1,0},{2,3},{3,2},{4,5},{5,4},{6,7},{7,6},{8,9},{9,8},{10,11... | collective-permute-start | bytes 11796488 | tf_op jit(solution)/shard_map/ppermute | solution.py:37
  356.6 30.1 %copy-start.38 = (bf16[4,128,768]{2,1,0:T(8,128)(2,1)S(1)}, bf16[4,128,768]{2,1,0:T(8,128)(2,1)}, u32[]{:S(2)}) copy-start(bf16[4,128,768]{2,1,0:T(8,128)(2,1)} %get-tuple-element.160) | copy-start | bytes 2359300
  369.6 19.1 %copy-start.7 = (bf16[4,128,768]{2,1,0:T(8,128)(2,1)S(1)}, bf16[4,128,768]{2,1,0:T(8,128)(2,1)}, u32[]{:S(2)}) copy-start(bf16[4,128,768]{2,1,0:T(8,128)(2,1)} %get-tuple-element.128.second_ref) | copy-start | bytes 2359300
  369.6 19.1 %copy-start.26 = (bf16[4,128,16]{2,1,0:T(8,128)(2,1)S(1)}, bf16[4,128,16]{2,1,0:T(8,128)(2,1)}, u32[]{:S(2)}) copy-start(bf16[4,128,16]{2,1,0:T(8,128)(2,1)} %get-tuple-element.162) | copy-start | bytes 49156
  369.6 37.1 %all-to-all-start.5 = ((bf16[16,3,64,128]{3,2,1,0:T(8,128)(2,1)}), bf16[16,3,64,128]{3,2,1,0:T(8,128)(2,1)S(1)}, u32[]{:S(2)}, u32[]{:S(2)}) async-start(bf16[16,3,64,128]{3,2,1,0:T(8,128)(2,1)} %get-tuple-element.158), calls=%async_computation.6 | async-start | bytes 1572864 | tf_op jit(solution)/shard_map/all_to_all | solution.py:1213
  388.4 2.2 collective-permute-start.12
  389.0 1.6 collective-permute-start.13
  407.6 52.5 %all-to-all-start.6 = ((bf16[16,48,1536]{2,1,0:T(8,128)(2,1)}), bf16[16,48,1536]{2,1,0:T(8,128)(2,1)S(1)}, u32[]{:S(2)}, u32[]{:S(2)}) async-start(bf16[16,48,1536]{2,1,0:T(8,128)(2,1)} %get-tuple-element.175), calls=%async_computation.8 | async-start | bytes 4718592 | tf_op jit(solution)/shard_map/all_to_all | solution.py:1239
  413.1 42.3 %reduce-scatter.11.cloned.1.call-start = ((), (), s32[]{:S(2)}) async-start(), calls=%async_computation.17 | async-start | bytes 983040 | tf_op jit(solution)/shard_map/reduce_scatter | solution.py:1026
  460.1 3.6 collective-permute-start.15
  467.5 61.5 %all-to-all-start.7 = ((bf16[16,9,64,128]{3,2,1,0:T(8,128)(2,1)}), bf16[16,9,64,128]{3,2,1,0:T(8,128)(2,1)S(1)}, u32[]{:S(2)}, u32[]{:S(2)}) async-start(bf16[16,9,64,128]{3,2,1,0:T(8,128)(2,1)} %pad_maximum_fusion), calls=%async_computation.10 | async-start | bytes 4718592 | tf_op jit(solution)/shard_map/all_to_all | solution.py:1246
  478.3 32.8 %reduce-scatter.13.cloned.1.call-start = ((), (), s32[]{:S(2)}) async-start(), calls=%async_computation.18 | async-start | bytes 245760 | tf_op jit(solution)/shard_map/reduce_scatter | solution.py:1031
  478.8 130.3 %reduce-scatter.15.cloned.1.call-start = ((), (), s32[]{:S(2)}) async-start(), calls=%async_computation.19 | async-start | bytes 2211840 | tf_op jit(solution)/shard_map/reduce_scatter | solution.py:1026
  535.3 4.9 collective-permute-start.22
  543.3 11.9 %copy-start.23 = (bf16[4,128,768]{2,1,0:T(8,128)(2,1)S(1)}, bf16[4,128,768]{2,1,0:T(8,128)(2,1)}, u32[]{:S(2)}) copy-start(bf16[4,128,768]{2,1,0:T(8,128)(2,1)} %get-tuple-element.167) | copy-start | bytes 2359300
  543.3 12.2 %copy-start.25 = (bf16[48,3072]{1,0:T(8,128)(2,1)S(1)}, bf16[48,3072]{1,0:T(8,128)(2,1)}, u32[]{:S(2)}) copy-start(bf16[48,3072]{1,0:T(8,128)(2,1)} %reduce-scatter.9.cloned.1.call-done) | copy-start | bytes 884740
  543.3 78.7 %all-to-all-start.8 = ((bf16[16,48,1536]{2,1,0:T(8,128)(2,1)}), bf16[16,48,1536]{2,1,0:T(8,128)(2,1)}, u32[]{:S(2)}, u32[]{:S(2)}) async-start(bf16[16,48,1536]{2,1,0:T(8,128)(2,1)} %get-tuple-element.194), calls=%async_computation.14 | async-start | bytes 4718592 | tf_op jit(solution)/shard_map/all_to_all | solution.py:1248
  555.1 77.5 %reduce-scatter.17.cloned.1.call-start = ((), (), s32[]{:S(2)}) async-start(), calls=%async_computation.20 | async-start | bytes 552960 | tf_op jit(solution)/shard_map/reduce_scatter | solution.py:1031
  555.2 12.4 %collective-permute-start.14 = (bf16[4,128,768]{2,1,0:T(8,128)(2,1)S(1)}, bf16[4,128,768]{2,1,0:T(8,128)(2,1)S(1)}, u32[]{:S(2)}, u32[]{:S(2)}) collective-permute-start(bf16[4,128,768]{2,1,0:T(8,128)(2,1)S(1)} %copy-done.23), channel_id=1, source_target_pairs={{0,1},{1,0},{2,3},{3,2},{4,5},{5,4},{6,7},{7,6},{8,9},{9,8},{10,11... | collective-permute-start | bytes 2359304 | tf_op jit(solution)/shard_map/ppermute | solution.py:37
  563.7 1.4 collective-permute-start.17
  565.7 5.3 collective-permute-start.18
  570.9 47.7 %collective-permute-start.16 = (bf16[4,128,768]{2,1,0:T(8,128)(2,1)S(1)}, bf16[4,128,768]{2,1,0:T(8,128)(2,1)S(1)}, u32[]{:S(2)}, u32[]{:S(2)}) collective-permute-start(bf16[4,128,768]{2,1,0:T(8,128)(2,1)S(1)} %copy-done.24), channel_id=1, source_target_pairs={{0,1},{1,0},{2,3},{3,2},{4,5},{5,4},{6,7},{7,6},{8,9},{9,8},{10,11... | collective-permute-start | bytes 2359304 | tf_op jit(solution)/shard_map/ppermute | solution.py:37
  571.1 38.8 %collective-permute-start.19 = (f32[1,768]{1,0:T(1,128)S(1)}, f32[1,768]{1,0:T(1,128)S(1)}, u32[]{:S(2)}, u32[]{:S(2)}) collective-permute-start(f32[1,768]{1,0:T(1,128)S(1)} %add.285), channel_id=1, source_target_pairs={{0,4},{2,6},{4,0},{6,2},{8,12},{10,14},{12,8},{14,10},{16,20},{18,... | collective-permute-start | bytes 9224 | tf_op jit(solution)/shard_map/ppermute | solution.py:62
  609.8 3.7 collective-permute-start.20
  613.5 4.5 collective-permute-start.21
  619.6 14.5 %copy-start.1 = (bf16[1,256,4,768]{3,2,1,0:T(4,128)(2,1)S(1)}, bf16[1,256,4,768]{3,2,1,0:T(4,128)(2,1)}, u32[]{:S(2)}) copy-start(bf16[1,256,4,768]{3,2,1,0:T(4,128)(2,1)} %param.18) | copy-start | bytes 4718596
  (30 other events, 84.7 us)
Sparse Core Ops, SparseCore 0:
  226.5 89.8 reduce-scatter.6
  348.7 40.5 reduce-scatter.8
  416.8 38.5 reduce-scatter.10
  481.0 29.9 reduce-scatter.12
  543.4 65.7 reduce-scatter.14
  611.4 21.1 reduce-scatter.16
